TPU v7x, 32 devices: a whole 2x2x4 slice. The times are simulated.
32 devices in a mesh: wide: 8 (over y, x, core), narrow: 4 (over z).
Axes of the slice: x: 2, y: 2, z: 4, core: 2. Of those that a mesh axis runs over, the one named last changes fastest.
Arguments:
- covariates: bfloat16 [65536, 128], P(('wide', 'narrow')), may hold values from -6 to 6
- level_codes: int32 [65536], P(('wide', 'narrow')), may hold values from 0 to 3
- sign_bits: int32 [65536], P(('wide', 'narrow')), may hold values from 0 to 1
- sample_rows: int32 [1024], P(('wide', 'narrow')), may hold values from 0 to 2047, as said below
- effects: float32 [512], replicated, may hold values from -6 to 6
- noise: float32 [65536], P(('wide', 'narrow')), may hold values from -8 to 8
Outputs:
- coefficients: float32 [512], replicated
- residual: float32 [65536], P(('wide', 'narrow'))
- factor: float32 [512, 512], replicated
Inputs may be any that keep to these rules, and one draw needn't show every extreme that they name: `sample_rows`: a local row offset on the device that owns the entry.
All inputs are finite; a program needn't handle non-finite values.
Results may differ from a plain program's by a relative error of at most 0.0006.
The roundings to bfloat16 on the way count: a program that leaves them out, or rounds other values in their place, can miss the bound.
Values may be sent and summed in bfloat16 or wider, within the bound.
No kernel may reach another device: no remote copies, remote signals or barrier semaphores. Data moves between devices by JAX's collectives and lax.ppermute only.
A program may use at most 64 MiB of HBM per device.

v0:
```python
import math

import jax
import jax.numpy as jnp
from jax import lax
from jax.sharding import PartitionSpec as P

COV = 128
LEVELS = 4
HB = 256
SKETCH = 1024
ITERS = 4


half_root = math.sqrt(0.5)


def partner(value, axis, apart):
    mask = 2**apart
    pairs = [(source, source ^ mask) for source in range(lax.axis_size(axis))]
    return lax.ppermute(value, axis, pairs)


def hadamard(size):
    left = jnp.arange(size, dtype=jnp.int32)[:, None]
    right = jnp.arange(size, dtype=jnp.int32)[None, :]
    common = jnp.bitwise_and(left, right)
    parity = jnp.zeros((size, size), jnp.int32)
    for place in range(size.bit_length()):
        parity = parity + jnp.bitwise_and(jnp.right_shift(common, place), 1)
    return (1 - 2 * (parity % 2)).astype(jnp.bfloat16)


def tri_solve(lower, vector, transpose):
    return lax.linalg.triangular_solve(
        lower, vector[:, None], left_side=True, lower=True, transpose_a=transpose
    )[:, 0]


def combine_pair(own, theirs, upper):
    own_wide = own.astype(jnp.float32)
    their_wide = theirs.astype(jnp.float32)
    low = jnp.where(upper, their_wide, own_wide)
    high = jnp.where(upper, own_wide, their_wide)
    return (jnp.where(upper, low - high, low + high) * half_root).astype(jnp.bfloat16)


def body(covariates, level_codes, sign_bits, sample_rows, effects, noise):
    rows_dev = covariates.shape[0]
    cols = LEVELS * COV
    onehot = (level_codes[:, None] == jnp.arange(LEVELS, dtype=jnp.int32)[None, :]).astype(
        jnp.float32
    )
    flipped = covariates * (1 - 2 * sign_bits).astype(jnp.bfloat16)[:, None]
    design = (onehot.astype(jnp.bfloat16)[:, :, None] * flipped[:, None, :]).reshape(
        rows_dev // HB, HB, cols
    )
    local = jnp.einsum("ij,gjc->gic", hadamard(HB), design, preferred_element_type=jnp.float32)
    local = (local * (1.0 / math.sqrt(HB))).astype(jnp.bfloat16).reshape(rows_dev, cols)
    wide_index = lax.axis_index("wide")
    mixed = local
    for place in range(3):
        upper = jnp.bitwise_and(jnp.right_shift(wide_index, place), 1) == 1
        theirs = partner(mixed, "wide", place)
        mixed = combine_pair(mixed, theirs, upper)
    sketch = mixed[sample_rows]
    gram = lax.psum(
        jnp.dot(sketch.T, sketch, preferred_element_type=jnp.float32), ("wide", "narrow")
    )
    lower = jnp.linalg.cholesky(gram)
    factor = lower.T * math.sqrt(LEVELS / SKETCH)
    wide_cov = covariates.astype(jnp.float32)

    def apply_design(vector):
        values = jnp.dot(wide_cov, vector.reshape(LEVELS, COV).T, precision=lax.Precision.HIGHEST)
        return jnp.sum(values * onehot, axis=1)

    def adjoint(vector):
        return jnp.dot(
            (onehot * vector[:, None]).T, wide_cov, precision=lax.Precision.HIGHEST
        ).reshape(cols)

    resid = apply_design(effects) + noise
    gradient_now = lax.psum(adjoint(resid), ("wide", "narrow"))
    steer = tri_solve(lower, gradient_now, False)
    direction = steer
    gamma = jnp.sum(steer * steer)
    solved = jnp.zeros((cols,), jnp.float32)
    for step in range(ITERS):
        image = apply_design(tri_solve(lower, direction, True))
        alpha = gamma / lax.psum(jnp.sum(image * image), ("wide", "narrow"))
        solved = solved + alpha * direction
        resid = resid - alpha * image
        gradient_now = lax.psum(adjoint(resid), ("wide", "narrow"))
        steer = tri_solve(lower, gradient_now, False)
        gamma_new = jnp.sum(steer * steer)
        direction = steer + gamma_new / gamma * direction
        gamma = gamma_new
    return (tri_solve(lower, solved, True), resid, factor)


def solution(mesh):
    return jax.shard_map(
        body,
        mesh=mesh,
        in_specs=(
            P(("wide", "narrow"), None),
            P(("wide", "narrow")),
            P(("wide", "narrow")),
            P(("wide", "narrow")),
            P(),
            P(("wide", "narrow")),
        ),
        out_specs=(P(), P(("wide", "narrow")), P()),
        check_vma=False,
    )
```

profile of v0, /device:TPU:0, one launch (start us, length us, event | category | flops | bytes accessed | tf_op | source)
XLA Modules:
  0.0 731.1 jit_solution(9117715083500408387)
XLA Ops:
  7.2 0.7 convert_convert_fusion
  8.3 0.7 subtract_convert_fusion
  9.0 1.4 broadcast_multiply_fusion.1
  10.4 7.2 broadcast_multiply_fusion
  17.6 2.2 mul.220
  19.8 2.6 multiply_convert_fusion.3
  22.9 3.9 collective-permute-done
  26.8 4.1 multiply_convert_fusion.2
  31.0 2.9 collective-permute-start.1
  33.8 46.2 %collective-permute-done.1 = bf16[2048,512]{1,0:T(8,128)(2,1)} collective-permute-done((bf16[2048,512]{1,0:T(8,128)(2,1)}, bf16[2048,512]{1,0:T(8,128)(2,1)}, u32[]{:S(2)}, u32[]{:S(2)}) %collective-permute-start.1) | collective-permute-done | bytes 2097184 | tf_op jit(solution)/shard_map/ppermute | solution.py:21
  80.1 3.4 multiply_convert_fusion.1
  83.5 1.8 collective-permute-start.2
  85.3 45.5 %collective-permute-done.2 = bf16[2048,512]{1,0:T(8,128)(2,1)} collective-permute-done((bf16[2048,512]{1,0:T(8,128)(2,1)S(1)}, bf16[2048,512]{1,0:T(8,128)(2,1)}, u32[]{:S(2)}, u32[]{:S(2)}) %collective-permute-start.2) | collective-permute-done | bytes 2097184 | tf_op jit(solution)/shard_map/ppermute | solution.py:21
  130.8 4.1 multiply_convert_fusion
  134.9 2.5 gather_fusion
  137.4 1.3 fusion.225
  139.7 41.2 %psum.64 = f32[512,1]{0,1:T(1,128)S(1)} all-reduce(f32[512,1]{0,1:T(1,128)S(1)} %bitcast.533), channel_id=1, replica_groups=mesh['wide'=8,'narrow'=4] {'wide','narrow'}, use_global_device_ids=true, to_apply=%region_10.11 | all-reduce | flops 512 | bytes 4096 | tf_op jit(solution)/shard_map/psum | solution.py:84
  180.8 89.3 %all-reduce.3.cloned.1.call-done = f32[512,512]{0,1:T(8,128)} async-done(((f32[512,512]{0,1:T(8,128)}), f32[512,512]{0,1:T(8,128)}) %all-reduce.3.cloned.1.call-update) | async-done | bytes 1048592 | tf_op jit(solution)/shard_map/psum | solution.py:67
  270.2 1.6 copy.11
  271.8 1.2 fusion.36
  273.0 0.8 cholesky.266
  273.9 11.7 %cholesky.104 = f32[128,128]{1,0:T(8,128)S(1)} custom-call(f32[128,128]{1,0:T(8,128)S(1)} %cholesky.266), custom_call_target="Cholesky" | custom-call | tf_op jit(solution)/shard_map/jit(cholesky)/cholesky | solution.py:70
  285.6 9.8 %custom-call.33 = f32[1,128,128]{1,2,0:T(8,128)S(1)} custom-call(f32[1,128,128]{2,1,0:T(8,128)S(1)} %get-tuple-element.104), custom_call_target="InvertDiagBlocksLowerTriangular" | custom-call | tf_op jit(solution)/shard_map/jit(cholesky)/cholesky | solution.py:70
  295.5 1.2 constant_dynamic-update-slice_fusion.3
  296.8 1.3 convolution_subtract_fusion
  298.1 11.7 %cholesky.217 = f32[128,128]{1,0:T(8,128)S(1)} custom-call(f32[128,128]{1,0:T(8,128)S(1)} %cholesky.270), custom_call_target="Cholesky" | custom-call | tf_op jit(solution)/shard_map/jit(cholesky)/cholesky | solution.py:70
  309.8 10.0 %custom-call.34 = f32[1,128,128]{1,2,0:T(8,128)S(1)} custom-call(f32[1,128,128]{2,1,0:T(8,128)S(1)} %get-tuple-element.101), custom_call_target="InvertDiagBlocksLowerTriangular" | custom-call | tf_op jit(solution)/shard_map/jit(cholesky)/cholesky | solution.py:70
  320.1 1.3 convolution_subtract_fusion.1
  321.4 11.7 %cholesky.238 = f32[128,128]{1,0:T(8,128)S(1)} custom-call(f32[128,128]{1,0:T(8,128)S(1)} %cholesky.275), custom_call_target="Cholesky" | custom-call | tf_op jit(solution)/shard_map/jit(cholesky)/cholesky | solution.py:70
  333.1 0.7 compare_reduce_fusion.1
  333.8 9.8 %custom-call.35 = f32[1,128,128]{1,2,0:T(8,128)S(1)} custom-call(f32[1,128,128]{2,1,0:T(8,128)S(1)} %get-tuple-element.98), custom_call_target="InvertDiagBlocksLowerTriangular" | custom-call | tf_op jit(solution)/shard_map/jit(cholesky)/cholesky | solution.py:70
  343.9 1.2 convolution_subtract_fusion.2
  345.1 11.7 %cholesky.255 = f32[128,128]{1,0:T(8,128)S(1)} custom-call(f32[128,128]{1,0:T(8,128)S(1)} %convolution_subtract_fusion.2), custom_call_target="Cholesky" | custom-call | tf_op jit(solution)/shard_map/jit(cholesky)/cholesky | solution.py:70
  356.8 0.6 compare_reduce_fusion
  357.5 0.6 compare_reduce_fusion.2
  360.7 1.3 multiply_bitcast_fusion
  362.0 8.5 %while.18 = (s32[]{:T(128)}, f32[512,512]{1,0:T(8,128)S(1)}, s32[4,2]{0,1:T(2,128)S(1)}, f32[4,128,128]{2,1,0:T(8,128)S(1)}, s32[]{:T(128)}) while((s32[]{:T(128)}, f32[512,512]{1,0:T(8,128)S(1)}, s32[4,2]{0,1:T(2,128)S(1)}, f32[4,128,128]{2,1,0:T(8,128)S(1)}, s32[]{:T(128)}) %tuple.65), condition=%wide.while_cond.1.clone.3, body=%wide.while_body.1.clone.3.sunk | while | flops 2 | bytes 131181 | solution.py:35
  362.1 0.6 fusion.281
  362.7 1.4 bitcast_dynamic-update-slice_fusion.2
  364.2 0.6 fusion.281
  364.8 1.4 bitcast_dynamic-update-slice_fusion.2
  366.3 0.6 fusion.281
  366.9 1.4 bitcast_dynamic-update-slice_fusion.2
  368.4 0.6 fusion.281
  369.0 1.4 bitcast_dynamic-update-slice_fusion.2
  370.5 39.3 %custom-call.51 = f32[4,128,128]{1,2,0:T(8,128)S(1)} custom-call(f32[4,128,128]{2,1,0:T(8,128)S(1)} %get-tuple-element.71), custom_call_target="InvertDiagBlocksLowerTriangular" | custom-call | tf_op jit(solution)/shard_map/triangular_solve/custom-call.8 | solution.py:35
  413.3 0.6 multiply_reduce_fusion.3
  413.9 0.6 multiply_reduce_fusion.7
  414.5 39.4 %psum.65 = f32[]{:T(128)} all-reduce(f32[]{:T(128)} %multiply_reduce_fusion.3), channel_id=1, replica_groups=mesh['wide'=8,'narrow'=4] {'wide','narrow'}, use_global_device_ids=true, to_apply=%region_14.17 | all-reduce | flops 1 | bytes 8 | tf_op jit(solution)/shard_map/psum | solution.py:91
  455.5 40.2 %psum.66 = f32[512,1]{0,1:T(1,128)S(1)} all-reduce(f32[512,1]{0,1:T(1,128)S(1)} %bitcast.534), channel_id=1, replica_groups=mesh['wide'=8,'narrow'=4] {'wide','narrow'}, use_global_device_ids=true, to_apply=%region_15.18 | all-reduce | flops 512 | bytes 4096 | tf_op jit(solution)/shard_map/psum | solution.py:94
  497.2 0.6 multiply_reduce_fusion.6
  501.2 0.6 multiply_reduce_fusion.2
  501.8 40.2 %psum.67 = f32[]{:T(128)} all-reduce(f32[]{:T(128)} %multiply_reduce_fusion.2), channel_id=1, replica_groups=mesh['wide'=8,'narrow'=4] {'wide','narrow'}, use_global_device_ids=true, to_apply=%region_19.22 | all-reduce | flops 1 | bytes 8 | tf_op jit(solution)/shard_map/psum | solution.py:91
  543.6 40.2 %psum.68 = f32[512,1]{0,1:T(1,128)S(1)} all-reduce(f32[512,1]{0,1:T(1,128)S(1)} %bitcast.535), channel_id=1, replica_groups=mesh['wide'=8,'narrow'=4] {'wide','narrow'}, use_global_device_ids=true, to_apply=%region_20.23 | all-reduce | flops 512 | bytes 4096 | tf_op jit(solution)/shard_map/psum | solution.py:94
  585.3 0.6 multiply_reduce_fusion.5
  589.3 0.6 multiply_reduce_fusion.1
  589.9 40.2 %psum.69 = f32[]{:T(128)} all-reduce(f32[]{:T(128)} %multiply_reduce_fusion.1), channel_id=1, replica_groups=mesh['wide'=8,'narrow'=4] {'wide','narrow'}, use_global_device_ids=true, to_apply=%region_24.27 | all-reduce | flops 1 | bytes 8 | tf_op jit(solution)/shard_map/psum | solution.py:91
  631.7 40.5 %psum.70 = f32[512,1]{0,1:T(1,128)S(1)} all-reduce(f32[512,1]{0,1:T(1,128)S(1)} %bitcast.536), channel_id=1, replica_groups=mesh['wide'=8,'narrow'=4] {'wide','narrow'}, use_global_device_ids=true, to_apply=%region_25.28 | all-reduce | flops 512 | bytes 4096 | tf_op jit(solution)/shard_map/psum | solution.py:94
  673.7 0.6 multiply_reduce_fusion.4
  677.7 0.6 multiply_reduce_fusion
  678.3 40.1 %psum.71 = f32[]{:T(128)} all-reduce(f32[]{:T(128)} %multiply_reduce_fusion), channel_id=1, replica_groups=mesh['wide'=8,'narrow'=4] {'wide','narrow'}, use_global_device_ids=true, to_apply=%region_29.32 | all-reduce | flops 1 | bytes 8 | tf_op jit(solution)/shard_map/psum | solution.py:91
  719.8 0.6 multiply_subtract_fusion
  720.4 1.3 copy.12
  723.1 0.6 pad_maximum_fusion.8
  (120 shorter events, 19.2 us)
Async XLA Ops:
  7.2 131.6 %copy-start = (f32[512]{0:T(512)S(1)}, f32[512]{0:T(512)}, u32[]{:S(2)}) copy-start(f32[512]{0:T(512)} %param.14) | copy-start | bytes 6148
  7.2 263.0 %all-reduce.3.cloned.1.call-start = ((), (), s32[]{:S(2)}) async-start(), calls=%async_computation | async-start | bytes 2097152 | tf_op jit(solution)/shard_map/psum | solution.py:67
  22.4 4.4 collective-permute-start
  31.0 49.1 %collective-permute-start.1 = (bf16[2048,512]{1,0:T(8,128)(2,1)}, bf16[2048,512]{1,0:T(8,128)(2,1)}, u32[]{:S(2)}, u32[]{:S(2)}) collective-permute-start(bf16[2048,512]{1,0:T(8,128)(2,1)} %multiply_convert_fusion.2), channel_id=1, source_target_pairs={{0,8},{4,12},{8,0},{12,4},{16,24},{20,28},{24,16},{28,20},{1,9},{5... | collective-permute-start | bytes 6291464 | tf_op jit(solution)/shard_map/ppermute | solution.py:21
  33.8 51.5 %copy-start.6 = (s32[32]{0:T(128)S(1)}, s32[32]{0:T(128)}, u32[]{:S(2)}) copy-start(s32[32]{0:T(128)} %param.13) | copy-start | bytes 388
  83.5 47.3 %collective-permute-start.2 = (bf16[2048,512]{1,0:T(8,128)(2,1)S(1)}, bf16[2048,512]{1,0:T(8,128)(2,1)}, u32[]{:S(2)}, u32[]{:S(2)}) collective-permute-start(bf16[2048,512]{1,0:T(8,128)(2,1)S(1)} %multiply_convert_fusion.1), channel_id=1, source_target_pairs={{0,16},{4,20},{8,24},{12,28},{16,0},{20,4},{24,8},{28,12},{1,17},{... | collective-permute-start | bytes 6291464 | tf_op jit(solution)/shard_map/ppermute | solution.py:21
  134.9 3.9 copy-start.1
  134.9 3.9 copy-start.4
  134.9 4.5 copy-start.5
  270.2 1.7 copy-start.2
  584.4 136.0 %copy-start.3 = (f32[512,512]{0,1:T(8,128)S(1)}, f32[512,512]{0,1:T(8,128)}, u32[]{:S(2)}) copy-start(f32[512,512]{0,1:T(8,128)} %get-tuple-element.93) | copy-start | bytes 3145732
Sparse Core Ops, SparseCore 0:
  138.9 131.2 all-reduce.2
where the time goes:
time: 739 us; the launch traced here: 731 us
  blocking collectives  322 us (44%)
  waiting for transfers between devices  185 us (25%)
  other arithmetic  148 us (20%)
  between operations  26.8 us (4%)
  matrix products  26.4 us (4%)
  local copies, waits for them, and re-layouts  17.5 us (2%)
    psum x4, blocking collectives, body(): gradient_now = lax.psum(adjoint(resid), ('wide', 'narrow'))  162 us
    psum x4, blocking collectives, body(): alpha = gamma / lax.psum(jnp.sum(image * image), ('wide', 'narrow'))  160 us
    ppermute x3, waiting for transfers between devices, partner(): return lax.ppermute(value, axis, pairs)  95.6 us
    psum x1, waiting for transfers between devices, body(): lax.psum(jnp.dot(sketch.T, sketch, preferred_element_type=jnp.float32), (...  89.3 us
    another operation x14, other arithmetic, body(): lower = jnp.linalg.cholesky(gram)  78.6 us
    another operation x8, other arithmetic, tri_solve(): lax.linalg.triangular_solve(lower, vector[:, None], left_side=True, lower...  40 us
  transfers between devices with their start and end apart: 4, of which 4 were waited for; matrix products, arithmetic and copies ran while one was open for 0% of the time, Pallas kernels for 0%

commit v1 on v0

v1 whole, which is shorter than its diff:
```python
import math

import jax
import jax.numpy as jnp
from jax import lax
from jax.sharding import PartitionSpec as P

COV = 128
LEVELS = 4
HB = 256
SKETCH = 1024
ITERS = 4
MIX_BITS = 3

half_root = math.sqrt(0.5)
HIGHEST = lax.Precision.HIGHEST


def partner(value, axis, mask):
    pairs = [(source, source ^ mask) for source in range(lax.axis_size(axis))]
    return lax.ppermute(value, axis, pairs)


def rounded(value):
    return lax.reduce_precision(value, 8, 7).astype(jnp.bfloat16)


def hadamard_rows(rows, size):
    common = jnp.bitwise_and(rows[:, None], jnp.arange(size, dtype=jnp.int32)[None, :])
    for shift in (4, 2, 1):
        common = jnp.bitwise_xor(common, jnp.right_shift(common, shift))
    return 1 - 2 * jnp.bitwise_and(common, 1)


def mix(pieces):
    wide_index = lax.axis_index("wide")
    for place in range(MIX_BITS):
        bit = jnp.bitwise_and(jnp.right_shift(wide_index, place), 1)
        sign = (1 - 2 * bit).astype(jnp.float32)
        pieces = [
            rounded((sign * own.astype(jnp.float32) + other.astype(jnp.float32)) * half_root)
            for own, other in zip(pieces[0::2], pieces[1::2])
        ]
    return pieces[0]


def gather_rows(rows):
    wide, narrow = lax.axis_size("wide"), lax.axis_size("narrow")
    samp, cols = rows.shape
    rows = jnp.concatenate([rows] + [partner(rows, "narrow", m) for m in range(1, narrow)])
    rows = jnp.concatenate([rows] + [partner(rows, "wide", m) for m in range(2, wide, 2)])
    rows = jnp.concatenate([rows, partner(rows, "wide", 1)])
    apart_wide = jnp.bitwise_xor(jnp.arange(wide), lax.axis_index("wide"))
    apart_narrow = jnp.bitwise_xor(jnp.arange(narrow), lax.axis_index("narrow"))
    place = jnp.bitwise_and(apart_wide, 1) * (wide // 2) + jnp.right_shift(apart_wide, 1)
    order = (place[:, None] * narrow + apart_narrow[None, :]).reshape(-1)
    return rows.reshape(wide * narrow, samp, cols)[order].reshape(-1, cols)


def body(covariates, level_codes, sign_bits, sample_rows, effects, noise):
    rows_dev = covariates.shape[0]
    samp = sample_rows.shape[0]
    cols = LEVELS * COV
    wide_cov = covariates.astype(jnp.float32)
    onehot = level_codes[:, None] == jnp.arange(LEVELS, dtype=jnp.int32)[None, :]
    design = (onehot.astype(jnp.bfloat16)[:, :, None] * covariates[:, None, :]).reshape(rows_dev, cols)

    wanted = [sample_rows] + [partner(sample_rows, "wide", m) for m in range(1, 2**MIX_BITS)]

    normal = jnp.dot(design.T, covariates, preferred_element_type=jnp.float32)
    back = jnp.dot((onehot.astype(jnp.float32) * noise[:, None]).T, wide_cov, precision=HIGHEST)
    sums = lax.psum(jnp.concatenate([normal, back]), ("wide", "narrow"))

    want = jnp.concatenate(wanted)
    signs = 1 - 2 * sign_bits
    table = hadamard_rows(jnp.bitwise_and(want, HB - 1), HB)
    table = jnp.tile(table, (1, rows_dev // HB)) * signs[None, :]
    block = jnp.arange(rows_dev, dtype=jnp.int32) // HB
    table = jnp.where((want // HB)[:, None] == block[None, :], table, 0).astype(jnp.bfloat16)
    local = jnp.dot(table, design, preferred_element_type=jnp.float32)
    local = rounded(local * (1.0 / math.sqrt(HB)))
    local = [local[m * samp : (m + 1) * samp] for m in range(2**MIX_BITS)]
    pieces = [local[0]] + [partner(local[m], "wide", m) for m in range(1, 2**MIX_BITS)]
    sketch = gather_rows(mix(pieces))

    gram = jnp.dot(sketch.T, sketch, preferred_element_type=jnp.float32)
    lower = jnp.linalg.cholesky(gram)
    factor = lower.T * math.sqrt(LEVELS / SKETCH)
    inverse = lax.linalg.triangular_solve(lower, jnp.eye(cols, dtype=jnp.float32), left_side=True, lower=True)

    normal = sums[:cols].reshape(LEVELS, COV, COV)
    back = sums[cols:]

    def normal_times(vector):
        return jnp.einsum("lij,lj->li", normal, vector.reshape(LEVELS, COV), precision=HIGHEST).reshape(cols)

    def precondition(vector):
        steer = jnp.dot(inverse, vector, precision=HIGHEST)
        return jnp.dot(steer, inverse, precision=HIGHEST), jnp.sum(steer * steer)

    gradient = normal_times(effects) + back.reshape(cols)
    step_to, gamma = precondition(gradient)
    solved = jnp.zeros((cols,), jnp.float32)
    for step in range(ITERS):
        image = normal_times(step_to)
        alpha = gamma / jnp.sum(step_to * image)
        solved = solved + alpha * step_to
        if step == ITERS - 1:
            break
        gradient = gradient - alpha * image
        steer, gamma_new = precondition(gradient)
        step_to = steer + gamma_new / gamma * step_to
        gamma = gamma_new
    left = (effects - solved).reshape(LEVELS, COV)
    values = jnp.dot(wide_cov, left.T, precision=HIGHEST)
    resid = noise + jnp.sum(jnp.where(onehot, values, 0.0), axis=1)
    return (solved, resid, factor)


def solution(mesh):
    return jax.shard_map(
        body,
        mesh=mesh,
        in_specs=(
            P(("wide", "narrow"), None),
            P(("wide", "narrow")),
            P(("wide", "narrow")),
            P(("wide", "narrow")),
            P(),
            P(("wide", "narrow")),
        ),
        out_specs=(P(), P(("wide", "narrow")), P()),
        check_vma=False,
    )
```

time: 739 us -> 351 us (0.47)
  blocking collectives: 322 us -> 0 us
  waiting for transfers between devices: 185 us -> 101 us
  starting transfers between devices: 5.25 us -> 22 us
    psum x8 -> x0, blocking collectives: 322 us -> none  [the longest x4 162 us: body(): gradient_now = lax.psum(adjoint(resid), ('wide', 'narrow'))]
    ppermute x3 -> x21, waiting for transfers between devices: 95.6 us -> 13.1 us  [partner(): return lax.ppermute(value, axis, pairs)]
    ppermute x3 -> x21, starting transfers between devices: 5.21 us -> 22 us  [partner(): return lax.ppermute(value, axis, pairs)]
    convert_element_type x5 -> x3, other arithmetic: 13 us -> 2.85 us  [the longest x1 1.11 us: body(): jnp.eye(cols, dtype=jnp.float32)]
    dot_general x11 -> x18, matrix products: 7.91 us -> 15 us  [the longest x4 4.88 us: precondition(): steer = jnp.dot(inverse, vector, precision=HIGHEST)]
    another operation x8 -> x2, other arithmetic: 40 us -> 40.1 us  [body(): lax.linalg.triangular_solve(lower, jnp.eye(cols, dtype=jnp.float32), left...]
  transfers between devices with their start and end apart: 4 -> 22, of which waited for: 4 -> 11; matrix products, arithmetic and copies ran while one was open for 0% -> 7% of each run, Pallas kernels for 0% -> 0%
where the time goes in v1:
time: 351 us; the launch traced here: 346 us
  other arithmetic  143 us (41%)
  waiting for transfers between devices  101 us (29%)
  matrix products  29.7 us (8%)
  between operations  26.7 us (8%)
  local copies, waits for them, and re-layouts  23.3 us (7%)
  starting transfers between devices  22 us (6%)
    psum x1, waiting for transfers between devices, body(): sums = lax.psum(jnp.concatenate([normal, back]), ('wide', 'narrow'))  87.8 us
    another operation x14, other arithmetic, body(): lower = jnp.linalg.cholesky(gram)  79 us
    another operation x2, other arithmetic, body(): lax.linalg.triangular_solve(lower, jnp.eye(cols, dtype=jnp.float32), left...  40.1 us
    ppermute x21, starting transfers between devices, partner(): return lax.ppermute(value, axis, pairs)  22 us
    another operation x12, local copies, waits for them, and re-layouts  14.2 us
    ppermute x21, waiting for transfers between devices, partner(): return lax.ppermute(value, axis, pairs)  13.1 us
    mul x1, other arithmetic, body(): onehot.astype(jnp.bfloat16)[:, :, None] * covariates[:, None, :]  10.8 us
    another operation x7, matrix products, body(): lax.linalg.triangular_solve(lower, jnp.eye(cols, dtype=jnp.float32), left...  9.3 us
  transfers between devices with their start and end apart: 22, of which 11 were waited for; matrix products, arithmetic and copies ran while one was open for 7% of the time, Pallas kernels for 0%

profile of v1, /device:TPU:0, one launch (start us, length us, event | category | flops | bytes accessed | tf_op | source)
XLA Modules:
  0.0 345.6 jit_solution(10573437228343548254)
XLA Ops:
  7.7 2.6 collective-permute-start.1
  10.4 1.8 collective-permute-start.3
  12.1 0.7 fusion.52
  13.2 1.4 fusion.50
  14.6 10.8 %broadcast_multiply_fusion = bf16[2048,4,128]{2,1,0:T(4,128)(2,1)S(1)} fusion(bf16[2048,128]{1,0:T(8,128)(2,1)} %param.6, bf16[2048,4]{1,0:T(8,128)(2,1)S(1)} %copy.12), kind=kLoop, calls=%fused_computation.31 | loop fusion | flops 1048576 | bytes 2637824 | tf_op jit(solution)/shard_map/mul | solution.py:66
  25.4 0.7 fusion.1
  26.2 0.7 pad_maximum_fusion.1
  26.9 1.1 fusion.27
  28.3 2.7 collective-permute-start.5
  31.1 1.7 collective-permute-done.5
  32.8 2.0 collective-permute-done.6
  35.1 1.0 select_convert_fusion
  36.4 0.7 fusion.13
  37.4 2.6 collective-permute-start.12
  39.9 0.8 iota_compare_fusion
  40.9 1.5 collective-permute-start.10
  42.7 1.5 collective-permute-start.8
  44.3 0.9 collective-permute-done.10
  45.8 1.0 collective-permute-done.8
  46.9 0.7 constant_dynamic-update-slice_fusion.6
  47.6 1.5 collective-permute-start.14
  49.1 2.7 collective-permute-start.15
  52.0 2.7 collective-permute-done.15
  54.7 2.9 collective-permute-done.16
  57.5 1.3 collective-permute-start.17
  59.4 1.7 collective-permute-start.19
  64.5 1.1 collective-permute-done.19
  66.3 87.8 %all-reduce.3.cloned.1.call-done = f32[516,128]{1,0:T(8,128)} async-done(((f32[516,128]{1,0:T(8,128)}), f32[516,128]{1,0:T(8,128)}) %all-reduce.3.cloned.1.call-update) | async-done | bytes 264208 | tf_op jit(solution)/shard_map/psum | solution.py:72
  154.0 1.0 slice.164
  155.5 0.7 slice_add_fusion
  156.9 0.7 convolution_bitcast_fusion.1
  158.2 1.0 copy-done.2
  159.2 11.7 %cholesky.104 = f32[128,128]{1,0:T(8,128)S(1)} custom-call(f32[128,128]{1,0:T(8,128)S(1)} %cholesky.266), custom_call_target="Cholesky" | custom-call | tf_op jit(solution)/shard_map/jit(cholesky)/cholesky | solution.py:87
  171.0 9.8 %custom-call.30 = f32[1,128,128]{1,2,0:T(8,128)S(1)} custom-call(f32[1,128,128]{2,1,0:T(8,128)S(1)} %get-tuple-element.53), custom_call_target="InvertDiagBlocksLowerTriangular" | custom-call | tf_op jit(solution)/shard_map/jit(cholesky)/cholesky | solution.py:87
  180.9 1.2 constant_dynamic-update-slice_fusion.17
  182.1 1.3 convolution_subtract_fusion.3
  183.4 12.1 %cholesky.217 = f32[128,128]{1,0:T(8,128)S(1)} custom-call(f32[128,128]{1,0:T(8,128)S(1)} %cholesky.270), custom_call_target="Cholesky" | custom-call | tf_op jit(solution)/shard_map/jit(cholesky)/cholesky | solution.py:87
  195.5 9.8 %custom-call.31 = f32[1,128,128]{1,2,0:T(8,128)S(1)} custom-call(f32[1,128,128]{2,1,0:T(8,128)S(1)} %get-tuple-element.50), custom_call_target="InvertDiagBlocksLowerTriangular" | custom-call | tf_op jit(solution)/shard_map/jit(cholesky)/cholesky | solution.py:87
  205.6 1.3 convolution_subtract_fusion.4
  206.9 11.7 %cholesky.238 = f32[128,128]{1,0:T(8,128)S(1)} custom-call(f32[128,128]{1,0:T(8,128)S(1)} %cholesky.275), custom_call_target="Cholesky" | custom-call | tf_op jit(solution)/shard_map/jit(cholesky)/cholesky | solution.py:87
  218.7 9.8 %custom-call.32 = f32[1,128,128]{1,2,0:T(8,128)S(1)} custom-call(f32[1,128,128]{2,1,0:T(8,128)S(1)} %get-tuple-element.47), custom_call_target="InvertDiagBlocksLowerTriangular" | custom-call | tf_op jit(solution)/shard_map/jit(cholesky)/cholesky | solution.py:87
  228.7 1.2 convolution_subtract_fusion.5
  229.9 11.9 %cholesky.255 = f32[128,128]{1,0:T(8,128)S(1)} custom-call(f32[128,128]{1,0:T(8,128)S(1)} %convolution_subtract_fusion.5), custom_call_target="Cholesky" | custom-call | tf_op jit(solution)/shard_map/jit(cholesky)/cholesky | solution.py:87
  241.8 0.7 compare_reduce_fusion.1
  246.4 1.2 multiply_bitcast_fusion
  247.7 14.2 %while.1 = (s32[]{:T(128)}, f32[512,512]{1,0:T(8,128)}, s32[4,2]{0,1:T(2,128)S(1)}, f32[4,128,128]{2,1,0:T(8,128)}, s32[]{:T(128)}) while((s32[]{:T(128)}, f32[512,512]{1,0:T(8,128)}, s32[4,2]{0,1:T(2,128)S(1)}, f32[4,128,128]{2,1,0:T(8,128)}, s32[]{:T(128)}) %tuple.48), condition=%wide.while_cond, body=%wide.while_body.sunk | while | flops 2 | bytes 132205 | solution.py:89
  248.3 2.9 bitcast_dynamic-update-slice_fusion.2
  251.9 2.9 bitcast_dynamic-update-slice_fusion.2
  255.5 2.9 bitcast_dynamic-update-slice_fusion.2
  259.0 2.8 bitcast_dynamic-update-slice_fusion.2
  261.9 40.1 %custom-call.33 = f32[4,128,128]{1,2,0:T(8,128)S(1)} custom-call(f32[4,128,128]{2,1,0:T(8,128)} %get-tuple-element.10), custom_call_target="InvertDiagBlocksLowerTriangular" | custom-call | tf_op jit(solution)/shard_map/triangular_solve | solution.py:89
  302.0 1.2 fusion.32
  303.2 1.4 convolution_subtract_fusion.1
  304.6 1.3 fusion.44
  305.8 1.3 convolution_subtract_fusion
  307.2 1.3 fusion.42
  308.5 1.7 convolution_subtract_fusion.2
  310.1 1.3 fusion.41
  311.4 1.0 fusion.76
  316.1 1.9 fusion.75
  318.0 1.6 fusion.64
  324.0 1.0 fusion.74
  330.1 1.0 fusion.73
  337.3 1.3 copy.14
  (125 shorter events, 24.5 us)
Async XLA Ops:
  7.2 146.9 %all-reduce.3.cloned.1.call-start = ((), (), s32[]{:S(2)}) async-start(), calls=%async_computation | async-start | bytes 532480 | tf_op jit(solution)/shard_map/psum | solution.py:72
  7.2 21.0 %collective-permute-start = (s32[32]{0:T(128)}, s32[32]{0:T(128)S(1)}, u32[]{:S(2)}, u32[]{:S(2)}) collective-permute-start(s32[32]{0:T(128)} %param.9), channel_id=1, source_target_pairs={{0,4},{4,0},{8,12},{12,8},{16,20},{20,16},{24,28},{28,24},{1,5},{5... | collective-permute-start | bytes 392 | tf_op jit(solution)/shard_map/ppermute | solution.py:21
  7.7 23.2 %collective-permute-start.1 = (s32[32]{0:T(128)}, s32[32]{0:T(128)S(1)}, u32[]{:S(2)}, u32[]{:S(2)}) collective-permute-start(s32[32]{0:T(128)} %param.9), channel_id=1, source_target_pairs={{0,8},{4,12},{8,0},{12,4},{16,24},{20,28},{24,16},{28,20},{1,9},{5... | collective-permute-start | bytes 392 | tf_op jit(solution)/shard_map/ppermute | solution.py:21
  10.3 20.8 %collective-permute-start.2 = (s32[32]{0:T(128)}, s32[32]{0:T(128)S(1)}, u32[]{:S(2)}, u32[]{:S(2)}) collective-permute-start(s32[32]{0:T(128)} %param.9), channel_id=1, source_target_pairs={{0,12},{4,8},{8,4},{12,0},{16,28},{20,24},{24,20},{28,16},{1,13},{... | collective-permute-start | bytes 392 | tf_op jit(solution)/shard_map/ppermute | solution.py:21
  10.4 20.7 %collective-permute-start.3 = (s32[32]{0:T(128)}, s32[32]{0:T(128)S(1)}, u32[]{:S(2)}, u32[]{:S(2)}) collective-permute-start(s32[32]{0:T(128)} %param.9), channel_id=1, source_target_pairs={{0,16},{4,20},{8,24},{12,28},{16,0},{20,4},{24,8},{28,12},{1,17},{... | collective-permute-start | bytes 392 | tf_op jit(solution)/shard_map/ppermute | solution.py:21
  12.1 19.0 %collective-permute-start.4 = (s32[32]{0:T(128)}, s32[32]{0:T(128)S(1)}, u32[]{:S(2)}, u32[]{:S(2)}) collective-permute-start(s32[32]{0:T(128)} %param.9), channel_id=1, source_target_pairs={{0,20},{4,16},{8,28},{12,24},{16,4},{20,0},{24,12},{28,8},{1,21},{... | collective-permute-start | bytes 392 | tf_op jit(solution)/shard_map/ppermute | solution.py:21
  12.8 12.6 %copy-start = (bf16[2048,128]{1,0:T(8,128)(2,1)S(1)}, bf16[2048,128]{1,0:T(8,128)(2,1)}, u32[]{:S(2)}) copy-start(bf16[2048,128]{1,0:T(8,128)(2,1)} %param.6) | copy-start | bytes 1572868
  25.4 2.6 copy-start.10
  25.4 2.8 copy-start.11
  28.3 4.5 %collective-permute-start.5 = (s32[32]{0:T(128)S(1)}, s32[32]{0:T(128)S(1)}, u32[]{:S(2)}, u32[]{:S(2)}) collective-permute-start(s32[32]{0:T(128)S(1)} %copy-done.11), channel_id=1, source_target_pairs={{0,24},{4,28},{8,16},{12,20},{16,8},{20,12},{24,0},{28,4},{1,25},{... | collective-permute-start | bytes 392 | tf_op jit(solution)/shard_map/ppermute | solution.py:21
  31.0 3.9 %collective-permute-start.6 = (s32[32]{0:T(128)S(1)}, s32[32]{0:T(128)S(1)}, u32[]{:S(2)}, u32[]{:S(2)}) collective-permute-start(s32[32]{0:T(128)S(1)} %copy-done.11), channel_id=1, source_target_pairs={{0,28},{4,24},{8,20},{12,16},{16,12},{20,8},{24,4},{28,0},{1,29},{... | collective-permute-start | bytes 392 | tf_op jit(solution)/shard_map/ppermute | solution.py:21
  37.1 117.9 %copy-start.8 = (f32[512]{0:T(512)S(1)}, f32[512]{0:T(512)}, u32[]{:S(2)}) copy-start(f32[512]{0:T(512)} %param.10) | copy-start | bytes 6148
  37.2 5.6 %collective-permute-start.13 = (bf16[32,512]{1,0:T(8,128)(2,1)S(1)}, bf16[32,512]{1,0:T(8,128)(2,1)S(1)}, u32[]{:S(2)}, u32[]{:S(2)}) collective-permute-start(bf16[32,512]{1,0:T(8,128)(2,1)S(1)} %get-tuple-element.32), channel_id=1, source_target_pairs={{0,28},{4,24},{8,20},{12,16},{16,12},{20,8},{24,4},{28,0},{1,29},{... | collective-permute-start | bytes 98312 | tf_op jit(solution)/shard_map/ppermute | solution.py:21
  37.4 6.8 %collective-permute-start.12 = (bf16[32,512]{1,0:T(8,128)(2,1)S(1)}, bf16[32,512]{1,0:T(8,128)(2,1)S(1)}, u32[]{:S(2)}, u32[]{:S(2)}) collective-permute-start(bf16[32,512]{1,0:T(8,128)(2,1)S(1)} %get-tuple-element.33), channel_id=1, source_target_pairs={{0,24},{4,28},{8,16},{12,20},{16,8},{20,12},{24,0},{28,4},{1,25},{... | collective-permute-start | bytes 98312 | tf_op jit(solution)/shard_map/ppermute | solution.py:21
  40.7 3.6 %collective-permute-start.11 = (bf16[32,512]{1,0:T(8,128)(2,1)S(1)}, bf16[32,512]{1,0:T(8,128)(2,1)S(1)}, u32[]{:S(2)}, u32[]{:S(2)}) collective-permute-start(bf16[32,512]{1,0:T(8,128)(2,1)S(1)} %get-tuple-element.34), channel_id=1, source_target_pairs={{0,20},{4,16},{8,28},{12,24},{16,4},{20,0},{24,12},{28,8},{1,21},{... | collective-permute-start | bytes 98312 | tf_op jit(solution)/shard_map/ppermute | solution.py:21
  40.9 4.3 %collective-permute-start.10 = (bf16[32,512]{1,0:T(8,128)(2,1)S(1)}, bf16[32,512]{1,0:T(8,128)(2,1)S(1)}, u32[]{:S(2)}, u32[]{:S(2)}) collective-permute-start(bf16[32,512]{1,0:T(8,128)(2,1)S(1)} %get-tuple-element.35), channel_id=1, source_target_pairs={{0,16},{4,20},{8,24},{12,28},{16,0},{20,4},{24,8},{28,12},{1,17},{... | collective-permute-start | bytes 98312 | tf_op jit(solution)/shard_map/ppermute | solution.py:21
  42.4 3.4 collective-permute-start.9
  42.7 4.1 %collective-permute-start.8 = (bf16[32,512]{1,0:T(8,128)(2,1)S(1)}, bf16[32,512]{1,0:T(8,128)(2,1)S(1)}, u32[]{:S(2)}, u32[]{:S(2)}) collective-permute-start(bf16[32,512]{1,0:T(8,128)(2,1)S(1)} %get-tuple-element.37), channel_id=1, source_target_pairs={{0,8},{4,12},{8,0},{12,4},{16,24},{20,28},{24,16},{28,20},{1,9},{5... | collective-permute-start | bytes 98312 | tf_op jit(solution)/shard_map/ppermute | solution.py:21
  44.2 2.7 collective-permute-start.7
  47.6 4.4 %collective-permute-start.14 = (bf16[32,512]{1,0:T(8,128)(2,1)S(1)}, bf16[32,512]{1,0:T(8,128)(2,1)S(1)}, u32[]{:S(2)}, u32[]{:S(2)}) collective-permute-start(bf16[32,512]{1,0:T(8,128)(2,1)S(1)} %get-tuple-element.26), channel_id=1, source_target_pairs={{0,1},{1,0},{2,3},{3,2},{4,5},{5,4},{6,7},{7,6},{8,9},{9,8},{10,11... | collective-permute-start | bytes 98312 | tf_op jit(solution)/shard_map/ppermute | solution.py:21
  49.1 5.5 %collective-permute-start.15 = (bf16[32,512]{1,0:T(8,128)(2,1)S(1)}, bf16[32,512]{1,0:T(8,128)(2,1)S(1)}, u32[]{:S(2)}, u32[]{:S(2)}) collective-permute-start(bf16[32,512]{1,0:T(8,128)(2,1)S(1)} %get-tuple-element.26), channel_id=1, source_target_pairs={{0,2},{1,3},{2,0},{3,1},{4,6},{5,7},{6,4},{7,5},{8,10},{9,11},{10,... | collective-permute-start | bytes 98312 | tf_op jit(solution)/shard_map/ppermute | solution.py:21
  51.8 5.7 %collective-permute-start.16 = (bf16[32,512]{1,0:T(8,128)(2,1)S(1)}, bf16[32,512]{1,0:T(8,128)(2,1)S(1)}, u32[]{:S(2)}, u32[]{:S(2)}) collective-permute-start(bf16[32,512]{1,0:T(8,128)(2,1)S(1)} %get-tuple-element.26), channel_id=1, source_target_pairs={{0,3},{1,2},{2,1},{3,0},{4,7},{5,6},{6,5},{7,4},{8,11},{9,10},{10,... | collective-permute-start | bytes 98312 | tf_op jit(solution)/shard_map/ppermute | solution.py:21
  57.5 5.5 %collective-permute-start.17 = (bf16[128,512]{1,0:T(8,128)(2,1)S(1)}, bf16[128,512]{1,0:T(8,128)(2,1)S(1)}, u32[]{:S(2)}, u32[]{:S(2)}) collective-permute-start(bf16[128,512]{1,0:T(8,128)(2,1)S(1)} %pad_maximum_fusion.2), channel_id=1, source_target_pairs={{0,8},{4,12},{8,0},{12,4},{16,24},{20,28},{24,16},{28,20},{1,9},{5... | collective-permute-start | bytes 393224 | tf_op jit(solution)/shard_map/ppermute | solution.py:21
  58.8 5.0 %collective-permute-start.18 = (bf16[128,512]{1,0:T(8,128)(2,1)S(1)}, bf16[128,512]{1,0:T(8,128)(2,1)S(1)}, u32[]{:S(2)}, u32[]{:S(2)}) collective-permute-start(bf16[128,512]{1,0:T(8,128)(2,1)S(1)} %pad_maximum_fusion.2), channel_id=1, source_target_pairs={{0,16},{4,20},{8,24},{12,28},{16,0},{20,4},{24,8},{28,12},{1,17},{... | collective-permute-start | bytes 393224 | tf_op jit(solution)/shard_map/ppermute | solution.py:21
  59.4 6.2 %collective-permute-start.19 = (bf16[128,512]{1,0:T(8,128)(2,1)S(1)}, bf16[128,512]{1,0:T(8,128)(2,1)S(1)}, u32[]{:S(2)}, u32[]{:S(2)}) collective-permute-start(bf16[128,512]{1,0:T(8,128)(2,1)S(1)} %pad_maximum_fusion.2), channel_id=1, source_target_pairs={{0,24},{4,28},{8,16},{12,20},{16,8},{20,12},{24,0},{28,4},{1,25},{... | collective-permute-start | bytes 393224 | tf_op jit(solution)/shard_map/ppermute | solution.py:21
  66.2 90.0 %collective-permute-start.20 = (bf16[512,512]{1,0:T(8,128)(2,1)}, bf16[512,512]{1,0:T(8,128)(2,1)S(1)}, u32[]{:S(2)}, u32[]{:S(2)}) collective-permute-start(bf16[512,512]{1,0:T(8,128)(2,1)} %get-tuple-element.38), channel_id=1, source_target_pairs={{0,4},{4,0},{8,12},{12,8},{16,20},{20,16},{24,28},{28,24},{1,5},{5... | collective-permute-start | bytes 1572872 | tf_op jit(solution)/shard_map/ppermute | solution.py:21
  158.2 1.0 copy-start.2
  247.7 58.2 %copy-start.1 = (f32[512,512]{1,0:T(8,128)S(1)}, f32[512,512]{1,0:T(8,128)}, u32[]{:S(2)}) copy-start(f32[512,512]{1,0:T(8,128)} %fusion.27) | copy-start | bytes 3145732
  302.0 1.2 copy-start.5
  308.5 4.5 %copy-start.3 = (f32[128,512]{1,0:T(8,128)}, f32[128,512]{1,0:T(8,128)S(1)}, u32[]{:S(2)}) copy-start(f32[128,512]{1,0:T(8,128)S(1)} %fusion.42) | copy-start | bytes 786436
  313.5 10.5 %copy-start.4 = (f32[128,512]{1,0:T(8,128)S(1)}, f32[128,512]{1,0:T(8,128)}, u32[]{:S(2)}) copy-start(f32[128,512]{1,0:T(8,128)} %copy-done.3) | copy-start | bytes 786436
  325.6 10.5 %copy-start.6 = (s32[2048]{0:T(1024)S(1)}, s32[2048]{0:T(1024)}, u32[]{:S(2)}) copy-start(s32[2048]{0:T(1024)} %param.7) | copy-start | bytes 24580
  330.1 6.6 %copy-start.7 = (f32[2048]{0:T(1024)S(1)}, f32[2048]{0:T(1024)}, u32[]{:S(2)}) copy-start(f32[2048]{0:T(1024)} %param.11) | copy-start | bytes 24580
  336.1 2.5 copy-start.9
Sparse Core Ops, SparseCore 0:
  27.1 126.9 all-reduce.2

commit v2 on v1

--- a/solution.py
+++ b/solution.py
@@ -1,8 +1,11 @@
+import functools
 import math
 
 import jax
 import jax.numpy as jnp
 from jax import lax
+from jax.experimental import pallas as pl
+from jax.experimental.pallas import tpu as pltpu
 from jax.sharding import PartitionSpec as P
 
 COV = 128
@@ -14,6 +17,9 @@
 
 half_root = math.sqrt(0.5)
 HIGHEST = lax.Precision.HIGHEST
+f32 = jnp.float32
+SUB, LANE = 8, 128
+COUNT = 4
 
 
 def partner(value, axis, mask):
@@ -44,17 +50,165 @@
     return pieces[0]
 
 
+def spread(value):
+    return jnp.broadcast_to(value, (SUB, LANE))
+
+
+def eliminate(tiles, count):
+    lane = lax.broadcasted_iota(jnp.int32, (SUB, LANE), 1)
+    sub = lax.broadcasted_iota(jnp.int32, (SUB, LANE), 0)
+    tiles = list(tiles)
+    scales = [None] * len(tiles)
+    for first in range(0, LANE, count):
+        tile, offset = divmod(first, SUB)
+        window = (lane >= first) & (lane < first + count)
+        columns = [
+            [spread(tiles[i][:, first + k : first + k + 1]) for k in range(count)] for i in range(tile, len(tiles))
+        ]
+        pivot = [
+            [spread(columns[0][m][offset + k : offset + k + 1, :]) if m >= k else None for m in range(count)]
+            for k in range(count)
+        ]
+        rows = []
+        for k in range(count):
+            row = spread(tiles[tile][offset + k : offset + k + 1, :])
+            row = jnp.where(window, 0.0, row)
+            rows.append(jnp.where(lane == first + k, 1.0, row))
+        inverse, ratio = [], [[None] * count for _ in range(count)]
+        for k in range(count):
+            inverse.append(1.0 / pivot[k][k])
+            for m in range(k + 1, count):
+                ratio[k][m] = pivot[k][m] * inverse[k]
+                for n in range(m, count):
+                    pivot[m][n] = pivot[m][n] - ratio[k][m] * pivot[k][n]
+                rows[m] = rows[m] - ratio[k][m] * rows[k]
+        steps = [None] * count
+        for k in reversed(range(count)):
+            steps[k] = rows[k] * inverse[k]
+            for m in range(k + 1, count):
+                steps[k] = steps[k] - ratio[k][m] * steps[m]
+        old = tiles[tile]
+        scale = scales[tile]
+        for i in range(tile, len(tiles)):
+            new = jnp.where(window, 0.0, tiles[i])
+            for k in range(count):
+                new = new - columns[i - tile][k] * steps[k]
+            tiles[i] = new
+        fixed = old
+        if offset + count < SUB:
+            fixed = jnp.where(sub >= offset + count, tiles[tile], old)
+        for k in range(count):
+            kept = rows[k]
+            for m in range(k, count):
+                kept = jnp.where(lane == first + m, pivot[k][m], kept)
+            root = lax.rsqrt(pivot[k][k])
+            fixed = jnp.where(sub == offset + k, kept, fixed)
+            scale = root if scale is None else jnp.where(sub == offset + k, root, scale)
+        tiles[tile] = fixed
+        scales[tile] = scale
+    return tiles, scales
+
+
+def factor_kernel(samp, ratio, place_ref, *refs):
+    piece_refs, (factor_ref, inverse_ref, sketch, work, line) = refs[:-5], refs[-5:]
+    cols = work.shape[0]
+    at = 0
+    for piece in piece_refs:
+        for start in range(0, piece.shape[0], samp):
+            put = pl.multiple_of(place_ref[at] * samp, samp)
+            sketch[pl.ds(put, samp), :] = piece[start : start + samp, :]
+            at += 1
+    rows = sketch[...]
+    work[...] = lax.dot_general(rows, rows, (((0,), (0,)), ((), ())), preferred_element_type=f32)
+
+    row_in = lax.broadcasted_iota(jnp.int32, (LANE, LANE), 0)
+    lane_in = lax.broadcasted_iota(jnp.int32, (LANE, LANE), 1)
+    lane_all = lax.broadcasted_iota(jnp.int32, (LANE, cols), 1)
+    row_all = lax.broadcasted_iota(jnp.int32, (cols, LANE), 0)
+
+    def block_step(block, _):
+        base = pl.multiple_of(block * LANE, LANE)
+        here = pl.ds(base, LANE)
+        tiles = [work[pl.ds(base + SUB * i, SUB), here] for i in range(LANE // SUB)]
+        tiles, scales = eliminate(tiles, COUNT)
+        scale = jnp.concatenate(scales)
+        inner = jnp.concatenate(tiles) * scale
+        upper = jnp.where(lane_in >= row_in, inner, 0.0)
+        lower = jnp.where(lane_in < row_in, inner, jnp.where(lane_in == row_in, scale, 0.0))
+        line[...] = jnp.dot(lower, work[here, :], precision=HIGHEST, preferred_element_type=f32)
+        whole = line[...]
+        factor_ref[here, :] = jnp.where(lane_all >= base, whole, 0.0) * ratio
+        factor_ref[here, here] = upper * ratio
+        inverse_ref[here, :] = jnp.where(lane_all < base, whole, 0.0)
+        inverse_ref[here, here] = lower
+
+        @pl.when(block < cols // LANE - 1)
+        def _():
+            line[:, here] = lower
+            steps = jnp.dot(lower.T, line[...], precision=HIGHEST, preferred_element_type=f32)
+            panel = jnp.where(row_all >= base + LANE, work[:, here], 0.0)
+            work[:, here] = jnp.where(row_all >= base + LANE, 0.0, work[:, here])
+            work[...] -= jnp.dot(panel, steps, precision=HIGHEST, preferred_element_type=f32)
+
+        return 0
+
+    lax.fori_loop(0, cols // LANE, block_step, 0)
+
+
+def factorize(pieces, place, samp, ratio):
+    cols = pieces[0].shape[1]
+    total = sum(piece.shape[0] for piece in pieces)
+    if samp % (2 * SUB):
+        rows = jnp.concatenate(pieces).reshape(total // samp, samp, cols)
+        pieces = [jnp.zeros_like(rows).at[place].set(rows).reshape(total, cols)]
+        place, samp = jnp.zeros((1,), jnp.int32), total
+    vmem = pl.BlockSpec(memory_space=pltpu.VMEM)
+    return pl.pallas_call(
+        functools.partial(factor_kernel, samp, ratio),
+        out_shape=[jax.ShapeDtypeStruct((cols, cols), f32)] * 2,
+        in_specs=[pl.BlockSpec(memory_space=pltpu.SMEM)] + [vmem] * len(pieces),
+        out_specs=[vmem] * 2,
+        scratch_shapes=[
+            pltpu.VMEM((total, cols), jnp.bfloat16),
+            pltpu.VMEM((cols, cols), f32),
+            pltpu.VMEM((LANE, cols), f32),
+        ],
+        compiler_params=pltpu.CompilerParams(vmem_limit_bytes=32 * 2**20),
+        name="factor",
+    )(place, *pieces)
+
+
 def gather_rows(rows):
     wide, narrow = lax.axis_size("wide"), lax.axis_size("narrow")
-    samp, cols = rows.shape
     rows = jnp.concatenate([rows] + [partner(rows, "narrow", m) for m in range(1, narrow)])
-    rows = jnp.concatenate([rows] + [partner(rows, "wide", m) for m in range(2, wide, 2)])
-    rows = jnp.concatenate([rows, partner(rows, "wide", 1)])
-    apart_wide = jnp.bitwise_xor(jnp.arange(wide), lax.axis_index("wide"))
-    apart_narrow = jnp.bitwise_xor(jnp.arange(narrow), lax.axis_index("narrow"))
-    place = jnp.bitwise_and(apart_wide, 1) * (wide // 2) + jnp.right_shift(apart_wide, 1)
-    order = (place[:, None] * narrow + apart_narrow[None, :]).reshape(-1)
-    return rows.reshape(wide * narrow, samp, cols)[order].reshape(-1, cols)
+    pieces = [rows] + [partner(rows, "wide", m) for m in range(2, wide, 2)]
+    pieces += [partner(piece, "wide", 1) for piece in pieces]
+    apart = jnp.concatenate([jnp.arange(0, wide, 2), jnp.arange(1, wide, 2)])
+    wide_place = jnp.bitwise_xor(apart, lax.axis_index("wide"))
+    narrow_place = jnp.bitwise_xor(jnp.arange(narrow), lax.axis_index("narrow"))
+    return pieces, (wide_place[:, None] * narrow + narrow_place[None, :]).reshape(-1)
+
+
+def sum_everywhere(value):
+    wide, narrow = lax.axis_size("wide"), lax.axis_size("narrow")
+    wide_index = lax.axis_index("wide")
+    core, chip = jnp.bitwise_and(wide_index, 1), jnp.right_shift(wide_index, 1)
+    rows, lanes = value.shape
+    share = -(-rows // (SUB * wide)) * SUB
+    value = jnp.pad(value, ((0, share * wide - rows), (0, 0))).reshape(2, wide // 2, share, lanes)
+    value = value[core] + partner(value[1 - core], "wide", 1)
+    total = value[chip]
+    for m in range(1, wide // 2):
+        total = total + partner(value[jnp.bitwise_xor(chip, m)], "wide", 2 * m)
+    parts = [total] + [partner(total, "narrow", m) for m in range(1, narrow)]
+    while len(parts) > 1:
+        parts = [left + right for left, right in zip(parts[0::2], parts[1::2])]
+    shares = [parts[0]] + [partner(parts[0], "wide", m) for m in range(2, wide, 2)]
+    shares += [partner(piece, "wide", 1) for piece in shares]
+    order = jnp.concatenate([jnp.arange(0, wide, 2), jnp.arange(1, wide, 2)])
+    source = jnp.bitwise_xor(order, wide_index)
+    source = jnp.bitwise_and(source, 1) * (wide // 2) + jnp.right_shift(source, 1)
+    return jnp.stack(shares)[source].reshape(wide * share, lanes)[:rows]
 
 
 def body(covariates, level_codes, sign_bits, sample_rows, effects, noise):
@@ -69,7 +223,7 @@
 
     normal = jnp.dot(design.T, covariates, preferred_element_type=jnp.float32)
     back = jnp.dot((onehot.astype(jnp.float32) * noise[:, None]).T, wide_cov, precision=HIGHEST)
-    sums = lax.psum(jnp.concatenate([normal, back]), ("wide", "narrow"))
+    sums = sum_everywhere(jnp.concatenate([normal, back]))
 
     want = jnp.concatenate(wanted)
     signs = 1 - 2 * sign_bits
@@ -81,12 +235,8 @@
     local = rounded(local * (1.0 / math.sqrt(HB)))
     local = [local[m * samp : (m + 1) * samp] for m in range(2**MIX_BITS)]
     pieces = [local[0]] + [partner(local[m], "wide", m) for m in range(1, 2**MIX_BITS)]
-    sketch = gather_rows(mix(pieces))
-
-    gram = jnp.dot(sketch.T, sketch, preferred_element_type=jnp.float32)
-    lower = jnp.linalg.cholesky(gram)
-    factor = lower.T * math.sqrt(LEVELS / SKETCH)
-    inverse = lax.linalg.triangular_solve(lower, jnp.eye(cols, dtype=jnp.float32), left_side=True, lower=True)
+    rows, place = gather_rows(mix(pieces))
+    factor, inverse = factorize(rows, place, samp, math.sqrt(LEVELS / SKETCH))
 
     normal = sums[:cols].reshape(LEVELS, COV, COV)
     back = sums[cols:]

time: 351 us -> 131 us (0.37); the launches traced: 346 us -> 130 us
  other arithmetic: 143 us -> 19.3 us
  waiting for transfers between devices: 101 us -> 18.3 us
  Pallas kernels: 0 us -> 34.3 us
  local copies, waits for them, and re-layouts: 23.3 us -> 1.52 us
  matrix products: 29.7 us -> 12.3 us
  between operations: 26.7 us -> 10.4 us
  starting transfers between devices: 22 us -> 34.3 us
    another operation x16 -> x0, other arithmetic: 119 us -> none  [the longest x14 79 us: body(): lower = jnp.linalg.cholesky(gram)]
    psum x1 -> x0, waiting for transfers between devices: 87.8 us -> none  [body(): sums = lax.psum(jnp.concatenate([normal, back]), ('wide', 'narrow'))]
    pallas_call x0 -> x1, Pallas kernels: none -> 34.3 us  [factorize(): pl.pallas_call(functools.partial(factor_kernel, samp, ratio), out_shape=[...]
    another operation x13 -> x0, matrix products: 14.8 us -> none  [the longest x7 9.3 us: body(): lax.linalg.triangular_solve(lower, jnp.eye(cols, dtype=jnp.float32), left...]
    another operation x17 -> x1, local copies, waits for them, and re-layouts: 14.3 us -> 0.01 us  [sum_everywhere(): return jnp.stack(shares)[source].reshape(wide * share, lanes)[:rows]]
    ppermute x21 -> x38, starting transfers between devices: 22 us -> 34.3 us  [partner(): return lax.ppermute(value, axis, pairs)]
    unnamed x32 -> x19, local copies, waits for them, and re-layouts: 5.84 us -> 0.35 us
    ppermute x21 -> x38, waiting for transfers between devices: 13.1 us -> 18.3 us  [partner(): return lax.ppermute(value, axis, pairs)]
  transfers between devices with their start and end apart: 22 -> 38, of which waited for: 11 -> 14; matrix products, arithmetic and copies ran while one was open for 7% -> 14% of each run, Pallas kernels for 0% -> 0%
where the time goes in v2:
time: 131 us; the launch traced here: 130 us
  starting transfers between devices  34.3 us (26%)
  Pallas kernels  34.3 us (26%)
  other arithmetic  19.3 us (15%)
  waiting for transfers between devices  18.3 us (14%)
  matrix products  12.3 us (9%)
  between operations  10.4 us (8%)
  local copies, waits for them, and re-layouts  1.52 us (1%)
    pallas_call x1, Pallas kernels, factorize(): pl.pallas_call(functools.partial(factor_kernel, samp, ratio), out_shape=[...  34.3 us
    ppermute x38, starting transfers between devices, partner(): return lax.ppermute(value, axis, pairs)  34.3 us
    ppermute x38, waiting for transfers between devices, partner(): return lax.ppermute(value, axis, pairs)  18.3 us
    mul x1, other arithmetic, body(): onehot.astype(jnp.bfloat16)[:, :, None] * covariates[:, None, :]  10.8 us
    dot_general x4, matrix products, precondition(): steer = jnp.dot(inverse, vector, precision=HIGHEST)  3.93 us
  transfers between devices with their start and end apart: 38, of which 14 were waited for; matrix products, arithmetic and copies ran while one was open for 14% of the time, Pallas kernels for 0%

profile of v2, /device:TPU:0, one launch (start us, length us, event | category | flops | bytes accessed | tf_op | source)
XLA Modules:
  0.0 130.5 jit_solution(9747201567399958625)
XLA Ops:
  0.6 4.0 %collective-permute-start.5 = (s32[32]{0:T(128)}, s32[32]{0:T(128)S(1)}, u32[]{:S(2)}, u32[]{:S(2)}) collective-permute-start(s32[32]{0:T(128)} %param.9), channel_id=1, source_target_pairs={{0,24},{4,28},{8,16},{12,20},{16,8},{20,12},{24,0},{28,4},{1,25},{... | collective-permute-start | bytes 392 | tf_op jit(solution)/shard_map/ppermute | solution.py:27
  4.6 1.2 collective-permute-start.3
  5.8 0.8 collective-permute-start.2
  6.6 1.5 %collective-permute-start.1 = (s32[32]{0:T(128)}, s32[32]{0:T(128)S(1)}, u32[]{:S(2)}, u32[]{:S(2)}) collective-permute-start(s32[32]{0:T(128)} %param.9), channel_id=1, source_target_pairs={{0,8},{4,12},{8,0},{12,4},{16,24},{20,28},{24,16},{28,20},{1,9},{5... | collective-permute-start | bytes 392 | tf_op jit(solution)/shard_map/ppermute | solution.py:27
  8.1 0.7 multiply_subtract_fusion
  8.8 0.7 fusion.24
  9.9 1.4 %fusion.22 = f32[4,128]{1,0:T(4,128)S(1)} fusion(bf16[2048,128]{1,0:T(8,128)(2,1)} %param.6, f32[2048]{0:T(1024)} %param.11, s32[2048]{0:T(1024)} %param.7), kind=kOutput, calls=%fused_computation.48 | convolution fusion | flops 12599296 | bytes 542720 | tf_op jit(solution)/shard_map/dot_general | solution.py:225
  11.3 10.8 %broadcast_multiply_fusion = bf16[2048,4,128]{2,1,0:T(4,128)(2,1)S(1)} fusion(bf16[2048,128]{1,0:T(8,128)(2,1)} %param.6, bf16[2048,4]{1,0:T(8,128)(2,1)S(1)} %copy.10), kind=kLoop, calls=%fused_computation.14 | loop fusion | flops 1048576 | bytes 2637824 | tf_op jit(solution)/shard_map/mul | solution.py:220
  22.2 0.8 fusion.1
  23.9 0.5 collective-permute-done
  24.5 2.8 %collective-permute-done.6 = s32[32]{0:T(128)S(1)} collective-permute-done((s32[32]{0:T(128)S(1)}, s32[32]{0:T(128)S(1)}, u32[]{:S(2)}, u32[]{:S(2)}) %collective-permute-start.6) | collective-permute-done | bytes 160 | tf_op jit(solution)/shard_map/ppermute | solution.py:27
  27.5 0.9 select_convert_fusion
  28.7 0.7 fusion.13
  29.5 0.6 collective-permute-start.10
  30.1 1.3 collective-permute-start.13
  31.3 1.4 %collective-permute-start.12 = (bf16[32,512]{1,0:T(8,128)(2,1)S(1)}, bf16[32,512]{1,0:T(8,128)(2,1)S(1)}, u32[]{:S(2)}, u32[]{:S(2)}) collective-permute-start(bf16[32,512]{1,0:T(8,128)(2,1)S(1)} %get-tuple-element.11), channel_id=1, source_target_pairs={{0,24},{4,28},{8,16},{12,20},{16,8},{20,12},{24,0},{28,4},{1,25},{... | collective-permute-start | bytes 98312 | tf_op jit(solution)/shard_map/ppermute | solution.py:27
  32.7 1.2 collective-permute-start.11
  33.9 0.6 collective-permute-start.9
  34.6 1.6 %collective-permute-start.8 = (bf16[32,512]{1,0:T(8,128)(2,1)S(1)}, bf16[32,512]{1,0:T(8,128)(2,1)S(1)}, u32[]{:S(2)}, u32[]{:S(2)}) collective-permute-start(bf16[32,512]{1,0:T(8,128)(2,1)S(1)} %get-tuple-element.14), channel_id=1, source_target_pairs={{0,8},{4,12},{8,0},{12,4},{16,24},{20,28},{24,16},{28,20},{1,9},{5... | collective-permute-start | bytes 98312 | tf_op jit(solution)/shard_map/ppermute | solution.py:27
  36.2 1.6 %collective-permute-start.25 = (f32[72,128]{1,0:T(8,128)S(1)}, f32[72,128]{1,0:T(8,128)S(1)}, u32[]{:S(2)}, u32[]{:S(2)}) collective-permute-start(f32[72,128]{1,0:T(8,128)S(1)} %get-tuple-element.16), channel_id=1, source_target_pairs={{0,8},{4,12},{8,0},{12,4},{16,24},{20,28},{24,16},{28,20},{1,9},{5... | collective-permute-start | bytes 110600 | tf_op jit(solution)/shard_map/ppermute | solution.py:27
  38.3 1.4 %collective-permute-start.26 = (f32[72,128]{1,0:T(8,128)S(1)}, f32[72,128]{1,0:T(8,128)S(1)}, u32[]{:S(2)}, u32[]{:S(2)}) collective-permute-start(f32[72,128]{1,0:T(8,128)S(1)} %get-tuple-element.18), channel_id=1, source_target_pairs={{0,16},{4,20},{8,24},{12,28},{16,0},{20,4},{24,8},{28,12},{1,17},{... | collective-permute-start | bytes 110600 | tf_op jit(solution)/shard_map/ppermute | solution.py:27
  39.8 3.7 %collective-permute-start.16 = (bf16[32,512]{1,0:T(8,128)(2,1)S(1)}, bf16[32,512]{1,0:T(8,128)(2,1)S(1)}, u32[]{:S(2)}, u32[]{:S(2)}) collective-permute-start(bf16[32,512]{1,0:T(8,128)(2,1)S(1)} %reduce-precision_convert_fusion), channel_id=1, source_target_pairs={{0,3},{1,2},{2,1},{3,0},{4,7},{5,6},{6,5},{7,4},{8,11},{9,10},{10,... | collective-permute-start | bytes 98312 | tf_op jit(solution)/shard_map/ppermute | solution.py:27
  43.5 0.8 collective-permute-start.14
  44.3 3.7 %collective-permute-start.30 = (f32[72,128]{1,0:T(8,128)S(1)}, f32[72,128]{1,0:T(8,128)S(1)}, u32[]{:S(2)}, u32[]{:S(2)}) collective-permute-start(f32[72,128]{1,0:T(8,128)S(1)} %fusion.21), channel_id=1, source_target_pairs={{0,3},{1,2},{2,1},{3,0},{4,7},{5,6},{6,5},{7,4},{8,11},{9,10},{10,... | collective-permute-start | bytes 110600 | tf_op jit(solution)/shard_map/ppermute | solution.py:27
  48.0 0.8 collective-permute-start.28
  48.8 1.5 %collective-permute-start.19 = (bf16[128,512]{1,0:T(8,128)(2,1)S(1)}, bf16[128,512]{1,0:T(8,128)(2,1)S(1)}, u32[]{:S(2)}, u32[]{:S(2)}) collective-permute-start(bf16[128,512]{1,0:T(8,128)(2,1)S(1)} %pad_maximum_fusion.refs_0_), channel_id=1, source_target_pairs={{0,24},{4,28},{8,16},{12,20},{16,8},{20,12},{24,0},{28,4},{1,25},{... | collective-permute-start | bytes 393224 | tf_op jit(solution)/shard_map/ppermute | solution.py:27
  50.3 1.6 %collective-permute-start.18 = (bf16[128,512]{1,0:T(8,128)(2,1)S(1)}, bf16[128,512]{1,0:T(8,128)(2,1)S(1)}, u32[]{:S(2)}, u32[]{:S(2)}) collective-permute-start(bf16[128,512]{1,0:T(8,128)(2,1)S(1)} %pad_maximum_fusion.refs_0_), channel_id=1, source_target_pairs={{0,16},{4,20},{8,24},{12,28},{16,0},{20,4},{24,8},{28,12},{1,17},{... | collective-permute-start | bytes 393224 | tf_op jit(solution)/shard_map/ppermute | solution.py:27
  52.3 0.5 collective-permute-done.29
  52.8 1.7 %collective-permute-start.31 = (f32[72,128]{1,0:T(8,128)S(1)}, f32[72,128]{1,0:T(8,128)S(1)}, u32[]{:S(2)}, u32[]{:S(2)}) collective-permute-start(f32[72,128]{1,0:T(8,128)S(1)} %get-tuple-element.8), channel_id=1, source_target_pairs={{0,8},{4,12},{8,0},{12,4},{16,24},{20,28},{24,16},{28,20},{1,9},{5... | collective-permute-start | bytes 110600 | tf_op jit(solution)/shard_map/ppermute | solution.py:27
  54.6 0.6 collective-permute-done.19.refs_3_
  55.2 1.2 collective-permute-done.18.refs_2_
  56.4 0.5 collective-permute-done.17.refs_1_
  57.7 3.5 %collective-permute-done.32 = f32[72,128]{1,0:T(8,128)S(1)} collective-permute-done((f32[72,128]{1,0:T(8,128)S(1)}, f32[72,128]{1,0:T(8,128)S(1)}, u32[]{:S(2)}, u32[]{:S(2)}) %collective-permute-start.32) | collective-permute-done | bytes 36896 | tf_op jit(solution)/shard_map/ppermute | solution.py:27
  61.3 1.1 collective-permute-start.33
  62.4 3.7 %collective-permute-done.33 = f32[72,128]{1,0:T(8,128)S(1)} collective-permute-done((f32[72,128]{1,0:T(8,128)S(1)}, f32[72,128]{1,0:T(8,128)S(1)}, u32[]{:S(2)}, u32[]{:S(2)}) %collective-permute-start.33) | collective-permute-done | bytes 36896 | tf_op jit(solution)/shard_map/ppermute | solution.py:27
  66.1 1.2 collective-permute-done.34
  67.5 1.0 collective-permute-done.35
  68.7 1.0 collective-permute-done.36
  69.9 1.0 collective-permute-done.37
  71.0 0.6 gather_fusion
  71.6 0.5 fusion.47
  72.2 34.3 %factor.1 = (f32[512,512]{1,0:T(8,128)}, f32[512,512]{1,0:T(8,128)S(1)}) custom-call(s32[32]{0:T(128)S(1)} %add.156.place_ref, bf16[128,512]{1,0:T(8,128)(2,1)S(1)} %pad_maximum_fusion.refs_0_, bf16[128,512]{1,0:T(8,128)(2,1)S(1)} %collective-permute-done.17.refs_1_, bf16[128,512]{1,0:T(8,128)(2,1)S(1)} %collective-permute-done.18.refs_2_, ...), custom_call_target="tpu_custom_call" | custom-call | tf_op jit(solution)/shard_map/factor/pallas_call | solution.py:166
  106.5 1.0 fusion.48
  107.5 0.6 fusion.38
  108.1 0.6 multiply_reduce_fusion.7
  108.7 0.5 fusion.29
  109.2 0.6 multiply_reduce_fusion.6
  111.2 1.0 fusion.49
  112.2 0.6 fusion.36
  112.8 0.6 multiply_reduce_fusion.5
  114.7 0.5 fusion.50
  115.2 0.6 multiply_reduce_fusion.4
  117.2 1.0 fusion.51
  118.2 0.6 fusion.34
  118.8 0.6 multiply_reduce_fusion.3
  120.8 0.5 fusion.52
  121.3 0.6 multiply_reduce_fusion.2
  123.3 1.0 fusion.53
  124.3 0.6 fusion.32
  124.9 0.6 multiply_reduce_fusion.1
  126.8 0.5 fusion.54
  127.3 0.6 multiply_reduce_fusion
  129.3 0.5 fusion.16
  129.9 0.6 add.187
  (96 shorter events, 4.6 us)
Async XLA Ops:
  0.6 22.6 %collective-permute-start.5 = (s32[32]{0:T(128)}, s32[32]{0:T(128)S(1)}, u32[]{:S(2)}, u32[]{:S(2)}) collective-permute-start(s32[32]{0:T(128)} %param.9), channel_id=1, source_target_pairs={{0,24},{4,28},{8,16},{12,20},{16,8},{20,12},{24,0},{28,4},{1,25},{... | collective-permute-start | bytes 392 | tf_op jit(solution)/shard_map/ppermute | solution.py:27
  4.6 18.8 %collective-permute-start.4 = (s32[32]{0:T(128)}, s32[32]{0:T(128)S(1)}, u32[]{:S(2)}, u32[]{:S(2)}) collective-permute-start(s32[32]{0:T(128)} %param.9), channel_id=1, source_target_pairs={{0,20},{4,16},{8,28},{12,24},{16,4},{20,0},{24,12},{28,8},{1,21},{... | collective-permute-start | bytes 392 | tf_op jit(solution)/shard_map/ppermute | solution.py:27
  4.6 19.1 %collective-permute-start.3 = (s32[32]{0:T(128)}, s32[32]{0:T(128)S(1)}, u32[]{:S(2)}, u32[]{:S(2)}) collective-permute-start(s32[32]{0:T(128)} %param.9), channel_id=1, source_target_pairs={{0,16},{4,20},{8,24},{12,28},{16,0},{20,4},{24,8},{28,12},{1,17},{... | collective-permute-start | bytes 392 | tf_op jit(solution)/shard_map/ppermute | solution.py:27
  5.8 18.1 %collective-permute-start.2 = (s32[32]{0:T(128)}, s32[32]{0:T(128)S(1)}, u32[]{:S(2)}, u32[]{:S(2)}) collective-permute-start(s32[32]{0:T(128)} %param.9), channel_id=1, source_target_pairs={{0,12},{4,8},{8,4},{12,0},{16,28},{20,24},{24,20},{28,16},{1,13},{... | collective-permute-start | bytes 392 | tf_op jit(solution)/shard_map/ppermute | solution.py:27
  6.6 17.3 %collective-permute-start.1 = (s32[32]{0:T(128)}, s32[32]{0:T(128)S(1)}, u32[]{:S(2)}, u32[]{:S(2)}) collective-permute-start(s32[32]{0:T(128)} %param.9), channel_id=1, source_target_pairs={{0,8},{4,12},{8,0},{12,4},{16,24},{20,28},{24,16},{28,20},{1,9},{5... | collective-permute-start | bytes 392 | tf_op jit(solution)/shard_map/ppermute | solution.py:27
  9.6 12.6 %copy-start = (bf16[2048,128]{1,0:T(8,128)(2,1)S(1)}, bf16[2048,128]{1,0:T(8,128)(2,1)}, u32[]{:S(2)}) copy-start(bf16[2048,128]{1,0:T(8,128)(2,1)} %param.6) | copy-start | bytes 1572868
  22.2 1.1 copy-start.5
  23.3 1.2 collective-permute-start
  23.4 3.9 %collective-permute-start.6 = (s32[32]{0:T(128)S(1)}, s32[32]{0:T(128)S(1)}, u32[]{:S(2)}, u32[]{:S(2)}) collective-permute-start(s32[32]{0:T(128)S(1)} %copy-done.5), channel_id=1, source_target_pairs={{0,28},{4,24},{8,20},{12,16},{16,12},{20,8},{24,4},{28,0},{1,29},{... | collective-permute-start | bytes 392 | tf_op jit(solution)/shard_map/ppermute | solution.py:27
  23.7 10.2 %collective-permute-start.24 = (f32[4,72,128]{2,1,0:T(8,128)S(1)}, f32[4,72,128]{2,1,0:T(8,128)S(1)}, u32[]{:S(2)}, u32[]{:S(2)}) collective-permute-start(f32[4,72,128]{2,1,0:T(8,128)S(1)} %dynamic-slice_bitcast_fusion), channel_id=1, source_target_pairs={{0,4},{4,0},{8,12},{12,8},{16,20},{20,16},{24,28},{28,24},{1,5},{5... | collective-permute-start | bytes 442376 | tf_op jit(solution)/shard_map/ppermute | solution.py:27
  29.4 42.2 %copy-start.3 = (f32[512]{0:T(512)S(1)}, f32[512]{0:T(512)}, u32[]{:S(2)}) copy-start(f32[512]{0:T(512)} %param.10) | copy-start | bytes 6148
  29.5 5.1 %collective-permute-start.10 = (bf16[32,512]{1,0:T(8,128)(2,1)S(1)}, bf16[32,512]{1,0:T(8,128)(2,1)S(1)}, u32[]{:S(2)}, u32[]{:S(2)}) collective-permute-start(bf16[32,512]{1,0:T(8,128)(2,1)S(1)} %get-tuple-element.9), channel_id=1, source_target_pairs={{0,16},{4,20},{8,24},{12,28},{16,0},{20,4},{24,8},{28,12},{1,17},{... | collective-permute-start | bytes 98312 | tf_op jit(solution)/shard_map/ppermute | solution.py:27
  30.1 6.1 %collective-permute-start.13 = (bf16[32,512]{1,0:T(8,128)(2,1)S(1)}, bf16[32,512]{1,0:T(8,128)(2,1)S(1)}, u32[]{:S(2)}, u32[]{:S(2)}) collective-permute-start(bf16[32,512]{1,0:T(8,128)(2,1)S(1)} %get-tuple-element.10), channel_id=1, source_target_pairs={{0,28},{4,24},{8,20},{12,16},{16,12},{20,8},{24,4},{28,0},{1,29},{... | collective-permute-start | bytes 98312 | tf_op jit(solution)/shard_map/ppermute | solution.py:27
  31.3 4.9 %collective-permute-start.12 = (bf16[32,512]{1,0:T(8,128)(2,1)S(1)}, bf16[32,512]{1,0:T(8,128)(2,1)S(1)}, u32[]{:S(2)}, u32[]{:S(2)}) collective-permute-start(bf16[32,512]{1,0:T(8,128)(2,1)S(1)} %get-tuple-element.11), channel_id=1, source_target_pairs={{0,24},{4,28},{8,16},{12,20},{16,8},{20,12},{24,0},{28,4},{1,25},{... | collective-permute-start | bytes 98312 | tf_op jit(solution)/shard_map/ppermute | solution.py:27
  32.7 5.1 %collective-permute-start.11 = (bf16[32,512]{1,0:T(8,128)(2,1)S(1)}, bf16[32,512]{1,0:T(8,128)(2,1)S(1)}, u32[]{:S(2)}, u32[]{:S(2)}) collective-permute-start(bf16[32,512]{1,0:T(8,128)(2,1)S(1)} %get-tuple-element.12), channel_id=1, source_target_pairs={{0,20},{4,16},{8,28},{12,24},{16,4},{20,0},{24,12},{28,8},{1,21},{... | collective-permute-start | bytes 98312 | tf_op jit(solution)/shard_map/ppermute | solution.py:27
  33.9 4.4 %collective-permute-start.9 = (bf16[32,512]{1,0:T(8,128)(2,1)S(1)}, bf16[32,512]{1,0:T(8,128)(2,1)S(1)}, u32[]{:S(2)}, u32[]{:S(2)}) collective-permute-start(bf16[32,512]{1,0:T(8,128)(2,1)S(1)} %get-tuple-element.13), channel_id=1, source_target_pairs={{0,12},{4,8},{8,4},{12,0},{16,28},{20,24},{24,20},{28,16},{1,13},{... | collective-permute-start | bytes 98312 | tf_op jit(solution)/shard_map/ppermute | solution.py:27
  34.6 5.2 %collective-permute-start.8 = (bf16[32,512]{1,0:T(8,128)(2,1)S(1)}, bf16[32,512]{1,0:T(8,128)(2,1)S(1)}, u32[]{:S(2)}, u32[]{:S(2)}) collective-permute-start(bf16[32,512]{1,0:T(8,128)(2,1)S(1)} %get-tuple-element.14), channel_id=1, source_target_pairs={{0,8},{4,12},{8,0},{12,4},{16,24},{20,28},{24,16},{28,20},{1,9},{5... | collective-permute-start | bytes 98312 | tf_op jit(solution)/shard_map/ppermute | solution.py:27
  36.1 3.6 %collective-permute-start.7 = (bf16[32,512]{1,0:T(8,128)(2,1)S(1)}, bf16[32,512]{1,0:T(8,128)(2,1)S(1)}, u32[]{:S(2)}, u32[]{:S(2)}) collective-permute-start(bf16[32,512]{1,0:T(8,128)(2,1)S(1)} %get-tuple-element.15), channel_id=1, source_target_pairs={{0,4},{4,0},{8,12},{12,8},{16,20},{20,16},{24,28},{28,24},{1,5},{5... | collective-permute-start | bytes 98312 | tf_op jit(solution)/shard_map/ppermute | solution.py:27
  36.2 7.3 %collective-permute-start.25 = (f32[72,128]{1,0:T(8,128)S(1)}, f32[72,128]{1,0:T(8,128)S(1)}, u32[]{:S(2)}, u32[]{:S(2)}) collective-permute-start(f32[72,128]{1,0:T(8,128)S(1)} %get-tuple-element.16), channel_id=1, source_target_pairs={{0,8},{4,12},{8,0},{12,4},{16,24},{20,28},{24,16},{28,20},{1,9},{5... | collective-permute-start | bytes 110600 | tf_op jit(solution)/shard_map/ppermute | solution.py:27
  37.9 6.4 %collective-permute-start.27 = (f32[72,128]{1,0:T(8,128)S(1)}, f32[72,128]{1,0:T(8,128)S(1)}, u32[]{:S(2)}, u32[]{:S(2)}) collective-permute-start(f32[72,128]{1,0:T(8,128)S(1)} %get-tuple-element.17), channel_id=1, source_target_pairs={{0,24},{4,28},{8,16},{12,20},{16,8},{20,12},{24,0},{28,4},{1,25},{... | collective-permute-start | bytes 110600 | tf_op jit(solution)/shard_map/ppermute | solution.py:27
  38.3 6.0 %collective-permute-start.26 = (f32[72,128]{1,0:T(8,128)S(1)}, f32[72,128]{1,0:T(8,128)S(1)}, u32[]{:S(2)}, u32[]{:S(2)}) collective-permute-start(f32[72,128]{1,0:T(8,128)S(1)} %get-tuple-element.18), channel_id=1, source_target_pairs={{0,16},{4,20},{8,24},{12,28},{16,0},{20,4},{24,8},{28,12},{1,17},{... | collective-permute-start | bytes 110600 | tf_op jit(solution)/shard_map/ppermute | solution.py:27
  39.8 8.2 %collective-permute-start.16 = (bf16[32,512]{1,0:T(8,128)(2,1)S(1)}, bf16[32,512]{1,0:T(8,128)(2,1)S(1)}, u32[]{:S(2)}, u32[]{:S(2)}) collective-permute-start(bf16[32,512]{1,0:T(8,128)(2,1)S(1)} %reduce-precision_convert_fusion), channel_id=1, source_target_pairs={{0,3},{1,2},{2,1},{3,0},{4,7},{5,6},{6,5},{7,4},{8,11},{9,10},{10,... | collective-permute-start | bytes 98312 | tf_op jit(solution)/shard_map/ppermute | solution.py:27
  43.5 5.3 %collective-permute-start.15 = (bf16[32,512]{1,0:T(8,128)(2,1)S(1)}, bf16[32,512]{1,0:T(8,128)(2,1)S(1)}, u32[]{:S(2)}, u32[]{:S(2)}) collective-permute-start(bf16[32,512]{1,0:T(8,128)(2,1)S(1)} %reduce-precision_convert_fusion), channel_id=1, source_target_pairs={{0,2},{1,3},{2,0},{3,1},{4,6},{5,7},{6,4},{7,5},{8,10},{9,11},{10,... | collective-permute-start | bytes 98312 | tf_op jit(solution)/shard_map/ppermute | solution.py:27
  43.5 5.3 %collective-permute-start.14 = (bf16[32,512]{1,0:T(8,128)(2,1)S(1)}, bf16[32,512]{1,0:T(8,128)(2,1)S(1)}, u32[]{:S(2)}, u32[]{:S(2)}) collective-permute-start(bf16[32,512]{1,0:T(8,128)(2,1)S(1)} %reduce-precision_convert_fusion), channel_id=1, source_target_pairs={{0,1},{1,0},{2,3},{3,2},{4,5},{5,4},{6,7},{7,6},{8,9},{9,8},{10,11... | collective-permute-start | bytes 98312 | tf_op jit(solution)/shard_map/ppermute | solution.py:27
  44.3 7.6 %collective-permute-start.30 = (f32[72,128]{1,0:T(8,128)S(1)}, f32[72,128]{1,0:T(8,128)S(1)}, u32[]{:S(2)}, u32[]{:S(2)}) collective-permute-start(f32[72,128]{1,0:T(8,128)S(1)} %fusion.21), channel_id=1, source_target_pairs={{0,3},{1,2},{2,1},{3,0},{4,7},{5,6},{6,5},{7,4},{8,11},{9,10},{10,... | collective-permute-start | bytes 110600 | tf_op jit(solution)/shard_map/ppermute | solution.py:27
  48.0 4.9 %collective-permute-start.29 = (f32[72,128]{1,0:T(8,128)S(1)}, f32[72,128]{1,0:T(8,128)S(1)}, u32[]{:S(2)}, u32[]{:S(2)}) collective-permute-start(f32[72,128]{1,0:T(8,128)S(1)} %fusion.21), channel_id=1, source_target_pairs={{0,2},{1,3},{2,0},{3,1},{4,6},{5,7},{6,4},{7,5},{8,10},{9,11},{10,... | collective-permute-start | bytes 110600 | tf_op jit(solution)/shard_map/ppermute | solution.py:27
  48.0 4.9 %collective-permute-start.28 = (f32[72,128]{1,0:T(8,128)S(1)}, f32[72,128]{1,0:T(8,128)S(1)}, u32[]{:S(2)}, u32[]{:S(2)}) collective-permute-start(f32[72,128]{1,0:T(8,128)S(1)} %fusion.21), channel_id=1, source_target_pairs={{0,1},{1,0},{2,3},{3,2},{4,5},{5,4},{6,7},{7,6},{8,9},{9,8},{10,11... | collective-permute-start | bytes 110600 | tf_op jit(solution)/shard_map/ppermute | solution.py:27
  48.8 6.4 %collective-permute-start.19 = (bf16[128,512]{1,0:T(8,128)(2,1)S(1)}, bf16[128,512]{1,0:T(8,128)(2,1)S(1)}, u32[]{:S(2)}, u32[]{:S(2)}) collective-permute-start(bf16[128,512]{1,0:T(8,128)(2,1)S(1)} %pad_maximum_fusion.refs_0_), channel_id=1, source_target_pairs={{0,24},{4,28},{8,16},{12,20},{16,8},{20,12},{24,0},{28,4},{1,25},{... | collective-permute-start | bytes 393224 | tf_op jit(solution)/shard_map/ppermute | solution.py:27
  50.3 6.1 %collective-permute-start.18 = (bf16[128,512]{1,0:T(8,128)(2,1)S(1)}, bf16[128,512]{1,0:T(8,128)(2,1)S(1)}, u32[]{:S(2)}, u32[]{:S(2)}) collective-permute-start(bf16[128,512]{1,0:T(8,128)(2,1)S(1)} %pad_maximum_fusion.refs_0_), channel_id=1, source_target_pairs={{0,16},{4,20},{8,24},{12,28},{16,0},{20,4},{24,8},{28,12},{1,17},{... | collective-permute-start | bytes 393224 | tf_op jit(solution)/shard_map/ppermute | solution.py:27
  51.9 5.0 %collective-permute-start.17 = (bf16[128,512]{1,0:T(8,128)(2,1)S(1)}, bf16[128,512]{1,0:T(8,128)(2,1)S(1)}, u32[]{:S(2)}, u32[]{:S(2)}) collective-permute-start(bf16[128,512]{1,0:T(8,128)(2,1)S(1)} %pad_maximum_fusion.refs_0_), channel_id=1, source_target_pairs={{0,8},{4,12},{8,0},{12,4},{16,24},{20,28},{24,16},{28,20},{1,9},{5... | collective-permute-start | bytes 393224 | tf_op jit(solution)/shard_map/ppermute | solution.py:27
  52.8 4.5 %collective-permute-start.31 = (f32[72,128]{1,0:T(8,128)S(1)}, f32[72,128]{1,0:T(8,128)S(1)}, u32[]{:S(2)}, u32[]{:S(2)}) collective-permute-start(f32[72,128]{1,0:T(8,128)S(1)} %get-tuple-element.8), channel_id=1, source_target_pairs={{0,8},{4,12},{8,0},{12,4},{16,24},{20,28},{24,16},{28,20},{1,9},{5... | collective-permute-start | bytes 110600 | tf_op jit(solution)/shard_map/ppermute | solution.py:27
  54.6 17.5 %collective-permute-start.20 = (bf16[128,512]{1,0:T(8,128)(2,1)S(1)}, bf16[128,512]{1,0:T(8,128)(2,1)S(1)}, u32[]{:S(2)}, u32[]{:S(2)}) collective-permute-start(bf16[128,512]{1,0:T(8,128)(2,1)S(1)} %pad_maximum_fusion.refs_0_), channel_id=1, source_target_pairs={{0,4},{4,0},{8,12},{12,8},{16,20},{20,16},{24,28},{28,24},{1,5},{5... | collective-permute-start | bytes 393224 | tf_op jit(solution)/shard_map/ppermute | solution.py:27
  55.2 16.9 %collective-permute-start.23 = (bf16[128,512]{1,0:T(8,128)(2,1)S(1)}, bf16[128,512]{1,0:T(8,128)(2,1)S(1)}, u32[]{:S(2)}, u32[]{:S(2)}) collective-permute-start(bf16[128,512]{1,0:T(8,128)(2,1)S(1)} %collective-permute-done.19.refs_3_), channel_id=1, source_target_pairs={{0,4},{4,0},{8,12},{12,8},{16,20},{20,16},{24,28},{28,24},{1,5},{5... | collective-permute-start | bytes 393224 | tf_op jit(solution)/shard_map/ppermute | solution.py:27
  56.4 15.7 %collective-permute-start.22 = (bf16[128,512]{1,0:T(8,128)(2,1)S(1)}, bf16[128,512]{1,0:T(8,128)(2,1)S(1)}, u32[]{:S(2)}, u32[]{:S(2)}) collective-permute-start(bf16[128,512]{1,0:T(8,128)(2,1)S(1)} %collective-permute-done.18.refs_2_), channel_id=1, source_target_pairs={{0,4},{4,0},{8,12},{12,8},{16,20},{20,16},{24,28},{28,24},{1,5},{5... | collective-permute-start | bytes 393224 | tf_op jit(solution)/shard_map/ppermute | solution.py:27
  56.9 15.2 %collective-permute-start.21 = (bf16[128,512]{1,0:T(8,128)(2,1)S(1)}, bf16[128,512]{1,0:T(8,128)(2,1)S(1)}, u32[]{:S(2)}, u32[]{:S(2)}) collective-permute-start(bf16[128,512]{1,0:T(8,128)(2,1)S(1)} %collective-permute-done.17.refs_1_), channel_id=1, source_target_pairs={{0,4},{4,0},{8,12},{12,8},{16,20},{20,16},{24,28},{28,24},{1,5},{5... | collective-permute-start | bytes 393224 | tf_op jit(solution)/shard_map/ppermute | solution.py:27
  57.3 4.0 %collective-permute-start.32 = (f32[72,128]{1,0:T(8,128)S(1)}, f32[72,128]{1,0:T(8,128)S(1)}, u32[]{:S(2)}, u32[]{:S(2)}) collective-permute-start(f32[72,128]{1,0:T(8,128)S(1)} %get-tuple-element.8), channel_id=1, source_target_pairs={{0,16},{4,20},{8,24},{12,28},{16,0},{20,4},{24,8},{28,12},{1,17},{... | collective-permute-start | bytes 110600 | tf_op jit(solution)/shard_map/ppermute | solution.py:27
  61.3 4.9 %collective-permute-start.33 = (f32[72,128]{1,0:T(8,128)S(1)}, f32[72,128]{1,0:T(8,128)S(1)}, u32[]{:S(2)}, u32[]{:S(2)}) collective-permute-start(f32[72,128]{1,0:T(8,128)S(1)} %get-tuple-element.8), channel_id=1, source_target_pairs={{0,24},{4,28},{8,16},{12,20},{16,8},{20,12},{24,0},{28,4},{1,25},{... | collective-permute-start | bytes 110600 | tf_op jit(solution)/shard_map/ppermute | solution.py:27
  66.1 1.2 collective-permute-start.34
  67.3 1.2 collective-permute-start.35
  68.6 1.2 collective-permute-start.36
  69.8 1.2 collective-permute-start.37
  118.2 11.1 %copy-start.1 = (s32[2048]{0:T(1024)S(1)}, s32[2048]{0:T(1024)}, u32[]{:S(2)}) copy-start(s32[2048]{0:T(1024)} %param.7) | copy-start | bytes 24580
  118.2 11.7 %copy-start.2 = (f32[2048]{0:T(1024)S(1)}, f32[2048]{0:T(1024)}, u32[]{:S(2)}) copy-start(f32[2048]{0:T(1024)} %param.11) | copy-start | bytes 24580
  129.3 1.2 copy-start.4

commit v3 on v2

--- a/solution.py
+++ b/solution.py
@@ -22,9 +22,13 @@
 COUNT = 4
 
 
-def partner(value, axis, mask):
-    pairs = [(source, source ^ mask) for source in range(lax.axis_size(axis))]
-    return lax.ppermute(value, axis, pairs)
+def swap(value, axis, groups=None):
+    return lax.all_to_all(value, axis, 0, 0, axis_index_groups=groups)
+
+
+def share_all(value, axis, groups=None):
+    count = len(groups[0]) if groups else lax.axis_size(axis)
+    return swap(jnp.broadcast_to(value, (count,) + value.shape), axis, groups)
 
 
 def rounded(value):
@@ -44,8 +48,8 @@
         bit = jnp.bitwise_and(jnp.right_shift(wide_index, place), 1)
         sign = (1 - 2 * bit).astype(jnp.float32)
         pieces = [
-            rounded((sign * own.astype(jnp.float32) + other.astype(jnp.float32)) * half_root)
-            for own, other in zip(pieces[0::2], pieces[1::2])
+            rounded((low.astype(jnp.float32) + sign * high.astype(jnp.float32)) * half_root)
+            for low, high in zip(pieces[0::2], pieces[1::2])
         ]
     return pieces[0]
 
@@ -109,16 +113,9 @@
     return tiles, scales
 
 
-def factor_kernel(samp, ratio, place_ref, *refs):
-    piece_refs, (factor_ref, inverse_ref, sketch, work, line) = refs[:-5], refs[-5:]
+def factor_kernel(ratio, sketch_ref, factor_ref, inverse_ref, work, line):
     cols = work.shape[0]
-    at = 0
-    for piece in piece_refs:
-        for start in range(0, piece.shape[0], samp):
-            put = pl.multiple_of(place_ref[at] * samp, samp)
-            sketch[pl.ds(put, samp), :] = piece[start : start + samp, :]
-            at += 1
-    rows = sketch[...]
+    rows = sketch_ref[...]
     work[...] = lax.dot_general(rows, rows, (((0,), (0,)), ((), ())), preferred_element_type=f32)
 
     row_in = lax.broadcasted_iota(jnp.int32, (LANE, LANE), 0)
@@ -155,60 +152,28 @@
     lax.fori_loop(0, cols // LANE, block_step, 0)
 
 
-def factorize(pieces, place, samp, ratio):
-    cols = pieces[0].shape[1]
-    total = sum(piece.shape[0] for piece in pieces)
-    if samp % (2 * SUB):
-        rows = jnp.concatenate(pieces).reshape(total // samp, samp, cols)
-        pieces = [jnp.zeros_like(rows).at[place].set(rows).reshape(total, cols)]
-        place, samp = jnp.zeros((1,), jnp.int32), total
+def factorize(sketch, ratio):
+    cols = sketch.shape[1]
     vmem = pl.BlockSpec(memory_space=pltpu.VMEM)
     return pl.pallas_call(
-        functools.partial(factor_kernel, samp, ratio),
+        functools.partial(factor_kernel, ratio),
         out_shape=[jax.ShapeDtypeStruct((cols, cols), f32)] * 2,
-        in_specs=[pl.BlockSpec(memory_space=pltpu.SMEM)] + [vmem] * len(pieces),
+        in_specs=[vmem],
         out_specs=[vmem] * 2,
-        scratch_shapes=[
-            pltpu.VMEM((total, cols), jnp.bfloat16),
-            pltpu.VMEM((cols, cols), f32),
-            pltpu.VMEM((LANE, cols), f32),
-        ],
+        scratch_shapes=[pltpu.VMEM((cols, cols), f32), pltpu.VMEM((LANE, cols), f32)],
         compiler_params=pltpu.CompilerParams(vmem_limit_bytes=32 * 2**20),
         name="factor",
-    )(place, *pieces)
-
-
-def gather_rows(rows):
-    wide, narrow = lax.axis_size("wide"), lax.axis_size("narrow")
-    rows = jnp.concatenate([rows] + [partner(rows, "narrow", m) for m in range(1, narrow)])
-    pieces = [rows] + [partner(rows, "wide", m) for m in range(2, wide, 2)]
-    pieces += [partner(piece, "wide", 1) for piece in pieces]
-    apart = jnp.concatenate([jnp.arange(0, wide, 2), jnp.arange(1, wide, 2)])
-    wide_place = jnp.bitwise_xor(apart, lax.axis_index("wide"))
-    narrow_place = jnp.bitwise_xor(jnp.arange(narrow), lax.axis_index("narrow"))
-    return pieces, (wide_place[:, None] * narrow + narrow_place[None, :]).reshape(-1)
+    )(sketch)
 
 
 def sum_everywhere(value):
-    wide, narrow = lax.axis_size("wide"), lax.axis_size("narrow")
-    wide_index = lax.axis_index("wide")
-    core, chip = jnp.bitwise_and(wide_index, 1), jnp.right_shift(wide_index, 1)
+    wide = lax.axis_size("wide")
     rows, lanes = value.shape
     share = -(-rows // (SUB * wide)) * SUB
-    value = jnp.pad(value, ((0, share * wide - rows), (0, 0))).reshape(2, wide // 2, share, lanes)
-    value = value[core] + partner(value[1 - core], "wide", 1)
-    total = value[chip]
-    for m in range(1, wide // 2):
-        total = total + partner(value[jnp.bitwise_xor(chip, m)], "wide", 2 * m)
-    parts = [total] + [partner(total, "narrow", m) for m in range(1, narrow)]
-    while len(parts) > 1:
-        parts = [left + right for left, right in zip(parts[0::2], parts[1::2])]
-    shares = [parts[0]] + [partner(parts[0], "wide", m) for m in range(2, wide, 2)]
-    shares += [partner(piece, "wide", 1) for piece in shares]
-    order = jnp.concatenate([jnp.arange(0, wide, 2), jnp.arange(1, wide, 2)])
-    source = jnp.bitwise_xor(order, wide_index)
-    source = jnp.bitwise_and(source, 1) * (wide // 2) + jnp.right_shift(source, 1)
-    return jnp.stack(shares)[source].reshape(wide * share, lanes)[:rows]
+    value = jnp.pad(value, ((0, share * wide - rows), (0, 0))).reshape(wide, share, lanes)
+    value = jnp.sum(swap(value, "wide"), axis=0)
+    value = jnp.sum(share_all(value, "narrow"), axis=0)
+    return share_all(value, "wide").reshape(wide * share, lanes)[:rows]
 
 
 def body(covariates, level_codes, sign_bits, sample_rows, effects, noise):
@@ -219,13 +184,14 @@
     onehot = level_codes[:, None] == jnp.arange(LEVELS, dtype=jnp.int32)[None, :]
     design = (onehot.astype(jnp.bfloat16)[:, :, None] * covariates[:, None, :]).reshape(rows_dev, cols)
 
-    wanted = [sample_rows] + [partner(sample_rows, "wide", m) for m in range(1, 2**MIX_BITS)]
+    mates = 2**MIX_BITS
+    groups = [[first + e for e in range(mates)] for first in range(0, lax.axis_size("wide"), mates)]
+    want = share_all(sample_rows, "wide", groups).reshape(-1)
 
     normal = jnp.dot(design.T, covariates, preferred_element_type=jnp.float32)
     back = jnp.dot((onehot.astype(jnp.float32) * noise[:, None]).T, wide_cov, precision=HIGHEST)
     sums = sum_everywhere(jnp.concatenate([normal, back]))
 
-    want = jnp.concatenate(wanted)
     signs = 1 - 2 * sign_bits
     table = hadamard_rows(jnp.bitwise_and(want, HB - 1), HB)
     table = jnp.tile(table, (1, rows_dev // HB)) * signs[None, :]
@@ -233,10 +199,9 @@
     table = jnp.where((want // HB)[:, None] == block[None, :], table, 0).astype(jnp.bfloat16)
     local = jnp.dot(table, design, preferred_element_type=jnp.float32)
     local = rounded(local * (1.0 / math.sqrt(HB)))
-    local = [local[m * samp : (m + 1) * samp] for m in range(2**MIX_BITS)]
-    pieces = [local[0]] + [partner(local[m], "wide", m) for m in range(1, 2**MIX_BITS)]
-    rows, place = gather_rows(mix(pieces))
-    factor, inverse = factorize(rows, place, samp, math.sqrt(LEVELS / SKETCH))
+    sketch = mix(list(swap(local.reshape(mates, samp, cols), "wide", groups)))
+    sketch = share_all(share_all(sketch, "narrow"), "wide").reshape(-1, cols)
+    factor, inverse = factorize(sketch, math.sqrt(LEVELS / SKETCH))
 
     normal = sums[:cols].reshape(LEVELS, COV, COV)
     back = sums[cols:]

time: 131 us -> 153 us (1.17)
  waiting for transfers between devices: 18.3 us -> 36.5 us
  blocking collectives: 0 us -> 9.66 us
  starting transfers between devices: 34.3 us -> 24.7 us
  local copies, waits for them, and re-layouts: 1.52 us -> 4.94 us
    all_to_all x0 -> x6, waiting for transfers between devices: none -> 36.5 us  [swap(): return lax.all_to_all(value, axis, 0, 0, axis_index_groups=groups)]
    ppermute x38 -> x0, starting transfers between devices: 34.3 us -> none  [partner(): return lax.ppermute(value, axis, pairs)]
    all_to_all x0 -> x6, starting transfers between devices: none -> 24.7 us  [swap(): return lax.all_to_all(value, axis, 0, 0, axis_index_groups=groups)]
    ppermute x38 -> x0, waiting for transfers between devices: 18.3 us -> none  [partner(): return lax.ppermute(value, axis, pairs)]
    all_to_all x0 -> x1, blocking collectives: none -> 9.66 us  [swap(): return lax.all_to_all(value, axis, 0, 0, axis_index_groups=groups)]
    broadcast_in_dim x0 -> x5, local copies, waits for them, and re-layouts: none -> 3.69 us  [share_all(): return swap(jnp.broadcast_to(value, (count,) + value.shape), axis, groups)]
  transfers between devices with their start and end apart: 38 -> 6, of which waited for: 14 -> 5; matrix products, arithmetic and copies ran while one was open for 14% -> 13% of each run, Pallas kernels for 0% -> 0%
where the time goes in v3:
time: 153 us; the launch traced here: 152 us
  waiting for transfers between devices  36.5 us (24%)
  Pallas kernels  33.6 us (22%)
  starting transfers between devices  24.7 us (16%)
  other arithmetic  19.8 us (13%)
  matrix products  13 us (8%)
  between operations  10.3 us (7%)
  blocking collectives  9.66 us (6%)
  local copies, waits for them, and re-layouts  4.94 us (3%)
    all_to_all x6, waiting for transfers between devices, swap(): return lax.all_to_all(value, axis, 0, 0, axis_index_groups=groups)  36.5 us
    pallas_call x1, Pallas kernels, factorize(): pl.pallas_call(functools.partial(factor_kernel, ratio), out_shape=[jax.Sh...  33.6 us
    all_to_all x6, starting transfers between devices, swap(): return lax.all_to_all(value, axis, 0, 0, axis_index_groups=groups)  24.7 us
    mul x1, other arithmetic, body(): onehot.astype(jnp.bfloat16)[:, :, None] * covariates[:, None, :]  10.8 us
    all_to_all x1, blocking collectives, swap(): return lax.all_to_all(value, axis, 0, 0, axis_index_groups=groups)  9.66 us
    dot_general x4, matrix products, precondition(): steer = jnp.dot(inverse, vector, precision=HIGHEST)  3.93 us
    broadcast_in_dim x5, local copies, waits for them, and re-layouts, share_all(): return swap(jnp.broadcast_to(value, (count,) + value.shape), axis, groups)  3.69 us
  transfers between devices with their start and end apart: 6, of which 5 were waited for; matrix products, arithmetic and copies ran while one was open for 13% of the time, Pallas kernels for 0%

profile of v3, /device:TPU:0, one launch (start us, length us, event | category | flops | bytes accessed | tf_op | source)
XLA Modules:
  0.0 152.4 jit_solution(9848597906987909178)
XLA Ops:
  0.6 1.3 broadcast_in_dim.15
  1.9 5.2 %all-to-all-start = ((s32[8,1,32]{2,1,0:T(1,128)}), s32[8,1,32]{2,1,0:T(1,128)S(1)}, u32[]{:S(2)}, u32[]{:S(2)}) async-start(s32[8,1,32]{2,1,0:T(1,128)} %broadcast_in_dim.15), calls=%async_computation | async-start | bytes 8192 | tf_op jit(solution)/shard_map/all_to_all | solution.py:26
  7.1 0.7 multiply_subtract_fusion
  7.8 0.7 fusion.23
  8.5 0.0 copy-start
  8.5 0.3 copy.10
  8.8 1.4 fusion.21
  10.2 10.8 %broadcast_multiply_fusion = bf16[2048,4,128]{2,1,0:T(4,128)(2,1)S(1)} fusion(bf16[2048,128]{1,0:T(8,128)(2,1)} %param.6, bf16[2048,4]{1,0:T(8,128)(2,1)S(1)} %copy.10), kind=kLoop, calls=%fused_computation.13 | loop fusion | flops 1048576 | bytes 2637824 | tf_op jit(solution)/shard_map/mul | solution.py:185
  21.0 0.0 copy-done
  21.0 0.7 fusion.1
  21.8 0.7 select_maximum_fusion
  22.5 0.0 all-to-all-done
  22.5 4.2 %all-to-all-start.4 = ((f32[8,72,128]{2,1,0:T(8,128)}), f32[8,72,128]{2,1,0:T(8,128)S(1)}, u32[]{:S(2)}, u32[]{:S(2)}) async-start(f32[8,72,128]{2,1,0:T(8,128)} %bitcast.3), calls=%async_computation.4 | async-start | bytes 589824 | tf_op jit(solution)/shard_map/all_to_all | solution.py:26
  26.8 0.5 broadcast.277
  27.3 0.7 reduce.3
  27.9 0.1 reshape.289
  28.0 0.2 fusion.19
  28.2 0.9 select_convert_fusion
  29.1 0.3 copy.21
  29.4 1.4 fusion.13
  30.8 3.3 %all-to-all-done.4 = f32[8,72,128]{2,1,0:T(8,128)S(1)} async-done(((f32[8,72,128]{2,1,0:T(8,128)}), f32[8,72,128]{2,1,0:T(8,128)S(1)}, u32[]{:S(2)}, u32[]{:S(2)}) %all-to-all-start.4) | async-done | bytes 294944 | tf_op jit(solution)/shard_map/all_to_all | solution.py:26
  34.0 3.4 %all-to-all-start.1 = ((bf16[8,32,512]{2,1,0:T(8,128)(2,1)}), bf16[8,32,512]{2,1,0:T(8,128)(2,1)S(1)}, u32[]{:S(2)}, u32[]{:S(2)}) async-start(bf16[8,32,512]{2,1,0:T(8,128)(2,1)} %bitcast), calls=%async_computation.1 | async-start | bytes 524288 | tf_op jit(solution)/shard_map/all_to_all | solution.py:26
  37.5 6.8 %all-to-all-done.1 = bf16[8,32,512]{2,1,0:T(8,128)(2,1)S(1)} async-done(((bf16[8,32,512]{2,1,0:T(8,128)(2,1)}), bf16[8,32,512]{2,1,0:T(8,128)(2,1)S(1)}, u32[]{:S(2)}, u32[]{:S(2)}) %all-to-all-start.1) | async-done | bytes 262176 | tf_op jit(solution)/shard_map/all_to_all | solution.py:26
  44.3 0.7 broadcast_in_dim.35
  45.0 4.9 %all-to-all-start.5 = ((f32[4,72,128]{2,1,0:T(8,128)}), f32[4,72,128]{2,1,0:T(8,128)S(1)}, u32[]{:S(2)}, u32[]{:S(2)}) async-start(f32[4,72,128]{2,1,0:T(8,128)} %broadcast_in_dim.35), calls=%async_computation.5 | async-start | bytes 294912 | tf_op jit(solution)/shard_map/all_to_all | solution.py:26
  49.9 0.1 fusion.20
  50.0 5.9 %all-to-all-done.5 = f32[4,72,128]{2,1,0:T(8,128)S(1)} async-done(((f32[4,72,128]{2,1,0:T(8,128)}), f32[4,72,128]{2,1,0:T(8,128)S(1)}, u32[]{:S(2)}, u32[]{:S(2)}) %all-to-all-start.5) | async-done | bytes 147488 | tf_op jit(solution)/shard_map/all_to_all | solution.py:26
  55.8 0.7 broadcast_in_dim.17
  56.5 3.3 %all-to-all-start.2 = ((bf16[4,32,512]{2,1,0:T(8,128)(2,1)}), bf16[4,32,512]{2,1,0:T(8,128)(2,1)S(1)}, u32[]{:S(2)}, u32[]{:S(2)}) async-start(bf16[4,32,512]{2,1,0:T(8,128)(2,1)} %broadcast_in_dim.17), calls=%async_computation.2 | async-start | bytes 262144 | tf_op jit(solution)/shard_map/all_to_all | solution.py:26
  59.9 5.9 %all-to-all-done.2 = bf16[4,32,512]{2,1,0:T(8,128)(2,1)S(1)} async-done(((bf16[4,32,512]{2,1,0:T(8,128)(2,1)}), bf16[4,32,512]{2,1,0:T(8,128)(2,1)S(1)}, u32[]{:S(2)}, u32[]{:S(2)}) %all-to-all-start.2) | async-done | bytes 131104 | tf_op jit(solution)/shard_map/all_to_all | solution.py:26
  65.7 0.0 copy-start.3
  65.8 9.7 %all_to_all.36 = f32[8,72,128]{2,1,0:T(8,128)S(1)} all-to-all(f32[8,72,128]{2,1,0:T(8,128)S(1)} %broadcast_in_dim.36), channel_id=1, replica_groups=mesh['wide'=8,'narrow'=4] {'wide'}, dimensions={0} | all-to-all | bytes 589824 | tf_op jit(solution)/shard_map/all_to_all | solution.py:26
  75.4 1.1 broadcast_in_dim.34
  76.5 3.7 %all-to-all-start.3 = ((bf16[8,4,32,512]{3,2,1,0:T(8,128)(2,1)}), bf16[8,4,32,512]{3,2,1,0:T(8,128)(2,1)S(1)}, u32[]{:S(2)}, u32[]{:S(2)}) async-start(bf16[8,4,32,512]{3,2,1,0:T(8,128)(2,1)} %broadcast_in_dim.34), calls=%async_computation.3 | async-start | bytes 2097152 | tf_op jit(solution)/shard_map/all_to_all | solution.py:26
  80.3 0.0 copy-done.3
  80.3 0.5 fusion.41
  80.8 14.6 %all-to-all-done.3 = bf16[8,4,32,512]{3,2,1,0:T(8,128)(2,1)S(1)} async-done(((bf16[8,4,32,512]{3,2,1,0:T(8,128)(2,1)}), bf16[8,4,32,512]{3,2,1,0:T(8,128)(2,1)S(1)}, u32[]{:S(2)}, u32[]{:S(2)}) %all-to-all-start.3) | async-done | bytes 1048608 | tf_op jit(solution)/shard_map/all_to_all | solution.py:26
  95.4 33.6 %factor.1 = (f32[512,512]{1,0:T(8,128)}, f32[512,512]{1,0:T(8,128)S(1)}) custom-call(bf16[1024,512]{1,0:T(8,128)(2,1)S(1)} %bitcast.130), custom_call_target="tpu_custom_call" | custom-call | tf_op jit(solution)/shard_map/factor/pallas_call | solution.py:158
  129.0 1.0 fusion.42
  130.0 0.6 fusion.37
  130.6 0.5 fusion.28
  131.1 0.6 multiply_reduce_fusion.6
  133.1 1.0 fusion.43
  134.1 0.6 fusion.35
  134.7 0.6 multiply_reduce_fusion.5
  136.6 0.5 fusion.44
  137.1 0.6 multiply_reduce_fusion.4
  139.1 1.0 fusion.45
  140.1 0.0 copy-start.1
  140.1 0.6 fusion.33
  140.7 0.6 multiply_reduce_fusion.3
  142.7 0.5 fusion.46
  143.2 0.6 multiply_reduce_fusion.2
  145.2 1.0 fusion.47
  146.1 0.6 fusion.31
  146.8 0.6 multiply_reduce_fusion.1
  148.7 0.5 fusion.48
  149.2 0.6 multiply_reduce_fusion
  151.2 0.0 copy-done.1
  151.2 0.0 copy-start.4
  151.2 0.5 fusion.16
  151.8 0.0 copy-done.2
  151.8 0.6 add.82
  152.4 0.0 copy-done.4
  (16 shorter events, 0.1 us)
Async XLA Ops:
  1.9 20.7 %all-to-all-start = ((s32[8,1,32]{2,1,0:T(1,128)}), s32[8,1,32]{2,1,0:T(1,128)S(1)}, u32[]{:S(2)}, u32[]{:S(2)}) async-start(s32[8,1,32]{2,1,0:T(1,128)} %broadcast_in_dim.15), calls=%async_computation | async-start | bytes 8192 | tf_op jit(solution)/shard_map/all_to_all | solution.py:26
  8.5 12.6 %copy-start = (bf16[2048,128]{1,0:T(8,128)(2,1)S(1)}, bf16[2048,128]{1,0:T(8,128)(2,1)}, u32[]{:S(2)}) copy-start(bf16[2048,128]{1,0:T(8,128)(2,1)} %param.6) | copy-start | bytes 1572868
  22.5 11.5 %all-to-all-start.4 = ((f32[8,72,128]{2,1,0:T(8,128)}), f32[8,72,128]{2,1,0:T(8,128)S(1)}, u32[]{:S(2)}, u32[]{:S(2)}) async-start(f32[8,72,128]{2,1,0:T(8,128)} %bitcast.3), calls=%async_computation.4 | async-start | bytes 589824 | tf_op jit(solution)/shard_map/all_to_all | solution.py:26
  34.0 10.3 %all-to-all-start.1 = ((bf16[8,32,512]{2,1,0:T(8,128)(2,1)}), bf16[8,32,512]{2,1,0:T(8,128)(2,1)S(1)}, u32[]{:S(2)}, u32[]{:S(2)}) async-start(bf16[8,32,512]{2,1,0:T(8,128)(2,1)} %bitcast), calls=%async_computation.1 | async-start | bytes 524288 | tf_op jit(solution)/shard_map/all_to_all | solution.py:26
  45.0 10.8 %all-to-all-start.5 = ((f32[4,72,128]{2,1,0:T(8,128)}), f32[4,72,128]{2,1,0:T(8,128)S(1)}, u32[]{:S(2)}, u32[]{:S(2)}) async-start(f32[4,72,128]{2,1,0:T(8,128)} %broadcast_in_dim.35), calls=%async_computation.5 | async-start | bytes 294912 | tf_op jit(solution)/shard_map/all_to_all | solution.py:26
  56.5 9.2 %all-to-all-start.2 = ((bf16[4,32,512]{2,1,0:T(8,128)(2,1)}), bf16[4,32,512]{2,1,0:T(8,128)(2,1)S(1)}, u32[]{:S(2)}, u32[]{:S(2)}) async-start(bf16[4,32,512]{2,1,0:T(8,128)(2,1)} %broadcast_in_dim.17), calls=%async_computation.2 | async-start | bytes 262144 | tf_op jit(solution)/shard_map/all_to_all | solution.py:26
  65.7 14.5 %copy-start.3 = (f32[512]{0:T(512)S(1)}, f32[512]{0:T(512)}, u32[]{:S(2)}) copy-start(f32[512]{0:T(512)} %param.10) | copy-start | bytes 6148
  76.5 18.9 %all-to-all-start.3 = ((bf16[8,4,32,512]{3,2,1,0:T(8,128)(2,1)}), bf16[8,4,32,512]{3,2,1,0:T(8,128)(2,1)S(1)}, u32[]{:S(2)}, u32[]{:S(2)}) async-start(bf16[8,4,32,512]{3,2,1,0:T(8,128)(2,1)} %broadcast_in_dim.34), calls=%async_computation.3 | async-start | bytes 2097152 | tf_op jit(solution)/shard_map/all_to_all | solution.py:26
  140.1 11.1 %copy-start.1 = (s32[2048]{0:T(1024)S(1)}, s32[2048]{0:T(1024)}, u32[]{:S(2)}) copy-start(s32[2048]{0:T(1024)} %param.7) | copy-start | bytes 24580
  140.1 11.7 %copy-start.2 = (f32[2048]{0:T(1024)S(1)}, f32[2048]{0:T(1024)}, u32[]{:S(2)}) copy-start(f32[2048]{0:T(1024)} %param.11) | copy-start | bytes 24580
  151.2 1.2 copy-start.4

commit v4 on v3

v4 whole, which is shorter than its diff:
```python
import functools
import math

import jax
import jax.numpy as jnp
from jax import lax
from jax.experimental import pallas as pl
from jax.experimental.pallas import tpu as pltpu
from jax.sharding import PartitionSpec as P

COV = 128
LEVELS = 4
HB = 256
SKETCH = 1024
ITERS = 4
MIX_BITS = 3
MATES = 2**MIX_BITS

half_root = math.sqrt(0.5)
HIGHEST = lax.Precision.HIGHEST
f32, bf16 = jnp.float32, jnp.bfloat16
SUB, LANE = 8, 128
PACK = 16
COUNT = 4
NT = (((1,), (1,)), ((), ()))
VMEM = pl.BlockSpec(memory_space=pltpu.VMEM)
SMEM = pl.BlockSpec(memory_space=pltpu.SMEM)


def partner(value, axis, mask):
    pairs = [(source, source ^ mask) for source in range(lax.axis_size(axis))]
    return lax.ppermute(value, axis, pairs)


def whole_up(number, unit):
    return -(-number // unit) * unit


def eye():
    rows = lax.broadcasted_iota(jnp.int32, (LANE, LANE), 0)
    lanes = lax.broadcasted_iota(jnp.int32, (LANE, LANE), 1)
    return rows, lanes, rows == lanes


def to_column(row, same):
    return jnp.sum(jnp.where(same, row, 0.0), axis=1, keepdims=True)


def to_row(column, same):
    return jnp.sum(jnp.where(same, column, 0.0), axis=0, keepdims=True)


def split(value):
    parts = []
    for _ in range(3):
        parts.append(value.astype(bf16))
        value = value - parts[-1].astype(f32)
    return parts


def tree_sum(values):
    while len(values) > 1:
        values = [left + right for left, right in zip(values[0::2], values[1::2])]
    return values[0]


def put_sums(ref, start, share, extra):
    rows = share.shape[0]
    for k, part in enumerate(split(share)):
        ref[start : start + rows, k * LANE : (k + 1) * LANE] = part
    tail = jnp.zeros((rows - 3 * SUB, LANE), bf16)
    ref[start : start + rows, 3 * LANE :] = jnp.concatenate(split(extra) + [tail])


def take_sums(ref, start, rows):
    block = ref[start : start + rows, :].astype(f32)
    share = block[:, :LANE] + block[:, LANE : 2 * LANE] + block[:, 2 * LANE : 3 * LANE]
    tail = block[:, 3 * LANE :]
    return share, tail[:SUB] + tail[SUB : 2 * SUB] + tail[2 * SUB : 3 * SUB]


def local_kernel(samp, share, index_ref, want_ref, cov_ref, codes_ref, signs_ref, noise_ref, *refs):
    out_refs, (design, table, packed) = refs[:-3], refs[-3:]
    chunks = codes_ref.shape[0]
    rows, lanes, same = eye()
    zero = jnp.zeros((LANE, LANE), f32)

    masks, halves = [], []
    for c in range(want_ref.shape[0]):
        want = to_column(want_ref[c : c + 1, :].astype(f32), same).astype(jnp.int32)
        masks.append(jnp.right_shift(want, HB.bit_length() - 1))
        line = []
        for h in range(HB // LANE):
            common = jnp.bitwise_and(want, lanes + h * LANE)
            for shift in (4, 2, 1):
                common = jnp.bitwise_xor(common, jnp.right_shift(common, shift))
            line.append((1 - 2 * jnp.bitwise_and(common, 1)).astype(f32))
        halves.append(line)

    for r in range(chunks):
        here = slice(r * LANE, (r + 1) * LANE)
        code = codes_ref[r : r + 1, :]
        turned = cov_ref[here, :].astype(f32).T
        for level in range(LEVELS):
            design[level * LANE : (level + 1) * LANE, here] = jnp.where(code == level, turned, zero).astype(bf16)
        noise = jnp.concatenate([noise_ref[r : r + 1, :]] * LEVELS + [jnp.zeros((PACK - LEVELS, LANE), f32)])
        level = lax.broadcasted_iota(jnp.int32, (PACK, LANE), 0)
        noise = jnp.where(code == level, noise, 0.0)
        for k, part in enumerate(split(noise)):
            design[LEVELS * LANE + k * PACK : LEVELS * LANE + (k + 1) * PACK, here] = part
        sign = (1 - 2 * signs_ref[r : r + 1, :]).astype(f32)
        block, h = divmod(r * LANE, HB)
        for c, (mask, line) in enumerate(zip(masks, halves)):
            value = jnp.where(mask == block, line[h // LANE] * sign, zero)
            table[c * LANE : (c + 1) * LANE, here] = value.astype(bf16)

    sums = jnp.dot(design[...], cov_ref[...], preferred_element_type=f32)
    normal = [sums[level * LANE : (level + 1) * LANE] for level in range(LEVELS)]
    back = sums[LEVELS * LANE :]
    back = back[:SUB] + back[PACK : PACK + SUB] + back[2 * PACK : 2 * PACK + SUB]
    extra = [jnp.sum(jnp.where(same, normal[level], 0.0), axis=0, keepdims=True) for level in (1, 3)]
    extra = jnp.concatenate([back[:LEVELS]] + extra + [jnp.zeros((2, LANE), f32)])
    for pair in range(LEVELS // 2):
        packed[pair * LANE : (pair + 1) * LANE, :] = jnp.where(rows >= lanes, normal[2 * pair], normal[2 * pair + 1])
    if packed.shape[0] > 2 * LANE:
        packed[2 * LANE :, :] = jnp.zeros((packed.shape[0] - 2 * LANE, LANE), f32)

    local = lax.dot_general(table[...], design[: LEVELS * LANE, :], NT, preferred_element_type=f32)
    local = (local * (1.0 / math.sqrt(HB))).astype(bf16)
    for m, out_ref in enumerate(out_refs):
        start = 0
        if m < MATES:
            out_ref[:samp, :] = local[m * samp : (m + 1) * samp]
            start = samp
        at = pl.multiple_of(jnp.bitwise_xor(index_ref[0], m) * share, share)
        put_sums(out_ref, start, packed[pl.ds(at, share), :], extra)


def mix_kernel(samp, share, index_ref, *refs):
    piece_refs, out_ref = refs[:-1], refs[-1]
    pieces = [ref[:samp, :].astype(f32) for ref in piece_refs[:MATES]]
    for place in range(MIX_BITS):
        bit = jnp.bitwise_and(jnp.right_shift(index_ref[0], place), 1)
        sign = (1 - 2 * bit).astype(f32)
        pieces = [
            ((sign * own + other) * half_root).astype(bf16).astype(f32)
            for own, other in zip(pieces[0::2], pieces[1::2])
        ]
    out_ref[:samp, :] = pieces[0].astype(bf16)
    sums = [take_sums(ref, samp if m < MATES else 0, share) for m, ref in enumerate(piece_refs)]
    put_sums(out_ref, samp, tree_sum([one for one, _ in sums]), tree_sum([one for _, one in sums]))


def stack_kernel(samp, share, index_ref, *refs):
    piece_refs, out_ref = refs[:-1], refs[-1]
    for m, ref in enumerate(piece_refs):
        at = pl.multiple_of(jnp.bitwise_xor(index_ref[1], m) * samp, samp)
        out_ref[pl.ds(at, samp), :] = ref[:samp, :]
    sums = [take_sums(ref, samp, share) for ref in piece_refs]
    put_sums(
        out_ref, samp * len(piece_refs), tree_sum([one for one, _ in sums]), tree_sum([one for _, one in sums])
    )


def spread(value):
    return jnp.broadcast_to(value, (SUB, LANE))


def eliminate(tiles, count):
    lane = lax.broadcasted_iota(jnp.int32, (SUB, LANE), 1)
    sub = lax.broadcasted_iota(jnp.int32, (SUB, LANE), 0)
    tiles = list(tiles)
    scales = [None] * len(tiles)
    for first in range(0, LANE, count):
        tile, offset = divmod(first, SUB)
        window = (lane >= first) & (lane < first + count)
        columns = [
            [spread(tiles[i][:, first + k : first + k + 1]) for k in range(count)] for i in range(tile, len(tiles))
        ]
        pivot = [
            [spread(columns[0][m][offset + k : offset + k + 1, :]) if m >= k else None for m in range(count)]
            for k in range(count)
        ]
        rows = []
        for k in range(count):
            row = spread(tiles[tile][offset + k : offset + k + 1, :])
            row = jnp.where(window, 0.0, row)
            rows.append(jnp.where(lane == first + k, 1.0, row))
        inverse, ratio = [], [[None] * count for _ in range(count)]
        for k in range(count):
            inverse.append(1.0 / pivot[k][k])
            for m in range(k + 1, count):
                ratio[k][m] = pivot[k][m] * inverse[k]
                for n in range(m, count):
                    pivot[m][n] = pivot[m][n] - ratio[k][m] * pivot[k][n]
                rows[m] = rows[m] - ratio[k][m] * rows[k]
        steps = [None] * count
        for k in reversed(range(count)):
            steps[k] = rows[k] * inverse[k]
            for m in range(k + 1, count):
                steps[k] = steps[k] - ratio[k][m] * steps[m]
        old = tiles[tile]
        scale = scales[tile]
        for i in range(tile, len(tiles)):
            new = jnp.where(window, 0.0, tiles[i])
            for k in range(count):
                new = new - columns[i - tile][k] * steps[k]
            tiles[i] = new
        fixed = old
        if offset + count < SUB:
            fixed = jnp.where(sub >= offset + count, tiles[tile], old)
        for k in range(count):
            kept = rows[k]
            for m in range(k, count):
                kept = jnp.where(lane == first + m, pivot[k][m], kept)
            root = lax.rsqrt(pivot[k][k])
            fixed = jnp.where(sub == offset + k, kept, fixed)
            scale = root if scale is None else jnp.where(sub == offset + k, root, scale)
        tiles[tile] = fixed
        scales[tile] = scale
    return tiles, scales


def factor_kernel(ratio, apart, rows_in, index_ref, *refs):
    piece_refs, (factor_ref, inverse_ref, sketch, work, line) = refs[:-5], refs[-5:]
    cols = work.shape[0]
    for mask, ref in zip(apart, piece_refs):
        at = pl.multiple_of(jnp.bitwise_xor(index_ref[0], mask) * rows_in, rows_in)
        sketch[pl.ds(at, rows_in), :] = ref[:rows_in, :]
    rows = sketch[...]
    work[...] = lax.dot_general(rows, rows, (((0,), (0,)), ((), ())), preferred_element_type=f32)

    row_in = lax.broadcasted_iota(jnp.int32, (LANE, LANE), 0)
    lane_in = lax.broadcasted_iota(jnp.int32, (LANE, LANE), 1)
    lane_all = lax.broadcasted_iota(jnp.int32, (LANE, cols), 1)
    row_all = lax.broadcasted_iota(jnp.int32, (cols, LANE), 0)

    def block_step(block, _):
        base = pl.multiple_of(block * LANE, LANE)
        here = pl.ds(base, LANE)
        tiles = [work[pl.ds(base + SUB * i, SUB), here] for i in range(LANE // SUB)]
        tiles, scales = eliminate(tiles, COUNT)
        scale = jnp.concatenate(scales)
        inner = jnp.concatenate(tiles) * scale
        upper = jnp.where(lane_in >= row_in, inner, 0.0)
        lower = jnp.where(lane_in < row_in, inner, jnp.where(lane_in == row_in, scale, 0.0))
        line[...] = jnp.dot(lower, work[here, :], precision=HIGHEST, preferred_element_type=f32)
        whole = line[...]
        factor_ref[here, :] = jnp.where(lane_all >= base, whole, 0.0) * ratio
        factor_ref[here, here] = upper * ratio
        inverse_ref[here, :] = jnp.where(lane_all < base, whole, 0.0)
        inverse_ref[here, here] = lower

        @pl.when(block < cols // LANE - 1)
        def _():
            line[:, here] = lower
            steps = jnp.dot(lower.T, line[...], precision=HIGHEST, preferred_element_type=f32)
            panel = jnp.where(row_all >= base + LANE, work[:, here], 0.0)
            work[:, here] = jnp.where(row_all >= base + LANE, 0.0, work[:, here])
            work[...] -= jnp.dot(panel, steps, precision=HIGHEST, preferred_element_type=f32)

        return 0

    lax.fori_loop(0, cols // LANE, block_step, 0)


def solve_kernel(apart, rows_in, share, index_ref, inverse_ref, effects_ref, cov_ref, codes_ref, noise_ref, *refs):
    piece_refs, (solved_ref, resid_ref, packed, kernel) = refs[:-4], refs[-4:]
    rows, lanes, same = eye()
    extra = None
    for mask, ref in zip(apart, piece_refs):
        at = pl.multiple_of(jnp.bitwise_xor(index_ref[0], mask) * share, share)
        packed[pl.ds(at, share), :], more = take_sums(ref, rows_in, share)
        extra = more if extra is None else extra
    normal = []
    for pair in range(LEVELS // 2):
        both = packed[pair * LANE : (pair + 1) * LANE, :]
        turned = both.T
        normal.append(jnp.where(rows >= lanes, both, turned))
        diagonal = jnp.where(same, extra[LEVELS + pair : LEVELS + pair + 1], turned)
        normal.append(jnp.where(rows < lanes, both, diagonal))

    inverse = inverse_ref[...]
    for level in range(LEVELS):
        here = slice(level * LANE, (level + 1) * LANE)
        kernel[:, here] = jnp.dot(inverse[:, here], normal[level], precision=HIGHEST, preferred_element_type=f32)
    kernel[...] = lax.dot_general(kernel[...], inverse, NT, precision=HIGHEST, preferred_element_type=f32)
    square = kernel[...]

    gradient = []
    for level in range(LEVELS):
        column = to_column(effects_ref[level : level + 1, :], same)
        gradient.append(jnp.sum(normal[level] * column, axis=0, keepdims=True) + extra[level : level + 1])
    gradient = jnp.concatenate(gradient, axis=1)
    steer_col = jnp.sum(inverse * gradient, axis=1, keepdims=True)
    steer_row = jnp.concatenate(
        [to_row(steer_col[level * LANE : (level + 1) * LANE], same) for level in range(LEVELS)], axis=1
    )
    go_row, go_col = steer_row, steer_col
    gamma = jnp.sum(steer_row * steer_row, axis=1, keepdims=True)
    solved_col = jnp.zeros_like(steer_col)
    for step in range(ITERS):
        image_row = jnp.sum(square * go_col, axis=0, keepdims=True)
        alpha = gamma / jnp.sum(go_row * image_row, axis=1, keepdims=True)
        solved_col = solved_col + alpha * go_col
        if step == ITERS - 1:
            break
        image_col = jnp.sum(square * go_row, axis=1, keepdims=True)
        steer_row = steer_row - alpha * image_row
        steer_col = steer_col - alpha * image_col
        gamma_new = jnp.sum(steer_row * steer_row, axis=1, keepdims=True)
        go_row = steer_row + gamma_new / gamma * go_row
        go_col = steer_col + gamma_new / gamma * go_col
        gamma = gamma_new
    solved = jnp.sum(inverse * solved_col, axis=0, keepdims=True)
    solved = jnp.concatenate([solved[:, level * LANE : (level + 1) * LANE] for level in range(LEVELS)])
    solved_ref[...] = solved

    left = jnp.concatenate([effects_ref[...] - solved, jnp.zeros((PACK - LEVELS, LANE), f32)])
    values = jnp.zeros((SUB, cov_ref.shape[0]), f32)
    for part in split(left):
        values = values + lax.dot_general(part, cov_ref[...], NT, preferred_element_type=f32)[:SUB]
    for r in range(codes_ref.shape[0]):
        code = codes_ref[r : r + 1, :]
        total = noise_ref[r : r + 1, :]
        for level in range(LEVELS):
            total = total + jnp.where(code == level, values[level : level + 1, r * LANE : (r + 1) * LANE], 0.0)
        resid_ref[r : r + 1, :] = total


def call(kernel, name, outs, scratch, index, *operands):
    return pl.pallas_call(
        kernel,
        out_shape=[jax.ShapeDtypeStruct(shape, dtype) for shape, dtype in outs],
        in_specs=[SMEM] + [VMEM] * len(operands),
        out_specs=[VMEM] * len(outs),
        scratch_shapes=[pltpu.VMEM(shape, dtype) for shape, dtype in scratch],
        compiler_params=pltpu.CompilerParams(vmem_limit_bytes=40 * 2**20),
        name=name,
    )(index, *operands)


def body(covariates, level_codes, sign_bits, sample_rows, effects, noise):
    wide, narrow = lax.axis_size("wide"), lax.axis_size("narrow")
    index = jnp.stack([lax.axis_index("wide"), lax.axis_index("narrow")]).astype(jnp.int32)
    rows_dev, cols = covariates.shape[0], LEVELS * COV
    samp = whole_up(sample_rows.shape[0], PACK)
    share = whole_up(max(2 * LANE // wide, 3 * SUB), PACK)
    sample_rows = jnp.pad(sample_rows, (0, samp - sample_rows.shape[0]), constant_values=-1)
    codes, signs, noise = [array.reshape(-1, LANE) for array in (level_codes, sign_bits, noise)]
    effects = effects.reshape(LEVELS, COV)

    want = jnp.concatenate([sample_rows] + [partner(sample_rows, "wide", m) for m in range(1, MATES)])
    pieces = call(
        functools.partial(local_kernel, samp, share),
        "local",
        [((samp * (m < MATES) + share, cols), bf16) for m in range(wide)],
        [
            ((cols + 3 * PACK, rows_dev), bf16),
            ((MATES * samp, rows_dev), bf16),
            ((share * wide, LANE), f32),
        ],
        index,
        want.reshape(-1, LANE),
        covariates,
        codes,
        signs,
        noise,
    )
    pieces = [pieces[0]] + [partner(pieces[m], "wide", m) for m in range(1, wide)]
    (piece,) = call(
        functools.partial(mix_kernel, samp, share), "mix", [((samp + share, cols), bf16)], [], index, *pieces
    )
    pieces = [piece] + [partner(piece, "narrow", m) for m in range(1, narrow)]
    rows_in = samp * narrow
    (piece,) = call(
        functools.partial(stack_kernel, samp, share), "stack", [((rows_in + share, cols), bf16)], [], index, *pieces
    )
    pieces = [piece] + [partner(piece, "wide", m) for m in range(2, wide, 2)]
    pieces += [partner(piece, "wide", 1) for piece in pieces]
    apart = [2 * m + core for core in range(2) for m in range(wide // 2)]
    factor, inverse = call(
        functools.partial(factor_kernel, math.sqrt(LEVELS / SKETCH), apart, rows_in),
        "factor",
        [((cols, cols), f32)] * 2,
        [((rows_in * wide, cols), bf16), ((cols, cols), f32), ((LANE, cols), f32)],
        index,
        *pieces,
    )
    solved, resid = call(
        functools.partial(solve_kernel, apart, rows_in, share),
        "solve",
        [((LEVELS, COV), f32), (codes.shape, f32)],
        [((share * wide, LANE), f32), ((cols, cols), f32)],
        index,
        inverse,
        effects,
        covariates,
        codes,
        noise,
        *pieces,
    )
    return solved.reshape(-1), resid.reshape(-1), factor


def solution(mesh):
    return jax.shard_map(
        body,
        mesh=mesh,
        in_specs=(
            P(("wide", "narrow"), None),
            P(("wide", "narrow")),
            P(("wide", "narrow")),
            P(("wide", "narrow")),
            P(),
            P(("wide", "narrow")),
        ),
        out_specs=(P(), P(("wide", "narrow")), P()),
        check_vma=False,
    )
```

time: 153 us -> 90.5 us (0.59)
  other arithmetic: 19.8 us -> 0.08 us
  waiting for transfers between devices: 36.5 us -> 21.6 us
  matrix products: 13 us -> 0 us
  Pallas kernels: 33.6 us -> 43.7 us
  blocking collectives: 9.66 us -> 0 us
  between operations: 10.3 us -> 0.71 us
  starting transfers between devices: 24.7 us -> 21.8 us
  local copies, waits for them, and re-layouts: 4.94 us -> 2.41 us
    all_to_all x6 -> x0, waiting for transfers between devices: 36.5 us -> none  [swap(): return lax.all_to_all(value, axis, 0, 0, axis_index_groups=groups)]
    all_to_all x6 -> x0, starting transfers between devices: 24.7 us -> none  [swap(): return lax.all_to_all(value, axis, 0, 0, axis_index_groups=groups)]
    ppermute x0 -> x24, starting transfers between devices: none -> 21.8 us  [partner(): return lax.ppermute(value, axis, pairs)]
    ppermute x0 -> x24, waiting for transfers between devices: none -> 21.6 us  [partner(): return lax.ppermute(value, axis, pairs)]
    dot_general x17 -> x0, matrix products: 13 us -> none  [the longest x4 3.93 us: precondition(): steer = jnp.dot(inverse, vector, precision=HIGHEST)]
    mul x1 -> x0, other arithmetic: 10.8 us -> none  [body(): onehot.astype(jnp.bfloat16)[:, :, None] * covariates[:, None, :]]
    pallas_call x1 -> x5, Pallas kernels: 33.6 us -> 43.7 us  [call(): pl.pallas_call(kernel, out_shape=[jax.ShapeDtypeStruct(shape, dtype) for...]
    all_to_all x1 -> x0, blocking collectives: 9.66 us -> none  [swap(): return lax.all_to_all(value, axis, 0, 0, axis_index_groups=groups)]
  transfers between devices with their start and end apart: 6 -> 24, of which waited for: 5 -> 13; matrix products, arithmetic and copies ran while one was open for 13% -> 0% of each run, Pallas kernels for 0% -> 0%
where the time goes in v4:
time: 90.5 us; the launch traced here: 90.3 us
  Pallas kernels  43.7 us (48%)
  starting transfers between devices  21.8 us (24%)
  waiting for transfers between devices  21.6 us (24%)
  local copies, waits for them, and re-layouts  2.41 us (3%)
    pallas_call x5, Pallas kernels, call(): pl.pallas_call(kernel, out_shape=[jax.ShapeDtypeStruct(shape, dtype) for...  43.7 us
    ppermute x24, starting transfers between devices, partner(): return lax.ppermute(value, axis, pairs)  21.8 us
    ppermute x24, waiting for transfers between devices, partner(): return lax.ppermute(value, axis, pairs)  21.6 us
    unnamed x14, local copies, waits for them, and re-layouts  2.33 us
  transfers between devices with their start and end apart: 24, of which 13 were waited for; matrix products, arithmetic and copies ran while one was open for 0% of the time, Pallas kernels for 0%

profile of v4, /device:TPU:0, one launch (start us, length us, event | category | flops | bytes accessed | tf_op | source)
XLA Modules:
  0.0 90.3 jit_solution(10249986178450401578)
XLA Ops:
  0.6 4.0 %collective-permute-start.5 = (s32[32]{0:T(128)}, s32[32]{0:T(128)S(1)}, u32[]{:S(2)}, u32[]{:S(2)}) collective-permute-start(s32[32]{0:T(128)} %param.9), channel_id=1, source_target_pairs={{0,24},{4,28},{8,16},{12,20},{16,8},{20,12},{24,0},{28,4},{1,25},{... | collective-permute-start | bytes 392 | tf_op jit(solution)/shard_map/ppermute | solution.py:32
  4.6 0.0 collective-permute-start.4
  4.6 1.2 %collective-permute-start.3 = (s32[32]{0:T(128)}, s32[32]{0:T(128)S(1)}, u32[]{:S(2)}, u32[]{:S(2)}) collective-permute-start(s32[32]{0:T(128)} %param.9), channel_id=1, source_target_pairs={{0,16},{4,20},{8,24},{12,28},{16,0},{20,4},{24,8},{28,12},{1,17},{... | collective-permute-start | bytes 392 | tf_op jit(solution)/shard_map/ppermute | solution.py:32
  5.8 0.8 collective-permute-start.2
  6.6 1.5 %collective-permute-start.1 = (s32[32]{0:T(128)}, s32[32]{0:T(128)S(1)}, u32[]{:S(2)}, u32[]{:S(2)}) collective-permute-start(s32[32]{0:T(128)} %param.9), channel_id=1, source_target_pairs={{0,8},{4,12},{8,0},{12,4},{16,24},{20,28},{24,16},{28,20},{1,9},{5... | collective-permute-start | bytes 392 | tf_op jit(solution)/shard_map/ppermute | solution.py:32
  8.1 0.1 pad_add_fusion.index_ref
  8.2 0.0 collective-permute-done.5
  8.2 0.6 copy-done.6
  8.8 0.0 collective-permute-start
  8.8 0.0 collective-permute-done.4
  8.8 0.5 collective-permute-start.6
  9.3 0.0 collective-permute-done.3
  9.3 0.0 collective-permute-done.2
  9.3 1.0 %collective-permute-done.1 = s32[32]{0:T(128)S(1)} collective-permute-done((s32[32]{0:T(128)}, s32[32]{0:T(128)S(1)}, u32[]{:S(2)}, u32[]{:S(2)}) %collective-permute-start.1) | collective-permute-done | bytes 160 | tf_op jit(solution)/shard_map/ppermute | solution.py:32
  10.3 0.0 collective-permute-done
  10.3 2.4 %collective-permute-done.6 = s32[32]{0:T(128)S(1)} collective-permute-done((s32[32]{0:T(128)S(1)}, s32[32]{0:T(128)S(1)}, u32[]{:S(2)}, u32[]{:S(2)}) %collective-permute-start.6) | collective-permute-done | bytes 160 | tf_op jit(solution)/shard_map/ppermute | solution.py:32
  12.6 0.1 concatenate.3
  12.7 0.0 copy-done.4
  12.7 0.0 copy-done.2
  12.7 0.0 copy-done.3
  12.7 0.0 copy-start
  12.8 1.0 %copy-done = bf16[2048,128]{1,0:T(8,128)(2,1)S(1)} copy-done((bf16[2048,128]{1,0:T(8,128)(2,1)S(1)}, bf16[2048,128]{1,0:T(8,128)(2,1)}, u32[]{:S(2)}) %copy-start) | copy-done | bytes 524312
  13.8 2.5 %local.1 = (bf16[64,512]{1,0:T(8,128)(2,1)S(1)}, bf16[64,512]{1,0:T(8,128)(2,1)S(1)}, bf16[64,512]{1,0:T(8,128)(2,1)S(1)}, bf16[64,512]{1,0:T(8,128)(2,1)S(1)}, ...) custom-call(s32[2]{0:T(128)S(1)} %pad_add_fusion.index_ref, ...), custom_call_target="tpu_custom_call" | custom-call | tf_op jit(solution)/shard_map/local/pallas_call | solution.py:332
  16.3 0.6 collective-permute-start.7
  16.9 0.5 collective-permute-start.8
  17.4 0.9 collective-permute-start.9
  18.3 0.5 collective-permute-start.10
  18.8 1.6 %collective-permute-start.11 = (bf16[64,512]{1,0:T(8,128)(2,1)S(1)}, bf16[64,512]{1,0:T(8,128)(2,1)S(1)}, u32[]{:S(2)}, u32[]{:S(2)}) collective-permute-start(bf16[64,512]{1,0:T(8,128)(2,1)S(1)} %get-tuple-element.20), channel_id=1, source_target_pairs={{0,20},{4,16},{8,28},{12,24},{16,4},{20,0},{24,12},{28,8},{1,21},{... | collective-permute-start | bytes 196616 | tf_op jit(solution)/shard_map/ppermute | solution.py:32
  20.4 0.0 collective-permute-done.7.refs_1_
  20.4 0.4 collective-permute-start.12
  20.8 1.0 %collective-permute-done.8.refs_2_ = bf16[64,512]{1,0:T(8,128)(2,1)S(1)} collective-permute-done((bf16[64,512]{1,0:T(8,128)(2,1)S(1)}, bf16[64,512]{1,0:T(8,128)(2,1)S(1)}, u32[]{:S(2)}, u32[]{:S(2)}) %collective-permute-start.8) | collective-permute-done | bytes 65568 | tf_op jit(solution)/shard_map/ppermute | solution.py:32
  21.8 0.9 collective-permute-start.13
  22.7 0.0 collective-permute-done.9.refs_3_
  22.7 0.6 collective-permute-done.10.refs_4_
  23.3 1.6 %collective-permute-done.11.refs_5_ = bf16[64,512]{1,0:T(8,128)(2,1)S(1)} collective-permute-done((bf16[64,512]{1,0:T(8,128)(2,1)S(1)}, bf16[64,512]{1,0:T(8,128)(2,1)S(1)}, u32[]{:S(2)}, u32[]{:S(2)}) %collective-permute-start.11) | collective-permute-done | bytes 65568 | tf_op jit(solution)/shard_map/ppermute | solution.py:32
  24.9 0.7 collective-permute-done.12.refs_6_
  25.6 1.4 %collective-permute-done.13.refs_7_ = bf16[64,512]{1,0:T(8,128)(2,1)S(1)} collective-permute-done((bf16[64,512]{1,0:T(8,128)(2,1)S(1)}, bf16[64,512]{1,0:T(8,128)(2,1)S(1)}, u32[]{:S(2)}, u32[]{:S(2)}) %collective-permute-start.13) | collective-permute-done | bytes 65568 | tf_op jit(solution)/shard_map/ppermute | solution.py:32
  27.0 0.7 mix.1.refs_0_
  27.7 3.7 %collective-permute-start.16 = (bf16[64,512]{1,0:T(8,128)(2,1)S(1)}, bf16[64,512]{1,0:T(8,128)(2,1)S(1)}, u32[]{:S(2)}, u32[]{:S(2)}) collective-permute-start(bf16[64,512]{1,0:T(8,128)(2,1)S(1)} %mix.1.refs_0_), channel_id=1, source_target_pairs={{0,3},{1,2},{2,1},{3,0},{4,7},{5,6},{6,5},{7,4},{8,11},{9,10},{10,... | collective-permute-start | bytes 196616 | tf_op jit(solution)/shard_map/ppermute | solution.py:32
  31.4 0.0 collective-permute-start.15
  31.4 0.8 collective-permute-start.14
  32.1 2.0 %collective-permute-done.16.refs_3_ = bf16[64,512]{1,0:T(8,128)(2,1)S(1)} collective-permute-done((bf16[64,512]{1,0:T(8,128)(2,1)S(1)}, bf16[64,512]{1,0:T(8,128)(2,1)S(1)}, u32[]{:S(2)}, u32[]{:S(2)}) %collective-permute-start.16) | collective-permute-done | bytes 65568 | tf_op jit(solution)/shard_map/ppermute | solution.py:32
  34.1 3.1 %collective-permute-done.15.refs_2_ = bf16[64,512]{1,0:T(8,128)(2,1)S(1)} collective-permute-done((bf16[64,512]{1,0:T(8,128)(2,1)S(1)}, bf16[64,512]{1,0:T(8,128)(2,1)S(1)}, u32[]{:S(2)}, u32[]{:S(2)}) %collective-permute-start.15) | collective-permute-done | bytes 65568 | tf_op jit(solution)/shard_map/ppermute | solution.py:32
  37.2 0.0 collective-permute-done.14.refs_1_
  37.2 0.6 stack.13.refs_0_
  37.8 0.0 copy-start.1
  37.8 1.6 %collective-permute-start.19 = (bf16[160,512]{1,0:T(8,128)(2,1)S(1)}, bf16[160,512]{1,0:T(8,128)(2,1)S(1)}, u32[]{:S(2)}, u32[]{:S(2)}) collective-permute-start(bf16[160,512]{1,0:T(8,128)(2,1)S(1)} %stack.13.refs_0_), channel_id=1, source_target_pairs={{0,24},{4,28},{8,16},{12,20},{16,8},{20,12},{24,0},{28,4},{1,25},{... | collective-permute-start | bytes 491528 | tf_op jit(solution)/shard_map/ppermute | solution.py:32
  39.4 0.6 collective-permute-start.18
  40.0 1.4 %collective-permute-start.17 = (bf16[160,512]{1,0:T(8,128)(2,1)S(1)}, bf16[160,512]{1,0:T(8,128)(2,1)S(1)}, u32[]{:S(2)}, u32[]{:S(2)}) collective-permute-start(bf16[160,512]{1,0:T(8,128)(2,1)S(1)} %stack.13.refs_0_), channel_id=1, source_target_pairs={{0,8},{4,12},{8,0},{12,4},{16,24},{20,28},{24,16},{28,20},{1,9},{5... | collective-permute-start | bytes 491528 | tf_op jit(solution)/shard_map/ppermute | solution.py:32
  41.3 0.0 collective-permute-start.20
  41.3 4.5 %collective-permute-done.19.refs_3_ = bf16[160,512]{1,0:T(8,128)(2,1)S(1)} collective-permute-done((bf16[160,512]{1,0:T(8,128)(2,1)S(1)}, bf16[160,512]{1,0:T(8,128)(2,1)S(1)}, u32[]{:S(2)}, u32[]{:S(2)}) %collective-permute-start.19) | collective-permute-done | bytes 163872 | tf_op jit(solution)/shard_map/ppermute | solution.py:32
  45.9 0.0 collective-permute-start.23
  45.9 2.1 %collective-permute-done.18.refs_2_ = bf16[160,512]{1,0:T(8,128)(2,1)S(1)} collective-permute-done((bf16[160,512]{1,0:T(8,128)(2,1)S(1)}, bf16[160,512]{1,0:T(8,128)(2,1)S(1)}, u32[]{:S(2)}, u32[]{:S(2)}) %collective-permute-start.18) | collective-permute-done | bytes 163872 | tf_op jit(solution)/shard_map/ppermute | solution.py:32
  48.0 0.0 collective-permute-start.22
  48.0 0.0 collective-permute-done.17.refs_1_
  48.1 0.5 collective-permute-start.21
  48.5 0.0 collective-permute-done.20.refs_4_
  48.5 0.0 collective-permute-done.23.refs_7_
  48.6 0.9 collective-permute-done.22.refs_6_
  49.4 0.2 collective-permute-done.21.refs_5_
  49.7 34.3 %factor.1 = (f32[512,512]{1,0:T(8,128)}, f32[512,512]{1,0:T(8,128)S(1)}) custom-call(s32[2]{0:T(128)S(1)} %pad_add_fusion.index_ref, bf16[160,512]{1,0:T(8,128)(2,1)S(1)} %stack.13.refs_0_, bf16[160,512]{1,0:T(8,128)(2,1)S(1)} %collective-permute-done.17.refs_1_, bf16[160,512]{1,0:T(8,128)(2,1)S(1)} %collective-permute-done.18.refs_2_, ...), custom_call_target="tpu_custom_call" | custom-call | tf_op jit(solution)/shard_map/factor/pallas_call | solution.py:332
  84.0 0.0 copy-done.1
  84.0 0.7 copy-done.5
  84.7 5.6 %solve.1 = (f32[4,128]{1,0:T(4,128)}, f32[16,128]{1,0:T(8,128)}) custom-call(s32[2]{0:T(128)S(1)} %pad_add_fusion.index_ref, f32[512,512]{1,0:T(8,128)S(1)} %get-tuple-element.23.inverse_ref, f32[4,128]{1,0:T(4,128)S(1)} %bitcast.15, bf16[2048,128]{1,0:T(8,128)(2,1)S(1)} %copy-done.1, s32[16,128]{1,0:T(8,128)S(1)} %bitcast.10, f32[16,128]{1,0:T(8,128)S(1)} %bitcast.12, ...), custom_call_target="tpu_custom_call" | custom-call | tf_op jit(solution)/shard_map/solve/pallas_call | solution.py:332
  (5 shorter events, 0.0 us)
Async XLA Ops:
  0.6 7.5 %collective-permute-start.5 = (s32[32]{0:T(128)}, s32[32]{0:T(128)S(1)}, u32[]{:S(2)}, u32[]{:S(2)}) collective-permute-start(s32[32]{0:T(128)} %param.9), channel_id=1, source_target_pairs={{0,24},{4,28},{8,16},{12,20},{16,8},{20,12},{24,0},{28,4},{1,25},{... | collective-permute-start | bytes 392 | tf_op jit(solution)/shard_map/ppermute | solution.py:32
  4.6 4.2 %collective-permute-start.4 = (s32[32]{0:T(128)}, s32[32]{0:T(128)S(1)}, u32[]{:S(2)}, u32[]{:S(2)}) collective-permute-start(s32[32]{0:T(128)} %param.9), channel_id=1, source_target_pairs={{0,20},{4,16},{8,28},{12,24},{16,4},{20,0},{24,12},{28,8},{1,21},{... | collective-permute-start | bytes 392 | tf_op jit(solution)/shard_map/ppermute | solution.py:32
  4.6 4.7 %collective-permute-start.3 = (s32[32]{0:T(128)}, s32[32]{0:T(128)S(1)}, u32[]{:S(2)}, u32[]{:S(2)}) collective-permute-start(s32[32]{0:T(128)} %param.9), channel_id=1, source_target_pairs={{0,16},{4,20},{8,24},{12,28},{16,0},{20,4},{24,8},{28,12},{1,17},{... | collective-permute-start | bytes 392 | tf_op jit(solution)/shard_map/ppermute | solution.py:32
  5.8 3.5 %collective-permute-start.2 = (s32[32]{0:T(128)}, s32[32]{0:T(128)S(1)}, u32[]{:S(2)}, u32[]{:S(2)}) collective-permute-start(s32[32]{0:T(128)} %param.9), channel_id=1, source_target_pairs={{0,12},{4,8},{8,4},{12,0},{16,28},{20,24},{24,20},{28,16},{1,13},{... | collective-permute-start | bytes 392 | tf_op jit(solution)/shard_map/ppermute | solution.py:32
  6.6 3.7 %collective-permute-start.1 = (s32[32]{0:T(128)}, s32[32]{0:T(128)S(1)}, u32[]{:S(2)}, u32[]{:S(2)}) collective-permute-start(s32[32]{0:T(128)} %param.9), channel_id=1, source_target_pairs={{0,8},{4,12},{8,0},{12,4},{16,24},{20,28},{24,16},{28,20},{1,9},{5... | collective-permute-start | bytes 392 | tf_op jit(solution)/shard_map/ppermute | solution.py:32
  8.1 4.6 %copy-start.4 = (s32[2048]{0:T(1024)S(1)}, s32[2048]{0:T(1024)}, u32[]{:S(2)}) copy-start(s32[2048]{0:T(1024)} %param.8) | copy-start | bytes 24580
  8.1 0.7 copy-start.6
  8.1 4.6 %copy-start.2 = (s32[2048]{0:T(1024)S(1)}, s32[2048]{0:T(1024)}, u32[]{:S(2)}) copy-start(s32[2048]{0:T(1024)} %param.7) | copy-start | bytes 24580
  8.1 4.6 %copy-start.3 = (f32[2048]{0:T(1024)S(1)}, f32[2048]{0:T(1024)}, u32[]{:S(2)}) copy-start(f32[2048]{0:T(1024)} %param.11) | copy-start | bytes 24580
  8.8 1.5 %collective-permute-start = (s32[32]{0:T(128)S(1)}, s32[32]{0:T(128)S(1)}, u32[]{:S(2)}, u32[]{:S(2)}) collective-permute-start(s32[32]{0:T(128)S(1)} %copy-done.6), channel_id=1, source_target_pairs={{0,4},{4,0},{8,12},{12,8},{16,20},{20,16},{24,28},{28,24},{1,5},{5... | collective-permute-start | bytes 392 | tf_op jit(solution)/shard_map/ppermute | solution.py:32
  8.8 3.9 %collective-permute-start.6 = (s32[32]{0:T(128)S(1)}, s32[32]{0:T(128)S(1)}, u32[]{:S(2)}, u32[]{:S(2)}) collective-permute-start(s32[32]{0:T(128)S(1)} %copy-done.6), channel_id=1, source_target_pairs={{0,28},{4,24},{8,20},{12,16},{16,12},{20,8},{24,4},{28,0},{1,29},{... | collective-permute-start | bytes 392 | tf_op jit(solution)/shard_map/ppermute | solution.py:32
  12.7 1.0 %copy-start = (bf16[2048,128]{1,0:T(8,128)(2,1)S(1)}, bf16[2048,128]{1,0:T(8,128)(2,1)}, u32[]{:S(2)}) copy-start(bf16[2048,128]{1,0:T(8,128)(2,1)} %cov_ref.3) | copy-start | bytes 1572868
  16.3 4.1 %collective-permute-start.7 = (bf16[64,512]{1,0:T(8,128)(2,1)S(1)}, bf16[64,512]{1,0:T(8,128)(2,1)S(1)}, u32[]{:S(2)}, u32[]{:S(2)}) collective-permute-start(bf16[64,512]{1,0:T(8,128)(2,1)S(1)} %get-tuple-element.16), channel_id=1, source_target_pairs={{0,4},{4,0},{8,12},{12,8},{16,20},{20,16},{24,28},{28,24},{1,5},{5... | collective-permute-start | bytes 196616 | tf_op jit(solution)/shard_map/ppermute | solution.py:32
  16.9 4.9 %collective-permute-start.8 = (bf16[64,512]{1,0:T(8,128)(2,1)S(1)}, bf16[64,512]{1,0:T(8,128)(2,1)S(1)}, u32[]{:S(2)}, u32[]{:S(2)}) collective-permute-start(bf16[64,512]{1,0:T(8,128)(2,1)S(1)} %get-tuple-element.17), channel_id=1, source_target_pairs={{0,8},{4,12},{8,0},{12,4},{16,24},{20,28},{24,16},{28,20},{1,9},{5... | collective-permute-start | bytes 196616 | tf_op jit(solution)/shard_map/ppermute | solution.py:32
  17.4 5.3 %collective-permute-start.9 = (bf16[64,512]{1,0:T(8,128)(2,1)S(1)}, bf16[64,512]{1,0:T(8,128)(2,1)S(1)}, u32[]{:S(2)}, u32[]{:S(2)}) collective-permute-start(bf16[64,512]{1,0:T(8,128)(2,1)S(1)} %get-tuple-element.18), channel_id=1, source_target_pairs={{0,12},{4,8},{8,4},{12,0},{16,28},{20,24},{24,20},{28,16},{1,13},{... | collective-permute-start | bytes 196616 | tf_op jit(solution)/shard_map/ppermute | solution.py:32
  18.3 5.0 %collective-permute-start.10 = (bf16[64,512]{1,0:T(8,128)(2,1)S(1)}, bf16[64,512]{1,0:T(8,128)(2,1)S(1)}, u32[]{:S(2)}, u32[]{:S(2)}) collective-permute-start(bf16[64,512]{1,0:T(8,128)(2,1)S(1)} %get-tuple-element.19), channel_id=1, source_target_pairs={{0,16},{4,20},{8,24},{12,28},{16,0},{20,4},{24,8},{28,12},{1,17},{... | collective-permute-start | bytes 196616 | tf_op jit(solution)/shard_map/ppermute | solution.py:32
  18.8 6.1 %collective-permute-start.11 = (bf16[64,512]{1,0:T(8,128)(2,1)S(1)}, bf16[64,512]{1,0:T(8,128)(2,1)S(1)}, u32[]{:S(2)}, u32[]{:S(2)}) collective-permute-start(bf16[64,512]{1,0:T(8,128)(2,1)S(1)} %get-tuple-element.20), channel_id=1, source_target_pairs={{0,20},{4,16},{8,28},{12,24},{16,4},{20,0},{24,12},{28,8},{1,21},{... | collective-permute-start | bytes 196616 | tf_op jit(solution)/shard_map/ppermute | solution.py:32
  20.4 5.2 %collective-permute-start.12 = (bf16[64,512]{1,0:T(8,128)(2,1)S(1)}, bf16[64,512]{1,0:T(8,128)(2,1)S(1)}, u32[]{:S(2)}, u32[]{:S(2)}) collective-permute-start(bf16[64,512]{1,0:T(8,128)(2,1)S(1)} %get-tuple-element.21), channel_id=1, source_target_pairs={{0,24},{4,28},{8,16},{12,20},{16,8},{20,12},{24,0},{28,4},{1,25},{... | collective-permute-start | bytes 196616 | tf_op jit(solution)/shard_map/ppermute | solution.py:32
  21.8 5.2 %collective-permute-start.13 = (bf16[64,512]{1,0:T(8,128)(2,1)S(1)}, bf16[64,512]{1,0:T(8,128)(2,1)S(1)}, u32[]{:S(2)}, u32[]{:S(2)}) collective-permute-start(bf16[64,512]{1,0:T(8,128)(2,1)S(1)} %get-tuple-element.22), channel_id=1, source_target_pairs={{0,28},{4,24},{8,20},{12,16},{16,12},{20,8},{24,4},{28,0},{1,29},{... | collective-permute-start | bytes 196616 | tf_op jit(solution)/shard_map/ppermute | solution.py:32
  27.7 6.4 %collective-permute-start.16 = (bf16[64,512]{1,0:T(8,128)(2,1)S(1)}, bf16[64,512]{1,0:T(8,128)(2,1)S(1)}, u32[]{:S(2)}, u32[]{:S(2)}) collective-permute-start(bf16[64,512]{1,0:T(8,128)(2,1)S(1)} %mix.1.refs_0_), channel_id=1, source_target_pairs={{0,3},{1,2},{2,1},{3,0},{4,7},{5,6},{6,5},{7,4},{8,11},{9,10},{10,... | collective-permute-start | bytes 196616 | tf_op jit(solution)/shard_map/ppermute | solution.py:32
  31.4 5.8 %collective-permute-start.15 = (bf16[64,512]{1,0:T(8,128)(2,1)S(1)}, bf16[64,512]{1,0:T(8,128)(2,1)S(1)}, u32[]{:S(2)}, u32[]{:S(2)}) collective-permute-start(bf16[64,512]{1,0:T(8,128)(2,1)S(1)} %mix.1.refs_0_), channel_id=1, source_target_pairs={{0,2},{1,3},{2,0},{3,1},{4,6},{5,7},{6,4},{7,5},{8,10},{9,11},{10,... | collective-permute-start | bytes 196616 | tf_op jit(solution)/shard_map/ppermute | solution.py:32
  31.4 5.8 %collective-permute-start.14 = (bf16[64,512]{1,0:T(8,128)(2,1)S(1)}, bf16[64,512]{1,0:T(8,128)(2,1)S(1)}, u32[]{:S(2)}, u32[]{:S(2)}) collective-permute-start(bf16[64,512]{1,0:T(8,128)(2,1)S(1)} %mix.1.refs_0_), channel_id=1, source_target_pairs={{0,1},{1,0},{2,3},{3,2},{4,5},{5,4},{6,7},{7,6},{8,9},{9,8},{10,11... | collective-permute-start | bytes 196616 | tf_op jit(solution)/shard_map/ppermute | solution.py:32
  37.8 46.2 %copy-start.1 = (bf16[2048,128]{1,0:T(8,128)(2,1)S(1)}, bf16[2048,128]{1,0:T(8,128)(2,1)}, u32[]{:S(2)}) copy-start(bf16[2048,128]{1,0:T(8,128)(2,1)} %cov_ref.3) | copy-start | bytes 1572868
  37.8 8.1 %collective-permute-start.19 = (bf16[160,512]{1,0:T(8,128)(2,1)S(1)}, bf16[160,512]{1,0:T(8,128)(2,1)S(1)}, u32[]{:S(2)}, u32[]{:S(2)}) collective-permute-start(bf16[160,512]{1,0:T(8,128)(2,1)S(1)} %stack.13.refs_0_), channel_id=1, source_target_pairs={{0,24},{4,28},{8,16},{12,20},{16,8},{20,12},{24,0},{28,4},{1,25},{... | collective-permute-start | bytes 491528 | tf_op jit(solution)/shard_map/ppermute | solution.py:32
  39.4 8.6 %collective-permute-start.18 = (bf16[160,512]{1,0:T(8,128)(2,1)S(1)}, bf16[160,512]{1,0:T(8,128)(2,1)S(1)}, u32[]{:S(2)}, u32[]{:S(2)}) collective-permute-start(bf16[160,512]{1,0:T(8,128)(2,1)S(1)} %stack.13.refs_0_), channel_id=1, source_target_pairs={{0,16},{4,20},{8,24},{12,28},{16,0},{20,4},{24,8},{28,12},{1,17},{... | collective-permute-start | bytes 491528 | tf_op jit(solution)/shard_map/ppermute | solution.py:32
  40.0 8.1 %collective-permute-start.17 = (bf16[160,512]{1,0:T(8,128)(2,1)S(1)}, bf16[160,512]{1,0:T(8,128)(2,1)S(1)}, u32[]{:S(2)}, u32[]{:S(2)}) collective-permute-start(bf16[160,512]{1,0:T(8,128)(2,1)S(1)} %stack.13.refs_0_), channel_id=1, source_target_pairs={{0,8},{4,12},{8,0},{12,4},{16,24},{20,28},{24,16},{28,20},{1,9},{5... | collective-permute-start | bytes 491528 | tf_op jit(solution)/shard_map/ppermute | solution.py:32
  41.3 7.2 %collective-permute-start.20 = (bf16[160,512]{1,0:T(8,128)(2,1)S(1)}, bf16[160,512]{1,0:T(8,128)(2,1)S(1)}, u32[]{:S(2)}, u32[]{:S(2)}) collective-permute-start(bf16[160,512]{1,0:T(8,128)(2,1)S(1)} %stack.13.refs_0_), channel_id=1, source_target_pairs={{0,4},{4,0},{8,12},{12,8},{16,20},{20,16},{24,28},{28,24},{1,5},{5... | collective-permute-start | bytes 491528 | tf_op jit(solution)/shard_map/ppermute | solution.py:32
  45.9 2.7 %collective-permute-start.23 = (bf16[160,512]{1,0:T(8,128)(2,1)S(1)}, bf16[160,512]{1,0:T(8,128)(2,1)S(1)}, u32[]{:S(2)}, u32[]{:S(2)}) collective-permute-start(bf16[160,512]{1,0:T(8,128)(2,1)S(1)} %collective-permute-done.19.refs_3_), channel_id=1, source_target_pairs={{0,4},{4,0},{8,12},{12,8},{16,20},{20,16},{24,28},{28,24},{1,5},{5... | collective-permute-start | bytes 491528 | tf_op jit(solution)/shard_map/ppermute | solution.py:32
  48.0 1.4 %collective-permute-start.22 = (bf16[160,512]{1,0:T(8,128)(2,1)S(1)}, bf16[160,512]{1,0:T(8,128)(2,1)S(1)}, u32[]{:S(2)}, u32[]{:S(2)}) collective-permute-start(bf16[160,512]{1,0:T(8,128)(2,1)S(1)} %collective-permute-done.18.refs_2_), channel_id=1, source_target_pairs={{0,4},{4,0},{8,12},{12,8},{16,20},{20,16},{24,28},{28,24},{1,5},{5... | collective-permute-start | bytes 491528 | tf_op jit(solution)/shard_map/ppermute | solution.py:32
  48.1 1.6 %collective-permute-start.21 = (bf16[160,512]{1,0:T(8,128)(2,1)S(1)}, bf16[160,512]{1,0:T(8,128)(2,1)S(1)}, u32[]{:S(2)}, u32[]{:S(2)}) collective-permute-start(bf16[160,512]{1,0:T(8,128)(2,1)S(1)} %collective-permute-done.17.refs_1_), channel_id=1, source_target_pairs={{0,4},{4,0},{8,12},{12,8},{16,20},{20,16},{24,28},{28,24},{1,5},{5... | collective-permute-start | bytes 491528 | tf_op jit(solution)/shard_map/ppermute | solution.py:32
  84.0 0.7 copy-start.5

commit v5 on v4

--- a/solution.py
+++ b/solution.py
@@ -21,7 +21,6 @@
 f32, bf16 = jnp.float32, jnp.bfloat16
 SUB, LANE = 8, 128
 PACK = 16
-COUNT = 4
 NT = (((1,), (1,)), ((), ()))
 VMEM = pl.BlockSpec(memory_space=pltpu.VMEM)
 SMEM = pl.BlockSpec(memory_space=pltpu.SMEM)
@@ -166,58 +165,70 @@
     return jnp.broadcast_to(value, (SUB, LANE))
 
 
-def eliminate(tiles, count):
+def reciprocal(value):
+    rough = pl.reciprocal(value, approx=True)
+    rough = rough * (2.0 - value * rough)
+    return rough * (2.0 - value * rough)
+
+
+def eliminate(tiles):
     lane = lax.broadcasted_iota(jnp.int32, (SUB, LANE), 1)
     sub = lax.broadcasted_iota(jnp.int32, (SUB, LANE), 0)
     tiles = list(tiles)
-    scales = [None] * len(tiles)
-    for first in range(0, LANE, count):
-        tile, offset = divmod(first, SUB)
-        window = (lane >= first) & (lane < first + count)
-        columns = [
-            [spread(tiles[i][:, first + k : first + k + 1]) for k in range(count)] for i in range(tile, len(tiles))
-        ]
-        pivot = [
-            [spread(columns[0][m][offset + k : offset + k + 1, :]) if m >= k else None for m in range(count)]
-            for k in range(count)
-        ]
-        rows = []
-        for k in range(count):
-            row = spread(tiles[tile][offset + k : offset + k + 1, :])
-            row = jnp.where(window, 0.0, row)
-            rows.append(jnp.where(lane == first + k, 1.0, row))
-        inverse, ratio = [], [[None] * count for _ in range(count)]
-        for k in range(count):
-            inverse.append(1.0 / pivot[k][k])
-            for m in range(k + 1, count):
-                ratio[k][m] = pivot[k][m] * inverse[k]
-                for n in range(m, count):
-                    pivot[m][n] = pivot[m][n] - ratio[k][m] * pivot[k][n]
-                rows[m] = rows[m] - ratio[k][m] * rows[k]
-        steps = [None] * count
-        for k in reversed(range(count)):
-            steps[k] = rows[k] * inverse[k]
-            for m in range(k + 1, count):
-                steps[k] = steps[k] - ratio[k][m] * steps[m]
+    scales = []
+    for tile in range(len(tiles)):
+        first = tile * SUB
+        window = (lane >= first) & (lane < first + SUB)
+        marks = [lane == first + k for k in range(SUB)]
         old = tiles[tile]
-        scale = scales[tile]
-        for i in range(tile, len(tiles)):
-            new = jnp.where(window, 0.0, tiles[i])
-            for k in range(count):
-                new = new - columns[i - tile][k] * steps[k]
-            tiles[i] = new
-        fixed = old
-        if offset + count < SUB:
-            fixed = jnp.where(sub >= offset + count, tiles[tile], old)
-        for k in range(count):
-            kept = rows[k]
-            for m in range(k, count):
-                kept = jnp.where(lane == first + m, pivot[k][m], kept)
-            root = lax.rsqrt(pivot[k][k])
-            fixed = jnp.where(sub == offset + k, kept, fixed)
-            scale = root if scale is None else jnp.where(sub == offset + k, root, scale)
-        tiles[tile] = fixed
-        scales[tile] = scale
+        columns = [spread(old[:, first + k : first + k + 1]) for k in range(SUB)]
+        pivot = [[spread(columns[m][k : k + 1, :]) if m >= k else None for m in range(SUB)] for k in range(SUB)]
+        cleared = jnp.where(window, 0.0, old)
+        rows = [jnp.where(marks[k], 1.0, spread(cleared[k : k + 1, :])) for k in range(SUB)]
+        steps, near, far = [None] * SUB, {}, {}
+        kept, scale = [None] * SUB, None
+        for k in range(0, SUB, 2):
+            low, cross, high = pivot[k][k], pivot[k][k + 1], pivot[k + 1][k + 1]
+            area = low * high - cross * cross
+            over = reciprocal(area)
+            rest = range(k + 2, SUB)
+            for m in rest:
+                near[k, m] = high * pivot[k][m] - cross * pivot[k + 1][m]
+                far[k, m] = low * pivot[k + 1][m] - cross * pivot[k][m]
+            for m in rest:
+                for n in range(m, SUB):
+                    pivot[m][n] = pivot[m][n] - over * (pivot[k][m] * near[k, n] + pivot[k + 1][m] * far[k, n])
+            for m in rest:
+                near[k, m] = over * near[k, m]
+                far[k, m] = over * far[k, m]
+                rows[m] = rows[m] - (near[k, m] * rows[k] + far[k, m] * rows[k + 1])
+            steps[k] = over * (high * rows[k] - cross * rows[k + 1])
+            steps[k + 1] = over * (low * rows[k + 1] - cross * rows[k])
+            inner = reciprocal(low)
+            ratio = cross * inner
+            kept[k] = rows[k]
+            kept[k + 1] = rows[k + 1] - ratio * rows[k]
+            for m in range(k, SUB):
+                kept[k] = jnp.where(marks[m], pivot[k][m], kept[k])
+            last = area * inner
+            kept[k + 1] = jnp.where(marks[k + 1], last, kept[k + 1])
+            for m in rest:
+                kept[k + 1] = jnp.where(marks[m], pivot[k + 1][m] - ratio * pivot[k][m], kept[k + 1])
+            roots = lax.rsqrt(low), lax.rsqrt(last)
+            scale = roots[0] if scale is None else jnp.where(sub >= k, roots[0], scale)
+            scale = jnp.where(sub >= k + 1, roots[1], scale)
+        for k in reversed(range(0, SUB, 2)):
+            for m in range(k + 2, SUB):
+                steps[k] = steps[k] - near[k, m] * steps[m]
+                steps[k + 1] = steps[k + 1] - far[k, m] * steps[m]
+        for i in range(tile + 1, len(tiles)):
+            change = [spread(tiles[i][:, first + k : first + k + 1]) * steps[k] for k in range(SUB)]
+            tiles[i] = jnp.where(window, 0.0, tiles[i]) - tree_sum(change)
+        new = kept[0]
+        for k in range(1, SUB):
+            new = jnp.where(sub >= k, kept[k], new)
+        tiles[tile] = new
+        scales.append(scale)
     return tiles, scales
 
 
@@ -228,7 +239,18 @@
         at = pl.multiple_of(jnp.bitwise_xor(index_ref[0], mask) * rows_in, rows_in)
         sketch[pl.ds(at, rows_in), :] = ref[:rows_in, :]
     rows = sketch[...]
-    work[...] = lax.dot_general(rows, rows, (((0,), (0,)), ((), ())), preferred_element_type=f32)
+    gram = lax.dot_general(rows, rows, (((0,), (0,)), ((), ())), preferred_element_type=f32)
+    work[...] = gram
+    _, _, same = eye()
+    diagonal = []
+    for at in range(0, cols, LANE):
+        block = work[at : at + LANE, at : at + LANE]
+        diagonal.append(jnp.sum(jnp.where(same, block, 0.0), axis=0, keepdims=True))
+    unit = [lax.rsqrt(part) for part in diagonal]
+    level = jnp.concatenate([part * one for part, one in zip(diagonal, unit)], axis=1) * ratio
+    unit_row = jnp.concatenate(unit, axis=1)
+    for at, one in zip(range(0, cols, LANE), unit):
+        work[at : at + LANE, :] = work[at : at + LANE, :] * to_column(one, same) * unit_row
 
     row_in = lax.broadcasted_iota(jnp.int32, (LANE, LANE), 0)
     lane_in = lax.broadcasted_iota(jnp.int32, (LANE, LANE), 1)
@@ -239,21 +261,19 @@
         base = pl.multiple_of(block * LANE, LANE)
         here = pl.ds(base, LANE)
         tiles = [work[pl.ds(base + SUB * i, SUB), here] for i in range(LANE // SUB)]
-        tiles, scales = eliminate(tiles, COUNT)
+        tiles, scales = eliminate(tiles)
         scale = jnp.concatenate(scales)
         inner = jnp.concatenate(tiles) * scale
         upper = jnp.where(lane_in >= row_in, inner, 0.0)
         lower = jnp.where(lane_in < row_in, inner, jnp.where(lane_in == row_in, scale, 0.0))
         line[...] = jnp.dot(lower, work[here, :], precision=HIGHEST, preferred_element_type=f32)
-        whole = line[...]
-        factor_ref[here, :] = jnp.where(lane_all >= base, whole, 0.0) * ratio
-        factor_ref[here, here] = upper * ratio
-        inverse_ref[here, :] = jnp.where(lane_all < base, whole, 0.0)
-        inverse_ref[here, here] = lower
+        line[:, here] = upper
+        factor_ref[here, :] = jnp.where(lane_all >= base, line[...], 0.0) * level
+        line[:, here] = lower
+        inverse_ref[here, :] = jnp.where(lane_all < base + LANE, line[...], 0.0) * unit_row
 
         @pl.when(block < cols // LANE - 1)
         def _():
-            line[:, here] = lower
             steps = jnp.dot(lower.T, line[...], precision=HIGHEST, preferred_element_type=f32)
             panel = jnp.where(row_all >= base + LANE, work[:, here], 0.0)
             work[:, here] = jnp.where(row_all >= base + LANE, 0.0, work[:, here])
@@ -265,7 +285,7 @@
 
 
 def solve_kernel(apart, rows_in, share, index_ref, inverse_ref, effects_ref, cov_ref, codes_ref, noise_ref, *refs):
-    piece_refs, (solved_ref, resid_ref, packed, kernel) = refs[:-4], refs[-4:]
+    piece_refs, (solved_ref, resid_ref, packed) = refs[:-3], refs[-3:]
     rows, lanes, same = eye()
     extra = None
     for mask, ref in zip(apart, piece_refs):
@@ -281,39 +301,30 @@
         normal.append(jnp.where(rows < lanes, both, diagonal))
 
     inverse = inverse_ref[...]
-    for level in range(LEVELS):
-        here = slice(level * LANE, (level + 1) * LANE)
-        kernel[:, here] = jnp.dot(inverse[:, here], normal[level], precision=HIGHEST, preferred_element_type=f32)
-    kernel[...] = lax.dot_general(kernel[...], inverse, NT, precision=HIGHEST, preferred_element_type=f32)
-    square = kernel[...]
-
+    spans = [slice(level * LANE, (level + 1) * LANE) for level in range(LEVELS)]
     gradient = []
     for level in range(LEVELS):
         column = to_column(effects_ref[level : level + 1, :], same)
         gradient.append(jnp.sum(normal[level] * column, axis=0, keepdims=True) + extra[level : level + 1])
-    gradient = jnp.concatenate(gradient, axis=1)
-    steer_col = jnp.sum(inverse * gradient, axis=1, keepdims=True)
-    steer_row = jnp.concatenate(
-        [to_row(steer_col[level * LANE : (level + 1) * LANE], same) for level in range(LEVELS)], axis=1
-    )
-    go_row, go_col = steer_row, steer_col
-    gamma = jnp.sum(steer_row * steer_row, axis=1, keepdims=True)
-    solved_col = jnp.zeros_like(steer_col)
+    steer = jnp.sum(inverse * jnp.concatenate(gradient, axis=1), axis=1, keepdims=True)
+    direction = steer
+    gamma = jnp.sum(steer * steer, axis=0, keepdims=True)
+    solved = jnp.zeros((1, cov_ref.shape[1] * LEVELS), f32)
     for step in range(ITERS):
-        image_row = jnp.sum(square * go_col, axis=0, keepdims=True)
-        alpha = gamma / jnp.sum(go_row * image_row, axis=1, keepdims=True)
-        solved_col = solved_col + alpha * go_col
+        move = jnp.sum(inverse * direction, axis=0, keepdims=True)
+        image = []
+        for level, span in enumerate(spans):
+            image.append(jnp.sum(normal[level] * to_column(move[:, span], same), axis=0, keepdims=True))
+        image = jnp.concatenate(image, axis=1)
+        alpha = gamma / jnp.sum(move * image, axis=1, keepdims=True)
+        solved = solved + alpha * move
         if step == ITERS - 1:
             break
-        image_col = jnp.sum(square * go_row, axis=1, keepdims=True)
-        steer_row = steer_row - alpha * image_row
-        steer_col = steer_col - alpha * image_col
-        gamma_new = jnp.sum(steer_row * steer_row, axis=1, keepdims=True)
-        go_row = steer_row + gamma_new / gamma * go_row
-        go_col = steer_col + gamma_new / gamma * go_col
+        steer = steer - alpha * jnp.sum(inverse * image, axis=1, keepdims=True)
+        gamma_new = jnp.sum(steer * steer, axis=0, keepdims=True)
+        direction = steer + gamma_new / gamma * direction
         gamma = gamma_new
-    solved = jnp.sum(inverse * solved_col, axis=0, keepdims=True)
-    solved = jnp.concatenate([solved[:, level * LANE : (level + 1) * LANE] for level in range(LEVELS)])
+    solved = jnp.concatenate([solved[:, span] for span in spans])
     solved_ref[...] = solved
 
     left = jnp.concatenate([effects_ref[...] - solved, jnp.zeros((PACK - LEVELS, LANE), f32)])
@@ -391,7 +402,7 @@
         functools.partial(solve_kernel, apart, rows_in, share),
         "solve",
         [((LEVELS, COV), f32), (codes.shape, f32)],
-        [((share * wide, LANE), f32), ((cols, cols), f32)],
+        [((share * wide, LANE), f32)],
         index,
         inverse,
         effects,

time: 90.5 us -> 82.4 us (0.910)
  Pallas kernels: 43.7 us -> 35.6 us
    pallas_call x5, Pallas kernels: 43.7 us -> 35.6 us  [call(): pl.pallas_call(kernel, out_shape=[jax.ShapeDtypeStruct(shape, dtype) for...]
where the time goes in v5:
time: 82.4 us; the launch traced here: 82.2 us
  Pallas kernels  35.6 us (43%)
  starting transfers between devices  21.8 us (26%)
  waiting for transfers between devices  21.6 us (26%)
  local copies, waits for them, and re-layouts  2.41 us (3%)
    pallas_call x5, Pallas kernels, call(): pl.pallas_call(kernel, out_shape=[jax.ShapeDtypeStruct(shape, dtype) for...  35.6 us
    ppermute x24, starting transfers between devices, partner(): return lax.ppermute(value, axis, pairs)  21.8 us
    ppermute x24, waiting for transfers between devices, partner(): return lax.ppermute(value, axis, pairs)  21.6 us
    unnamed x14, local copies, waits for them, and re-layouts  2.33 us
  transfers between devices with their start and end apart: 24, of which 13 were waited for; matrix products, arithmetic and copies ran while one was open for 0% of the time, Pallas kernels for 0%

profile of v5, /device:TPU:0, one launch (start us, length us, event | category | flops | bytes accessed | tf_op | source)
XLA Modules:
  0.0 82.2 jit_solution(7178257941332088892)
XLA Ops:
  0.6 4.0 %collective-permute-start.5 = (s32[32]{0:T(128)}, s32[32]{0:T(128)S(1)}, u32[]{:S(2)}, u32[]{:S(2)}) collective-permute-start(s32[32]{0:T(128)} %param.9), channel_id=1, source_target_pairs={{0,24},{4,28},{8,16},{12,20},{16,8},{20,12},{24,0},{28,4},{1,25},{... | collective-permute-start | bytes 392 | tf_op jit(solution)/shard_map/ppermute | solution.py:31
  4.6 0.0 collective-permute-start.4
  4.6 1.2 %collective-permute-start.3 = (s32[32]{0:T(128)}, s32[32]{0:T(128)S(1)}, u32[]{:S(2)}, u32[]{:S(2)}) collective-permute-start(s32[32]{0:T(128)} %param.9), channel_id=1, source_target_pairs={{0,16},{4,20},{8,24},{12,28},{16,0},{20,4},{24,8},{28,12},{1,17},{... | collective-permute-start | bytes 392 | tf_op jit(solution)/shard_map/ppermute | solution.py:31
  5.8 0.8 collective-permute-start.2
  6.6 1.5 %collective-permute-start.1 = (s32[32]{0:T(128)}, s32[32]{0:T(128)S(1)}, u32[]{:S(2)}, u32[]{:S(2)}) collective-permute-start(s32[32]{0:T(128)} %param.9), channel_id=1, source_target_pairs={{0,8},{4,12},{8,0},{12,4},{16,24},{20,28},{24,16},{28,20},{1,9},{5... | collective-permute-start | bytes 392 | tf_op jit(solution)/shard_map/ppermute | solution.py:31
  8.1 0.1 pad_add_fusion.index_ref
  8.2 0.0 collective-permute-done.5
  8.2 0.6 copy-done.6
  8.8 0.0 collective-permute-start
  8.8 0.0 collective-permute-done.4
  8.8 0.5 collective-permute-start.6
  9.3 0.0 collective-permute-done.3
  9.3 0.0 collective-permute-done.2
  9.3 1.0 %collective-permute-done.1 = s32[32]{0:T(128)S(1)} collective-permute-done((s32[32]{0:T(128)}, s32[32]{0:T(128)S(1)}, u32[]{:S(2)}, u32[]{:S(2)}) %collective-permute-start.1) | collective-permute-done | bytes 160 | tf_op jit(solution)/shard_map/ppermute | solution.py:31
  10.3 0.0 collective-permute-done
  10.3 2.4 %collective-permute-done.6 = s32[32]{0:T(128)S(1)} collective-permute-done((s32[32]{0:T(128)S(1)}, s32[32]{0:T(128)S(1)}, u32[]{:S(2)}, u32[]{:S(2)}) %collective-permute-start.6) | collective-permute-done | bytes 160 | tf_op jit(solution)/shard_map/ppermute | solution.py:31
  12.6 0.1 concatenate.3
  12.7 0.0 copy-done.4
  12.7 0.0 copy-done.2
  12.7 0.0 copy-done.3
  12.7 0.0 copy-start
  12.8 1.0 %copy-done = bf16[2048,128]{1,0:T(8,128)(2,1)S(1)} copy-done((bf16[2048,128]{1,0:T(8,128)(2,1)S(1)}, bf16[2048,128]{1,0:T(8,128)(2,1)}, u32[]{:S(2)}) %copy-start) | copy-done | bytes 524312
  13.8 2.5 %local.1 = (bf16[64,512]{1,0:T(8,128)(2,1)S(1)}, bf16[64,512]{1,0:T(8,128)(2,1)S(1)}, bf16[64,512]{1,0:T(8,128)(2,1)S(1)}, bf16[64,512]{1,0:T(8,128)(2,1)S(1)}, ...) custom-call(s32[2]{0:T(128)S(1)} %pad_add_fusion.index_ref, ...), custom_call_target="tpu_custom_call" | custom-call | tf_op jit(solution)/shard_map/local/pallas_call | solution.py:343
  16.3 0.6 collective-permute-start.7
  16.9 0.5 collective-permute-start.8
  17.4 0.9 %collective-permute-start.9 = (bf16[64,512]{1,0:T(8,128)(2,1)S(1)}, bf16[64,512]{1,0:T(8,128)(2,1)S(1)}, u32[]{:S(2)}, u32[]{:S(2)}) collective-permute-start(bf16[64,512]{1,0:T(8,128)(2,1)S(1)} %get-tuple-element.18), channel_id=1, source_target_pairs={{0,12},{4,8},{8,4},{12,0},{16,28},{20,24},{24,20},{28,16},{1,13},{... | collective-permute-start | bytes 196616 | tf_op jit(solution)/shard_map/ppermute | solution.py:31
  18.3 0.5 collective-permute-start.10
  18.8 1.6 %collective-permute-start.11 = (bf16[64,512]{1,0:T(8,128)(2,1)S(1)}, bf16[64,512]{1,0:T(8,128)(2,1)S(1)}, u32[]{:S(2)}, u32[]{:S(2)}) collective-permute-start(bf16[64,512]{1,0:T(8,128)(2,1)S(1)} %get-tuple-element.20), channel_id=1, source_target_pairs={{0,20},{4,16},{8,28},{12,24},{16,4},{20,0},{24,12},{28,8},{1,21},{... | collective-permute-start | bytes 196616 | tf_op jit(solution)/shard_map/ppermute | solution.py:31
  20.4 0.0 collective-permute-done.7.refs_1_
  20.4 0.4 collective-permute-start.12
  20.8 1.0 %collective-permute-done.8.refs_2_ = bf16[64,512]{1,0:T(8,128)(2,1)S(1)} collective-permute-done((bf16[64,512]{1,0:T(8,128)(2,1)S(1)}, bf16[64,512]{1,0:T(8,128)(2,1)S(1)}, u32[]{:S(2)}, u32[]{:S(2)}) %collective-permute-start.8) | collective-permute-done | bytes 65568 | tf_op jit(solution)/shard_map/ppermute | solution.py:31
  21.8 0.9 %collective-permute-start.13 = (bf16[64,512]{1,0:T(8,128)(2,1)S(1)}, bf16[64,512]{1,0:T(8,128)(2,1)S(1)}, u32[]{:S(2)}, u32[]{:S(2)}) collective-permute-start(bf16[64,512]{1,0:T(8,128)(2,1)S(1)} %get-tuple-element.22), channel_id=1, source_target_pairs={{0,28},{4,24},{8,20},{12,16},{16,12},{20,8},{24,4},{28,0},{1,29},{... | collective-permute-start | bytes 196616 | tf_op jit(solution)/shard_map/ppermute | solution.py:31
  22.7 0.0 collective-permute-done.9.refs_3_
  22.7 0.6 collective-permute-done.10.refs_4_
  23.3 1.6 %collective-permute-done.11.refs_5_ = bf16[64,512]{1,0:T(8,128)(2,1)S(1)} collective-permute-done((bf16[64,512]{1,0:T(8,128)(2,1)S(1)}, bf16[64,512]{1,0:T(8,128)(2,1)S(1)}, u32[]{:S(2)}, u32[]{:S(2)}) %collective-permute-start.11) | collective-permute-done | bytes 65568 | tf_op jit(solution)/shard_map/ppermute | solution.py:31
  24.9 0.7 collective-permute-done.12.refs_6_
  25.6 1.4 %collective-permute-done.13.refs_7_ = bf16[64,512]{1,0:T(8,128)(2,1)S(1)} collective-permute-done((bf16[64,512]{1,0:T(8,128)(2,1)S(1)}, bf16[64,512]{1,0:T(8,128)(2,1)S(1)}, u32[]{:S(2)}, u32[]{:S(2)}) %collective-permute-start.13) | collective-permute-done | bytes 65568 | tf_op jit(solution)/shard_map/ppermute | solution.py:31
  27.0 0.7 mix.1.refs_0_
  27.7 3.7 %collective-permute-start.16 = (bf16[64,512]{1,0:T(8,128)(2,1)S(1)}, bf16[64,512]{1,0:T(8,128)(2,1)S(1)}, u32[]{:S(2)}, u32[]{:S(2)}) collective-permute-start(bf16[64,512]{1,0:T(8,128)(2,1)S(1)} %mix.1.refs_0_), channel_id=1, source_target_pairs={{0,3},{1,2},{2,1},{3,0},{4,7},{5,6},{6,5},{7,4},{8,11},{9,10},{10,... | collective-permute-start | bytes 196616 | tf_op jit(solution)/shard_map/ppermute | solution.py:31
  31.4 0.0 collective-permute-start.15
  31.4 0.8 collective-permute-start.14
  32.1 2.0 %collective-permute-done.16.refs_3_ = bf16[64,512]{1,0:T(8,128)(2,1)S(1)} collective-permute-done((bf16[64,512]{1,0:T(8,128)(2,1)S(1)}, bf16[64,512]{1,0:T(8,128)(2,1)S(1)}, u32[]{:S(2)}, u32[]{:S(2)}) %collective-permute-start.16) | collective-permute-done | bytes 65568 | tf_op jit(solution)/shard_map/ppermute | solution.py:31
  34.1 3.1 %collective-permute-done.15.refs_2_ = bf16[64,512]{1,0:T(8,128)(2,1)S(1)} collective-permute-done((bf16[64,512]{1,0:T(8,128)(2,1)S(1)}, bf16[64,512]{1,0:T(8,128)(2,1)S(1)}, u32[]{:S(2)}, u32[]{:S(2)}) %collective-permute-start.15) | collective-permute-done | bytes 65568 | tf_op jit(solution)/shard_map/ppermute | solution.py:31
  37.2 0.0 collective-permute-done.14.refs_1_
  37.2 0.6 stack.13.refs_0_
  37.8 0.0 copy-start.1
  37.8 1.6 %collective-permute-start.19 = (bf16[160,512]{1,0:T(8,128)(2,1)S(1)}, bf16[160,512]{1,0:T(8,128)(2,1)S(1)}, u32[]{:S(2)}, u32[]{:S(2)}) collective-permute-start(bf16[160,512]{1,0:T(8,128)(2,1)S(1)} %stack.13.refs_0_), channel_id=1, source_target_pairs={{0,24},{4,28},{8,16},{12,20},{16,8},{20,12},{24,0},{28,4},{1,25},{... | collective-permute-start | bytes 491528 | tf_op jit(solution)/shard_map/ppermute | solution.py:31
  39.4 0.6 collective-permute-start.18
  40.0 1.4 %collective-permute-start.17 = (bf16[160,512]{1,0:T(8,128)(2,1)S(1)}, bf16[160,512]{1,0:T(8,128)(2,1)S(1)}, u32[]{:S(2)}, u32[]{:S(2)}) collective-permute-start(bf16[160,512]{1,0:T(8,128)(2,1)S(1)} %stack.13.refs_0_), channel_id=1, source_target_pairs={{0,8},{4,12},{8,0},{12,4},{16,24},{20,28},{24,16},{28,20},{1,9},{5... | collective-permute-start | bytes 491528 | tf_op jit(solution)/shard_map/ppermute | solution.py:31
  41.3 0.0 collective-permute-start.20
  41.3 4.5 %collective-permute-done.19.refs_3_ = bf16[160,512]{1,0:T(8,128)(2,1)S(1)} collective-permute-done((bf16[160,512]{1,0:T(8,128)(2,1)S(1)}, bf16[160,512]{1,0:T(8,128)(2,1)S(1)}, u32[]{:S(2)}, u32[]{:S(2)}) %collective-permute-start.19) | collective-permute-done | bytes 163872 | tf_op jit(solution)/shard_map/ppermute | solution.py:31
  45.9 0.0 collective-permute-start.23
  45.9 2.1 %collective-permute-done.18.refs_2_ = bf16[160,512]{1,0:T(8,128)(2,1)S(1)} collective-permute-done((bf16[160,512]{1,0:T(8,128)(2,1)S(1)}, bf16[160,512]{1,0:T(8,128)(2,1)S(1)}, u32[]{:S(2)}, u32[]{:S(2)}) %collective-permute-start.18) | collective-permute-done | bytes 163872 | tf_op jit(solution)/shard_map/ppermute | solution.py:31
  48.0 0.0 collective-permute-start.22
  48.0 0.0 collective-permute-done.17.refs_1_
  48.1 0.5 collective-permute-start.21
  48.5 0.0 collective-permute-done.20.refs_4_
  48.5 0.0 collective-permute-done.23.refs_7_
  48.6 0.9 %collective-permute-done.22.refs_6_ = bf16[160,512]{1,0:T(8,128)(2,1)S(1)} collective-permute-done((bf16[160,512]{1,0:T(8,128)(2,1)S(1)}, bf16[160,512]{1,0:T(8,128)(2,1)S(1)}, u32[]{:S(2)}, u32[]{:S(2)}) %collective-permute-start.22) | collective-permute-done | bytes 163872 | tf_op jit(solution)/shard_map/ppermute | solution.py:31
  49.4 0.2 collective-permute-done.21.refs_5_
  49.7 28.3 %factor.1 = (f32[512,512]{1,0:T(8,128)}, f32[512,512]{1,0:T(8,128)S(1)}) custom-call(s32[2]{0:T(128)S(1)} %pad_add_fusion.index_ref, bf16[160,512]{1,0:T(8,128)(2,1)S(1)} %stack.13.refs_0_, bf16[160,512]{1,0:T(8,128)(2,1)S(1)} %collective-permute-done.17.refs_1_, bf16[160,512]{1,0:T(8,128)(2,1)S(1)} %collective-permute-done.18.refs_2_, ...), custom_call_target="tpu_custom_call" | custom-call | tf_op jit(solution)/shard_map/factor/pallas_call | solution.py:343
  78.0 0.0 copy-done.1
  78.0 0.7 copy-done.5
  78.7 3.5 %solve.1 = (f32[4,128]{1,0:T(4,128)}, f32[16,128]{1,0:T(8,128)}) custom-call(s32[2]{0:T(128)S(1)} %pad_add_fusion.index_ref, f32[512,512]{1,0:T(8,128)S(1)} %get-tuple-element.23.inverse_ref, f32[4,128]{1,0:T(4,128)S(1)} %bitcast.15, bf16[2048,128]{1,0:T(8,128)(2,1)S(1)} %copy-done.1, s32[16,128]{1,0:T(8,128)S(1)} %bitcast.10, f32[16,128]{1,0:T(8,128)S(1)} %bitcast.12, ...), custom_call_target="tpu_custom_call" | custom-call | tf_op jit(solution)/shard_map/solve/pallas_call | solution.py:343
  (5 shorter events, 0.0 us)
Async XLA Ops:
  0.6 7.5 %collective-permute-start.5 = (s32[32]{0:T(128)}, s32[32]{0:T(128)S(1)}, u32[]{:S(2)}, u32[]{:S(2)}) collective-permute-start(s32[32]{0:T(128)} %param.9), channel_id=1, source_target_pairs={{0,24},{4,28},{8,16},{12,20},{16,8},{20,12},{24,0},{28,4},{1,25},{... | collective-permute-start | bytes 392 | tf_op jit(solution)/shard_map/ppermute | solution.py:31
  4.6 4.2 %collective-permute-start.4 = (s32[32]{0:T(128)}, s32[32]{0:T(128)S(1)}, u32[]{:S(2)}, u32[]{:S(2)}) collective-permute-start(s32[32]{0:T(128)} %param.9), channel_id=1, source_target_pairs={{0,20},{4,16},{8,28},{12,24},{16,4},{20,0},{24,12},{28,8},{1,21},{... | collective-permute-start | bytes 392 | tf_op jit(solution)/shard_map/ppermute | solution.py:31
  4.6 4.7 %collective-permute-start.3 = (s32[32]{0:T(128)}, s32[32]{0:T(128)S(1)}, u32[]{:S(2)}, u32[]{:S(2)}) collective-permute-start(s32[32]{0:T(128)} %param.9), channel_id=1, source_target_pairs={{0,16},{4,20},{8,24},{12,28},{16,0},{20,4},{24,8},{28,12},{1,17},{... | collective-permute-start | bytes 392 | tf_op jit(solution)/shard_map/ppermute | solution.py:31
  5.8 3.5 %collective-permute-start.2 = (s32[32]{0:T(128)}, s32[32]{0:T(128)S(1)}, u32[]{:S(2)}, u32[]{:S(2)}) collective-permute-start(s32[32]{0:T(128)} %param.9), channel_id=1, source_target_pairs={{0,12},{4,8},{8,4},{12,0},{16,28},{20,24},{24,20},{28,16},{1,13},{... | collective-permute-start | bytes 392 | tf_op jit(solution)/shard_map/ppermute | solution.py:31
  6.6 3.7 %collective-permute-start.1 = (s32[32]{0:T(128)}, s32[32]{0:T(128)S(1)}, u32[]{:S(2)}, u32[]{:S(2)}) collective-permute-start(s32[32]{0:T(128)} %param.9), channel_id=1, source_target_pairs={{0,8},{4,12},{8,0},{12,4},{16,24},{20,28},{24,16},{28,20},{1,9},{5... | collective-permute-start | bytes 392 | tf_op jit(solution)/shard_map/ppermute | solution.py:31
  8.1 4.6 %copy-start.4 = (s32[2048]{0:T(1024)S(1)}, s32[2048]{0:T(1024)}, u32[]{:S(2)}) copy-start(s32[2048]{0:T(1024)} %param.8) | copy-start | bytes 24580
  8.1 0.7 copy-start.6
  8.1 4.6 %copy-start.2 = (s32[2048]{0:T(1024)S(1)}, s32[2048]{0:T(1024)}, u32[]{:S(2)}) copy-start(s32[2048]{0:T(1024)} %param.7) | copy-start | bytes 24580
  8.1 4.6 %copy-start.3 = (f32[2048]{0:T(1024)S(1)}, f32[2048]{0:T(1024)}, u32[]{:S(2)}) copy-start(f32[2048]{0:T(1024)} %param.11) | copy-start | bytes 24580
  8.8 1.5 %collective-permute-start = (s32[32]{0:T(128)S(1)}, s32[32]{0:T(128)S(1)}, u32[]{:S(2)}, u32[]{:S(2)}) collective-permute-start(s32[32]{0:T(128)S(1)} %copy-done.6), channel_id=1, source_target_pairs={{0,4},{4,0},{8,12},{12,8},{16,20},{20,16},{24,28},{28,24},{1,5},{5... | collective-permute-start | bytes 392 | tf_op jit(solution)/shard_map/ppermute | solution.py:31
  8.8 3.9 %collective-permute-start.6 = (s32[32]{0:T(128)S(1)}, s32[32]{0:T(128)S(1)}, u32[]{:S(2)}, u32[]{:S(2)}) collective-permute-start(s32[32]{0:T(128)S(1)} %copy-done.6), channel_id=1, source_target_pairs={{0,28},{4,24},{8,20},{12,16},{16,12},{20,8},{24,4},{28,0},{1,29},{... | collective-permute-start | bytes 392 | tf_op jit(solution)/shard_map/ppermute | solution.py:31
  12.7 1.0 %copy-start = (bf16[2048,128]{1,0:T(8,128)(2,1)S(1)}, bf16[2048,128]{1,0:T(8,128)(2,1)}, u32[]{:S(2)}) copy-start(bf16[2048,128]{1,0:T(8,128)(2,1)} %cov_ref.3) | copy-start | bytes 1572868
  16.3 4.1 %collective-permute-start.7 = (bf16[64,512]{1,0:T(8,128)(2,1)S(1)}, bf16[64,512]{1,0:T(8,128)(2,1)S(1)}, u32[]{:S(2)}, u32[]{:S(2)}) collective-permute-start(bf16[64,512]{1,0:T(8,128)(2,1)S(1)} %get-tuple-element.16), channel_id=1, source_target_pairs={{0,4},{4,0},{8,12},{12,8},{16,20},{20,16},{24,28},{28,24},{1,5},{5... | collective-permute-start | bytes 196616 | tf_op jit(solution)/shard_map/ppermute | solution.py:31
  16.9 4.9 %collective-permute-start.8 = (bf16[64,512]{1,0:T(8,128)(2,1)S(1)}, bf16[64,512]{1,0:T(8,128)(2,1)S(1)}, u32[]{:S(2)}, u32[]{:S(2)}) collective-permute-start(bf16[64,512]{1,0:T(8,128)(2,1)S(1)} %get-tuple-element.17), channel_id=1, source_target_pairs={{0,8},{4,12},{8,0},{12,4},{16,24},{20,28},{24,16},{28,20},{1,9},{5... | collective-permute-start | bytes 196616 | tf_op jit(solution)/shard_map/ppermute | solution.py:31
  17.4 5.3 %collective-permute-start.9 = (bf16[64,512]{1,0:T(8,128)(2,1)S(1)}, bf16[64,512]{1,0:T(8,128)(2,1)S(1)}, u32[]{:S(2)}, u32[]{:S(2)}) collective-permute-start(bf16[64,512]{1,0:T(8,128)(2,1)S(1)} %get-tuple-element.18), channel_id=1, source_target_pairs={{0,12},{4,8},{8,4},{12,0},{16,28},{20,24},{24,20},{28,16},{1,13},{... | collective-permute-start | bytes 196616 | tf_op jit(solution)/shard_map/ppermute | solution.py:31
  18.3 5.0 %collective-permute-start.10 = (bf16[64,512]{1,0:T(8,128)(2,1)S(1)}, bf16[64,512]{1,0:T(8,128)(2,1)S(1)}, u32[]{:S(2)}, u32[]{:S(2)}) collective-permute-start(bf16[64,512]{1,0:T(8,128)(2,1)S(1)} %get-tuple-element.19), channel_id=1, source_target_pairs={{0,16},{4,20},{8,24},{12,28},{16,0},{20,4},{24,8},{28,12},{1,17},{... | collective-permute-start | bytes 196616 | tf_op jit(solution)/shard_map/ppermute | solution.py:31
  18.8 6.1 %collective-permute-start.11 = (bf16[64,512]{1,0:T(8,128)(2,1)S(1)}, bf16[64,512]{1,0:T(8,128)(2,1)S(1)}, u32[]{:S(2)}, u32[]{:S(2)}) collective-permute-start(bf16[64,512]{1,0:T(8,128)(2,1)S(1)} %get-tuple-element.20), channel_id=1, source_target_pairs={{0,20},{4,16},{8,28},{12,24},{16,4},{20,0},{24,12},{28,8},{1,21},{... | collective-permute-start | bytes 196616 | tf_op jit(solution)/shard_map/ppermute | solution.py:31
  20.4 5.2 %collective-permute-start.12 = (bf16[64,512]{1,0:T(8,128)(2,1)S(1)}, bf16[64,512]{1,0:T(8,128)(2,1)S(1)}, u32[]{:S(2)}, u32[]{:S(2)}) collective-permute-start(bf16[64,512]{1,0:T(8,128)(2,1)S(1)} %get-tuple-element.21), channel_id=1, source_target_pairs={{0,24},{4,28},{8,16},{12,20},{16,8},{20,12},{24,0},{28,4},{1,25},{... | collective-permute-start | bytes 196616 | tf_op jit(solution)/shard_map/ppermute | solution.py:31
  21.8 5.2 %collective-permute-start.13 = (bf16[64,512]{1,0:T(8,128)(2,1)S(1)}, bf16[64,512]{1,0:T(8,128)(2,1)S(1)}, u32[]{:S(2)}, u32[]{:S(2)}) collective-permute-start(bf16[64,512]{1,0:T(8,128)(2,1)S(1)} %get-tuple-element.22), channel_id=1, source_target_pairs={{0,28},{4,24},{8,20},{12,16},{16,12},{20,8},{24,4},{28,0},{1,29},{... | collective-permute-start | bytes 196616 | tf_op jit(solution)/shard_map/ppermute | solution.py:31
  27.7 6.4 %collective-permute-start.16 = (bf16[64,512]{1,0:T(8,128)(2,1)S(1)}, bf16[64,512]{1,0:T(8,128)(2,1)S(1)}, u32[]{:S(2)}, u32[]{:S(2)}) collective-permute-start(bf16[64,512]{1,0:T(8,128)(2,1)S(1)} %mix.1.refs_0_), channel_id=1, source_target_pairs={{0,3},{1,2},{2,1},{3,0},{4,7},{5,6},{6,5},{7,4},{8,11},{9,10},{10,... | collective-permute-start | bytes 196616 | tf_op jit(solution)/shard_map/ppermute | solution.py:31
  31.4 5.8 %collective-permute-start.15 = (bf16[64,512]{1,0:T(8,128)(2,1)S(1)}, bf16[64,512]{1,0:T(8,128)(2,1)S(1)}, u32[]{:S(2)}, u32[]{:S(2)}) collective-permute-start(bf16[64,512]{1,0:T(8,128)(2,1)S(1)} %mix.1.refs_0_), channel_id=1, source_target_pairs={{0,2},{1,3},{2,0},{3,1},{4,6},{5,7},{6,4},{7,5},{8,10},{9,11},{10,... | collective-permute-start | bytes 196616 | tf_op jit(solution)/shard_map/ppermute | solution.py:31
  31.4 5.8 %collective-permute-start.14 = (bf16[64,512]{1,0:T(8,128)(2,1)S(1)}, bf16[64,512]{1,0:T(8,128)(2,1)S(1)}, u32[]{:S(2)}, u32[]{:S(2)}) collective-permute-start(bf16[64,512]{1,0:T(8,128)(2,1)S(1)} %mix.1.refs_0_), channel_id=1, source_target_pairs={{0,1},{1,0},{2,3},{3,2},{4,5},{5,4},{6,7},{7,6},{8,9},{9,8},{10,11... | collective-permute-start | bytes 196616 | tf_op jit(solution)/shard_map/ppermute | solution.py:31
  37.8 40.2 %copy-start.1 = (bf16[2048,128]{1,0:T(8,128)(2,1)S(1)}, bf16[2048,128]{1,0:T(8,128)(2,1)}, u32[]{:S(2)}) copy-start(bf16[2048,128]{1,0:T(8,128)(2,1)} %cov_ref.3) | copy-start | bytes 1572868
  37.8 8.1 %collective-permute-start.19 = (bf16[160,512]{1,0:T(8,128)(2,1)S(1)}, bf16[160,512]{1,0:T(8,128)(2,1)S(1)}, u32[]{:S(2)}, u32[]{:S(2)}) collective-permute-start(bf16[160,512]{1,0:T(8,128)(2,1)S(1)} %stack.13.refs_0_), channel_id=1, source_target_pairs={{0,24},{4,28},{8,16},{12,20},{16,8},{20,12},{24,0},{28,4},{1,25},{... | collective-permute-start | bytes 491528 | tf_op jit(solution)/shard_map/ppermute | solution.py:31
  39.4 8.6 %collective-permute-start.18 = (bf16[160,512]{1,0:T(8,128)(2,1)S(1)}, bf16[160,512]{1,0:T(8,128)(2,1)S(1)}, u32[]{:S(2)}, u32[]{:S(2)}) collective-permute-start(bf16[160,512]{1,0:T(8,128)(2,1)S(1)} %stack.13.refs_0_), channel_id=1, source_target_pairs={{0,16},{4,20},{8,24},{12,28},{16,0},{20,4},{24,8},{28,12},{1,17},{... | collective-permute-start | bytes 491528 | tf_op jit(solution)/shard_map/ppermute | solution.py:31
  40.0 8.1 %collective-permute-start.17 = (bf16[160,512]{1,0:T(8,128)(2,1)S(1)}, bf16[160,512]{1,0:T(8,128)(2,1)S(1)}, u32[]{:S(2)}, u32[]{:S(2)}) collective-permute-start(bf16[160,512]{1,0:T(8,128)(2,1)S(1)} %stack.13.refs_0_), channel_id=1, source_target_pairs={{0,8},{4,12},{8,0},{12,4},{16,24},{20,28},{24,16},{28,20},{1,9},{5... | collective-permute-start | bytes 491528 | tf_op jit(solution)/shard_map/ppermute | solution.py:31
  41.3 7.2 %collective-permute-start.20 = (bf16[160,512]{1,0:T(8,128)(2,1)S(1)}, bf16[160,512]{1,0:T(8,128)(2,1)S(1)}, u32[]{:S(2)}, u32[]{:S(2)}) collective-permute-start(bf16[160,512]{1,0:T(8,128)(2,1)S(1)} %stack.13.refs_0_), channel_id=1, source_target_pairs={{0,4},{4,0},{8,12},{12,8},{16,20},{20,16},{24,28},{28,24},{1,5},{5... | collective-permute-start | bytes 491528 | tf_op jit(solution)/shard_map/ppermute | solution.py:31
  45.9 2.7 %collective-permute-start.23 = (bf16[160,512]{1,0:T(8,128)(2,1)S(1)}, bf16[160,512]{1,0:T(8,128)(2,1)S(1)}, u32[]{:S(2)}, u32[]{:S(2)}) collective-permute-start(bf16[160,512]{1,0:T(8,128)(2,1)S(1)} %collective-permute-done.19.refs_3_), channel_id=1, source_target_pairs={{0,4},{4,0},{8,12},{12,8},{16,20},{20,16},{24,28},{28,24},{1,5},{5... | collective-permute-start | bytes 491528 | tf_op jit(solution)/shard_map/ppermute | solution.py:31
  48.0 1.4 %collective-permute-start.22 = (bf16[160,512]{1,0:T(8,128)(2,1)S(1)}, bf16[160,512]{1,0:T(8,128)(2,1)S(1)}, u32[]{:S(2)}, u32[]{:S(2)}) collective-permute-start(bf16[160,512]{1,0:T(8,128)(2,1)S(1)} %collective-permute-done.18.refs_2_), channel_id=1, source_target_pairs={{0,4},{4,0},{8,12},{12,8},{16,20},{20,16},{24,28},{28,24},{1,5},{5... | collective-permute-start | bytes 491528 | tf_op jit(solution)/shard_map/ppermute | solution.py:31
  48.1 1.6 %collective-permute-start.21 = (bf16[160,512]{1,0:T(8,128)(2,1)S(1)}, bf16[160,512]{1,0:T(8,128)(2,1)S(1)}, u32[]{:S(2)}, u32[]{:S(2)}) collective-permute-start(bf16[160,512]{1,0:T(8,128)(2,1)S(1)} %collective-permute-done.17.refs_1_), channel_id=1, source_target_pairs={{0,4},{4,0},{8,12},{12,8},{16,20},{20,16},{24,28},{28,24},{1,5},{5... | collective-permute-start | bytes 491528 | tf_op jit(solution)/shard_map/ppermute | solution.py:31
  78.0 0.7 copy-start.5

commit v6 on v5

--- a/solution.py
+++ b/solution.py
@@ -78,25 +78,10 @@
     return share, tail[:SUB] + tail[SUB : 2 * SUB] + tail[2 * SUB : 3 * SUB]
 
 
-def local_kernel(samp, share, index_ref, want_ref, cov_ref, codes_ref, signs_ref, noise_ref, *refs):
-    out_refs, (design, table, packed) = refs[:-3], refs[-3:]
-    chunks = codes_ref.shape[0]
+def design_kernel(cov_ref, codes_ref, noise_ref, design, packed):
     rows, lanes, same = eye()
     zero = jnp.zeros((LANE, LANE), f32)
-
-    masks, halves = [], []
-    for c in range(want_ref.shape[0]):
-        want = to_column(want_ref[c : c + 1, :].astype(f32), same).astype(jnp.int32)
-        masks.append(jnp.right_shift(want, HB.bit_length() - 1))
-        line = []
-        for h in range(HB // LANE):
-            common = jnp.bitwise_and(want, lanes + h * LANE)
-            for shift in (4, 2, 1):
-                common = jnp.bitwise_xor(common, jnp.right_shift(common, shift))
-            line.append((1 - 2 * jnp.bitwise_and(common, 1)).astype(f32))
-        halves.append(line)
-
-    for r in range(chunks):
+    for r in range(codes_ref.shape[0]):
         here = slice(r * LANE, (r + 1) * LANE)
         code = codes_ref[r : r + 1, :]
         turned = cov_ref[here, :].astype(f32).T
@@ -107,46 +92,88 @@
         noise = jnp.where(code == level, noise, 0.0)
         for k, part in enumerate(split(noise)):
             design[LEVELS * LANE + k * PACK : LEVELS * LANE + (k + 1) * PACK, here] = part
-        sign = (1 - 2 * signs_ref[r : r + 1, :]).astype(f32)
-        block, h = divmod(r * LANE, HB)
-        for c, (mask, line) in enumerate(zip(masks, halves)):
-            value = jnp.where(mask == block, line[h // LANE] * sign, zero)
-            table[c * LANE : (c + 1) * LANE, here] = value.astype(bf16)
 
     sums = jnp.dot(design[...], cov_ref[...], preferred_element_type=f32)
     normal = [sums[level * LANE : (level + 1) * LANE] for level in range(LEVELS)]
     back = sums[LEVELS * LANE :]
     back = back[:SUB] + back[PACK : PACK + SUB] + back[2 * PACK : 2 * PACK + SUB]
     extra = [jnp.sum(jnp.where(same, normal[level], 0.0), axis=0, keepdims=True) for level in (1, 3)]
-    extra = jnp.concatenate([back[:LEVELS]] + extra + [jnp.zeros((2, LANE), f32)])
     for pair in range(LEVELS // 2):
         packed[pair * LANE : (pair + 1) * LANE, :] = jnp.where(rows >= lanes, normal[2 * pair], normal[2 * pair + 1])
-    if packed.shape[0] > 2 * LANE:
-        packed[2 * LANE :, :] = jnp.zeros((packed.shape[0] - 2 * LANE, LANE), f32)
-
-    local = lax.dot_general(table[...], design[: LEVELS * LANE, :], NT, preferred_element_type=f32)
+    rest = packed.shape[0] - SUB - 2 * LANE
+    if rest:
+        packed[2 * LANE : 2 * LANE + rest, :] = jnp.zeros((rest, LANE), f32)
+    packed[2 * LANE + rest :, :] = jnp.concatenate([back[:LEVELS]] + extra + [jnp.zeros((2, LANE), f32)])
+
+
+def local_kernel(samp, share, starts, index_ref, design_ref, packed_ref, signs_ref, *refs):
+    want_refs, (stay_ref, go_ref, table) = refs[:-3], refs[-3:]
+    chunks = signs_ref.shape[0]
+    lanes = lax.broadcasted_iota(jnp.int32, (1, LANE), 1)
+    wide_lanes, same = eye()[1:]
+    zero = jnp.zeros((LANE, LANE), f32)
+    pairs = LANE // (2 * samp)
+
+    masks, halves = [], []
+    for c in range(MATES // 2 // pairs):
+        want = want_refs[c * pairs][...]
+        for q in range(1, pairs):
+            want = jnp.where(lanes >= 2 * samp * q, want_refs[c * pairs + q][...], want)
+        want = to_column(want.astype(f32), same).astype(jnp.int32)
+        masks.append(jnp.right_shift(want, HB.bit_length() - 1))
+        line = []
+        for h in range(HB // LANE):
+            common = jnp.bitwise_and(want, wide_lanes + h * LANE)
+            for shift in (4, 2, 1):
+                common = jnp.bitwise_xor(common, jnp.right_shift(common, shift))
+            line.append((1 - 2 * jnp.bitwise_and(common, 1)).astype(f32))
+        halves.append(line)
+    for r in range(chunks):
+        sign = (1 - 2 * signs_ref[r : r + 1, :]).astype(f32)
+        block, h = divmod(r * LANE, HB)
+        for c, (mask, line) in enumerate(zip(masks, halves)):
+            value = jnp.where(mask == block, line[h // LANE] * sign, zero)
+            table[c * LANE : (c + 1) * LANE, r * LANE : (r + 1) * LANE] = value.astype(bf16)
+
+    local = lax.dot_general(table[...], design_ref[: LEVELS * LANE, :], NT, preferred_element_type=f32)
     local = (local * (1.0 / math.sqrt(HB))).astype(bf16)
-    for m, out_ref in enumerate(out_refs):
-        start = 0
+    extra = packed_ref[packed_ref.shape[0] - SUB :, :]
+    for m in range(2 * len(starts)):
+        out_ref, start = (stay_ref, go_ref)[m % 2], starts[m // 2]
         if m < MATES:
-            out_ref[:samp, :] = local[m * samp : (m + 1) * samp]
-            start = samp
+            out_ref[start : start + samp, :] = local[m * samp : (m + 1) * samp]
+            start += samp
         at = pl.multiple_of(jnp.bitwise_xor(index_ref[0], m) * share, share)
-        put_sums(out_ref, start, packed[pl.ds(at, share), :], extra)
+        put_sums(out_ref, start, packed_ref[pl.ds(at, share), :], extra)
+
+
+def butterfly(pieces, place, index):
+    bit = jnp.bitwise_and(jnp.right_shift(index, place), 1)
+    sign = (1 - 2 * bit).astype(f32)
+    return [
+        ((sign * own + other) * half_root).astype(bf16).astype(f32) for own, other in zip(pieces[0::2], pieces[1::2])
+    ]
+
+
+def pair_kernel(samp, share, starts, index_ref, stay_ref, came_ref, *out_refs):
+    for m, (start, out_ref) in enumerate(zip(starts, out_refs)):
+        put = 0
+        if 2 * m < MATES:
+            here = slice(start, start + samp)
+            pieces = [ref[here, :].astype(f32) for ref in (stay_ref, came_ref)]
+            out_ref[:samp, :] = butterfly(pieces, 0, index_ref[0])[0].astype(bf16)
+            put, start = samp, start + samp
+        (own, own_extra), (other, other_extra) = [take_sums(ref, start, share) for ref in (stay_ref, came_ref)]
+        put_sums(out_ref, put, own + other, own_extra + other_extra)
 
 
 def mix_kernel(samp, share, index_ref, *refs):
     piece_refs, out_ref = refs[:-1], refs[-1]
-    pieces = [ref[:samp, :].astype(f32) for ref in piece_refs[:MATES]]
-    for place in range(MIX_BITS):
-        bit = jnp.bitwise_and(jnp.right_shift(index_ref[0], place), 1)
-        sign = (1 - 2 * bit).astype(f32)
-        pieces = [
-            ((sign * own + other) * half_root).astype(bf16).astype(f32)
-            for own, other in zip(pieces[0::2], pieces[1::2])
-        ]
+    pieces = [ref[:samp, :].astype(f32) for ref in piece_refs[: MATES // 2]]
+    for place in range(1, MIX_BITS):
+        pieces = butterfly(pieces, place, index_ref[0])
     out_ref[:samp, :] = pieces[0].astype(bf16)
-    sums = [take_sums(ref, samp if m < MATES else 0, share) for m, ref in enumerate(piece_refs)]
+    sums = [take_sums(ref, samp if 2 * m < MATES else 0, share) for m, ref in enumerate(piece_refs)]
     put_sums(out_ref, samp, tree_sum([one for one, _ in sums]), tree_sum([one for _, one in sums]))
 
 
@@ -339,16 +366,16 @@
         resid_ref[r : r + 1, :] = total
 
 
-def call(kernel, name, outs, scratch, index, *operands):
+def call(kernel, name, outs, scratch, *operands):
     return pl.pallas_call(
         kernel,
         out_shape=[jax.ShapeDtypeStruct(shape, dtype) for shape, dtype in outs],
-        in_specs=[SMEM] + [VMEM] * len(operands),
+        in_specs=[SMEM if operand.ndim == 1 else VMEM for operand in operands],
         out_specs=[VMEM] * len(outs),
         scratch_shapes=[pltpu.VMEM(shape, dtype) for shape, dtype in scratch],
         compiler_params=pltpu.CompilerParams(vmem_limit_bytes=40 * 2**20),
         name=name,
-    )(index, *operands)
+    )(*operands)
 
 
 def body(covariates, level_codes, sign_bits, sample_rows, effects, noise):
@@ -361,24 +388,43 @@
     codes, signs, noise = [array.reshape(-1, LANE) for array in (level_codes, sign_bits, noise)]
     effects = effects.reshape(LEVELS, COV)
 
-    want = jnp.concatenate([sample_rows] + [partner(sample_rows, "wide", m) for m in range(1, MATES)])
-    pieces = call(
-        functools.partial(local_kernel, samp, share),
-        "local",
-        [((samp * (m < MATES) + share, cols), bf16) for m in range(wide)],
-        [
-            ((cols + 3 * PACK, rows_dev), bf16),
-            ((MATES * samp, rows_dev), bf16),
-            ((share * wide, LANE), f32),
-        ],
-        index,
-        want.reshape(-1, LANE),
+    lane = jnp.arange(LANE, dtype=jnp.int32)[None, :]
+    want = jnp.tile(sample_rows, LANE // samp)[None, :]
+    want = jnp.where(jnp.bitwise_and(lane // samp, 1) == 0, want, partner(want, "wide", 1))
+    want = [want] + [partner(want, "wide", m) for m in range(2, MATES, 2)]
+
+    design, packed = call(
+        design_kernel,
+        "design",
+        [((cols + 3 * PACK, rows_dev), bf16), ((share * wide + SUB, LANE), f32)],
+        [],
         covariates,
         codes,
+        noise,
+    )
+    sizes = [samp * (2 * m < MATES) + share for m in range(wide // 2)]
+    starts = [sum(sizes[:m]) for m in range(wide // 2)]
+    stay, go = call(
+        functools.partial(local_kernel, samp, share, starts),
+        "local",
+        [((sum(sizes), cols), bf16)] * 2,
+        [((MATES * samp, rows_dev), bf16)],
+        index,
+        design,
+        packed,
         signs,
-        noise,
-    )
-    pieces = [pieces[0]] + [partner(pieces[m], "wide", m) for m in range(1, wide)]
+        *want,
+    )
+    pieces = call(
+        functools.partial(pair_kernel, samp, share, starts),
+        "pair",
+        [((size, cols), bf16) for size in sizes],
+        [],
+        index,
+        stay,
+        partner(go, "wide", 1),
+    )
+    pieces = [pieces[0]] + [partner(pieces[m], "wide", 2 * m) for m in range(1, wide // 2)]
     (piece,) = call(
         functools.partial(mix_kernel, samp, share), "mix", [((samp + share, cols), bf16)], [], index, *pieces
     )

time: 82.4 us -> 75.9 us (0.921)
  starting transfers between devices: 21.8 us -> 17.1 us
  waiting for transfers between devices: 21.6 us -> 17.7 us
  local copies, waits for them, and re-layouts: 2.41 us -> 3.88 us
    ppermute x24 -> x18, starting transfers between devices: 21.8 us -> 17.1 us  [partner(): return lax.ppermute(value, axis, pairs)]
    ppermute x24 -> x18, waiting for transfers between devices: 21.6 us -> 17.7 us  [partner(): return lax.ppermute(value, axis, pairs)]
    pallas_call x5 -> x7, Pallas kernels: 35.6 us -> 36.1 us  [call(): pl.pallas_call(kernel, out_shape=[jax.ShapeDtypeStruct(shape, dtype) for...]
  transfers between devices with their start and end apart: 24 -> 18, of which waited for: 13 -> 11; matrix products, arithmetic and copies ran while one was open for 0% -> 0% of each run, Pallas kernels for 0% -> 1%
where the time goes in v6:
time: 75.9 us; the launch traced here: 75.6 us
  Pallas kernels  36.1 us (48%)
  waiting for transfers between devices  17.7 us (23%)
  starting transfers between devices  17.1 us (23%)
  local copies, waits for them, and re-layouts  3.88 us (5%)
    pallas_call x7, Pallas kernels, call(): pl.pallas_call(kernel, out_shape=[jax.ShapeDtypeStruct(shape, dtype) for...  36.1 us
    ppermute x18, waiting for transfers between devices, partner(): return lax.ppermute(value, axis, pairs)  17.7 us
    ppermute x18, starting transfers between devices, partner(): return lax.ppermute(value, axis, pairs)  17.1 us
    unnamed x14, local copies, waits for them, and re-layouts  3.14 us
  transfers between devices with their start and end apart: 18, of which 11 were waited for; matrix products, arithmetic and copies ran while one was open for 0% of the time, Pallas kernels for 1%

profile of v6, /device:TPU:0, one launch (start us, length us, event | category | flops | bytes accessed | tf_op | source)
XLA Modules:
  0.0 75.6 jit_solution(11066706557448849813)
XLA Ops:
  0.6 0.7 tile.2
  1.3 0.1 broadcast_in_dim_tile.3
  1.4 0.5 collective-permute-start
  1.8 0.8 %collective-permute-done = s32[1,128]{1,0:T(1,128)S(1)} collective-permute-done((s32[1,128]{1,0:T(1,128)S(1)}, s32[1,128]{1,0:T(1,128)S(1)}, u32[]{:S(2)}, u32[]{:S(2)}) %collective-permute-start) | collective-permute-done | bytes 544 | tf_op jit(solution)/shard_map/ppermute | solution.py:31
  2.7 3.8 %collective-permute-start.3 = (s32[1,128]{1,0:T(1,128)S(1)}, s32[1,128]{1,0:T(1,128)S(1)}, u32[]{:S(2)}, u32[]{:S(2)}) collective-permute-start(s32[1,128]{1,0:T(1,128)S(1)} %compare_select_fusion.refs_0_), channel_id=1, source_target_pairs={{0,24},{4,28},{8,16},{12,20},{16,8},{20,12},{24,0},{28,4},{1,25},{... | collective-permute-start | bytes 1544 | tf_op jit(solution)/shard_map/ppermute | solution.py:31
  6.5 0.5 collective-permute-start.2
  7.0 0.1 collective-permute-start.1
  7.1 0.1 pad_add_fusion.index_ref
  7.2 0.0 copy-start
  7.2 1.0 %copy-done = bf16[2048,128]{1,0:T(8,128)(2,1)S(1)} copy-done((bf16[2048,128]{1,0:T(8,128)(2,1)S(1)}, bf16[2048,128]{1,0:T(8,128)(2,1)}, u32[]{:S(2)}) %copy-start) | copy-done | bytes 524312
  8.2 0.0 copy-start.2
  8.2 0.7 copy-done.2
  8.9 0.0 copy-start.3
  8.9 0.7 copy-done.3
  9.6 1.0 %design.1 = (bf16[560,2048]{1,0:T(8,128)(2,1)S(1)}, f32[264,128]{1,0:T(8,128)S(1)}) custom-call(bf16[2048,128]{1,0:T(8,128)(2,1)S(1)} %copy-done, s32[16,128]{1,0:T(8,128)S(1)} %bitcast.8, f32[16,128]{1,0:T(8,128)S(1)} %bitcast.10), custom_call_target="tpu_custom_call" | custom-call | tf_op jit(solution)/shard_map/design/pallas_call | solution.py:370
  10.6 0.0 collective-permute-done.3.refs_3_
  10.6 0.0 collective-permute-done.2.refs_2_
  10.7 0.0 collective-permute-done.1.refs_1_
  10.7 0.0 copy-start.5
  10.7 0.7 copy-done.5
  11.4 0.0 copy-start.1
  11.4 0.0 copy-start.4
  11.4 0.0 copy-start.6
  11.4 1.4 %local.1 = (bf16[256,512]{1,0:T(8,128)(2,1)S(1)}, bf16[256,512]{1,0:T(8,128)(2,1)S(1)}) custom-call(s32[2]{0:T(128)S(1)} %pad_add_fusion.index_ref, bf16[560,2048]{1,0:T(8,128)(2,1)S(1)} %get-tuple-element.15.design_ref, f32[264,128]{1,0:T(8,128)S(1)} %get-tuple-element.16.packed_ref, s32[16,128]{1,0:T(8,128)S(1)} %bitcast.12, ...), custom_call_target="tpu_custom_call" | custom-call | tf_op jit(solution)/shard_map/local/pallas_call | solution.py:370
  12.8 0.1 collective-permute-start.4
  12.9 1.5 %collective-permute-done.4.came_ref = bf16[256,512]{1,0:T(8,128)(2,1)S(1)} collective-permute-done((bf16[256,512]{1,0:T(8,128)(2,1)S(1)}, bf16[256,512]{1,0:T(8,128)(2,1)S(1)}, u32[]{:S(2)}, u32[]{:S(2)}) %collective-permute-start.4) | collective-permute-done | bytes 262176 | tf_op jit(solution)/shard_map/ppermute | solution.py:31
  14.4 0.6 pair.1
  15.1 2.0 %collective-permute-start.5 = (bf16[64,512]{1,0:T(8,128)(2,1)S(1)}, bf16[64,512]{1,0:T(8,128)(2,1)S(1)}, u32[]{:S(2)}, u32[]{:S(2)}) collective-permute-start(bf16[64,512]{1,0:T(8,128)(2,1)S(1)} %get-tuple-element.20), channel_id=1, source_target_pairs={{0,8},{4,12},{8,0},{12,4},{16,24},{20,28},{24,16},{28,20},{1,9},{5... | collective-permute-start | bytes 196616 | tf_op jit(solution)/shard_map/ppermute | solution.py:31
  17.0 1.5 %collective-permute-start.6 = (bf16[64,512]{1,0:T(8,128)(2,1)S(1)}, bf16[64,512]{1,0:T(8,128)(2,1)S(1)}, u32[]{:S(2)}, u32[]{:S(2)}) collective-permute-start(bf16[64,512]{1,0:T(8,128)(2,1)S(1)} %get-tuple-element.21), channel_id=1, source_target_pairs={{0,16},{4,20},{8,24},{12,28},{16,0},{20,4},{24,8},{28,12},{1,17},{... | collective-permute-start | bytes 196616 | tf_op jit(solution)/shard_map/ppermute | solution.py:31
  18.6 0.1 collective-permute-start.7
  18.6 0.8 %collective-permute-done.5.refs_1_ = bf16[64,512]{1,0:T(8,128)(2,1)S(1)} collective-permute-done((bf16[64,512]{1,0:T(8,128)(2,1)S(1)}, bf16[64,512]{1,0:T(8,128)(2,1)S(1)}, u32[]{:S(2)}, u32[]{:S(2)}) %collective-permute-start.5) | collective-permute-done | bytes 65568 | tf_op jit(solution)/shard_map/ppermute | solution.py:31
  19.4 1.9 %collective-permute-done.6.refs_2_ = bf16[64,512]{1,0:T(8,128)(2,1)S(1)} collective-permute-done((bf16[64,512]{1,0:T(8,128)(2,1)S(1)}, bf16[64,512]{1,0:T(8,128)(2,1)S(1)}, u32[]{:S(2)}, u32[]{:S(2)}) %collective-permute-start.6) | collective-permute-done | bytes 65568 | tf_op jit(solution)/shard_map/ppermute | solution.py:31
  21.3 2.4 %collective-permute-done.7.refs_3_ = bf16[64,512]{1,0:T(8,128)(2,1)S(1)} collective-permute-done((bf16[64,512]{1,0:T(8,128)(2,1)S(1)}, bf16[64,512]{1,0:T(8,128)(2,1)S(1)}, u32[]{:S(2)}, u32[]{:S(2)}) %collective-permute-start.7) | collective-permute-done | bytes 65568 | tf_op jit(solution)/shard_map/ppermute | solution.py:31
  23.7 0.6 mix.1.refs_0_
  24.3 3.7 %collective-permute-start.10 = (bf16[64,512]{1,0:T(8,128)(2,1)S(1)}, bf16[64,512]{1,0:T(8,128)(2,1)S(1)}, u32[]{:S(2)}, u32[]{:S(2)}) collective-permute-start(bf16[64,512]{1,0:T(8,128)(2,1)S(1)} %mix.1.refs_0_), channel_id=1, source_target_pairs={{0,3},{1,2},{2,1},{3,0},{4,7},{5,6},{6,5},{7,4},{8,11},{9,10},{10,... | collective-permute-start | bytes 196616 | tf_op jit(solution)/shard_map/ppermute | solution.py:31
  28.0 0.0 collective-permute-start.9
  28.0 0.8 %collective-permute-start.8 = (bf16[64,512]{1,0:T(8,128)(2,1)S(1)}, bf16[64,512]{1,0:T(8,128)(2,1)S(1)}, u32[]{:S(2)}, u32[]{:S(2)}) collective-permute-start(bf16[64,512]{1,0:T(8,128)(2,1)S(1)} %mix.1.refs_0_), channel_id=1, source_target_pairs={{0,1},{1,0},{2,3},{3,2},{4,5},{5,4},{6,7},{7,6},{8,9},{9,8},{10,11... | collective-permute-start | bytes 196616 | tf_op jit(solution)/shard_map/ppermute | solution.py:31
  28.8 1.7 %collective-permute-done.10.refs_3_ = bf16[64,512]{1,0:T(8,128)(2,1)S(1)} collective-permute-done((bf16[64,512]{1,0:T(8,128)(2,1)S(1)}, bf16[64,512]{1,0:T(8,128)(2,1)S(1)}, u32[]{:S(2)}, u32[]{:S(2)}) %collective-permute-start.10) | collective-permute-done | bytes 65568 | tf_op jit(solution)/shard_map/ppermute | solution.py:31
  30.5 2.7 %collective-permute-done.9.refs_2_ = bf16[64,512]{1,0:T(8,128)(2,1)S(1)} collective-permute-done((bf16[64,512]{1,0:T(8,128)(2,1)S(1)}, bf16[64,512]{1,0:T(8,128)(2,1)S(1)}, u32[]{:S(2)}, u32[]{:S(2)}) %collective-permute-start.9) | collective-permute-done | bytes 65568 | tf_op jit(solution)/shard_map/ppermute | solution.py:31
  33.2 0.0 collective-permute-done.8.refs_1_
  33.2 0.6 stack.13.refs_0_
  33.8 0.5 collective-permute-start.13
  34.3 1.5 %collective-permute-start.12 = (bf16[160,512]{1,0:T(8,128)(2,1)S(1)}, bf16[160,512]{1,0:T(8,128)(2,1)S(1)}, u32[]{:S(2)}, u32[]{:S(2)}) collective-permute-start(bf16[160,512]{1,0:T(8,128)(2,1)S(1)} %stack.13.refs_0_), channel_id=1, source_target_pairs={{0,16},{4,20},{8,24},{12,28},{16,0},{20,4},{24,8},{28,12},{1,17},{... | collective-permute-start | bytes 491528 | tf_op jit(solution)/shard_map/ppermute | solution.py:31
  35.8 1.5 %collective-permute-start.11 = (bf16[160,512]{1,0:T(8,128)(2,1)S(1)}, bf16[160,512]{1,0:T(8,128)(2,1)S(1)}, u32[]{:S(2)}, u32[]{:S(2)}) collective-permute-start(bf16[160,512]{1,0:T(8,128)(2,1)S(1)} %stack.13.refs_0_), channel_id=1, source_target_pairs={{0,8},{4,12},{8,0},{12,4},{16,24},{20,28},{24,16},{28,20},{1,9},{5... | collective-permute-start | bytes 491528 | tf_op jit(solution)/shard_map/ppermute | solution.py:31
  37.3 0.0 collective-permute-start.14
  37.3 3.5 %collective-permute-done.13.refs_3_ = bf16[160,512]{1,0:T(8,128)(2,1)S(1)} collective-permute-done((bf16[160,512]{1,0:T(8,128)(2,1)S(1)}, bf16[160,512]{1,0:T(8,128)(2,1)S(1)}, u32[]{:S(2)}, u32[]{:S(2)}) %collective-permute-start.13) | collective-permute-done | bytes 163872 | tf_op jit(solution)/shard_map/ppermute | solution.py:31
  40.8 0.0 collective-permute-start.17
  40.8 1.3 %collective-permute-done.12.refs_2_ = bf16[160,512]{1,0:T(8,128)(2,1)S(1)} collective-permute-done((bf16[160,512]{1,0:T(8,128)(2,1)S(1)}, bf16[160,512]{1,0:T(8,128)(2,1)S(1)}, u32[]{:S(2)}, u32[]{:S(2)}) %collective-permute-start.12) | collective-permute-done | bytes 163872 | tf_op jit(solution)/shard_map/ppermute | solution.py:31
  42.1 0.0 collective-permute-start.16
  42.1 0.0 collective-permute-done.11.refs_1_
  42.1 0.5 collective-permute-start.15
  42.6 0.0 collective-permute-done.14.refs_4_
  42.6 0.0 collective-permute-done.17.refs_7_
  42.6 0.9 %collective-permute-done.16.refs_6_ = bf16[160,512]{1,0:T(8,128)(2,1)S(1)} collective-permute-done((bf16[160,512]{1,0:T(8,128)(2,1)S(1)}, bf16[160,512]{1,0:T(8,128)(2,1)S(1)}, u32[]{:S(2)}, u32[]{:S(2)}) %collective-permute-start.16) | collective-permute-done | bytes 163872 | tf_op jit(solution)/shard_map/ppermute | solution.py:31
  43.5 0.2 collective-permute-done.15.refs_5_
  43.7 28.3 %factor.1 = (f32[512,512]{1,0:T(8,128)}, f32[512,512]{1,0:T(8,128)S(1)}) custom-call(s32[2]{0:T(128)S(1)} %pad_add_fusion.index_ref, bf16[160,512]{1,0:T(8,128)(2,1)S(1)} %stack.13.refs_0_, bf16[160,512]{1,0:T(8,128)(2,1)S(1)} %collective-permute-done.11.refs_1_, bf16[160,512]{1,0:T(8,128)(2,1)S(1)} %collective-permute-done.12.refs_2_, ...), custom_call_target="tpu_custom_call" | custom-call | tf_op jit(solution)/shard_map/factor/pallas_call | solution.py:370
  72.1 0.0 copy-done.1
  72.1 0.0 copy-done.4
  72.1 0.0 copy-done.6
  72.1 3.5 %solve.1 = (f32[4,128]{1,0:T(4,128)}, f32[16,128]{1,0:T(8,128)}) custom-call(s32[2]{0:T(128)S(1)} %pad_add_fusion.index_ref, f32[512,512]{1,0:T(8,128)S(1)} %get-tuple-element.23.inverse_ref, f32[4,128]{1,0:T(4,128)S(1)} %bitcast.13, bf16[2048,128]{1,0:T(8,128)(2,1)S(1)} %copy-done.1, s32[16,128]{1,0:T(8,128)S(1)} %bitcast.9, f32[16,128]{1,0:T(8,128)S(1)} %bitcast.11, ...), custom_call_target="tpu_custom_call" | custom-call | tf_op jit(solution)/shard_map/solve/pallas_call | solution.py:370
  (1 shorter events, 0.0 us)
Async XLA Ops:
  1.4 1.3 %collective-permute-start = (s32[1,128]{1,0:T(1,128)S(1)}, s32[1,128]{1,0:T(1,128)S(1)}, u32[]{:S(2)}, u32[]{:S(2)}) collective-permute-start(s32[1,128]{1,0:T(1,128)S(1)} %broadcast_in_dim_tile.3), channel_id=1, source_target_pairs={{0,4},{4,0},{8,12},{12,8},{16,20},{20,16},{24,28},{28,24},{1,5},{5... | collective-permute-start | bytes 1544 | tf_op jit(solution)/shard_map/ppermute | solution.py:31
  2.7 8.0 %collective-permute-start.3 = (s32[1,128]{1,0:T(1,128)S(1)}, s32[1,128]{1,0:T(1,128)S(1)}, u32[]{:S(2)}, u32[]{:S(2)}) collective-permute-start(s32[1,128]{1,0:T(1,128)S(1)} %compare_select_fusion.refs_0_), channel_id=1, source_target_pairs={{0,24},{4,28},{8,16},{12,20},{16,8},{20,12},{24,0},{28,4},{1,25},{... | collective-permute-start | bytes 1544 | tf_op jit(solution)/shard_map/ppermute | solution.py:31
  6.5 4.2 %collective-permute-start.2 = (s32[1,128]{1,0:T(1,128)S(1)}, s32[1,128]{1,0:T(1,128)S(1)}, u32[]{:S(2)}, u32[]{:S(2)}) collective-permute-start(s32[1,128]{1,0:T(1,128)S(1)} %compare_select_fusion.refs_0_), channel_id=1, source_target_pairs={{0,16},{4,20},{8,24},{12,28},{16,0},{20,4},{24,8},{28,12},{1,17},{... | collective-permute-start | bytes 1544 | tf_op jit(solution)/shard_map/ppermute | solution.py:31
  7.0 3.7 %collective-permute-start.1 = (s32[1,128]{1,0:T(1,128)S(1)}, s32[1,128]{1,0:T(1,128)S(1)}, u32[]{:S(2)}, u32[]{:S(2)}) collective-permute-start(s32[1,128]{1,0:T(1,128)S(1)} %compare_select_fusion.refs_0_), channel_id=1, source_target_pairs={{0,8},{4,12},{8,0},{12,4},{16,24},{20,28},{24,16},{28,20},{1,9},{5... | collective-permute-start | bytes 1544 | tf_op jit(solution)/shard_map/ppermute | solution.py:31
  7.2 1.0 %copy-start = (bf16[2048,128]{1,0:T(8,128)(2,1)S(1)}, bf16[2048,128]{1,0:T(8,128)(2,1)}, u32[]{:S(2)}) copy-start(bf16[2048,128]{1,0:T(8,128)(2,1)} %cov_ref.3) | copy-start | bytes 1572868
  8.2 0.7 copy-start.2
  8.9 0.7 copy-start.3
  10.7 0.7 copy-start.5
  11.4 60.7 %copy-start.1 = (bf16[2048,128]{1,0:T(8,128)(2,1)S(1)}, bf16[2048,128]{1,0:T(8,128)(2,1)}, u32[]{:S(2)}) copy-start(bf16[2048,128]{1,0:T(8,128)(2,1)} %cov_ref.3) | copy-start | bytes 1572868
  11.4 60.7 %copy-start.4 = (f32[2048]{0:T(1024)S(1)}, f32[2048]{0:T(1024)}, u32[]{:S(2)}) copy-start(f32[2048]{0:T(1024)} %param.11) | copy-start | bytes 24580
  11.4 60.7 %copy-start.6 = (f32[512]{0:T(512)S(1)}, f32[512]{0:T(512)}, u32[]{:S(2)}) copy-start(f32[512]{0:T(512)} %param.10) | copy-start | bytes 6148
  12.8 1.6 %collective-permute-start.4 = (bf16[256,512]{1,0:T(8,128)(2,1)S(1)}, bf16[256,512]{1,0:T(8,128)(2,1)S(1)}, u32[]{:S(2)}, u32[]{:S(2)}) collective-permute-start(bf16[256,512]{1,0:T(8,128)(2,1)S(1)} %get-tuple-element.18), channel_id=1, source_target_pairs={{0,4},{4,0},{8,12},{12,8},{16,20},{20,16},{24,28},{28,24},{1,5},{5... | collective-permute-start | bytes 786440 | tf_op jit(solution)/shard_map/ppermute | solution.py:31
  15.1 4.4 %collective-permute-start.5 = (bf16[64,512]{1,0:T(8,128)(2,1)S(1)}, bf16[64,512]{1,0:T(8,128)(2,1)S(1)}, u32[]{:S(2)}, u32[]{:S(2)}) collective-permute-start(bf16[64,512]{1,0:T(8,128)(2,1)S(1)} %get-tuple-element.20), channel_id=1, source_target_pairs={{0,8},{4,12},{8,0},{12,4},{16,24},{20,28},{24,16},{28,20},{1,9},{5... | collective-permute-start | bytes 196616 | tf_op jit(solution)/shard_map/ppermute | solution.py:31
  17.0 4.3 %collective-permute-start.6 = (bf16[64,512]{1,0:T(8,128)(2,1)S(1)}, bf16[64,512]{1,0:T(8,128)(2,1)S(1)}, u32[]{:S(2)}, u32[]{:S(2)}) collective-permute-start(bf16[64,512]{1,0:T(8,128)(2,1)S(1)} %get-tuple-element.21), channel_id=1, source_target_pairs={{0,16},{4,20},{8,24},{12,28},{16,0},{20,4},{24,8},{28,12},{1,17},{... | collective-permute-start | bytes 196616 | tf_op jit(solution)/shard_map/ppermute | solution.py:31
  18.6 5.2 %collective-permute-start.7 = (bf16[64,512]{1,0:T(8,128)(2,1)S(1)}, bf16[64,512]{1,0:T(8,128)(2,1)S(1)}, u32[]{:S(2)}, u32[]{:S(2)}) collective-permute-start(bf16[64,512]{1,0:T(8,128)(2,1)S(1)} %get-tuple-element.22), channel_id=1, source_target_pairs={{0,24},{4,28},{8,16},{12,20},{16,8},{20,12},{24,0},{28,4},{1,25},{... | collective-permute-start | bytes 196616 | tf_op jit(solution)/shard_map/ppermute | solution.py:31
  24.3 6.1 %collective-permute-start.10 = (bf16[64,512]{1,0:T(8,128)(2,1)S(1)}, bf16[64,512]{1,0:T(8,128)(2,1)S(1)}, u32[]{:S(2)}, u32[]{:S(2)}) collective-permute-start(bf16[64,512]{1,0:T(8,128)(2,1)S(1)} %mix.1.refs_0_), channel_id=1, source_target_pairs={{0,3},{1,2},{2,1},{3,0},{4,7},{5,6},{6,5},{7,4},{8,11},{9,10},{10,... | collective-permute-start | bytes 196616 | tf_op jit(solution)/shard_map/ppermute | solution.py:31
  28.0 5.2 %collective-permute-start.9 = (bf16[64,512]{1,0:T(8,128)(2,1)S(1)}, bf16[64,512]{1,0:T(8,128)(2,1)S(1)}, u32[]{:S(2)}, u32[]{:S(2)}) collective-permute-start(bf16[64,512]{1,0:T(8,128)(2,1)S(1)} %mix.1.refs_0_), channel_id=1, source_target_pairs={{0,2},{1,3},{2,0},{3,1},{4,6},{5,7},{6,4},{7,5},{8,10},{9,11},{10,... | collective-permute-start | bytes 196616 | tf_op jit(solution)/shard_map/ppermute | solution.py:31
  28.0 5.2 %collective-permute-start.8 = (bf16[64,512]{1,0:T(8,128)(2,1)S(1)}, bf16[64,512]{1,0:T(8,128)(2,1)S(1)}, u32[]{:S(2)}, u32[]{:S(2)}) collective-permute-start(bf16[64,512]{1,0:T(8,128)(2,1)S(1)} %mix.1.refs_0_), channel_id=1, source_target_pairs={{0,1},{1,0},{2,3},{3,2},{4,5},{5,4},{6,7},{7,6},{8,9},{9,8},{10,11... | collective-permute-start | bytes 196616 | tf_op jit(solution)/shard_map/ppermute | solution.py:31
  33.8 7.1 %collective-permute-start.13 = (bf16[160,512]{1,0:T(8,128)(2,1)S(1)}, bf16[160,512]{1,0:T(8,128)(2,1)S(1)}, u32[]{:S(2)}, u32[]{:S(2)}) collective-permute-start(bf16[160,512]{1,0:T(8,128)(2,1)S(1)} %stack.13.refs_0_), channel_id=1, source_target_pairs={{0,24},{4,28},{8,16},{12,20},{16,8},{20,12},{24,0},{28,4},{1,25},{... | collective-permute-start | bytes 491528 | tf_op jit(solution)/shard_map/ppermute | solution.py:31
  34.3 7.8 %collective-permute-start.12 = (bf16[160,512]{1,0:T(8,128)(2,1)S(1)}, bf16[160,512]{1,0:T(8,128)(2,1)S(1)}, u32[]{:S(2)}, u32[]{:S(2)}) collective-permute-start(bf16[160,512]{1,0:T(8,128)(2,1)S(1)} %stack.13.refs_0_), channel_id=1, source_target_pairs={{0,16},{4,20},{8,24},{12,28},{16,0},{20,4},{24,8},{28,12},{1,17},{... | collective-permute-start | bytes 491528 | tf_op jit(solution)/shard_map/ppermute | solution.py:31
  35.8 6.3 %collective-permute-start.11 = (bf16[160,512]{1,0:T(8,128)(2,1)S(1)}, bf16[160,512]{1,0:T(8,128)(2,1)S(1)}, u32[]{:S(2)}, u32[]{:S(2)}) collective-permute-start(bf16[160,512]{1,0:T(8,128)(2,1)S(1)} %stack.13.refs_0_), channel_id=1, source_target_pairs={{0,8},{4,12},{8,0},{12,4},{16,24},{20,28},{24,16},{28,20},{1,9},{5... | collective-permute-start | bytes 491528 | tf_op jit(solution)/shard_map/ppermute | solution.py:31
  37.3 5.3 %collective-permute-start.14 = (bf16[160,512]{1,0:T(8,128)(2,1)S(1)}, bf16[160,512]{1,0:T(8,128)(2,1)S(1)}, u32[]{:S(2)}, u32[]{:S(2)}) collective-permute-start(bf16[160,512]{1,0:T(8,128)(2,1)S(1)} %stack.13.refs_0_), channel_id=1, source_target_pairs={{0,4},{4,0},{8,12},{12,8},{16,20},{20,16},{24,28},{28,24},{1,5},{5... | collective-permute-start | bytes 491528 | tf_op jit(solution)/shard_map/ppermute | solution.py:31
  40.8 1.8 %collective-permute-start.17 = (bf16[160,512]{1,0:T(8,128)(2,1)S(1)}, bf16[160,512]{1,0:T(8,128)(2,1)S(1)}, u32[]{:S(2)}, u32[]{:S(2)}) collective-permute-start(bf16[160,512]{1,0:T(8,128)(2,1)S(1)} %collective-permute-done.13.refs_3_), channel_id=1, source_target_pairs={{0,4},{4,0},{8,12},{12,8},{16,20},{20,16},{24,28},{28,24},{1,5},{5... | collective-permute-start | bytes 491528 | tf_op jit(solution)/shard_map/ppermute | solution.py:31
  42.1 1.4 %collective-permute-start.16 = (bf16[160,512]{1,0:T(8,128)(2,1)S(1)}, bf16[160,512]{1,0:T(8,128)(2,1)S(1)}, u32[]{:S(2)}, u32[]{:S(2)}) collective-permute-start(bf16[160,512]{1,0:T(8,128)(2,1)S(1)} %collective-permute-done.12.refs_2_), channel_id=1, source_target_pairs={{0,4},{4,0},{8,12},{12,8},{16,20},{20,16},{24,28},{28,24},{1,5},{5... | collective-permute-start | bytes 491528 | tf_op jit(solution)/shard_map/ppermute | solution.py:31
  42.1 1.6 %collective-permute-start.15 = (bf16[160,512]{1,0:T(8,128)(2,1)S(1)}, bf16[160,512]{1,0:T(8,128)(2,1)S(1)}, u32[]{:S(2)}, u32[]{:S(2)}) collective-permute-start(bf16[160,512]{1,0:T(8,128)(2,1)S(1)} %collective-permute-done.11.refs_1_), channel_id=1, source_target_pairs={{0,4},{4,0},{8,12},{12,8},{16,20},{20,16},{24,28},{28,24},{1,5},{5... | collective-permute-start | bytes 491528 | tf_op jit(solution)/shard_map/ppermute | solution.py:31

commit v7 on v6

--- a/solution.py
+++ b/solution.py
@@ -193,9 +193,7 @@
 
 
 def reciprocal(value):
-    rough = pl.reciprocal(value, approx=True)
-    rough = rough * (2.0 - value * rough)
-    return rough * (2.0 - value * rough)
+    return pltpu.reciprocal(value, approx=True)
 
 
 def eliminate(tiles):
@@ -213,54 +211,90 @@
         cleared = jnp.where(window, 0.0, old)
         rows = [jnp.where(marks[k], 1.0, spread(cleared[k : k + 1, :])) for k in range(SUB)]
         steps, near, far = [None] * SUB, {}, {}
-        kept, scale = [None] * SUB, None
-        for k in range(0, SUB, 2):
+        kept, roots = [None] * SUB, [None] * SUB
+
+        def keep(k, low, ratio, values, others):
+            last = others[k + 1]
+            kept[k] = rows[k]
+            for m in range(k, SUB):
+                kept[k] = jnp.where(marks[m], values[m], kept[k])
+            kept[k + 1] = rows[k + 1] - ratio * rows[k]
+            for m in range(k + 1, SUB):
+                kept[k + 1] = jnp.where(marks[m], others[m], kept[k + 1])
+            roots[k], roots[k + 1] = lax.rsqrt(low), lax.rsqrt(last)
+
+        for k in range(0, SUB, 4):
             low, cross, high = pivot[k][k], pivot[k][k + 1], pivot[k + 1][k + 1]
             area = low * high - cross * cross
-            over = reciprocal(area)
-            rest = range(k + 2, SUB)
-            for m in rest:
+            drop = {}
+            for m in range(k + 2, SUB):
                 near[k, m] = high * pivot[k][m] - cross * pivot[k + 1][m]
                 far[k, m] = low * pivot[k + 1][m] - cross * pivot[k][m]
-            for m in rest:
+            for m in range(k + 2, SUB):
                 for n in range(m, SUB):
-                    pivot[m][n] = pivot[m][n] - over * (pivot[k][m] * near[k, n] + pivot[k + 1][m] * far[k, n])
-            for m in rest:
-                near[k, m] = over * near[k, m]
-                far[k, m] = over * far[k, m]
+                    drop[m, n] = pivot[k][m] * near[k, n] + pivot[k + 1][m] * far[k, n]
+            c, d = k + 2, k + 3
+            grown = {(m, n): area * pivot[m][n] - drop[m, n] for m in (c, d) for n in range(m, SUB)}
+            low2, cross2, high2 = grown[c, c], grown[c, d], grown[d, d]
+            area2 = low2 * high2 - cross2 * cross2
+            over, over2 = reciprocal(area), reciprocal(area2)
+            for m in range(k + 4, SUB):
+                near[c, m] = high2 * grown[c, m] - cross2 * grown[d, m]
+                far[c, m] = low2 * grown[d, m] - cross2 * grown[c, m]
+            for m in range(k + 4, SUB):
+                for n in range(m, SUB):
+                    drop2 = grown[c, m] * near[c, n] + grown[d, m] * far[c, n]
+                    pivot[m][n] = pivot[m][n] - over * (drop[m, n] + over2 * drop2)
+            for m in range(k + 2, SUB):
+                near[k, m], far[k, m] = over * near[k, m], over * far[k, m]
                 rows[m] = rows[m] - (near[k, m] * rows[k] + far[k, m] * rows[k + 1])
+            for m in range(k + 4, SUB):
+                near[c, m], far[c, m] = over2 * near[c, m], over2 * far[c, m]
+                rows[m] = rows[m] - (near[c, m] * rows[c] + far[c, m] * rows[d])
             steps[k] = over * (high * rows[k] - cross * rows[k + 1])
             steps[k + 1] = over * (low * rows[k + 1] - cross * rows[k])
+            both = area * over2
+            steps[c] = both * (high2 * rows[c] - cross2 * rows[d])
+            steps[d] = both * (low2 * rows[d] - cross2 * rows[c])
+
             inner = reciprocal(low)
             ratio = cross * inner
-            kept[k] = rows[k]
-            kept[k + 1] = rows[k + 1] - ratio * rows[k]
-            for m in range(k, SUB):
-                kept[k] = jnp.where(marks[m], pivot[k][m], kept[k])
-            last = area * inner
-            kept[k + 1] = jnp.where(marks[k + 1], last, kept[k + 1])
-            for m in rest:
-                kept[k + 1] = jnp.where(marks[m], pivot[k + 1][m] - ratio * pivot[k][m], kept[k + 1])
-            roots = lax.rsqrt(low), lax.rsqrt(last)
-            scale = roots[0] if scale is None else jnp.where(sub >= k, roots[0], scale)
-            scale = jnp.where(sub >= k + 1, roots[1], scale)
+            values = {m: pivot[k][m] for m in range(k, SUB)}
+            others = {m: pivot[k + 1][m] - ratio * pivot[k][m] for m in range(k + 2, SUB)}
+            others[k + 1] = area * inner
+            keep(k, low, ratio, values, others)
+            inner = reciprocal(low2)
+            ratio = cross2 * inner
+            values = {m: over * grown[c, m] for m in range(c, SUB)}
+            others = {m: over * (grown[d, m] - ratio * grown[c, m]) for m in range(c + 2, SUB)}
+            others[d] = over * (area2 * inner)
+            keep(c, values[c], ratio, values, others)
         for k in reversed(range(0, SUB, 2)):
-            for m in range(k + 2, SUB):
+            for m in reversed(range(k + 2, SUB)):
                 steps[k] = steps[k] - near[k, m] * steps[m]
                 steps[k + 1] = steps[k + 1] - far[k, m] * steps[m]
         for i in range(tile + 1, len(tiles)):
             change = [spread(tiles[i][:, first + k : first + k + 1]) * steps[k] for k in range(SUB)]
-            tiles[i] = jnp.where(window, 0.0, tiles[i]) - tree_sum(change)
-        new = kept[0]
+            tiles[i] = jnp.where(window, 0.0, tiles[i]) - tree_sum(change[::-1])
+        new, scale = kept[0], roots[0]
         for k in range(1, SUB):
             new = jnp.where(sub >= k, kept[k], new)
+            scale = jnp.where(sub >= k, roots[k], scale)
         tiles[tile] = new
         scales.append(scale)
     return tiles, scales
 
 
+LEFT, RIGHT = (0, 1, 0, 1, 2, 0), (0, 0, 1, 1, 0, 2)
+
+
+def parts_of(value, order, axis):
+    parts = split(value)
+    return jnp.concatenate([parts[k] for k in order], axis=axis)
+
+
 def factor_kernel(ratio, apart, rows_in, index_ref, *refs):
-    piece_refs, (factor_ref, inverse_ref, sketch, work, line) = refs[:-5], refs[-5:]
+    piece_refs, (factor_ref, inverse_ref, sketch, work) = refs[:-4], refs[-4:]
     cols = work.shape[0]
     for mask, ref in zip(apart, piece_refs):
         at = pl.multiple_of(jnp.bitwise_xor(index_ref[0], mask) * rows_in, rows_in)
@@ -281,34 +315,35 @@
 
     row_in = lax.broadcasted_iota(jnp.int32, (LANE, LANE), 0)
     lane_in = lax.broadcasted_iota(jnp.int32, (LANE, LANE), 1)
-    lane_all = lax.broadcasted_iota(jnp.int32, (LANE, cols), 1)
-    row_all = lax.broadcasted_iota(jnp.int32, (cols, LANE), 0)
-
-    def block_step(block, _):
-        base = pl.multiple_of(block * LANE, LANE)
-        here = pl.ds(base, LANE)
-        tiles = [work[pl.ds(base + SUB * i, SUB), here] for i in range(LANE // SUB)]
+    for base in range(0, cols, LANE):
+        end = base + LANE
+        here = slice(base, end)
+        tiles = [work[base + SUB * i : base + SUB * (i + 1), here] for i in range(LANE // SUB)]
         tiles, scales = eliminate(tiles)
         scale = jnp.concatenate(scales)
         inner = jnp.concatenate(tiles) * scale
         upper = jnp.where(lane_in >= row_in, inner, 0.0)
         lower = jnp.where(lane_in < row_in, inner, jnp.where(lane_in == row_in, scale, 0.0))
-        line[...] = jnp.dot(lower, work[here, :], precision=HIGHEST, preferred_element_type=f32)
-        line[:, here] = upper
-        factor_ref[here, :] = jnp.where(lane_all >= base, line[...], 0.0) * level
-        line[:, here] = lower
-        inverse_ref[here, :] = jnp.where(lane_all < base + LANE, line[...], 0.0) * unit_row
-
-        @pl.when(block < cols // LANE - 1)
-        def _():
-            steps = jnp.dot(lower.T, line[...], precision=HIGHEST, preferred_element_type=f32)
-            panel = jnp.where(row_all >= base + LANE, work[:, here], 0.0)
-            work[:, here] = jnp.where(row_all >= base + LANE, 0.0, work[:, here])
-            work[...] -= jnp.dot(panel, steps, precision=HIGHEST, preferred_element_type=f32)
-
-        return 0
-
-    lax.fori_loop(0, cols // LANE, block_step, 0)
+        line = jnp.dot(parts_of(lower, LEFT, 1), parts_of(work[here, :], RIGHT, 0), preferred_element_type=f32)
+        if end < cols:
+            panel = parts_of(work[end:, here], LEFT, 1)
+            panel = lax.dot_general(panel, parts_of(lower, RIGHT, 1), NT, preferred_element_type=f32)
+            panel = parts_of(panel, LEFT, 1)
+            steps = ([line[:, :base]] if base else []) + [lower, line[:, end:]]
+            steps = parts_of(jnp.concatenate(steps, axis=1), RIGHT, 0)
+            work[end:, here] = jnp.zeros((cols - end, LANE), f32)
+            for start, stop in ((0, LANE), (LANE, cols - end)):
+                if start < stop:
+                    change = jnp.dot(panel[start:stop], steps, preferred_element_type=f32)
+                    work[end + start : end + stop, :] = work[end + start : end + stop, :] - change
+        factor_ref[here, here] = upper * level[:, here]
+        inverse_ref[here, here] = lower * unit_row[:, here]
+        if base:
+            factor_ref[here, :base] = jnp.zeros((LANE, base), f32)
+            inverse_ref[here, :base] = line[:, :base] * unit_row[:, :base]
+        if end < cols:
+            factor_ref[here, end:] = line[:, end:] * level[:, end:]
+            inverse_ref[here, end:] = jnp.zeros((LANE, cols - end), f32)
 
 
 def solve_kernel(apart, rows_in, share, index_ref, inverse_ref, effects_ref, cov_ref, codes_ref, noise_ref, *refs):
@@ -440,7 +475,7 @@
         functools.partial(factor_kernel, math.sqrt(LEVELS / SKETCH), apart, rows_in),
         "factor",
         [((cols, cols), f32)] * 2,
-        [((rows_in * wide, cols), bf16), ((cols, cols), f32), ((LANE, cols), f32)],
+        [((rows_in * wide, cols), bf16), ((cols, cols), f32)],
         index,
         *pieces,
     )

time: 75.9 us -> 68.6 us (0.904)
  Pallas kernels: 36.1 us -> 28.9 us
    pallas_call x7, Pallas kernels: 36.1 us -> 28.9 us  [call(): pl.pallas_call(kernel, out_shape=[jax.ShapeDtypeStruct(shape, dtype) for...]
where the time goes in v7:
time: 68.6 us; the launch traced here: 68.3 us
  Pallas kernels  28.9 us (42%)
  waiting for transfers between devices  17.7 us (26%)
  starting transfers between devices  17.1 us (25%)
  local copies, waits for them, and re-layouts  3.88 us (6%)
  between operations  0.73 us (1%)
    pallas_call x7, Pallas kernels, call(): pl.pallas_call(kernel, out_shape=[jax.ShapeDtypeStruct(shape, dtype) for...  28.9 us
    ppermute x18, waiting for transfers between devices, partner(): return lax.ppermute(value, axis, pairs)  17.7 us
    ppermute x18, starting transfers between devices, partner(): return lax.ppermute(value, axis, pairs)  17.1 us
    unnamed x14, local copies, waits for them, and re-layouts  3.14 us
  transfers between devices with their start and end apart: 18, of which 11 were waited for; matrix products, arithmetic and copies ran while one was open for 0% of the time, Pallas kernels for 1%

profile of v7, /device:TPU:0, one launch (start us, length us, event | category | flops | bytes accessed | tf_op | source)
XLA Modules:
  0.0 68.3 jit_solution(4996581967133614726)
XLA Ops:
  0.6 0.7 tile.2
  1.3 0.1 broadcast_in_dim_tile.3
  1.4 0.5 collective-permute-start
  1.8 0.8 %collective-permute-done = s32[1,128]{1,0:T(1,128)S(1)} collective-permute-done((s32[1,128]{1,0:T(1,128)S(1)}, s32[1,128]{1,0:T(1,128)S(1)}, u32[]{:S(2)}, u32[]{:S(2)}) %collective-permute-start) | collective-permute-done | bytes 544 | tf_op jit(solution)/shard_map/ppermute | solution.py:31
  2.7 3.8 %collective-permute-start.3 = (s32[1,128]{1,0:T(1,128)S(1)}, s32[1,128]{1,0:T(1,128)S(1)}, u32[]{:S(2)}, u32[]{:S(2)}) collective-permute-start(s32[1,128]{1,0:T(1,128)S(1)} %compare_select_fusion.refs_0_), channel_id=1, source_target_pairs={{0,24},{4,28},{8,16},{12,20},{16,8},{20,12},{24,0},{28,4},{1,25},{... | collective-permute-start | bytes 1544 | tf_op jit(solution)/shard_map/ppermute | solution.py:31
  6.5 0.5 collective-permute-start.2
  7.0 0.1 collective-permute-start.1
  7.1 0.1 pad_add_fusion.index_ref
  7.2 0.0 copy-start
  7.2 1.0 %copy-done = bf16[2048,128]{1,0:T(8,128)(2,1)S(1)} copy-done((bf16[2048,128]{1,0:T(8,128)(2,1)S(1)}, bf16[2048,128]{1,0:T(8,128)(2,1)}, u32[]{:S(2)}) %copy-start) | copy-done | bytes 524312
  8.2 0.0 copy-start.2
  8.2 0.7 %copy-done.2 = s32[2048]{0:T(1024)S(1)} copy-done((s32[2048]{0:T(1024)S(1)}, s32[2048]{0:T(1024)}, u32[]{:S(2)}) %copy-start.2) | copy-done | bytes 8216
  8.9 0.0 copy-start.3
  8.9 0.7 %copy-done.3 = f32[2048]{0:T(1024)S(1)} copy-done((f32[2048]{0:T(1024)S(1)}, f32[2048]{0:T(1024)}, u32[]{:S(2)}) %copy-start.3) | copy-done | bytes 8216
  9.6 1.0 %design.1 = (bf16[560,2048]{1,0:T(8,128)(2,1)S(1)}, f32[264,128]{1,0:T(8,128)S(1)}) custom-call(bf16[2048,128]{1,0:T(8,128)(2,1)S(1)} %copy-done, s32[16,128]{1,0:T(8,128)S(1)} %bitcast.8, f32[16,128]{1,0:T(8,128)S(1)} %bitcast.10), custom_call_target="tpu_custom_call" | custom-call | tf_op jit(solution)/shard_map/design/pallas_call | solution.py:405
  10.6 0.0 collective-permute-done.3.refs_3_
  10.7 0.0 collective-permute-done.2.refs_2_
  10.7 0.0 collective-permute-done.1.refs_1_
  10.7 0.0 copy-start.5
  10.7 0.7 %copy-done.5 = s32[2048]{0:T(1024)S(1)} copy-done((s32[2048]{0:T(1024)S(1)}, s32[2048]{0:T(1024)}, u32[]{:S(2)}) %copy-start.5) | copy-done | bytes 8216
  11.4 0.0 copy-start.1
  11.4 0.0 copy-start.4
  11.4 0.0 copy-start.6
  11.4 1.4 %local.1 = (bf16[256,512]{1,0:T(8,128)(2,1)S(1)}, bf16[256,512]{1,0:T(8,128)(2,1)S(1)}) custom-call(s32[2]{0:T(128)S(1)} %pad_add_fusion.index_ref, bf16[560,2048]{1,0:T(8,128)(2,1)S(1)} %get-tuple-element.15.design_ref, f32[264,128]{1,0:T(8,128)S(1)} %get-tuple-element.16.packed_ref, s32[16,128]{1,0:T(8,128)S(1)} %bitcast.12, ...), custom_call_target="tpu_custom_call" | custom-call | tf_op jit(solution)/shard_map/local/pallas_call | solution.py:405
  12.8 0.1 collective-permute-start.4
  12.9 1.5 %collective-permute-done.4.came_ref = bf16[256,512]{1,0:T(8,128)(2,1)S(1)} collective-permute-done((bf16[256,512]{1,0:T(8,128)(2,1)S(1)}, bf16[256,512]{1,0:T(8,128)(2,1)S(1)}, u32[]{:S(2)}, u32[]{:S(2)}) %collective-permute-start.4) | collective-permute-done | bytes 262176 | tf_op jit(solution)/shard_map/ppermute | solution.py:31
  14.4 0.6 pair.1
  15.1 2.0 %collective-permute-start.5 = (bf16[64,512]{1,0:T(8,128)(2,1)S(1)}, bf16[64,512]{1,0:T(8,128)(2,1)S(1)}, u32[]{:S(2)}, u32[]{:S(2)}) collective-permute-start(bf16[64,512]{1,0:T(8,128)(2,1)S(1)} %get-tuple-element.20), channel_id=1, source_target_pairs={{0,8},{4,12},{8,0},{12,4},{16,24},{20,28},{24,16},{28,20},{1,9},{5... | collective-permute-start | bytes 196616 | tf_op jit(solution)/shard_map/ppermute | solution.py:31
  17.0 1.5 %collective-permute-start.6 = (bf16[64,512]{1,0:T(8,128)(2,1)S(1)}, bf16[64,512]{1,0:T(8,128)(2,1)S(1)}, u32[]{:S(2)}, u32[]{:S(2)}) collective-permute-start(bf16[64,512]{1,0:T(8,128)(2,1)S(1)} %get-tuple-element.21), channel_id=1, source_target_pairs={{0,16},{4,20},{8,24},{12,28},{16,0},{20,4},{24,8},{28,12},{1,17},{... | collective-permute-start | bytes 196616 | tf_op jit(solution)/shard_map/ppermute | solution.py:31
  18.5 0.1 collective-permute-start.7
  18.6 0.8 %collective-permute-done.5.refs_1_ = bf16[64,512]{1,0:T(8,128)(2,1)S(1)} collective-permute-done((bf16[64,512]{1,0:T(8,128)(2,1)S(1)}, bf16[64,512]{1,0:T(8,128)(2,1)S(1)}, u32[]{:S(2)}, u32[]{:S(2)}) %collective-permute-start.5) | collective-permute-done | bytes 65568 | tf_op jit(solution)/shard_map/ppermute | solution.py:31
  19.4 1.9 %collective-permute-done.6.refs_2_ = bf16[64,512]{1,0:T(8,128)(2,1)S(1)} collective-permute-done((bf16[64,512]{1,0:T(8,128)(2,1)S(1)}, bf16[64,512]{1,0:T(8,128)(2,1)S(1)}, u32[]{:S(2)}, u32[]{:S(2)}) %collective-permute-start.6) | collective-permute-done | bytes 65568 | tf_op jit(solution)/shard_map/ppermute | solution.py:31
  21.3 2.4 %collective-permute-done.7.refs_3_ = bf16[64,512]{1,0:T(8,128)(2,1)S(1)} collective-permute-done((bf16[64,512]{1,0:T(8,128)(2,1)S(1)}, bf16[64,512]{1,0:T(8,128)(2,1)S(1)}, u32[]{:S(2)}, u32[]{:S(2)}) %collective-permute-start.7) | collective-permute-done | bytes 65568 | tf_op jit(solution)/shard_map/ppermute | solution.py:31
  23.7 0.6 mix.1.refs_0_
  24.3 3.7 %collective-permute-start.10 = (bf16[64,512]{1,0:T(8,128)(2,1)S(1)}, bf16[64,512]{1,0:T(8,128)(2,1)S(1)}, u32[]{:S(2)}, u32[]{:S(2)}) collective-permute-start(bf16[64,512]{1,0:T(8,128)(2,1)S(1)} %mix.1.refs_0_), channel_id=1, source_target_pairs={{0,3},{1,2},{2,1},{3,0},{4,7},{5,6},{6,5},{7,4},{8,11},{9,10},{10,... | collective-permute-start | bytes 196616 | tf_op jit(solution)/shard_map/ppermute | solution.py:31
  28.0 0.0 collective-permute-start.9
  28.0 0.8 %collective-permute-start.8 = (bf16[64,512]{1,0:T(8,128)(2,1)S(1)}, bf16[64,512]{1,0:T(8,128)(2,1)S(1)}, u32[]{:S(2)}, u32[]{:S(2)}) collective-permute-start(bf16[64,512]{1,0:T(8,128)(2,1)S(1)} %mix.1.refs_0_), channel_id=1, source_target_pairs={{0,1},{1,0},{2,3},{3,2},{4,5},{5,4},{6,7},{7,6},{8,9},{9,8},{10,11... | collective-permute-start | bytes 196616 | tf_op jit(solution)/shard_map/ppermute | solution.py:31
  28.8 1.7 %collective-permute-done.10.refs_3_ = bf16[64,512]{1,0:T(8,128)(2,1)S(1)} collective-permute-done((bf16[64,512]{1,0:T(8,128)(2,1)S(1)}, bf16[64,512]{1,0:T(8,128)(2,1)S(1)}, u32[]{:S(2)}, u32[]{:S(2)}) %collective-permute-start.10) | collective-permute-done | bytes 65568 | tf_op jit(solution)/shard_map/ppermute | solution.py:31
  30.5 2.7 %collective-permute-done.9.refs_2_ = bf16[64,512]{1,0:T(8,128)(2,1)S(1)} collective-permute-done((bf16[64,512]{1,0:T(8,128)(2,1)S(1)}, bf16[64,512]{1,0:T(8,128)(2,1)S(1)}, u32[]{:S(2)}, u32[]{:S(2)}) %collective-permute-start.9) | collective-permute-done | bytes 65568 | tf_op jit(solution)/shard_map/ppermute | solution.py:31
  33.2 0.0 collective-permute-done.8.refs_1_
  33.2 0.6 stack.13.refs_0_
  33.8 0.5 collective-permute-start.13
  34.3 1.5 %collective-permute-start.12 = (bf16[160,512]{1,0:T(8,128)(2,1)S(1)}, bf16[160,512]{1,0:T(8,128)(2,1)S(1)}, u32[]{:S(2)}, u32[]{:S(2)}) collective-permute-start(bf16[160,512]{1,0:T(8,128)(2,1)S(1)} %stack.13.refs_0_), channel_id=1, source_target_pairs={{0,16},{4,20},{8,24},{12,28},{16,0},{20,4},{24,8},{28,12},{1,17},{... | collective-permute-start | bytes 491528 | tf_op jit(solution)/shard_map/ppermute | solution.py:31
  35.8 1.5 %collective-permute-start.11 = (bf16[160,512]{1,0:T(8,128)(2,1)S(1)}, bf16[160,512]{1,0:T(8,128)(2,1)S(1)}, u32[]{:S(2)}, u32[]{:S(2)}) collective-permute-start(bf16[160,512]{1,0:T(8,128)(2,1)S(1)} %stack.13.refs_0_), channel_id=1, source_target_pairs={{0,8},{4,12},{8,0},{12,4},{16,24},{20,28},{24,16},{28,20},{1,9},{5... | collective-permute-start | bytes 491528 | tf_op jit(solution)/shard_map/ppermute | solution.py:31
  37.3 0.0 collective-permute-start.14
  37.3 3.5 %collective-permute-done.13.refs_3_ = bf16[160,512]{1,0:T(8,128)(2,1)S(1)} collective-permute-done((bf16[160,512]{1,0:T(8,128)(2,1)S(1)}, bf16[160,512]{1,0:T(8,128)(2,1)S(1)}, u32[]{:S(2)}, u32[]{:S(2)}) %collective-permute-start.13) | collective-permute-done | bytes 163872 | tf_op jit(solution)/shard_map/ppermute | solution.py:31
  40.8 0.0 collective-permute-start.17
  40.8 1.3 %collective-permute-done.12.refs_2_ = bf16[160,512]{1,0:T(8,128)(2,1)S(1)} collective-permute-done((bf16[160,512]{1,0:T(8,128)(2,1)S(1)}, bf16[160,512]{1,0:T(8,128)(2,1)S(1)}, u32[]{:S(2)}, u32[]{:S(2)}) %collective-permute-start.12) | collective-permute-done | bytes 163872 | tf_op jit(solution)/shard_map/ppermute | solution.py:31
  42.1 0.0 collective-permute-start.16
  42.1 0.0 collective-permute-done.11.refs_1_
  42.1 0.5 collective-permute-start.15
  42.6 0.0 collective-permute-done.14.refs_4_
  42.6 0.0 collective-permute-done.17.refs_7_
  42.6 0.9 %collective-permute-done.16.refs_6_ = bf16[160,512]{1,0:T(8,128)(2,1)S(1)} collective-permute-done((bf16[160,512]{1,0:T(8,128)(2,1)S(1)}, bf16[160,512]{1,0:T(8,128)(2,1)S(1)}, u32[]{:S(2)}, u32[]{:S(2)}) %collective-permute-start.16) | collective-permute-done | bytes 163872 | tf_op jit(solution)/shard_map/ppermute | solution.py:31
  43.5 0.2 collective-permute-done.15.refs_5_
  43.7 21.1 %factor.1 = (f32[512,512]{1,0:T(8,128)}, f32[512,512]{1,0:T(8,128)S(1)}) custom-call(s32[2]{0:T(128)S(1)} %pad_add_fusion.index_ref, bf16[160,512]{1,0:T(8,128)(2,1)S(1)} %stack.13.refs_0_, bf16[160,512]{1,0:T(8,128)(2,1)S(1)} %collective-permute-done.11.refs_1_, bf16[160,512]{1,0:T(8,128)(2,1)S(1)} %collective-permute-done.12.refs_2_, ...), custom_call_target="tpu_custom_call" | custom-call | tf_op jit(solution)/shard_map/factor/pallas_call | solution.py:405
  64.8 0.0 copy-done.1
  64.8 0.0 copy-done.4
  64.8 0.0 copy-done.6
  64.8 3.5 %solve.1 = (f32[4,128]{1,0:T(4,128)}, f32[16,128]{1,0:T(8,128)}) custom-call(s32[2]{0:T(128)S(1)} %pad_add_fusion.index_ref, f32[512,512]{1,0:T(8,128)S(1)} %get-tuple-element.23.inverse_ref, f32[4,128]{1,0:T(4,128)S(1)} %bitcast.13, bf16[2048,128]{1,0:T(8,128)(2,1)S(1)} %copy-done.1, s32[16,128]{1,0:T(8,128)S(1)} %bitcast.9, f32[16,128]{1,0:T(8,128)S(1)} %bitcast.11, ...), custom_call_target="tpu_custom_call" | custom-call | tf_op jit(solution)/shard_map/solve/pallas_call | solution.py:405
  (1 shorter events, 0.0 us)
Async XLA Ops:
  1.4 1.3 %collective-permute-start = (s32[1,128]{1,0:T(1,128)S(1)}, s32[1,128]{1,0:T(1,128)S(1)}, u32[]{:S(2)}, u32[]{:S(2)}) collective-permute-start(s32[1,128]{1,0:T(1,128)S(1)} %broadcast_in_dim_tile.3), channel_id=1, source_target_pairs={{0,4},{4,0},{8,12},{12,8},{16,20},{20,16},{24,28},{28,24},{1,5},{5... | collective-permute-start | bytes 1544 | tf_op jit(solution)/shard_map/ppermute | solution.py:31
  2.7 8.0 %collective-permute-start.3 = (s32[1,128]{1,0:T(1,128)S(1)}, s32[1,128]{1,0:T(1,128)S(1)}, u32[]{:S(2)}, u32[]{:S(2)}) collective-permute-start(s32[1,128]{1,0:T(1,128)S(1)} %compare_select_fusion.refs_0_), channel_id=1, source_target_pairs={{0,24},{4,28},{8,16},{12,20},{16,8},{20,12},{24,0},{28,4},{1,25},{... | collective-permute-start | bytes 1544 | tf_op jit(solution)/shard_map/ppermute | solution.py:31
  6.5 4.2 %collective-permute-start.2 = (s32[1,128]{1,0:T(1,128)S(1)}, s32[1,128]{1,0:T(1,128)S(1)}, u32[]{:S(2)}, u32[]{:S(2)}) collective-permute-start(s32[1,128]{1,0:T(1,128)S(1)} %compare_select_fusion.refs_0_), channel_id=1, source_target_pairs={{0,16},{4,20},{8,24},{12,28},{16,0},{20,4},{24,8},{28,12},{1,17},{... | collective-permute-start | bytes 1544 | tf_op jit(solution)/shard_map/ppermute | solution.py:31
  7.0 3.7 %collective-permute-start.1 = (s32[1,128]{1,0:T(1,128)S(1)}, s32[1,128]{1,0:T(1,128)S(1)}, u32[]{:S(2)}, u32[]{:S(2)}) collective-permute-start(s32[1,128]{1,0:T(1,128)S(1)} %compare_select_fusion.refs_0_), channel_id=1, source_target_pairs={{0,8},{4,12},{8,0},{12,4},{16,24},{20,28},{24,16},{28,20},{1,9},{5... | collective-permute-start | bytes 1544 | tf_op jit(solution)/shard_map/ppermute | solution.py:31
  7.2 1.0 %copy-start = (bf16[2048,128]{1,0:T(8,128)(2,1)S(1)}, bf16[2048,128]{1,0:T(8,128)(2,1)}, u32[]{:S(2)}) copy-start(bf16[2048,128]{1,0:T(8,128)(2,1)} %cov_ref.3) | copy-start | bytes 1572868
  8.2 0.7 %copy-start.2 = (s32[2048]{0:T(1024)S(1)}, s32[2048]{0:T(1024)}, u32[]{:S(2)}) copy-start(s32[2048]{0:T(1024)} %param.7) | copy-start | bytes 24580
  8.9 0.7 %copy-start.3 = (f32[2048]{0:T(1024)S(1)}, f32[2048]{0:T(1024)}, u32[]{:S(2)}) copy-start(f32[2048]{0:T(1024)} %param.11) | copy-start | bytes 24580
  10.7 0.7 %copy-start.5 = (s32[2048]{0:T(1024)S(1)}, s32[2048]{0:T(1024)}, u32[]{:S(2)}) copy-start(s32[2048]{0:T(1024)} %param.8) | copy-start | bytes 24580
  11.4 53.4 %copy-start.1 = (bf16[2048,128]{1,0:T(8,128)(2,1)S(1)}, bf16[2048,128]{1,0:T(8,128)(2,1)}, u32[]{:S(2)}) copy-start(bf16[2048,128]{1,0:T(8,128)(2,1)} %cov_ref.3) | copy-start | bytes 1572868
  11.4 53.4 %copy-start.4 = (f32[2048]{0:T(1024)S(1)}, f32[2048]{0:T(1024)}, u32[]{:S(2)}) copy-start(f32[2048]{0:T(1024)} %param.11) | copy-start | bytes 24580
  11.4 53.4 %copy-start.6 = (f32[512]{0:T(512)S(1)}, f32[512]{0:T(512)}, u32[]{:S(2)}) copy-start(f32[512]{0:T(512)} %param.10) | copy-start | bytes 6148
  12.8 1.6 %collective-permute-start.4 = (bf16[256,512]{1,0:T(8,128)(2,1)S(1)}, bf16[256,512]{1,0:T(8,128)(2,1)S(1)}, u32[]{:S(2)}, u32[]{:S(2)}) collective-permute-start(bf16[256,512]{1,0:T(8,128)(2,1)S(1)} %get-tuple-element.18), channel_id=1, source_target_pairs={{0,4},{4,0},{8,12},{12,8},{16,20},{20,16},{24,28},{28,24},{1,5},{5... | collective-permute-start | bytes 786440 | tf_op jit(solution)/shard_map/ppermute | solution.py:31
  15.1 4.3 %collective-permute-start.5 = (bf16[64,512]{1,0:T(8,128)(2,1)S(1)}, bf16[64,512]{1,0:T(8,128)(2,1)S(1)}, u32[]{:S(2)}, u32[]{:S(2)}) collective-permute-start(bf16[64,512]{1,0:T(8,128)(2,1)S(1)} %get-tuple-element.20), channel_id=1, source_target_pairs={{0,8},{4,12},{8,0},{12,4},{16,24},{20,28},{24,16},{28,20},{1,9},{5... | collective-permute-start | bytes 196616 | tf_op jit(solution)/shard_map/ppermute | solution.py:31
  17.0 4.3 %collective-permute-start.6 = (bf16[64,512]{1,0:T(8,128)(2,1)S(1)}, bf16[64,512]{1,0:T(8,128)(2,1)S(1)}, u32[]{:S(2)}, u32[]{:S(2)}) collective-permute-start(bf16[64,512]{1,0:T(8,128)(2,1)S(1)} %get-tuple-element.21), channel_id=1, source_target_pairs={{0,16},{4,20},{8,24},{12,28},{16,0},{20,4},{24,8},{28,12},{1,17},{... | collective-permute-start | bytes 196616 | tf_op jit(solution)/shard_map/ppermute | solution.py:31
  18.5 5.2 %collective-permute-start.7 = (bf16[64,512]{1,0:T(8,128)(2,1)S(1)}, bf16[64,512]{1,0:T(8,128)(2,1)S(1)}, u32[]{:S(2)}, u32[]{:S(2)}) collective-permute-start(bf16[64,512]{1,0:T(8,128)(2,1)S(1)} %get-tuple-element.22), channel_id=1, source_target_pairs={{0,24},{4,28},{8,16},{12,20},{16,8},{20,12},{24,0},{28,4},{1,25},{... | collective-permute-start | bytes 196616 | tf_op jit(solution)/shard_map/ppermute | solution.py:31
  24.3 6.1 %collective-permute-start.10 = (bf16[64,512]{1,0:T(8,128)(2,1)S(1)}, bf16[64,512]{1,0:T(8,128)(2,1)S(1)}, u32[]{:S(2)}, u32[]{:S(2)}) collective-permute-start(bf16[64,512]{1,0:T(8,128)(2,1)S(1)} %mix.1.refs_0_), channel_id=1, source_target_pairs={{0,3},{1,2},{2,1},{3,0},{4,7},{5,6},{6,5},{7,4},{8,11},{9,10},{10,... | collective-permute-start | bytes 196616 | tf_op jit(solution)/shard_map/ppermute | solution.py:31
  28.0 5.2 %collective-permute-start.9 = (bf16[64,512]{1,0:T(8,128)(2,1)S(1)}, bf16[64,512]{1,0:T(8,128)(2,1)S(1)}, u32[]{:S(2)}, u32[]{:S(2)}) collective-permute-start(bf16[64,512]{1,0:T(8,128)(2,1)S(1)} %mix.1.refs_0_), channel_id=1, source_target_pairs={{0,2},{1,3},{2,0},{3,1},{4,6},{5,7},{6,4},{7,5},{8,10},{9,11},{10,... | collective-permute-start | bytes 196616 | tf_op jit(solution)/shard_map/ppermute | solution.py:31
  28.0 5.2 %collective-permute-start.8 = (bf16[64,512]{1,0:T(8,128)(2,1)S(1)}, bf16[64,512]{1,0:T(8,128)(2,1)S(1)}, u32[]{:S(2)}, u32[]{:S(2)}) collective-permute-start(bf16[64,512]{1,0:T(8,128)(2,1)S(1)} %mix.1.refs_0_), channel_id=1, source_target_pairs={{0,1},{1,0},{2,3},{3,2},{4,5},{5,4},{6,7},{7,6},{8,9},{9,8},{10,11... | collective-permute-start | bytes 196616 | tf_op jit(solution)/shard_map/ppermute | solution.py:31
  33.8 7.1 %collective-permute-start.13 = (bf16[160,512]{1,0:T(8,128)(2,1)S(1)}, bf16[160,512]{1,0:T(8,128)(2,1)S(1)}, u32[]{:S(2)}, u32[]{:S(2)}) collective-permute-start(bf16[160,512]{1,0:T(8,128)(2,1)S(1)} %stack.13.refs_0_), channel_id=1, source_target_pairs={{0,24},{4,28},{8,16},{12,20},{16,8},{20,12},{24,0},{28,4},{1,25},{... | collective-permute-start | bytes 491528 | tf_op jit(solution)/shard_map/ppermute | solution.py:31
  34.3 7.8 %collective-permute-start.12 = (bf16[160,512]{1,0:T(8,128)(2,1)S(1)}, bf16[160,512]{1,0:T(8,128)(2,1)S(1)}, u32[]{:S(2)}, u32[]{:S(2)}) collective-permute-start(bf16[160,512]{1,0:T(8,128)(2,1)S(1)} %stack.13.refs_0_), channel_id=1, source_target_pairs={{0,16},{4,20},{8,24},{12,28},{16,0},{20,4},{24,8},{28,12},{1,17},{... | collective-permute-start | bytes 491528 | tf_op jit(solution)/shard_map/ppermute | solution.py:31
  35.8 6.3 %collective-permute-start.11 = (bf16[160,512]{1,0:T(8,128)(2,1)S(1)}, bf16[160,512]{1,0:T(8,128)(2,1)S(1)}, u32[]{:S(2)}, u32[]{:S(2)}) collective-permute-start(bf16[160,512]{1,0:T(8,128)(2,1)S(1)} %stack.13.refs_0_), channel_id=1, source_target_pairs={{0,8},{4,12},{8,0},{12,4},{16,24},{20,28},{24,16},{28,20},{1,9},{5... | collective-permute-start | bytes 491528 | tf_op jit(solution)/shard_map/ppermute | solution.py:31
  37.3 5.3 %collective-permute-start.14 = (bf16[160,512]{1,0:T(8,128)(2,1)S(1)}, bf16[160,512]{1,0:T(8,128)(2,1)S(1)}, u32[]{:S(2)}, u32[]{:S(2)}) collective-permute-start(bf16[160,512]{1,0:T(8,128)(2,1)S(1)} %stack.13.refs_0_), channel_id=1, source_target_pairs={{0,4},{4,0},{8,12},{12,8},{16,20},{20,16},{24,28},{28,24},{1,5},{5... | collective-permute-start | bytes 491528 | tf_op jit(solution)/shard_map/ppermute | solution.py:31
  40.8 1.8 %collective-permute-start.17 = (bf16[160,512]{1,0:T(8,128)(2,1)S(1)}, bf16[160,512]{1,0:T(8,128)(2,1)S(1)}, u32[]{:S(2)}, u32[]{:S(2)}) collective-permute-start(bf16[160,512]{1,0:T(8,128)(2,1)S(1)} %collective-permute-done.13.refs_3_), channel_id=1, source_target_pairs={{0,4},{4,0},{8,12},{12,8},{16,20},{20,16},{24,28},{28,24},{1,5},{5... | collective-permute-start | bytes 491528 | tf_op jit(solution)/shard_map/ppermute | solution.py:31
  42.1 1.4 %collective-permute-start.16 = (bf16[160,512]{1,0:T(8,128)(2,1)S(1)}, bf16[160,512]{1,0:T(8,128)(2,1)S(1)}, u32[]{:S(2)}, u32[]{:S(2)}) collective-permute-start(bf16[160,512]{1,0:T(8,128)(2,1)S(1)} %collective-permute-done.12.refs_2_), channel_id=1, source_target_pairs={{0,4},{4,0},{8,12},{12,8},{16,20},{20,16},{24,28},{28,24},{1,5},{5... | collective-permute-start | bytes 491528 | tf_op jit(solution)/shard_map/ppermute | solution.py:31
  42.1 1.6 %collective-permute-start.15 = (bf16[160,512]{1,0:T(8,128)(2,1)S(1)}, bf16[160,512]{1,0:T(8,128)(2,1)S(1)}, u32[]{:S(2)}, u32[]{:S(2)}) collective-permute-start(bf16[160,512]{1,0:T(8,128)(2,1)S(1)} %collective-permute-done.11.refs_1_), channel_id=1, source_target_pairs={{0,4},{4,0},{8,12},{12,8},{16,20},{20,16},{24,28},{28,24},{1,5},{5... | collective-permute-start | bytes 491528 | tf_op jit(solution)/shard_map/ppermute | solution.py:31

commit v8 on v7

--- a/solution.py
+++ b/solution.py
@@ -78,7 +78,19 @@
     return share, tail[:SUB] + tail[SUB : 2 * SUB] + tail[2 * SUB : 3 * SUB]
 
 
-def design_kernel(cov_ref, codes_ref, noise_ref, design, packed):
+def design_kernel(cov_hbm, codes_hbm, signs_hbm, noise_hbm, design, packed, signs, *scratch):
+    cov_ref, codes_ref, signs_ref, noise_ref, arrived = scratch
+    moves = [
+        pltpu.make_async_copy(source, target, arrived.at[k])
+        for k, (source, target) in enumerate(
+            ((cov_hbm, cov_ref), (codes_hbm, codes_ref), (signs_hbm, signs_ref), (noise_hbm, noise_ref))
+        )
+    ]
+    for move in moves:
+        move.start()
+    for move in moves:
+        move.wait()
+    signs[...] = (1 - 2 * signs_ref[...]).astype(f32)
     rows, lanes, same = eye()
     zero = jnp.zeros((LANE, LANE), f32)
     for r in range(codes_ref.shape[0]):
@@ -129,7 +141,7 @@
             line.append((1 - 2 * jnp.bitwise_and(common, 1)).astype(f32))
         halves.append(line)
     for r in range(chunks):
-        sign = (1 - 2 * signs_ref[r : r + 1, :]).astype(f32)
+        sign = signs_ref[r : r + 1, :]
         block, h = divmod(r * LANE, HB)
         for c, (mask, line) in enumerate(zip(masks, halves)):
             value = jnp.where(mask == block, line[h // LANE] * sign, zero)
@@ -293,15 +305,23 @@
     return jnp.concatenate([parts[k] for k in order], axis=axis)
 
 
-def factor_kernel(ratio, apart, rows_in, index_ref, *refs):
+def take_gram(rows_in, index_ref, piece_refs, sketch):
+    for m, ref in enumerate(piece_refs):
+        at = jnp.bitwise_xor(jnp.right_shift(index_ref[0], 1), m) * rows_in
+        sketch[pl.ds(pl.multiple_of(at, rows_in), rows_in), :] = ref[:rows_in, :]
+    rows = sketch[...]
+    return lax.dot_general(rows, rows, (((0,), (0,)), ((), ())), preferred_element_type=f32)
+
+
+def gram_kernel(rows_in, index_ref, *refs):
+    piece_refs, (gram_ref, sketch) = refs[:-2], refs[-2:]
+    gram_ref[...] = take_gram(rows_in, index_ref, piece_refs, sketch)
+
+
+def factor_kernel(ratio, rows_in, index_ref, gram_ref, *refs):
     piece_refs, (factor_ref, inverse_ref, sketch, work) = refs[:-4], refs[-4:]
     cols = work.shape[0]
-    for mask, ref in zip(apart, piece_refs):
-        at = pl.multiple_of(jnp.bitwise_xor(index_ref[0], mask) * rows_in, rows_in)
-        sketch[pl.ds(at, rows_in), :] = ref[:rows_in, :]
-    rows = sketch[...]
-    gram = lax.dot_general(rows, rows, (((0,), (0,)), ((), ())), preferred_element_type=f32)
-    work[...] = gram
+    work[...] = gram_ref[...] + take_gram(rows_in, index_ref, piece_refs, sketch)
     _, _, same = eye()
     diagonal = []
     for at in range(0, cols, LANE):
@@ -423,20 +443,25 @@
     codes, signs, noise = [array.reshape(-1, LANE) for array in (level_codes, sign_bits, noise)]
     effects = effects.reshape(LEVELS, COV)
 
-    lane = jnp.arange(LANE, dtype=jnp.int32)[None, :]
-    want = jnp.tile(sample_rows, LANE // samp)[None, :]
-    want = jnp.where(jnp.bitwise_and(lane // samp, 1) == 0, want, partner(want, "wide", 1))
+    want = jnp.concatenate([sample_rows, partner(sample_rows, "wide", 1)] * (LANE // (2 * samp)))[None, :]
     want = [want] + [partner(want, "wide", m) for m in range(2, MATES, 2)]
 
-    design, packed = call(
+    anywhere = pl.BlockSpec(memory_space=pl.ANY)
+    operands = (covariates, codes, signs, noise)
+    design, packed, signs = pl.pallas_call(
         design_kernel,
-        "design",
-        [((cols + 3 * PACK, rows_dev), bf16), ((share * wide + SUB, LANE), f32)],
-        [],
-        covariates,
-        codes,
-        noise,
-    )
+        out_shape=[
+            jax.ShapeDtypeStruct((cols + 3 * PACK, rows_dev), bf16),
+            jax.ShapeDtypeStruct((share * wide + SUB, LANE), f32),
+            jax.ShapeDtypeStruct(signs.shape, f32),
+        ],
+        in_specs=[anywhere] * 4,
+        out_specs=[VMEM] * 3,
+        scratch_shapes=[pltpu.VMEM(operand.shape, operand.dtype) for operand in operands]
+        + [pltpu.SemaphoreType.DMA((4,))],
+        compiler_params=pltpu.CompilerParams(vmem_limit_bytes=40 * 2**20),
+        name="design",
+    )(*operands)
     sizes = [samp * (2 * m < MATES) + share for m in range(wide // 2)]
     starts = [sum(sizes[:m]) for m in range(wide // 2)]
     stay, go = call(
@@ -469,16 +494,21 @@
         functools.partial(stack_kernel, samp, share), "stack", [((rows_in + share, cols), bf16)], [], index, *pieces
     )
     pieces = [piece] + [partner(piece, "wide", m) for m in range(2, wide, 2)]
-    pieces += [partner(piece, "wide", 1) for piece in pieces]
+    theirs = [partner(piece, "wide", 1) for piece in pieces]
+    sketch = [((rows_in * (wide // 2), cols), bf16)]
+    square = ((cols, cols), f32)
+    (gram,) = call(functools.partial(gram_kernel, rows_in), "gram", [square], sketch, index, *pieces)
+    factor, inverse = call(
+        functools.partial(factor_kernel, math.sqrt(LEVELS / SKETCH), rows_in),
+        "factor",
+        [square] * 2,
+        sketch + [square],
+        index,
+        gram,
+        *theirs,
+    )
+    pieces += theirs
     apart = [2 * m + core for core in range(2) for m in range(wide // 2)]
-    factor, inverse = call(
-        functools.partial(factor_kernel, math.sqrt(LEVELS / SKETCH), apart, rows_in),
-        "factor",
-        [((cols, cols), f32)] * 2,
-        [((rows_in * wide, cols), bf16), ((cols, cols), f32)],
-        index,
-        *pieces,
-    )
     solved, resid = call(
         functools.partial(solve_kernel, apart, rows_in, share),
         "solve",

time: 68.6 us -> 68.1 us (level)
  waiting for transfers between devices: 17.7 us -> 16.7 us
  other arithmetic: 0.08 us -> 0.88 us
  local copies, waits for them, and re-layouts: 3.88 us -> 3.14 us
    pallas_call x0 -> x1, Pallas kernels: none -> 1.11 us  [body(): pl.pallas_call(design_kernel, out_shape=[jax.ShapeDtypeStruct((cols + 3 *...]
    ppermute x18, waiting for transfers between devices: 17.7 us -> 16.7 us  [partner(): return lax.ppermute(value, axis, pairs)]
    broadcast_in_dim x0 -> x1, other arithmetic: none -> 0.81 us  [body(): jnp.concatenate([sample_rows, partner(sample_rows, 'wide', 1)] * (LANE //...]
    another operation x2 -> x0, local copies, waits for them, and re-layouts: 0.74 us -> none  [body(): want = jnp.tile(sample_rows, LANE // samp)[None, :]]
    pallas_call x7, Pallas kernels: 28.9 us -> 28.2 us  [call(): pl.pallas_call(kernel, out_shape=[jax.ShapeDtypeStruct(shape, dtype) for...]
    unnamed x14 -> x12, local copies, waits for them, and re-layouts: 3.14 us -> 3.14 us
  transfers between devices with their start and end apart: 18 -> 18, of which waited for: 11 -> 9; matrix products, arithmetic and copies ran while one was open for 0% -> 0% of each run, Pallas kernels for 1% -> 3%
where the time goes in v8:
time: 68.1 us; the launch traced here: 67.8 us
  Pallas kernels  29.3 us (43%)
  starting transfers between devices  17.1 us (25%)
  waiting for transfers between devices  16.7 us (25%)
  local copies, waits for them, and re-layouts  3.14 us (5%)
  other arithmetic  0.88 us (1%)
  between operations  0.75 us (1%)
    pallas_call x7, Pallas kernels, call(): pl.pallas_call(kernel, out_shape=[jax.ShapeDtypeStruct(shape, dtype) for...  28.2 us
    ppermute x18, starting transfers between devices, partner(): return lax.ppermute(value, axis, pairs)  17.1 us
    ppermute x18, waiting for transfers between devices, partner(): return lax.ppermute(value, axis, pairs)  16.7 us
    unnamed x12, local copies, waits for them, and re-layouts  3.14 us
  transfers between devices with their start and end apart: 18, of which 9 were waited for; matrix products, arithmetic and copies ran while one was open for 0% of the time, Pallas kernels for 3%

profile of v8, /device:TPU:0, one launch (start us, length us, event | category | flops | bytes accessed | tf_op | source)
XLA Modules:
  0.0 67.8 jit_solution(2384945901609227848)
XLA Ops:
  0.6 0.5 collective-permute-start
  1.1 0.1 pad_add_fusion.index_ref
  1.2 0.9 %collective-permute-done = s32[32]{0:T(128)S(1)} collective-permute-done((s32[32]{0:T(128)}, s32[32]{0:T(128)S(1)}, u32[]{:S(2)}, u32[]{:S(2)}) %collective-permute-start) | collective-permute-done | bytes 160 | tf_op jit(solution)/shard_map/ppermute | solution.py:31
  2.1 0.8 %add_bitcast_fusion.refs_0_ = s32[1,128]{1,0:T(1,128)S(1)} fusion(s32[32]{0:T(128)S(1)} %collective-permute-done, s32[32]{0:T(128)} %param.9), kind=kLoop, calls=%fused_computation.1 | loop fusion | flops 384 | bytes 768 | tf_op jit(solution)/shard_map/broadcast_in_dim | solution.py:446
  2.9 3.7 %collective-permute-start.3 = (s32[1,128]{1,0:T(1,128)S(1)}, s32[1,128]{1,0:T(1,128)S(1)}, u32[]{:S(2)}, u32[]{:S(2)}) collective-permute-start(s32[1,128]{1,0:T(1,128)S(1)} %add_bitcast_fusion.refs_0_), channel_id=1, source_target_pairs={{0,24},{4,28},{8,16},{12,20},{16,8},{20,12},{24,0},{28,4},{1,25},{... | collective-permute-start | bytes 1544 | tf_op jit(solution)/shard_map/ppermute | solution.py:31
  6.7 0.5 collective-permute-start.2
  7.2 0.1 collective-permute-start.1
  7.3 0.0 copy-start
  7.3 1.0 %copy-done = bf16[2048,128]{1,0:T(8,128)(2,1)S(1)} copy-done((bf16[2048,128]{1,0:T(8,128)(2,1)S(1)}, bf16[2048,128]{1,0:T(8,128)(2,1)}, u32[]{:S(2)}) %copy-start) | copy-done | bytes 524312
  8.3 0.0 copy-start.2
  8.3 0.7 %copy-done.2 = s32[2048]{0:T(1024)S(1)} copy-done((s32[2048]{0:T(1024)S(1)}, s32[2048]{0:T(1024)}, u32[]{:S(2)}) %copy-start.2) | copy-done | bytes 8216
  9.0 0.0 copy-start.3
  9.0 0.7 %copy-done.3 = f32[2048]{0:T(1024)S(1)} copy-done((f32[2048]{0:T(1024)S(1)}, f32[2048]{0:T(1024)}, u32[]{:S(2)}) %copy-start.3) | copy-done | bytes 8216
  9.7 0.0 copy-start.4
  9.7 0.7 %copy-done.4 = s32[2048]{0:T(1024)S(1)} copy-done((s32[2048]{0:T(1024)S(1)}, s32[2048]{0:T(1024)}, u32[]{:S(2)}) %copy-start.4) | copy-done | bytes 8216
  10.4 1.1 %design.1 = (bf16[560,2048]{1,0:T(8,128)(2,1)S(1)}, f32[264,128]{1,0:T(8,128)S(1)}, f32[16,128]{1,0:T(8,128)S(1)}) custom-call(bf16[2048,128]{1,0:T(8,128)(2,1)S(1)} %copy-done, s32[16,128]{1,0:T(8,128)S(1)} %bitcast.10, s32[16,128]{1,0:T(8,128)S(1)} %bitcast.14, f32[16,128]{1,0:T(8,128)S(1)} %bitcast.12), custom_call_target="tpu_custom_call" | custom-call | tf_op jit(solution)/shard_map/design/pallas_call | solution.py:451
  11.5 0.0 collective-permute-done.3.refs_3_
  11.6 0.0 collective-permute-done.2.refs_2_
  11.6 0.0 collective-permute-done.1.refs_1_
  11.6 1.4 %local.1 = (bf16[256,512]{1,0:T(8,128)(2,1)S(1)}, bf16[256,512]{1,0:T(8,128)(2,1)S(1)}) custom-call(s32[2]{0:T(128)S(1)} %pad_add_fusion.index_ref, bf16[560,2048]{1,0:T(8,128)(2,1)S(1)} %get-tuple-element.16.design_ref, f32[264,128]{1,0:T(8,128)S(1)} %get-tuple-element.17.packed_ref, f32[16,128]{1,0:T(8,128)S(1)} %get-tuple-element.18.signs_ref, ...), custom_call_target="tpu_custom_call" | custom-call | tf_op jit(solution)/shard_map/local/pallas_call | solution.py:425
  13.0 0.1 collective-permute-start.4
  13.1 1.5 %collective-permute-done.4.came_ref = bf16[256,512]{1,0:T(8,128)(2,1)S(1)} collective-permute-done((bf16[256,512]{1,0:T(8,128)(2,1)S(1)}, bf16[256,512]{1,0:T(8,128)(2,1)S(1)}, u32[]{:S(2)}, u32[]{:S(2)}) %collective-permute-start.4) | collective-permute-done | bytes 262176 | tf_op jit(solution)/shard_map/ppermute | solution.py:31
  14.6 0.0 copy-start.1
  14.6 0.0 copy-start.5
  14.6 0.6 pair.1
  15.3 2.0 %collective-permute-start.5 = (bf16[64,512]{1,0:T(8,128)(2,1)S(1)}, bf16[64,512]{1,0:T(8,128)(2,1)S(1)}, u32[]{:S(2)}, u32[]{:S(2)}) collective-permute-start(bf16[64,512]{1,0:T(8,128)(2,1)S(1)} %get-tuple-element.22), channel_id=1, source_target_pairs={{0,8},{4,12},{8,0},{12,4},{16,24},{20,28},{24,16},{28,20},{1,9},{5... | collective-permute-start | bytes 196616 | tf_op jit(solution)/shard_map/ppermute | solution.py:31
  17.2 1.5 %collective-permute-start.6 = (bf16[64,512]{1,0:T(8,128)(2,1)S(1)}, bf16[64,512]{1,0:T(8,128)(2,1)S(1)}, u32[]{:S(2)}, u32[]{:S(2)}) collective-permute-start(bf16[64,512]{1,0:T(8,128)(2,1)S(1)} %get-tuple-element.23), channel_id=1, source_target_pairs={{0,16},{4,20},{8,24},{12,28},{16,0},{20,4},{24,8},{28,12},{1,17},{... | collective-permute-start | bytes 196616 | tf_op jit(solution)/shard_map/ppermute | solution.py:31
  18.8 0.1 collective-permute-start.7
  18.8 0.8 %collective-permute-done.5.refs_1_ = bf16[64,512]{1,0:T(8,128)(2,1)S(1)} collective-permute-done((bf16[64,512]{1,0:T(8,128)(2,1)S(1)}, bf16[64,512]{1,0:T(8,128)(2,1)S(1)}, u32[]{:S(2)}, u32[]{:S(2)}) %collective-permute-start.5) | collective-permute-done | bytes 65568 | tf_op jit(solution)/shard_map/ppermute | solution.py:31
  19.6 1.9 %collective-permute-done.6.refs_2_ = bf16[64,512]{1,0:T(8,128)(2,1)S(1)} collective-permute-done((bf16[64,512]{1,0:T(8,128)(2,1)S(1)}, bf16[64,512]{1,0:T(8,128)(2,1)S(1)}, u32[]{:S(2)}, u32[]{:S(2)}) %collective-permute-start.6) | collective-permute-done | bytes 65568 | tf_op jit(solution)/shard_map/ppermute | solution.py:31
  21.5 2.4 %collective-permute-done.7.refs_3_ = bf16[64,512]{1,0:T(8,128)(2,1)S(1)} collective-permute-done((bf16[64,512]{1,0:T(8,128)(2,1)S(1)}, bf16[64,512]{1,0:T(8,128)(2,1)S(1)}, u32[]{:S(2)}, u32[]{:S(2)}) %collective-permute-start.7) | collective-permute-done | bytes 65568 | tf_op jit(solution)/shard_map/ppermute | solution.py:31
  23.9 0.6 mix.1.refs_0_
  24.5 3.7 %collective-permute-start.10 = (bf16[64,512]{1,0:T(8,128)(2,1)S(1)}, bf16[64,512]{1,0:T(8,128)(2,1)S(1)}, u32[]{:S(2)}, u32[]{:S(2)}) collective-permute-start(bf16[64,512]{1,0:T(8,128)(2,1)S(1)} %mix.1.refs_0_), channel_id=1, source_target_pairs={{0,3},{1,2},{2,1},{3,0},{4,7},{5,6},{6,5},{7,4},{8,11},{9,10},{10,... | collective-permute-start | bytes 196616 | tf_op jit(solution)/shard_map/ppermute | solution.py:31
  28.2 0.0 collective-permute-start.9
  28.2 0.8 %collective-permute-start.8 = (bf16[64,512]{1,0:T(8,128)(2,1)S(1)}, bf16[64,512]{1,0:T(8,128)(2,1)S(1)}, u32[]{:S(2)}, u32[]{:S(2)}) collective-permute-start(bf16[64,512]{1,0:T(8,128)(2,1)S(1)} %mix.1.refs_0_), channel_id=1, source_target_pairs={{0,1},{1,0},{2,3},{3,2},{4,5},{5,4},{6,7},{7,6},{8,9},{9,8},{10,11... | collective-permute-start | bytes 196616 | tf_op jit(solution)/shard_map/ppermute | solution.py:31
  29.0 1.7 %collective-permute-done.10.refs_3_ = bf16[64,512]{1,0:T(8,128)(2,1)S(1)} collective-permute-done((bf16[64,512]{1,0:T(8,128)(2,1)S(1)}, bf16[64,512]{1,0:T(8,128)(2,1)S(1)}, u32[]{:S(2)}, u32[]{:S(2)}) %collective-permute-start.10) | collective-permute-done | bytes 65568 | tf_op jit(solution)/shard_map/ppermute | solution.py:31
  30.7 2.7 %collective-permute-done.9.refs_2_ = bf16[64,512]{1,0:T(8,128)(2,1)S(1)} collective-permute-done((bf16[64,512]{1,0:T(8,128)(2,1)S(1)}, bf16[64,512]{1,0:T(8,128)(2,1)S(1)}, u32[]{:S(2)}, u32[]{:S(2)}) %collective-permute-start.9) | collective-permute-done | bytes 65568 | tf_op jit(solution)/shard_map/ppermute | solution.py:31
  33.4 0.0 collective-permute-done.8.refs_1_
  33.4 0.6 stack.13.refs_0_
  34.0 0.5 collective-permute-start.13
  34.5 1.5 %collective-permute-start.12 = (bf16[160,512]{1,0:T(8,128)(2,1)S(1)}, bf16[160,512]{1,0:T(8,128)(2,1)S(1)}, u32[]{:S(2)}, u32[]{:S(2)}) collective-permute-start(bf16[160,512]{1,0:T(8,128)(2,1)S(1)} %stack.13.refs_0_), channel_id=1, source_target_pairs={{0,16},{4,20},{8,24},{12,28},{16,0},{20,4},{24,8},{28,12},{1,17},{... | collective-permute-start | bytes 491528 | tf_op jit(solution)/shard_map/ppermute | solution.py:31
  36.0 1.5 %collective-permute-start.11 = (bf16[160,512]{1,0:T(8,128)(2,1)S(1)}, bf16[160,512]{1,0:T(8,128)(2,1)S(1)}, u32[]{:S(2)}, u32[]{:S(2)}) collective-permute-start(bf16[160,512]{1,0:T(8,128)(2,1)S(1)} %stack.13.refs_0_), channel_id=1, source_target_pairs={{0,8},{4,12},{8,0},{12,4},{16,24},{20,28},{24,16},{28,20},{1,9},{5... | collective-permute-start | bytes 491528 | tf_op jit(solution)/shard_map/ppermute | solution.py:31
  37.5 0.0 collective-permute-start.14
  37.5 3.5 %collective-permute-done.13.refs_3_ = bf16[160,512]{1,0:T(8,128)(2,1)S(1)} collective-permute-done((bf16[160,512]{1,0:T(8,128)(2,1)S(1)}, bf16[160,512]{1,0:T(8,128)(2,1)S(1)}, u32[]{:S(2)}, u32[]{:S(2)}) %collective-permute-start.13) | collective-permute-done | bytes 163872 | tf_op jit(solution)/shard_map/ppermute | solution.py:31
  41.0 0.0 collective-permute-start.17
  41.0 1.3 %collective-permute-done.12.refs_2_ = bf16[160,512]{1,0:T(8,128)(2,1)S(1)} collective-permute-done((bf16[160,512]{1,0:T(8,128)(2,1)S(1)}, bf16[160,512]{1,0:T(8,128)(2,1)S(1)}, u32[]{:S(2)}, u32[]{:S(2)}) %collective-permute-start.12) | collective-permute-done | bytes 163872 | tf_op jit(solution)/shard_map/ppermute | solution.py:31
  42.3 0.0 collective-permute-start.16
  42.3 0.0 collective-permute-done.11.refs_1_
  42.3 0.5 collective-permute-start.15
  42.8 1.0 %gram.1.gram_ref = f32[512,512]{1,0:T(8,128)S(1)} custom-call(s32[2]{0:T(128)S(1)} %pad_add_fusion.index_ref, bf16[160,512]{1,0:T(8,128)(2,1)S(1)} %stack.13.refs_0_, bf16[160,512]{1,0:T(8,128)(2,1)S(1)} %collective-permute-done.11.refs_1_, bf16[160,512]{1,0:T(8,128)(2,1)S(1)} %collective-permute-done.12.refs_2_, ...), custom_call_target="tpu_custom_call" | custom-call | tf_op jit(solution)/shard_map/gram/pallas_call | solution.py:425
  43.9 0.0 collective-permute-done.14.refs_0_.refs_4_
  43.9 0.0 collective-permute-done.17.refs_3_.refs_7_
  43.9 0.0 collective-permute-done.16.refs_2_.refs_6_
  43.9 0.0 collective-permute-done.15.refs_1_.refs_5_
  43.9 20.3 %factor.1 = (f32[512,512]{1,0:T(8,128)}, f32[512,512]{1,0:T(8,128)S(1)}) custom-call(s32[2]{0:T(128)S(1)} %pad_add_fusion.index_ref, f32[512,512]{1,0:T(8,128)S(1)} %gram.1.gram_ref, bf16[160,512]{1,0:T(8,128)(2,1)S(1)} %collective-permute-done.14.refs_0_.refs_4_, bf16[160,512]{1,0:T(8,128)(2,1)S(1)} %collective-permute-done.15.refs_1_.refs_5_, ...), custom_call_target="tpu_custom_call" | custom-call | tf_op jit(solution)/shard_map/factor/pallas_call | solution.py:425
  64.3 0.0 copy-done.1
  64.3 0.0 copy-done.5
  64.3 3.5 %solve.1 = (f32[4,128]{1,0:T(4,128)}, f32[16,128]{1,0:T(8,128)}) custom-call(s32[2]{0:T(128)S(1)} %pad_add_fusion.index_ref, f32[512,512]{1,0:T(8,128)S(1)} %get-tuple-element.25.inverse_ref, f32[4,128]{1,0:T(4,128)S(1)} %bitcast.15, bf16[2048,128]{1,0:T(8,128)(2,1)S(1)} %copy-done.1, s32[16,128]{1,0:T(8,128)S(1)} %bitcast.11, f32[16,128]{1,0:T(8,128)S(1)} %bitcast.13, ...), custom_call_target="tpu_custom_call" | custom-call | tf_op jit(solution)/shard_map/solve/pallas_call | solution.py:425
Async XLA Ops:
  0.6 1.5 %collective-permute-start = (s32[32]{0:T(128)}, s32[32]{0:T(128)S(1)}, u32[]{:S(2)}, u32[]{:S(2)}) collective-permute-start(s32[32]{0:T(128)} %param.9), channel_id=1, source_target_pairs={{0,4},{4,0},{8,12},{12,8},{16,20},{20,16},{24,28},{28,24},{1,5},{5... | collective-permute-start | bytes 392 | tf_op jit(solution)/shard_map/ppermute | solution.py:31
  2.9 8.6 %collective-permute-start.3 = (s32[1,128]{1,0:T(1,128)S(1)}, s32[1,128]{1,0:T(1,128)S(1)}, u32[]{:S(2)}, u32[]{:S(2)}) collective-permute-start(s32[1,128]{1,0:T(1,128)S(1)} %add_bitcast_fusion.refs_0_), channel_id=1, source_target_pairs={{0,24},{4,28},{8,16},{12,20},{16,8},{20,12},{24,0},{28,4},{1,25},{... | collective-permute-start | bytes 1544 | tf_op jit(solution)/shard_map/ppermute | solution.py:31
  6.7 4.9 %collective-permute-start.2 = (s32[1,128]{1,0:T(1,128)S(1)}, s32[1,128]{1,0:T(1,128)S(1)}, u32[]{:S(2)}, u32[]{:S(2)}) collective-permute-start(s32[1,128]{1,0:T(1,128)S(1)} %add_bitcast_fusion.refs_0_), channel_id=1, source_target_pairs={{0,16},{4,20},{8,24},{12,28},{16,0},{20,4},{24,8},{28,12},{1,17},{... | collective-permute-start | bytes 1544 | tf_op jit(solution)/shard_map/ppermute | solution.py:31
  7.2 4.4 %collective-permute-start.1 = (s32[1,128]{1,0:T(1,128)S(1)}, s32[1,128]{1,0:T(1,128)S(1)}, u32[]{:S(2)}, u32[]{:S(2)}) collective-permute-start(s32[1,128]{1,0:T(1,128)S(1)} %add_bitcast_fusion.refs_0_), channel_id=1, source_target_pairs={{0,8},{4,12},{8,0},{12,4},{16,24},{20,28},{24,16},{28,20},{1,9},{5... | collective-permute-start | bytes 1544 | tf_op jit(solution)/shard_map/ppermute | solution.py:31
  7.3 1.0 %copy-start = (bf16[2048,128]{1,0:T(8,128)(2,1)S(1)}, bf16[2048,128]{1,0:T(8,128)(2,1)}, u32[]{:S(2)}) copy-start(bf16[2048,128]{1,0:T(8,128)(2,1)} %cov_ref.1) | copy-start | bytes 1572868
  8.3 0.7 %copy-start.2 = (s32[2048]{0:T(1024)S(1)}, s32[2048]{0:T(1024)}, u32[]{:S(2)}) copy-start(s32[2048]{0:T(1024)} %param.7) | copy-start | bytes 24580
  9.0 0.7 %copy-start.3 = (f32[2048]{0:T(1024)S(1)}, f32[2048]{0:T(1024)}, u32[]{:S(2)}) copy-start(f32[2048]{0:T(1024)} %param.11) | copy-start | bytes 24580
  9.7 0.7 %copy-start.4 = (s32[2048]{0:T(1024)S(1)}, s32[2048]{0:T(1024)}, u32[]{:S(2)}) copy-start(s32[2048]{0:T(1024)} %param.8) | copy-start | bytes 24580
  13.0 1.6 %collective-permute-start.4 = (bf16[256,512]{1,0:T(8,128)(2,1)S(1)}, bf16[256,512]{1,0:T(8,128)(2,1)S(1)}, u32[]{:S(2)}, u32[]{:S(2)}) collective-permute-start(bf16[256,512]{1,0:T(8,128)(2,1)S(1)} %get-tuple-element.20), channel_id=1, source_target_pairs={{0,4},{4,0},{8,12},{12,8},{16,20},{20,16},{24,28},{28,24},{1,5},{5... | collective-permute-start | bytes 786440 | tf_op jit(solution)/shard_map/ppermute | solution.py:31
  14.6 49.6 %copy-start.1 = (bf16[2048,128]{1,0:T(8,128)(2,1)S(1)}, bf16[2048,128]{1,0:T(8,128)(2,1)}, u32[]{:S(2)}) copy-start(bf16[2048,128]{1,0:T(8,128)(2,1)} %cov_ref.1) | copy-start | bytes 1572868
  14.6 49.6 %copy-start.5 = (f32[512]{0:T(512)S(1)}, f32[512]{0:T(512)}, u32[]{:S(2)}) copy-start(f32[512]{0:T(512)} %param.10) | copy-start | bytes 6148
  15.3 4.3 %collective-permute-start.5 = (bf16[64,512]{1,0:T(8,128)(2,1)S(1)}, bf16[64,512]{1,0:T(8,128)(2,1)S(1)}, u32[]{:S(2)}, u32[]{:S(2)}) collective-permute-start(bf16[64,512]{1,0:T(8,128)(2,1)S(1)} %get-tuple-element.22), channel_id=1, source_target_pairs={{0,8},{4,12},{8,0},{12,4},{16,24},{20,28},{24,16},{28,20},{1,9},{5... | collective-permute-start | bytes 196616 | tf_op jit(solution)/shard_map/ppermute | solution.py:31
  17.2 4.3 %collective-permute-start.6 = (bf16[64,512]{1,0:T(8,128)(2,1)S(1)}, bf16[64,512]{1,0:T(8,128)(2,1)S(1)}, u32[]{:S(2)}, u32[]{:S(2)}) collective-permute-start(bf16[64,512]{1,0:T(8,128)(2,1)S(1)} %get-tuple-element.23), channel_id=1, source_target_pairs={{0,16},{4,20},{8,24},{12,28},{16,0},{20,4},{24,8},{28,12},{1,17},{... | collective-permute-start | bytes 196616 | tf_op jit(solution)/shard_map/ppermute | solution.py:31
  18.8 5.2 %collective-permute-start.7 = (bf16[64,512]{1,0:T(8,128)(2,1)S(1)}, bf16[64,512]{1,0:T(8,128)(2,1)S(1)}, u32[]{:S(2)}, u32[]{:S(2)}) collective-permute-start(bf16[64,512]{1,0:T(8,128)(2,1)S(1)} %get-tuple-element.24), channel_id=1, source_target_pairs={{0,24},{4,28},{8,16},{12,20},{16,8},{20,12},{24,0},{28,4},{1,25},{... | collective-permute-start | bytes 196616 | tf_op jit(solution)/shard_map/ppermute | solution.py:31
  24.5 6.1 %collective-permute-start.10 = (bf16[64,512]{1,0:T(8,128)(2,1)S(1)}, bf16[64,512]{1,0:T(8,128)(2,1)S(1)}, u32[]{:S(2)}, u32[]{:S(2)}) collective-permute-start(bf16[64,512]{1,0:T(8,128)(2,1)S(1)} %mix.1.refs_0_), channel_id=1, source_target_pairs={{0,3},{1,2},{2,1},{3,0},{4,7},{5,6},{6,5},{7,4},{8,11},{9,10},{10,... | collective-permute-start | bytes 196616 | tf_op jit(solution)/shard_map/ppermute | solution.py:31
  28.2 5.2 %collective-permute-start.9 = (bf16[64,512]{1,0:T(8,128)(2,1)S(1)}, bf16[64,512]{1,0:T(8,128)(2,1)S(1)}, u32[]{:S(2)}, u32[]{:S(2)}) collective-permute-start(bf16[64,512]{1,0:T(8,128)(2,1)S(1)} %mix.1.refs_0_), channel_id=1, source_target_pairs={{0,2},{1,3},{2,0},{3,1},{4,6},{5,7},{6,4},{7,5},{8,10},{9,11},{10,... | collective-permute-start | bytes 196616 | tf_op jit(solution)/shard_map/ppermute | solution.py:31
  28.2 5.2 %collective-permute-start.8 = (bf16[64,512]{1,0:T(8,128)(2,1)S(1)}, bf16[64,512]{1,0:T(8,128)(2,1)S(1)}, u32[]{:S(2)}, u32[]{:S(2)}) collective-permute-start(bf16[64,512]{1,0:T(8,128)(2,1)S(1)} %mix.1.refs_0_), channel_id=1, source_target_pairs={{0,1},{1,0},{2,3},{3,2},{4,5},{5,4},{6,7},{7,6},{8,9},{9,8},{10,11... | collective-permute-start | bytes 196616 | tf_op jit(solution)/shard_map/ppermute | solution.py:31
  34.0 7.1 %collective-permute-start.13 = (bf16[160,512]{1,0:T(8,128)(2,1)S(1)}, bf16[160,512]{1,0:T(8,128)(2,1)S(1)}, u32[]{:S(2)}, u32[]{:S(2)}) collective-permute-start(bf16[160,512]{1,0:T(8,128)(2,1)S(1)} %stack.13.refs_0_), channel_id=1, source_target_pairs={{0,24},{4,28},{8,16},{12,20},{16,8},{20,12},{24,0},{28,4},{1,25},{... | collective-permute-start | bytes 491528 | tf_op jit(solution)/shard_map/ppermute | solution.py:31
  34.5 7.8 %collective-permute-start.12 = (bf16[160,512]{1,0:T(8,128)(2,1)S(1)}, bf16[160,512]{1,0:T(8,128)(2,1)S(1)}, u32[]{:S(2)}, u32[]{:S(2)}) collective-permute-start(bf16[160,512]{1,0:T(8,128)(2,1)S(1)} %stack.13.refs_0_), channel_id=1, source_target_pairs={{0,16},{4,20},{8,24},{12,28},{16,0},{20,4},{24,8},{28,12},{1,17},{... | collective-permute-start | bytes 491528 | tf_op jit(solution)/shard_map/ppermute | solution.py:31
  36.0 6.3 %collective-permute-start.11 = (bf16[160,512]{1,0:T(8,128)(2,1)S(1)}, bf16[160,512]{1,0:T(8,128)(2,1)S(1)}, u32[]{:S(2)}, u32[]{:S(2)}) collective-permute-start(bf16[160,512]{1,0:T(8,128)(2,1)S(1)} %stack.13.refs_0_), channel_id=1, source_target_pairs={{0,8},{4,12},{8,0},{12,4},{16,24},{20,28},{24,16},{28,20},{1,9},{5... | collective-permute-start | bytes 491528 | tf_op jit(solution)/shard_map/ppermute | solution.py:31
  37.5 6.3 %collective-permute-start.14 = (bf16[160,512]{1,0:T(8,128)(2,1)S(1)}, bf16[160,512]{1,0:T(8,128)(2,1)S(1)}, u32[]{:S(2)}, u32[]{:S(2)}) collective-permute-start(bf16[160,512]{1,0:T(8,128)(2,1)S(1)} %stack.13.refs_0_), channel_id=1, source_target_pairs={{0,4},{4,0},{8,12},{12,8},{16,20},{20,16},{24,28},{28,24},{1,5},{5... | collective-permute-start | bytes 491528 | tf_op jit(solution)/shard_map/ppermute | solution.py:31
  41.0 2.8 %collective-permute-start.17 = (bf16[160,512]{1,0:T(8,128)(2,1)S(1)}, bf16[160,512]{1,0:T(8,128)(2,1)S(1)}, u32[]{:S(2)}, u32[]{:S(2)}) collective-permute-start(bf16[160,512]{1,0:T(8,128)(2,1)S(1)} %collective-permute-done.13.refs_3_), channel_id=1, source_target_pairs={{0,4},{4,0},{8,12},{12,8},{16,20},{20,16},{24,28},{28,24},{1,5},{5... | collective-permute-start | bytes 491528 | tf_op jit(solution)/shard_map/ppermute | solution.py:31
  42.3 1.6 %collective-permute-start.16 = (bf16[160,512]{1,0:T(8,128)(2,1)S(1)}, bf16[160,512]{1,0:T(8,128)(2,1)S(1)}, u32[]{:S(2)}, u32[]{:S(2)}) collective-permute-start(bf16[160,512]{1,0:T(8,128)(2,1)S(1)} %collective-permute-done.12.refs_2_), channel_id=1, source_target_pairs={{0,4},{4,0},{8,12},{12,8},{16,20},{20,16},{24,28},{28,24},{1,5},{5... | collective-permute-start | bytes 491528 | tf_op jit(solution)/shard_map/ppermute | solution.py:31
  42.3 1.6 %collective-permute-start.15 = (bf16[160,512]{1,0:T(8,128)(2,1)S(1)}, bf16[160,512]{1,0:T(8,128)(2,1)S(1)}, u32[]{:S(2)}, u32[]{:S(2)}) collective-permute-start(bf16[160,512]{1,0:T(8,128)(2,1)S(1)} %collective-permute-done.11.refs_1_), channel_id=1, source_target_pairs={{0,4},{4,0},{8,12},{12,8},{16,20},{20,16},{24,28},{28,24},{1,5},{5... | collective-permute-start | bytes 491528 | tf_op jit(solution)/shard_map/ppermute | solution.py:31

commit v9 on v8

--- a/solution.py
+++ b/solution.py
@@ -281,13 +281,23 @@
             others = {m: over * (grown[d, m] - ratio * grown[c, m]) for m in range(c + 2, SUB)}
             others[d] = over * (area2 * inner)
             keep(c, values[c], ratio, values, others)
+        if tile + 1 < len(tiles):
+            after = tiles[tile + 1]
+            ahead = [spread(after[:, first + k : first + k + 1]) for k in range(SUB)]
+            fresh = jnp.where(window, 0.0, after)
+            for k in range(0, SUB, 2):
+                for m in range(k + 2, SUB):
+                    ahead[m] = ahead[m] - (near[k, m] * ahead[k] + far[k, m] * ahead[k + 1])
+                fresh = fresh - (ahead[k] * steps[k] + ahead[k + 1] * steps[k + 1])
         for k in reversed(range(0, SUB, 2)):
             for m in reversed(range(k + 2, SUB)):
                 steps[k] = steps[k] - near[k, m] * steps[m]
                 steps[k + 1] = steps[k + 1] - far[k, m] * steps[m]
-        for i in range(tile + 1, len(tiles)):
+        for i in range(tile + 2, len(tiles)):
             change = [spread(tiles[i][:, first + k : first + k + 1]) * steps[k] for k in range(SUB)]
             tiles[i] = jnp.where(window, 0.0, tiles[i]) - tree_sum(change[::-1])
+        if tile + 1 < len(tiles):
+            tiles[tile + 1] = fresh
         new, scale = kept[0], roots[0]
         for k in range(1, SUB):
             new = jnp.where(sub >= k, kept[k], new)
@@ -446,7 +456,7 @@
     want = jnp.concatenate([sample_rows, partner(sample_rows, "wide", 1)] * (LANE // (2 * samp)))[None, :]
     want = [want] + [partner(want, "wide", m) for m in range(2, MATES, 2)]
 
-    anywhere = pl.BlockSpec(memory_space=pl.ANY)
+    in_hbm = pl.BlockSpec(memory_space=pltpu.HBM)
     operands = (covariates, codes, signs, noise)
     design, packed, signs = pl.pallas_call(
         design_kernel,
@@ -455,7 +465,7 @@
             jax.ShapeDtypeStruct((share * wide + SUB, LANE), f32),
             jax.ShapeDtypeStruct(signs.shape, f32),
         ],
-        in_specs=[anywhere] * 4,
+        in_specs=[in_hbm] * 4,
         out_specs=[VMEM] * 3,
         scratch_shapes=[pltpu.VMEM(operand.shape, operand.dtype) for operand in operands]
         + [pltpu.SemaphoreType.DMA((4,))],

time: 68.1 us -> 65.9 us (0.968)
  Pallas kernels: 29.3 us -> 27 us
    pallas_call x7, Pallas kernels: 28.2 us -> 25.9 us  [call(): pl.pallas_call(kernel, out_shape=[jax.ShapeDtypeStruct(shape, dtype) for...]
where the time goes in v9:
time: 65.9 us; the launch traced here: 65.6 us
  Pallas kernels  27 us (41%)
  starting transfers between devices  17.1 us (26%)
  waiting for transfers between devices  16.7 us (25%)
  local copies, waits for them, and re-layouts  3.14 us (5%)
  other arithmetic  0.88 us (1%)
  between operations  0.75 us (1%)
    pallas_call x7, Pallas kernels, call(): pl.pallas_call(kernel, out_shape=[jax.ShapeDtypeStruct(shape, dtype) for...  25.9 us
    ppermute x18, starting transfers between devices, partner(): return lax.ppermute(value, axis, pairs)  17.1 us
    ppermute x18, waiting for transfers between devices, partner(): return lax.ppermute(value, axis, pairs)  16.7 us
    unnamed x12, local copies, waits for them, and re-layouts  3.14 us
  transfers between devices with their start and end apart: 18, of which 9 were waited for; matrix products, arithmetic and copies ran while one was open for 0% of the time, Pallas kernels for 3%

profile of v9, /device:TPU:0, one launch (start us, length us, event | category | flops | bytes accessed | tf_op | source)
XLA Modules:
  0.0 65.6 jit_solution(14635275746825846978)
XLA Ops:
  0.6 0.5 collective-permute-start
  1.1 0.1 pad_add_fusion.index_ref
  1.2 0.9 %collective-permute-done = s32[32]{0:T(128)S(1)} collective-permute-done((s32[32]{0:T(128)}, s32[32]{0:T(128)S(1)}, u32[]{:S(2)}, u32[]{:S(2)}) %collective-permute-start) | collective-permute-done | bytes 160 | tf_op jit(solution)/shard_map/ppermute | solution.py:31
  2.1 0.8 %add_bitcast_fusion.refs_0_ = s32[1,128]{1,0:T(1,128)S(1)} fusion(s32[32]{0:T(128)S(1)} %collective-permute-done, s32[32]{0:T(128)} %param.9), kind=kLoop, calls=%fused_computation.1 | loop fusion | flops 384 | bytes 768 | tf_op jit(solution)/shard_map/broadcast_in_dim | solution.py:456
  2.9 3.7 %collective-permute-start.3 = (s32[1,128]{1,0:T(1,128)S(1)}, s32[1,128]{1,0:T(1,128)S(1)}, u32[]{:S(2)}, u32[]{:S(2)}) collective-permute-start(s32[1,128]{1,0:T(1,128)S(1)} %add_bitcast_fusion.refs_0_), channel_id=1, source_target_pairs={{0,24},{4,28},{8,16},{12,20},{16,8},{20,12},{24,0},{28,4},{1,25},{... | collective-permute-start | bytes 1544 | tf_op jit(solution)/shard_map/ppermute | solution.py:31
  6.7 0.5 collective-permute-start.2
  7.2 0.1 collective-permute-start.1
  7.3 0.0 copy-start
  7.3 1.0 %copy-done = bf16[2048,128]{1,0:T(8,128)(2,1)S(1)} copy-done((bf16[2048,128]{1,0:T(8,128)(2,1)S(1)}, bf16[2048,128]{1,0:T(8,128)(2,1)}, u32[]{:S(2)}) %copy-start) | copy-done | bytes 524312
  8.3 0.0 copy-start.2
  8.3 0.7 %copy-done.2 = s32[2048]{0:T(1024)S(1)} copy-done((s32[2048]{0:T(1024)S(1)}, s32[2048]{0:T(1024)}, u32[]{:S(2)}) %copy-start.2) | copy-done | bytes 8216
  9.0 0.0 copy-start.3
  9.0 0.7 %copy-done.3 = f32[2048]{0:T(1024)S(1)} copy-done((f32[2048]{0:T(1024)S(1)}, f32[2048]{0:T(1024)}, u32[]{:S(2)}) %copy-start.3) | copy-done | bytes 8216
  9.7 0.0 copy-start.4
  9.7 0.7 %copy-done.4 = s32[2048]{0:T(1024)S(1)} copy-done((s32[2048]{0:T(1024)S(1)}, s32[2048]{0:T(1024)}, u32[]{:S(2)}) %copy-start.4) | copy-done | bytes 8216
  10.4 1.1 %design.1 = (bf16[560,2048]{1,0:T(8,128)(2,1)S(1)}, f32[264,128]{1,0:T(8,128)S(1)}, f32[16,128]{1,0:T(8,128)S(1)}) custom-call(bf16[2048,128]{1,0:T(8,128)(2,1)S(1)} %copy-done, s32[16,128]{1,0:T(8,128)S(1)} %bitcast.10, s32[16,128]{1,0:T(8,128)S(1)} %bitcast.14, f32[16,128]{1,0:T(8,128)S(1)} %bitcast.12), custom_call_target="tpu_custom_call" | custom-call | tf_op jit(solution)/shard_map/design/pallas_call | solution.py:461
  11.5 0.0 collective-permute-done.3.refs_3_
  11.6 0.0 collective-permute-done.2.refs_2_
  11.6 0.0 collective-permute-done.1.refs_1_
  11.6 1.4 %local.1 = (bf16[256,512]{1,0:T(8,128)(2,1)S(1)}, bf16[256,512]{1,0:T(8,128)(2,1)S(1)}) custom-call(s32[2]{0:T(128)S(1)} %pad_add_fusion.index_ref, bf16[560,2048]{1,0:T(8,128)(2,1)S(1)} %get-tuple-element.16.design_ref, f32[264,128]{1,0:T(8,128)S(1)} %get-tuple-element.17.packed_ref, f32[16,128]{1,0:T(8,128)S(1)} %get-tuple-element.18.signs_ref, ...), custom_call_target="tpu_custom_call" | custom-call | tf_op jit(solution)/shard_map/local/pallas_call | solution.py:435
  13.0 0.1 collective-permute-start.4
  13.1 1.5 %collective-permute-done.4.came_ref = bf16[256,512]{1,0:T(8,128)(2,1)S(1)} collective-permute-done((bf16[256,512]{1,0:T(8,128)(2,1)S(1)}, bf16[256,512]{1,0:T(8,128)(2,1)S(1)}, u32[]{:S(2)}, u32[]{:S(2)}) %collective-permute-start.4) | collective-permute-done | bytes 262176 | tf_op jit(solution)/shard_map/ppermute | solution.py:31
  14.6 0.0 copy-start.1
  14.6 0.0 copy-start.5
  14.6 0.6 pair.1
  15.3 2.0 %collective-permute-start.5 = (bf16[64,512]{1,0:T(8,128)(2,1)S(1)}, bf16[64,512]{1,0:T(8,128)(2,1)S(1)}, u32[]{:S(2)}, u32[]{:S(2)}) collective-permute-start(bf16[64,512]{1,0:T(8,128)(2,1)S(1)} %get-tuple-element.22), channel_id=1, source_target_pairs={{0,8},{4,12},{8,0},{12,4},{16,24},{20,28},{24,16},{28,20},{1,9},{5... | collective-permute-start | bytes 196616 | tf_op jit(solution)/shard_map/ppermute | solution.py:31
  17.2 1.5 %collective-permute-start.6 = (bf16[64,512]{1,0:T(8,128)(2,1)S(1)}, bf16[64,512]{1,0:T(8,128)(2,1)S(1)}, u32[]{:S(2)}, u32[]{:S(2)}) collective-permute-start(bf16[64,512]{1,0:T(8,128)(2,1)S(1)} %get-tuple-element.23), channel_id=1, source_target_pairs={{0,16},{4,20},{8,24},{12,28},{16,0},{20,4},{24,8},{28,12},{1,17},{... | collective-permute-start | bytes 196616 | tf_op jit(solution)/shard_map/ppermute | solution.py:31
  18.8 0.1 collective-permute-start.7
  18.8 0.8 %collective-permute-done.5.refs_1_ = bf16[64,512]{1,0:T(8,128)(2,1)S(1)} collective-permute-done((bf16[64,512]{1,0:T(8,128)(2,1)S(1)}, bf16[64,512]{1,0:T(8,128)(2,1)S(1)}, u32[]{:S(2)}, u32[]{:S(2)}) %collective-permute-start.5) | collective-permute-done | bytes 65568 | tf_op jit(solution)/shard_map/ppermute | solution.py:31
  19.6 1.9 %collective-permute-done.6.refs_2_ = bf16[64,512]{1,0:T(8,128)(2,1)S(1)} collective-permute-done((bf16[64,512]{1,0:T(8,128)(2,1)S(1)}, bf16[64,512]{1,0:T(8,128)(2,1)S(1)}, u32[]{:S(2)}, u32[]{:S(2)}) %collective-permute-start.6) | collective-permute-done | bytes 65568 | tf_op jit(solution)/shard_map/ppermute | solution.py:31
  21.5 2.4 %collective-permute-done.7.refs_3_ = bf16[64,512]{1,0:T(8,128)(2,1)S(1)} collective-permute-done((bf16[64,512]{1,0:T(8,128)(2,1)S(1)}, bf16[64,512]{1,0:T(8,128)(2,1)S(1)}, u32[]{:S(2)}, u32[]{:S(2)}) %collective-permute-start.7) | collective-permute-done | bytes 65568 | tf_op jit(solution)/shard_map/ppermute | solution.py:31
  23.9 0.6 mix.1.refs_0_
  24.5 3.7 %collective-permute-start.10 = (bf16[64,512]{1,0:T(8,128)(2,1)S(1)}, bf16[64,512]{1,0:T(8,128)(2,1)S(1)}, u32[]{:S(2)}, u32[]{:S(2)}) collective-permute-start(bf16[64,512]{1,0:T(8,128)(2,1)S(1)} %mix.1.refs_0_), channel_id=1, source_target_pairs={{0,3},{1,2},{2,1},{3,0},{4,7},{5,6},{6,5},{7,4},{8,11},{9,10},{10,... | collective-permute-start | bytes 196616 | tf_op jit(solution)/shard_map/ppermute | solution.py:31
  28.2 0.0 collective-permute-start.9
  28.2 0.8 %collective-permute-start.8 = (bf16[64,512]{1,0:T(8,128)(2,1)S(1)}, bf16[64,512]{1,0:T(8,128)(2,1)S(1)}, u32[]{:S(2)}, u32[]{:S(2)}) collective-permute-start(bf16[64,512]{1,0:T(8,128)(2,1)S(1)} %mix.1.refs_0_), channel_id=1, source_target_pairs={{0,1},{1,0},{2,3},{3,2},{4,5},{5,4},{6,7},{7,6},{8,9},{9,8},{10,11... | collective-permute-start | bytes 196616 | tf_op jit(solution)/shard_map/ppermute | solution.py:31
  29.0 1.7 %collective-permute-done.10.refs_3_ = bf16[64,512]{1,0:T(8,128)(2,1)S(1)} collective-permute-done((bf16[64,512]{1,0:T(8,128)(2,1)S(1)}, bf16[64,512]{1,0:T(8,128)(2,1)S(1)}, u32[]{:S(2)}, u32[]{:S(2)}) %collective-permute-start.10) | collective-permute-done | bytes 65568 | tf_op jit(solution)/shard_map/ppermute | solution.py:31
  30.7 2.7 %collective-permute-done.9.refs_2_ = bf16[64,512]{1,0:T(8,128)(2,1)S(1)} collective-permute-done((bf16[64,512]{1,0:T(8,128)(2,1)S(1)}, bf16[64,512]{1,0:T(8,128)(2,1)S(1)}, u32[]{:S(2)}, u32[]{:S(2)}) %collective-permute-start.9) | collective-permute-done | bytes 65568 | tf_op jit(solution)/shard_map/ppermute | solution.py:31
  33.4 0.0 collective-permute-done.8.refs_1_
  33.4 0.6 stack.13.refs_0_
  34.0 0.5 collective-permute-start.13
  34.5 1.5 %collective-permute-start.12 = (bf16[160,512]{1,0:T(8,128)(2,1)S(1)}, bf16[160,512]{1,0:T(8,128)(2,1)S(1)}, u32[]{:S(2)}, u32[]{:S(2)}) collective-permute-start(bf16[160,512]{1,0:T(8,128)(2,1)S(1)} %stack.13.refs_0_), channel_id=1, source_target_pairs={{0,16},{4,20},{8,24},{12,28},{16,0},{20,4},{24,8},{28,12},{1,17},{... | collective-permute-start | bytes 491528 | tf_op jit(solution)/shard_map/ppermute | solution.py:31
  36.0 1.5 %collective-permute-start.11 = (bf16[160,512]{1,0:T(8,128)(2,1)S(1)}, bf16[160,512]{1,0:T(8,128)(2,1)S(1)}, u32[]{:S(2)}, u32[]{:S(2)}) collective-permute-start(bf16[160,512]{1,0:T(8,128)(2,1)S(1)} %stack.13.refs_0_), channel_id=1, source_target_pairs={{0,8},{4,12},{8,0},{12,4},{16,24},{20,28},{24,16},{28,20},{1,9},{5... | collective-permute-start | bytes 491528 | tf_op jit(solution)/shard_map/ppermute | solution.py:31
  37.5 0.0 collective-permute-start.14
  37.5 3.5 %collective-permute-done.13.refs_3_ = bf16[160,512]{1,0:T(8,128)(2,1)S(1)} collective-permute-done((bf16[160,512]{1,0:T(8,128)(2,1)S(1)}, bf16[160,512]{1,0:T(8,128)(2,1)S(1)}, u32[]{:S(2)}, u32[]{:S(2)}) %collective-permute-start.13) | collective-permute-done | bytes 163872 | tf_op jit(solution)/shard_map/ppermute | solution.py:31
  41.0 0.0 collective-permute-start.17
  41.0 1.3 %collective-permute-done.12.refs_2_ = bf16[160,512]{1,0:T(8,128)(2,1)S(1)} collective-permute-done((bf16[160,512]{1,0:T(8,128)(2,1)S(1)}, bf16[160,512]{1,0:T(8,128)(2,1)S(1)}, u32[]{:S(2)}, u32[]{:S(2)}) %collective-permute-start.12) | collective-permute-done | bytes 163872 | tf_op jit(solution)/shard_map/ppermute | solution.py:31
  42.3 0.0 collective-permute-start.16
  42.3 0.0 collective-permute-done.11.refs_1_
  42.3 0.5 collective-permute-start.15
  42.8 1.0 %gram.1.gram_ref = f32[512,512]{1,0:T(8,128)S(1)} custom-call(s32[2]{0:T(128)S(1)} %pad_add_fusion.index_ref, bf16[160,512]{1,0:T(8,128)(2,1)S(1)} %stack.13.refs_0_, bf16[160,512]{1,0:T(8,128)(2,1)S(1)} %collective-permute-done.11.refs_1_, bf16[160,512]{1,0:T(8,128)(2,1)S(1)} %collective-permute-done.12.refs_2_, ...), custom_call_target="tpu_custom_call" | custom-call | tf_op jit(solution)/shard_map/gram/pallas_call | solution.py:435
  43.9 0.0 collective-permute-done.14.refs_0_.refs_4_
  43.9 0.0 collective-permute-done.17.refs_3_.refs_7_
  43.9 0.0 collective-permute-done.16.refs_2_.refs_6_
  43.9 0.0 collective-permute-done.15.refs_1_.refs_5_
  43.9 18.1 %factor.1 = (f32[512,512]{1,0:T(8,128)}, f32[512,512]{1,0:T(8,128)S(1)}) custom-call(s32[2]{0:T(128)S(1)} %pad_add_fusion.index_ref, f32[512,512]{1,0:T(8,128)S(1)} %gram.1.gram_ref, bf16[160,512]{1,0:T(8,128)(2,1)S(1)} %collective-permute-done.14.refs_0_.refs_4_, bf16[160,512]{1,0:T(8,128)(2,1)S(1)} %collective-permute-done.15.refs_1_.refs_5_, ...), custom_call_target="tpu_custom_call" | custom-call | tf_op jit(solution)/shard_map/factor/pallas_call | solution.py:435
  62.0 0.0 copy-done.1
  62.0 0.0 copy-done.5
  62.0 3.5 %solve.1 = (f32[4,128]{1,0:T(4,128)}, f32[16,128]{1,0:T(8,128)}) custom-call(s32[2]{0:T(128)S(1)} %pad_add_fusion.index_ref, f32[512,512]{1,0:T(8,128)S(1)} %get-tuple-element.25.inverse_ref, f32[4,128]{1,0:T(4,128)S(1)} %bitcast.15, bf16[2048,128]{1,0:T(8,128)(2,1)S(1)} %copy-done.1, s32[16,128]{1,0:T(8,128)S(1)} %bitcast.11, f32[16,128]{1,0:T(8,128)S(1)} %bitcast.13, ...), custom_call_target="tpu_custom_call" | custom-call | tf_op jit(solution)/shard_map/solve/pallas_call | solution.py:435
Async XLA Ops:
  0.6 1.5 %collective-permute-start = (s32[32]{0:T(128)}, s32[32]{0:T(128)S(1)}, u32[]{:S(2)}, u32[]{:S(2)}) collective-permute-start(s32[32]{0:T(128)} %param.9), channel_id=1, source_target_pairs={{0,4},{4,0},{8,12},{12,8},{16,20},{20,16},{24,28},{28,24},{1,5},{5... | collective-permute-start | bytes 392 | tf_op jit(solution)/shard_map/ppermute | solution.py:31
  2.9 8.6 %collective-permute-start.3 = (s32[1,128]{1,0:T(1,128)S(1)}, s32[1,128]{1,0:T(1,128)S(1)}, u32[]{:S(2)}, u32[]{:S(2)}) collective-permute-start(s32[1,128]{1,0:T(1,128)S(1)} %add_bitcast_fusion.refs_0_), channel_id=1, source_target_pairs={{0,24},{4,28},{8,16},{12,20},{16,8},{20,12},{24,0},{28,4},{1,25},{... | collective-permute-start | bytes 1544 | tf_op jit(solution)/shard_map/ppermute | solution.py:31
  6.7 4.9 %collective-permute-start.2 = (s32[1,128]{1,0:T(1,128)S(1)}, s32[1,128]{1,0:T(1,128)S(1)}, u32[]{:S(2)}, u32[]{:S(2)}) collective-permute-start(s32[1,128]{1,0:T(1,128)S(1)} %add_bitcast_fusion.refs_0_), channel_id=1, source_target_pairs={{0,16},{4,20},{8,24},{12,28},{16,0},{20,4},{24,8},{28,12},{1,17},{... | collective-permute-start | bytes 1544 | tf_op jit(solution)/shard_map/ppermute | solution.py:31
  7.2 4.4 %collective-permute-start.1 = (s32[1,128]{1,0:T(1,128)S(1)}, s32[1,128]{1,0:T(1,128)S(1)}, u32[]{:S(2)}, u32[]{:S(2)}) collective-permute-start(s32[1,128]{1,0:T(1,128)S(1)} %add_bitcast_fusion.refs_0_), channel_id=1, source_target_pairs={{0,8},{4,12},{8,0},{12,4},{16,24},{20,28},{24,16},{28,20},{1,9},{5... | collective-permute-start | bytes 1544 | tf_op jit(solution)/shard_map/ppermute | solution.py:31
  7.3 1.0 %copy-start = (bf16[2048,128]{1,0:T(8,128)(2,1)S(1)}, bf16[2048,128]{1,0:T(8,128)(2,1)}, u32[]{:S(2)}) copy-start(bf16[2048,128]{1,0:T(8,128)(2,1)} %cov_ref.1) | copy-start | bytes 1572868
  8.3 0.7 %copy-start.2 = (s32[2048]{0:T(1024)S(1)}, s32[2048]{0:T(1024)}, u32[]{:S(2)}) copy-start(s32[2048]{0:T(1024)} %param.7) | copy-start | bytes 24580
  9.0 0.7 %copy-start.3 = (f32[2048]{0:T(1024)S(1)}, f32[2048]{0:T(1024)}, u32[]{:S(2)}) copy-start(f32[2048]{0:T(1024)} %param.11) | copy-start | bytes 24580
  9.7 0.7 %copy-start.4 = (s32[2048]{0:T(1024)S(1)}, s32[2048]{0:T(1024)}, u32[]{:S(2)}) copy-start(s32[2048]{0:T(1024)} %param.8) | copy-start | bytes 24580
  13.0 1.6 %collective-permute-start.4 = (bf16[256,512]{1,0:T(8,128)(2,1)S(1)}, bf16[256,512]{1,0:T(8,128)(2,1)S(1)}, u32[]{:S(2)}, u32[]{:S(2)}) collective-permute-start(bf16[256,512]{1,0:T(8,128)(2,1)S(1)} %get-tuple-element.20), channel_id=1, source_target_pairs={{0,4},{4,0},{8,12},{12,8},{16,20},{20,16},{24,28},{28,24},{1,5},{5... | collective-permute-start | bytes 786440 | tf_op jit(solution)/shard_map/ppermute | solution.py:31
  14.6 47.4 %copy-start.1 = (bf16[2048,128]{1,0:T(8,128)(2,1)S(1)}, bf16[2048,128]{1,0:T(8,128)(2,1)}, u32[]{:S(2)}) copy-start(bf16[2048,128]{1,0:T(8,128)(2,1)} %cov_ref.1) | copy-start | bytes 1572868
  14.6 47.4 %copy-start.5 = (f32[512]{0:T(512)S(1)}, f32[512]{0:T(512)}, u32[]{:S(2)}) copy-start(f32[512]{0:T(512)} %param.10) | copy-start | bytes 6148
  15.3 4.3 %collective-permute-start.5 = (bf16[64,512]{1,0:T(8,128)(2,1)S(1)}, bf16[64,512]{1,0:T(8,128)(2,1)S(1)}, u32[]{:S(2)}, u32[]{:S(2)}) collective-permute-start(bf16[64,512]{1,0:T(8,128)(2,1)S(1)} %get-tuple-element.22), channel_id=1, source_target_pairs={{0,8},{4,12},{8,0},{12,4},{16,24},{20,28},{24,16},{28,20},{1,9},{5... | collective-permute-start | bytes 196616 | tf_op jit(solution)/shard_map/ppermute | solution.py:31
  17.2 4.3 %collective-permute-start.6 = (bf16[64,512]{1,0:T(8,128)(2,1)S(1)}, bf16[64,512]{1,0:T(8,128)(2,1)S(1)}, u32[]{:S(2)}, u32[]{:S(2)}) collective-permute-start(bf16[64,512]{1,0:T(8,128)(2,1)S(1)} %get-tuple-element.23), channel_id=1, source_target_pairs={{0,16},{4,20},{8,24},{12,28},{16,0},{20,4},{24,8},{28,12},{1,17},{... | collective-permute-start | bytes 196616 | tf_op jit(solution)/shard_map/ppermute | solution.py:31
  18.8 5.2 %collective-permute-start.7 = (bf16[64,512]{1,0:T(8,128)(2,1)S(1)}, bf16[64,512]{1,0:T(8,128)(2,1)S(1)}, u32[]{:S(2)}, u32[]{:S(2)}) collective-permute-start(bf16[64,512]{1,0:T(8,128)(2,1)S(1)} %get-tuple-element.24), channel_id=1, source_target_pairs={{0,24},{4,28},{8,16},{12,20},{16,8},{20,12},{24,0},{28,4},{1,25},{... | collective-permute-start | bytes 196616 | tf_op jit(solution)/shard_map/ppermute | solution.py:31
  24.5 6.1 %collective-permute-start.10 = (bf16[64,512]{1,0:T(8,128)(2,1)S(1)}, bf16[64,512]{1,0:T(8,128)(2,1)S(1)}, u32[]{:S(2)}, u32[]{:S(2)}) collective-permute-start(bf16[64,512]{1,0:T(8,128)(2,1)S(1)} %mix.1.refs_0_), channel_id=1, source_target_pairs={{0,3},{1,2},{2,1},{3,0},{4,7},{5,6},{6,5},{7,4},{8,11},{9,10},{10,... | collective-permute-start | bytes 196616 | tf_op jit(solution)/shard_map/ppermute | solution.py:31
  28.2 5.2 %collective-permute-start.9 = (bf16[64,512]{1,0:T(8,128)(2,1)S(1)}, bf16[64,512]{1,0:T(8,128)(2,1)S(1)}, u32[]{:S(2)}, u32[]{:S(2)}) collective-permute-start(bf16[64,512]{1,0:T(8,128)(2,1)S(1)} %mix.1.refs_0_), channel_id=1, source_target_pairs={{0,2},{1,3},{2,0},{3,1},{4,6},{5,7},{6,4},{7,5},{8,10},{9,11},{10,... | collective-permute-start | bytes 196616 | tf_op jit(solution)/shard_map/ppermute | solution.py:31
  28.2 5.2 %collective-permute-start.8 = (bf16[64,512]{1,0:T(8,128)(2,1)S(1)}, bf16[64,512]{1,0:T(8,128)(2,1)S(1)}, u32[]{:S(2)}, u32[]{:S(2)}) collective-permute-start(bf16[64,512]{1,0:T(8,128)(2,1)S(1)} %mix.1.refs_0_), channel_id=1, source_target_pairs={{0,1},{1,0},{2,3},{3,2},{4,5},{5,4},{6,7},{7,6},{8,9},{9,8},{10,11... | collective-permute-start | bytes 196616 | tf_op jit(solution)/shard_map/ppermute | solution.py:31
  34.0 7.1 %collective-permute-start.13 = (bf16[160,512]{1,0:T(8,128)(2,1)S(1)}, bf16[160,512]{1,0:T(8,128)(2,1)S(1)}, u32[]{:S(2)}, u32[]{:S(2)}) collective-permute-start(bf16[160,512]{1,0:T(8,128)(2,1)S(1)} %stack.13.refs_0_), channel_id=1, source_target_pairs={{0,24},{4,28},{8,16},{12,20},{16,8},{20,12},{24,0},{28,4},{1,25},{... | collective-permute-start | bytes 491528 | tf_op jit(solution)/shard_map/ppermute | solution.py:31
  34.5 7.8 %collective-permute-start.12 = (bf16[160,512]{1,0:T(8,128)(2,1)S(1)}, bf16[160,512]{1,0:T(8,128)(2,1)S(1)}, u32[]{:S(2)}, u32[]{:S(2)}) collective-permute-start(bf16[160,512]{1,0:T(8,128)(2,1)S(1)} %stack.13.refs_0_), channel_id=1, source_target_pairs={{0,16},{4,20},{8,24},{12,28},{16,0},{20,4},{24,8},{28,12},{1,17},{... | collective-permute-start | bytes 491528 | tf_op jit(solution)/shard_map/ppermute | solution.py:31
  36.0 6.3 %collective-permute-start.11 = (bf16[160,512]{1,0:T(8,128)(2,1)S(1)}, bf16[160,512]{1,0:T(8,128)(2,1)S(1)}, u32[]{:S(2)}, u32[]{:S(2)}) collective-permute-start(bf16[160,512]{1,0:T(8,128)(2,1)S(1)} %stack.13.refs_0_), channel_id=1, source_target_pairs={{0,8},{4,12},{8,0},{12,4},{16,24},{20,28},{24,16},{28,20},{1,9},{5... | collective-permute-start | bytes 491528 | tf_op jit(solution)/shard_map/ppermute | solution.py:31
  37.5 6.3 %collective-permute-start.14 = (bf16[160,512]{1,0:T(8,128)(2,1)S(1)}, bf16[160,512]{1,0:T(8,128)(2,1)S(1)}, u32[]{:S(2)}, u32[]{:S(2)}) collective-permute-start(bf16[160,512]{1,0:T(8,128)(2,1)S(1)} %stack.13.refs_0_), channel_id=1, source_target_pairs={{0,4},{4,0},{8,12},{12,8},{16,20},{20,16},{24,28},{28,24},{1,5},{5... | collective-permute-start | bytes 491528 | tf_op jit(solution)/shard_map/ppermute | solution.py:31
  41.0 2.8 %collective-permute-start.17 = (bf16[160,512]{1,0:T(8,128)(2,1)S(1)}, bf16[160,512]{1,0:T(8,128)(2,1)S(1)}, u32[]{:S(2)}, u32[]{:S(2)}) collective-permute-start(bf16[160,512]{1,0:T(8,128)(2,1)S(1)} %collective-permute-done.13.refs_3_), channel_id=1, source_target_pairs={{0,4},{4,0},{8,12},{12,8},{16,20},{20,16},{24,28},{28,24},{1,5},{5... | collective-permute-start | bytes 491528 | tf_op jit(solution)/shard_map/ppermute | solution.py:31
  42.3 1.6 %collective-permute-start.16 = (bf16[160,512]{1,0:T(8,128)(2,1)S(1)}, bf16[160,512]{1,0:T(8,128)(2,1)S(1)}, u32[]{:S(2)}, u32[]{:S(2)}) collective-permute-start(bf16[160,512]{1,0:T(8,128)(2,1)S(1)} %collective-permute-done.12.refs_2_), channel_id=1, source_target_pairs={{0,4},{4,0},{8,12},{12,8},{16,20},{20,16},{24,28},{28,24},{1,5},{5... | collective-permute-start | bytes 491528 | tf_op jit(solution)/shard_map/ppermute | solution.py:31
  42.3 1.6 %collective-permute-start.15 = (bf16[160,512]{1,0:T(8,128)(2,1)S(1)}, bf16[160,512]{1,0:T(8,128)(2,1)S(1)}, u32[]{:S(2)}, u32[]{:S(2)}) collective-permute-start(bf16[160,512]{1,0:T(8,128)(2,1)S(1)} %collective-permute-done.11.refs_1_), channel_id=1, source_target_pairs={{0,4},{4,0},{8,12},{12,8},{16,20},{20,16},{24,28},{28,24},{1,5},{5... | collective-permute-start | bytes 491528 | tf_op jit(solution)/shard_map/ppermute | solution.py:31

commit v10 on v9

--- a/solution.py
+++ b/solution.py
@@ -78,24 +78,12 @@
     return share, tail[:SUB] + tail[SUB : 2 * SUB] + tail[2 * SUB : 3 * SUB]
 
 
-def design_kernel(cov_hbm, codes_hbm, signs_hbm, noise_hbm, design, packed, signs, *scratch):
-    cov_ref, codes_ref, signs_ref, noise_ref, arrived = scratch
-    moves = [
-        pltpu.make_async_copy(source, target, arrived.at[k])
-        for k, (source, target) in enumerate(
-            ((cov_hbm, cov_ref), (codes_hbm, codes_ref), (signs_hbm, signs_ref), (noise_hbm, noise_ref))
-        )
-    ]
-    for move in moves:
-        move.start()
-    for move in moves:
-        move.wait()
-    signs[...] = (1 - 2 * signs_ref[...]).astype(f32)
+def design_kernel(cov_ref, marks_ref, noise_ref, design, packed):
     rows, lanes, same = eye()
     zero = jnp.zeros((LANE, LANE), f32)
-    for r in range(codes_ref.shape[0]):
+    for r in range(marks_ref.shape[0]):
         here = slice(r * LANE, (r + 1) * LANE)
-        code = codes_ref[r : r + 1, :]
+        code = jnp.bitwise_and(marks_ref[r : r + 1, :], LEVELS - 1)
         turned = cov_ref[here, :].astype(f32).T
         for level in range(LEVELS):
             design[level * LANE : (level + 1) * LANE, here] = jnp.where(code == level, turned, zero).astype(bf16)
@@ -118,30 +106,28 @@
     packed[2 * LANE + rest :, :] = jnp.concatenate([back[:LEVELS]] + extra + [jnp.zeros((2, LANE), f32)])
 
 
-def local_kernel(samp, share, starts, index_ref, design_ref, packed_ref, signs_ref, *refs):
+def local_kernel(samp, share, starts, index_ref, design_ref, packed_ref, marks_ref, *refs):
     want_refs, (stay_ref, go_ref, table) = refs[:-3], refs[-3:]
-    chunks = signs_ref.shape[0]
-    lanes = lax.broadcasted_iota(jnp.int32, (1, LANE), 1)
-    wide_lanes, same = eye()[1:]
+    chunks = marks_ref.shape[0]
+    lanes = eye()[1]
     zero = jnp.zeros((LANE, LANE), f32)
-    pairs = LANE // (2 * samp)
+    per = LANE // samp
+    small = lax.broadcasted_iota(jnp.int32, (samp, samp), 0) == lax.broadcasted_iota(jnp.int32, (samp, samp), 1)
 
     masks, halves = [], []
-    for c in range(MATES // 2 // pairs):
-        want = want_refs[c * pairs][...]
-        for q in range(1, pairs):
-            want = jnp.where(lanes >= 2 * samp * q, want_refs[c * pairs + q][...], want)
-        want = to_column(want.astype(f32), same).astype(jnp.int32)
+    for c in range(MATES // per):
+        want = [to_column(ref[...].astype(f32), small) for ref in want_refs[c * per : (c + 1) * per]]
+        want = jnp.concatenate(want).astype(jnp.int32)
         masks.append(jnp.right_shift(want, HB.bit_length() - 1))
         line = []
         for h in range(HB // LANE):
-            common = jnp.bitwise_and(want, wide_lanes + h * LANE)
+            common = jnp.bitwise_and(want, lanes + h * LANE)
             for shift in (4, 2, 1):
                 common = jnp.bitwise_xor(common, jnp.right_shift(common, shift))
             line.append((1 - 2 * jnp.bitwise_and(common, 1)).astype(f32))
         halves.append(line)
     for r in range(chunks):
-        sign = signs_ref[r : r + 1, :]
+        sign = jnp.where(marks_ref[r : r + 1, :] < LEVELS, 1.0, -1.0)
         block, h = divmod(r * LANE, HB)
         for c, (mask, line) in enumerate(zip(masks, halves)):
             value = jnp.where(mask == block, line[h // LANE] * sign, zero)
@@ -376,7 +362,7 @@
             inverse_ref[here, end:] = jnp.zeros((LANE, cols - end), f32)
 
 
-def solve_kernel(apart, rows_in, share, index_ref, inverse_ref, effects_ref, cov_ref, codes_ref, noise_ref, *refs):
+def solve_kernel(apart, rows_in, share, index_ref, inverse_ref, effects_ref, cov_ref, marks_ref, noise_ref, *refs):
     piece_refs, (solved_ref, resid_ref, packed) = refs[:-3], refs[-3:]
     rows, lanes, same = eye()
     extra = None
@@ -423,8 +409,8 @@
     values = jnp.zeros((SUB, cov_ref.shape[0]), f32)
     for part in split(left):
         values = values + lax.dot_general(part, cov_ref[...], NT, preferred_element_type=f32)[:SUB]
-    for r in range(codes_ref.shape[0]):
-        code = codes_ref[r : r + 1, :]
+    for r in range(marks_ref.shape[0]):
+        code = jnp.bitwise_and(marks_ref[r : r + 1, :], LEVELS - 1)
         total = noise_ref[r : r + 1, :]
         for level in range(LEVELS):
             total = total + jnp.where(code == level, values[level : level + 1, r * LANE : (r + 1) * LANE], 0.0)
@@ -450,28 +436,23 @@
     samp = whole_up(sample_rows.shape[0], PACK)
     share = whole_up(max(2 * LANE // wide, 3 * SUB), PACK)
     sample_rows = jnp.pad(sample_rows, (0, samp - sample_rows.shape[0]), constant_values=-1)
-    codes, signs, noise = [array.reshape(-1, LANE) for array in (level_codes, sign_bits, noise)]
+    marks = (level_codes + LEVELS * sign_bits).reshape(-1, LANE)
+    noise = noise.reshape(-1, LANE)
     effects = effects.reshape(LEVELS, COV)
 
-    want = jnp.concatenate([sample_rows, partner(sample_rows, "wide", 1)] * (LANE // (2 * samp)))[None, :]
+    want = sample_rows[None, :]
     want = [want] + [partner(want, "wide", m) for m in range(2, MATES, 2)]
-
-    in_hbm = pl.BlockSpec(memory_space=pltpu.HBM)
-    operands = (covariates, codes, signs, noise)
-    design, packed, signs = pl.pallas_call(
+    want = [one for piece in want for one in (piece, partner(piece, "wide", 1))]
+
+    design, packed = call(
         design_kernel,
-        out_shape=[
-            jax.ShapeDtypeStruct((cols + 3 * PACK, rows_dev), bf16),
-            jax.ShapeDtypeStruct((share * wide + SUB, LANE), f32),
-            jax.ShapeDtypeStruct(signs.shape, f32),
-        ],
-        in_specs=[in_hbm] * 4,
-        out_specs=[VMEM] * 3,
-        scratch_shapes=[pltpu.VMEM(operand.shape, operand.dtype) for operand in operands]
-        + [pltpu.SemaphoreType.DMA((4,))],
-        compiler_params=pltpu.CompilerParams(vmem_limit_bytes=40 * 2**20),
-        name="design",
-    )(*operands)
+        "design",
+        [((cols + 3 * PACK, rows_dev), bf16), ((share * wide + SUB, LANE), f32)],
+        [],
+        covariates,
+        marks,
+        noise,
+    )
     sizes = [samp * (2 * m < MATES) + share for m in range(wide // 2)]
     starts = [sum(sizes[:m]) for m in range(wide // 2)]
     stay, go = call(
@@ -482,7 +463,7 @@
         index,
         design,
         packed,
-        signs,
+        marks,
         *want,
     )
     pieces = call(
@@ -522,13 +503,13 @@
     solved, resid = call(
         functools.partial(solve_kernel, apart, rows_in, share),
         "solve",
-        [((LEVELS, COV), f32), (codes.shape, f32)],
+        [((LEVELS, COV), f32), (noise.shape, f32)],
         [((share * wide, LANE), f32)],
         index,
         inverse,
         effects,
         covariates,
-        codes,
+        marks,
         noise,
         *pieces,
     )

time: 65.9 us -> 66 us (level)
  starting transfers between devices: 17.1 us -> 18.1 us
  local copies, waits for them, and re-layouts: 3.14 us -> 2.4 us
    pallas_call x7 -> x8, Pallas kernels: 25.9 us -> 27.1 us  [call(): pl.pallas_call(kernel, out_shape=[jax.ShapeDtypeStruct(shape, dtype) for...]
    pallas_call x1 -> x0, Pallas kernels: 1.11 us -> none  [body(): pl.pallas_call(design_kernel, out_shape=[jax.ShapeDtypeStruct((cols + 3 *...]
    ppermute x18 -> x21, starting transfers between devices: 17.1 us -> 18.1 us  [partner(): return lax.ppermute(value, axis, pairs)]
    broadcast_in_dim x1 -> x0, other arithmetic: 0.81 us -> none  [body(): jnp.concatenate([sample_rows, partner(sample_rows, 'wide', 1)] * (LANE //...]
    unnamed x12 -> x10, local copies, waits for them, and re-layouts: 3.14 us -> 2.4 us
    reshape x0 -> x1, other arithmetic: none -> 0.72 us  [body(): marks = (level_codes + LEVELS * sign_bits).reshape(-1, LANE)]
    ppermute x18 -> x21, waiting for transfers between devices: 16.7 us -> 16.5 us  [partner(): return lax.ppermute(value, axis, pairs)]
  transfers between devices with their start and end apart: 18 -> 21, of which waited for: 9 -> 11; matrix products, arithmetic and copies ran while one was open for 0% -> 1% of each run, Pallas kernels for 3% -> 3%
where the time goes in v10:
time: 66 us; the launch traced here: 65.7 us
  Pallas kernels  27.1 us (41%)
  starting transfers between devices  18.1 us (27%)
  waiting for transfers between devices  16.5 us (25%)
  local copies, waits for them, and re-layouts  2.4 us (4%)
  other arithmetic  0.79 us (1%)
  between operations  0.72 us (1%)
    pallas_call x8, Pallas kernels, call(): pl.pallas_call(kernel, out_shape=[jax.ShapeDtypeStruct(shape, dtype) for...  27.1 us
    ppermute x21, starting transfers between devices, partner(): return lax.ppermute(value, axis, pairs)  18.1 us
    ppermute x21, waiting for transfers between devices, partner(): return lax.ppermute(value, axis, pairs)  16.5 us
    unnamed x10, local copies, waits for them, and re-layouts  2.4 us
  transfers between devices with their start and end apart: 21, of which 11 were waited for; matrix products, arithmetic and copies ran while one was open for 1% of the time, Pallas kernels for 3%

profile of v10, /device:TPU:0, one launch (start us, length us, event | category | flops | bytes accessed | tf_op | source)
XLA Modules:
  0.0 65.7 jit_solution(15853252096272436738)
XLA Ops:
  0.6 4.0 %collective-permute-start.5 = (s32[1,32]{1,0:T(1,128)}, s32[1,32]{1,0:T(1,128)S(1)}, u32[]{:S(2)}, u32[]{:S(2)}) collective-permute-start(s32[1,32]{1,0:T(1,128)} %bitcast.12), channel_id=1, source_target_pairs={{0,24},{4,28},{8,16},{12,20},{16,8},{20,12},{24,0},{28,4},{1,25},{... | collective-permute-start | bytes 392 | tf_op jit(solution)/shard_map/ppermute | solution.py:31
  4.6 0.5 collective-permute-start.3
  5.1 0.1 collective-permute-start.1
  5.2 0.0 collective-permute-start
  5.2 0.1 pad_add_fusion.index_ref
  5.3 0.7 %add_bitcast_fusion.marks_ref = s32[16,128]{1,0:T(8,128)S(1)} fusion(s32[2048]{0:T(1024)} %param.7, s32[2048]{0:T(1024)} %param.8), kind=kLoop, calls=%fused_computation | loop fusion | flops 4096 | bytes 24576 | tf_op jit(solution)/shard_map/reshape | solution.py:439
  6.0 0.0 copy-start
  6.0 1.0 %copy-done = bf16[2048,128]{1,0:T(8,128)(2,1)S(1)} copy-done((bf16[2048,128]{1,0:T(8,128)(2,1)S(1)}, bf16[2048,128]{1,0:T(8,128)(2,1)}, u32[]{:S(2)}) %copy-start) | copy-done | bytes 524312
  7.1 0.0 copy-start.2
  7.1 0.7 %copy-done.2 = f32[2048]{0:T(1024)S(1)} copy-done((f32[2048]{0:T(1024)S(1)}, f32[2048]{0:T(1024)}, u32[]{:S(2)}) %copy-start.2) | copy-done | bytes 8216
  7.8 1.0 %design.1 = (bf16[560,2048]{1,0:T(8,128)(2,1)S(1)}, f32[264,128]{1,0:T(8,128)S(1)}) custom-call(bf16[2048,128]{1,0:T(8,128)(2,1)S(1)} %copy-done, s32[16,128]{1,0:T(8,128)S(1)} %add_bitcast_fusion.marks_ref, f32[16,128]{1,0:T(8,128)S(1)} %bitcast.9), custom_call_target="tpu_custom_call" | custom-call | tf_op jit(solution)/shard_map/design/pallas_call | solution.py:421
  8.8 0.0 collective-permute-done.5.refs_6_
  8.8 0.6 collective-permute-start.6
  9.4 0.0 collective-permute-done.3.refs_4_
  9.4 0.1 collective-permute-start.4
  9.5 0.0 collective-permute-done.1.refs_2_
  9.5 0.4 collective-permute-start.2
  9.9 0.0 collective-permute-done.refs_1_
  9.9 0.3 collective-permute-done.6.refs_7_
  10.2 0.3 collective-permute-done.4.refs_5_
  10.5 0.2 collective-permute-done.2.refs_3_
  10.7 0.0 copy-start.4
  10.7 0.7 copy-done.4
  11.4 1.6 %local.1 = (bf16[256,512]{1,0:T(8,128)(2,1)S(1)}, bf16[256,512]{1,0:T(8,128)(2,1)S(1)}) custom-call(s32[2]{0:T(128)S(1)} %pad_add_fusion.index_ref, bf16[560,2048]{1,0:T(8,128)(2,1)S(1)} %get-tuple-element.15.design_ref, f32[264,128]{1,0:T(8,128)S(1)} %get-tuple-element.16.packed_ref, s32[16,128]{1,0:T(8,128)S(1)} %add_bitcast_fusion.marks_ref, ...), custom_call_target="tpu_custom_call" | custom-call | tf_op jit(solution)/shard_map/local/pallas_call | solution.py:421
  12.9 0.4 collective-permute-start.7
  13.3 1.2 %collective-permute-done.7.came_ref = bf16[256,512]{1,0:T(8,128)(2,1)S(1)} collective-permute-done((bf16[256,512]{1,0:T(8,128)(2,1)S(1)}, bf16[256,512]{1,0:T(8,128)(2,1)S(1)}, u32[]{:S(2)}, u32[]{:S(2)}) %collective-permute-start.7) | collective-permute-done | bytes 262176 | tf_op jit(solution)/shard_map/ppermute | solution.py:31
  14.5 0.0 copy-start.1
  14.6 0.0 copy-start.3
  14.6 0.7 pair.1
  15.2 2.0 %collective-permute-start.8 = (bf16[64,512]{1,0:T(8,128)(2,1)S(1)}, bf16[64,512]{1,0:T(8,128)(2,1)S(1)}, u32[]{:S(2)}, u32[]{:S(2)}) collective-permute-start(bf16[64,512]{1,0:T(8,128)(2,1)S(1)} %get-tuple-element.20), channel_id=1, source_target_pairs={{0,8},{4,12},{8,0},{12,4},{16,24},{20,28},{24,16},{28,20},{1,9},{5... | collective-permute-start | bytes 196616 | tf_op jit(solution)/shard_map/ppermute | solution.py:31
  17.2 1.5 %collective-permute-start.9 = (bf16[64,512]{1,0:T(8,128)(2,1)S(1)}, bf16[64,512]{1,0:T(8,128)(2,1)S(1)}, u32[]{:S(2)}, u32[]{:S(2)}) collective-permute-start(bf16[64,512]{1,0:T(8,128)(2,1)S(1)} %get-tuple-element.21), channel_id=1, source_target_pairs={{0,16},{4,20},{8,24},{12,28},{16,0},{20,4},{24,8},{28,12},{1,17},{... | collective-permute-start | bytes 196616 | tf_op jit(solution)/shard_map/ppermute | solution.py:31
  18.7 0.1 collective-permute-start.10
  18.8 1.0 %collective-permute-done.8.refs_1_ = bf16[64,512]{1,0:T(8,128)(2,1)S(1)} collective-permute-done((bf16[64,512]{1,0:T(8,128)(2,1)S(1)}, bf16[64,512]{1,0:T(8,128)(2,1)S(1)}, u32[]{:S(2)}, u32[]{:S(2)}) %collective-permute-start.8) | collective-permute-done | bytes 65568 | tf_op jit(solution)/shard_map/ppermute | solution.py:31
  19.7 1.7 %collective-permute-done.9.refs_2_ = bf16[64,512]{1,0:T(8,128)(2,1)S(1)} collective-permute-done((bf16[64,512]{1,0:T(8,128)(2,1)S(1)}, bf16[64,512]{1,0:T(8,128)(2,1)S(1)}, u32[]{:S(2)}, u32[]{:S(2)}) %collective-permute-start.9) | collective-permute-done | bytes 65568 | tf_op jit(solution)/shard_map/ppermute | solution.py:31
  21.4 2.4 %collective-permute-done.10.refs_3_ = bf16[64,512]{1,0:T(8,128)(2,1)S(1)} collective-permute-done((bf16[64,512]{1,0:T(8,128)(2,1)S(1)}, bf16[64,512]{1,0:T(8,128)(2,1)S(1)}, u32[]{:S(2)}, u32[]{:S(2)}) %collective-permute-start.10) | collective-permute-done | bytes 65568 | tf_op jit(solution)/shard_map/ppermute | solution.py:31
  23.8 0.6 mix.1.refs_0_
  24.5 3.7 %collective-permute-start.13 = (bf16[64,512]{1,0:T(8,128)(2,1)S(1)}, bf16[64,512]{1,0:T(8,128)(2,1)S(1)}, u32[]{:S(2)}, u32[]{:S(2)}) collective-permute-start(bf16[64,512]{1,0:T(8,128)(2,1)S(1)} %mix.1.refs_0_), channel_id=1, source_target_pairs={{0,3},{1,2},{2,1},{3,0},{4,7},{5,6},{6,5},{7,4},{8,11},{9,10},{10,... | collective-permute-start | bytes 196616 | tf_op jit(solution)/shard_map/ppermute | solution.py:31
  28.1 0.0 collective-permute-start.12
  28.1 0.8 %collective-permute-start.11 = (bf16[64,512]{1,0:T(8,128)(2,1)S(1)}, bf16[64,512]{1,0:T(8,128)(2,1)S(1)}, u32[]{:S(2)}, u32[]{:S(2)}) collective-permute-start(bf16[64,512]{1,0:T(8,128)(2,1)S(1)} %mix.1.refs_0_), channel_id=1, source_target_pairs={{0,1},{1,0},{2,3},{3,2},{4,5},{5,4},{6,7},{7,6},{8,9},{9,8},{10,11... | collective-permute-start | bytes 196616 | tf_op jit(solution)/shard_map/ppermute | solution.py:31
  28.9 1.7 %collective-permute-done.13.refs_3_ = bf16[64,512]{1,0:T(8,128)(2,1)S(1)} collective-permute-done((bf16[64,512]{1,0:T(8,128)(2,1)S(1)}, bf16[64,512]{1,0:T(8,128)(2,1)S(1)}, u32[]{:S(2)}, u32[]{:S(2)}) %collective-permute-start.13) | collective-permute-done | bytes 65568 | tf_op jit(solution)/shard_map/ppermute | solution.py:31
  30.6 2.7 %collective-permute-done.12.refs_2_ = bf16[64,512]{1,0:T(8,128)(2,1)S(1)} collective-permute-done((bf16[64,512]{1,0:T(8,128)(2,1)S(1)}, bf16[64,512]{1,0:T(8,128)(2,1)S(1)}, u32[]{:S(2)}, u32[]{:S(2)}) %collective-permute-start.12) | collective-permute-done | bytes 65568 | tf_op jit(solution)/shard_map/ppermute | solution.py:31
  33.3 0.0 collective-permute-done.11.refs_1_
  33.3 0.6 stack.13.refs_0_
  33.9 0.6 collective-permute-start.16
  34.5 1.5 %collective-permute-start.15 = (bf16[160,512]{1,0:T(8,128)(2,1)S(1)}, bf16[160,512]{1,0:T(8,128)(2,1)S(1)}, u32[]{:S(2)}, u32[]{:S(2)}) collective-permute-start(bf16[160,512]{1,0:T(8,128)(2,1)S(1)} %stack.13.refs_0_), channel_id=1, source_target_pairs={{0,16},{4,20},{8,24},{12,28},{16,0},{20,4},{24,8},{28,12},{1,17},{... | collective-permute-start | bytes 491528 | tf_op jit(solution)/shard_map/ppermute | solution.py:31
  35.9 1.5 %collective-permute-start.14 = (bf16[160,512]{1,0:T(8,128)(2,1)S(1)}, bf16[160,512]{1,0:T(8,128)(2,1)S(1)}, u32[]{:S(2)}, u32[]{:S(2)}) collective-permute-start(bf16[160,512]{1,0:T(8,128)(2,1)S(1)} %stack.13.refs_0_), channel_id=1, source_target_pairs={{0,8},{4,12},{8,0},{12,4},{16,24},{20,28},{24,16},{28,20},{1,9},{5... | collective-permute-start | bytes 491528 | tf_op jit(solution)/shard_map/ppermute | solution.py:31
  37.4 0.0 collective-permute-start.17
  37.4 3.9 %collective-permute-done.16.refs_3_ = bf16[160,512]{1,0:T(8,128)(2,1)S(1)} collective-permute-done((bf16[160,512]{1,0:T(8,128)(2,1)S(1)}, bf16[160,512]{1,0:T(8,128)(2,1)S(1)}, u32[]{:S(2)}, u32[]{:S(2)}) %collective-permute-start.16) | collective-permute-done | bytes 163872 | tf_op jit(solution)/shard_map/ppermute | solution.py:31
  41.3 0.0 collective-permute-start.20
  41.3 1.0 %collective-permute-done.15.refs_2_ = bf16[160,512]{1,0:T(8,128)(2,1)S(1)} collective-permute-done((bf16[160,512]{1,0:T(8,128)(2,1)S(1)}, bf16[160,512]{1,0:T(8,128)(2,1)S(1)}, u32[]{:S(2)}, u32[]{:S(2)}) %collective-permute-start.15) | collective-permute-done | bytes 163872 | tf_op jit(solution)/shard_map/ppermute | solution.py:31
  42.4 0.0 collective-permute-start.19
  42.4 0.0 collective-permute-done.14.refs_1_
  42.4 0.5 collective-permute-start.18
  42.9 1.0 %gram.1.gram_ref = f32[512,512]{1,0:T(8,128)S(1)} custom-call(s32[2]{0:T(128)S(1)} %pad_add_fusion.index_ref, bf16[160,512]{1,0:T(8,128)(2,1)S(1)} %stack.13.refs_0_, bf16[160,512]{1,0:T(8,128)(2,1)S(1)} %collective-permute-done.14.refs_1_, bf16[160,512]{1,0:T(8,128)(2,1)S(1)} %collective-permute-done.15.refs_2_, ...), custom_call_target="tpu_custom_call" | custom-call | tf_op jit(solution)/shard_map/gram/pallas_call | solution.py:421
  43.9 0.0 collective-permute-done.17.refs_0_.refs_4_
  44.0 0.0 collective-permute-done.20.refs_3_.refs_7_
  44.0 0.0 collective-permute-done.19.refs_2_.refs_6_
  44.0 0.0 collective-permute-done.18.refs_1_.refs_5_
  44.0 18.1 %factor.1 = (f32[512,512]{1,0:T(8,128)}, f32[512,512]{1,0:T(8,128)S(1)}) custom-call(s32[2]{0:T(128)S(1)} %pad_add_fusion.index_ref, f32[512,512]{1,0:T(8,128)S(1)} %gram.1.gram_ref, bf16[160,512]{1,0:T(8,128)(2,1)S(1)} %collective-permute-done.17.refs_0_.refs_4_, bf16[160,512]{1,0:T(8,128)(2,1)S(1)} %collective-permute-done.18.refs_1_.refs_5_, ...), custom_call_target="tpu_custom_call" | custom-call | tf_op jit(solution)/shard_map/factor/pallas_call | solution.py:421
  62.1 0.0 copy-done.1
  62.1 0.0 copy-done.3
  62.1 3.5 %solve.1 = (f32[4,128]{1,0:T(4,128)}, f32[16,128]{1,0:T(8,128)}) custom-call(s32[2]{0:T(128)S(1)} %pad_add_fusion.index_ref, f32[512,512]{1,0:T(8,128)S(1)} %get-tuple-element.23.inverse_ref, f32[4,128]{1,0:T(4,128)S(1)} %bitcast.11, bf16[2048,128]{1,0:T(8,128)(2,1)S(1)} %copy-done.1, s32[16,128]{1,0:T(8,128)S(1)} %add_bitcast_fusion.marks_ref, ...), custom_call_target="tpu_custom_call" | custom-call | tf_op jit(solution)/shard_map/solve/pallas_call | solution.py:421
Async XLA Ops:
  0.6 8.2 %collective-permute-start.5 = (s32[1,32]{1,0:T(1,128)}, s32[1,32]{1,0:T(1,128)S(1)}, u32[]{:S(2)}, u32[]{:S(2)}) collective-permute-start(s32[1,32]{1,0:T(1,128)} %bitcast.12), channel_id=1, source_target_pairs={{0,24},{4,28},{8,16},{12,20},{16,8},{20,12},{24,0},{28,4},{1,25},{... | collective-permute-start | bytes 392 | tf_op jit(solution)/shard_map/ppermute | solution.py:31
  4.6 4.8 %collective-permute-start.3 = (s32[1,32]{1,0:T(1,128)}, s32[1,32]{1,0:T(1,128)S(1)}, u32[]{:S(2)}, u32[]{:S(2)}) collective-permute-start(s32[1,32]{1,0:T(1,128)} %bitcast.13), channel_id=1, source_target_pairs={{0,16},{4,20},{8,24},{12,28},{16,0},{20,4},{24,8},{28,12},{1,17},{... | collective-permute-start | bytes 392 | tf_op jit(solution)/shard_map/ppermute | solution.py:31
  5.1 4.4 %collective-permute-start.1 = (s32[1,32]{1,0:T(1,128)}, s32[1,32]{1,0:T(1,128)S(1)}, u32[]{:S(2)}, u32[]{:S(2)}) collective-permute-start(s32[1,32]{1,0:T(1,128)} %bitcast.14), channel_id=1, source_target_pairs={{0,8},{4,12},{8,0},{12,4},{16,24},{20,28},{24,16},{28,20},{1,9},{5... | collective-permute-start | bytes 392 | tf_op jit(solution)/shard_map/ppermute | solution.py:31
  5.2 4.7 %collective-permute-start = (s32[1,32]{1,0:T(1,128)}, s32[1,32]{1,0:T(1,128)S(1)}, u32[]{:S(2)}, u32[]{:S(2)}) collective-permute-start(s32[1,32]{1,0:T(1,128)} %bitcast.15), channel_id=1, source_target_pairs={{0,4},{4,0},{8,12},{12,8},{16,20},{20,16},{24,28},{28,24},{1,5},{5... | collective-permute-start | bytes 392 | tf_op jit(solution)/shard_map/ppermute | solution.py:31
  6.0 1.0 %copy-start = (bf16[2048,128]{1,0:T(8,128)(2,1)S(1)}, bf16[2048,128]{1,0:T(8,128)(2,1)}, u32[]{:S(2)}) copy-start(bf16[2048,128]{1,0:T(8,128)(2,1)} %cov_ref.3) | copy-start | bytes 1572868
  7.1 0.7 %copy-start.2 = (f32[2048]{0:T(1024)S(1)}, f32[2048]{0:T(1024)}, u32[]{:S(2)}) copy-start(f32[2048]{0:T(1024)} %param.11) | copy-start | bytes 24580
  8.8 1.4 %collective-permute-start.6 = (s32[1,32]{1,0:T(1,128)S(1)}, s32[1,32]{1,0:T(1,128)S(1)}, u32[]{:S(2)}, u32[]{:S(2)}) collective-permute-start(s32[1,32]{1,0:T(1,128)S(1)} %collective-permute-done.5.refs_6_), channel_id=1, source_target_pairs={{0,4},{4,0},{8,12},{12,8},{16,20},{20,16},{24,28},{28,24},{1,5},{5... | collective-permute-start | bytes 392 | tf_op jit(solution)/shard_map/ppermute | solution.py:31
  9.4 1.1 %collective-permute-start.4 = (s32[1,32]{1,0:T(1,128)S(1)}, s32[1,32]{1,0:T(1,128)S(1)}, u32[]{:S(2)}, u32[]{:S(2)}) collective-permute-start(s32[1,32]{1,0:T(1,128)S(1)} %collective-permute-done.3.refs_4_), channel_id=1, source_target_pairs={{0,4},{4,0},{8,12},{12,8},{16,20},{20,16},{24,28},{28,24},{1,5},{5... | collective-permute-start | bytes 392 | tf_op jit(solution)/shard_map/ppermute | solution.py:31
  9.5 1.2 %collective-permute-start.2 = (s32[1,32]{1,0:T(1,128)S(1)}, s32[1,32]{1,0:T(1,128)S(1)}, u32[]{:S(2)}, u32[]{:S(2)}) collective-permute-start(s32[1,32]{1,0:T(1,128)S(1)} %collective-permute-done.1.refs_2_), channel_id=1, source_target_pairs={{0,4},{4,0},{8,12},{12,8},{16,20},{20,16},{24,28},{28,24},{1,5},{5... | collective-permute-start | bytes 392 | tf_op jit(solution)/shard_map/ppermute | solution.py:31
  10.7 0.7 copy-start.4
  12.9 1.6 %collective-permute-start.7 = (bf16[256,512]{1,0:T(8,128)(2,1)S(1)}, bf16[256,512]{1,0:T(8,128)(2,1)S(1)}, u32[]{:S(2)}, u32[]{:S(2)}) collective-permute-start(bf16[256,512]{1,0:T(8,128)(2,1)S(1)} %get-tuple-element.18), channel_id=1, source_target_pairs={{0,4},{4,0},{8,12},{12,8},{16,20},{20,16},{24,28},{28,24},{1,5},{5... | collective-permute-start | bytes 786440 | tf_op jit(solution)/shard_map/ppermute | solution.py:31
  14.5 47.6 %copy-start.1 = (bf16[2048,128]{1,0:T(8,128)(2,1)S(1)}, bf16[2048,128]{1,0:T(8,128)(2,1)}, u32[]{:S(2)}) copy-start(bf16[2048,128]{1,0:T(8,128)(2,1)} %cov_ref.3) | copy-start | bytes 1572868
  14.6 47.6 %copy-start.3 = (f32[512]{0:T(512)S(1)}, f32[512]{0:T(512)}, u32[]{:S(2)}) copy-start(f32[512]{0:T(512)} %param.10) | copy-start | bytes 6148
  15.2 4.5 %collective-permute-start.8 = (bf16[64,512]{1,0:T(8,128)(2,1)S(1)}, bf16[64,512]{1,0:T(8,128)(2,1)S(1)}, u32[]{:S(2)}, u32[]{:S(2)}) collective-permute-start(bf16[64,512]{1,0:T(8,128)(2,1)S(1)} %get-tuple-element.20), channel_id=1, source_target_pairs={{0,8},{4,12},{8,0},{12,4},{16,24},{20,28},{24,16},{28,20},{1,9},{5... | collective-permute-start | bytes 196616 | tf_op jit(solution)/shard_map/ppermute | solution.py:31
  17.2 4.3 %collective-permute-start.9 = (bf16[64,512]{1,0:T(8,128)(2,1)S(1)}, bf16[64,512]{1,0:T(8,128)(2,1)S(1)}, u32[]{:S(2)}, u32[]{:S(2)}) collective-permute-start(bf16[64,512]{1,0:T(8,128)(2,1)S(1)} %get-tuple-element.21), channel_id=1, source_target_pairs={{0,16},{4,20},{8,24},{12,28},{16,0},{20,4},{24,8},{28,12},{1,17},{... | collective-permute-start | bytes 196616 | tf_op jit(solution)/shard_map/ppermute | solution.py:31
  18.7 5.2 %collective-permute-start.10 = (bf16[64,512]{1,0:T(8,128)(2,1)S(1)}, bf16[64,512]{1,0:T(8,128)(2,1)S(1)}, u32[]{:S(2)}, u32[]{:S(2)}) collective-permute-start(bf16[64,512]{1,0:T(8,128)(2,1)S(1)} %get-tuple-element.22), channel_id=1, source_target_pairs={{0,24},{4,28},{8,16},{12,20},{16,8},{20,12},{24,0},{28,4},{1,25},{... | collective-permute-start | bytes 196616 | tf_op jit(solution)/shard_map/ppermute | solution.py:31
  24.5 6.1 %collective-permute-start.13 = (bf16[64,512]{1,0:T(8,128)(2,1)S(1)}, bf16[64,512]{1,0:T(8,128)(2,1)S(1)}, u32[]{:S(2)}, u32[]{:S(2)}) collective-permute-start(bf16[64,512]{1,0:T(8,128)(2,1)S(1)} %mix.1.refs_0_), channel_id=1, source_target_pairs={{0,3},{1,2},{2,1},{3,0},{4,7},{5,6},{6,5},{7,4},{8,11},{9,10},{10,... | collective-permute-start | bytes 196616 | tf_op jit(solution)/shard_map/ppermute | solution.py:31
  28.1 5.2 %collective-permute-start.12 = (bf16[64,512]{1,0:T(8,128)(2,1)S(1)}, bf16[64,512]{1,0:T(8,128)(2,1)S(1)}, u32[]{:S(2)}, u32[]{:S(2)}) collective-permute-start(bf16[64,512]{1,0:T(8,128)(2,1)S(1)} %mix.1.refs_0_), channel_id=1, source_target_pairs={{0,2},{1,3},{2,0},{3,1},{4,6},{5,7},{6,4},{7,5},{8,10},{9,11},{10,... | collective-permute-start | bytes 196616 | tf_op jit(solution)/shard_map/ppermute | solution.py:31
  28.1 5.2 %collective-permute-start.11 = (bf16[64,512]{1,0:T(8,128)(2,1)S(1)}, bf16[64,512]{1,0:T(8,128)(2,1)S(1)}, u32[]{:S(2)}, u32[]{:S(2)}) collective-permute-start(bf16[64,512]{1,0:T(8,128)(2,1)S(1)} %mix.1.refs_0_), channel_id=1, source_target_pairs={{0,1},{1,0},{2,3},{3,2},{4,5},{5,4},{6,7},{7,6},{8,9},{9,8},{10,11... | collective-permute-start | bytes 196616 | tf_op jit(solution)/shard_map/ppermute | solution.py:31
  33.9 7.5 %collective-permute-start.16 = (bf16[160,512]{1,0:T(8,128)(2,1)S(1)}, bf16[160,512]{1,0:T(8,128)(2,1)S(1)}, u32[]{:S(2)}, u32[]{:S(2)}) collective-permute-start(bf16[160,512]{1,0:T(8,128)(2,1)S(1)} %stack.13.refs_0_), channel_id=1, source_target_pairs={{0,24},{4,28},{8,16},{12,20},{16,8},{20,12},{24,0},{28,4},{1,25},{... | collective-permute-start | bytes 491528 | tf_op jit(solution)/shard_map/ppermute | solution.py:31
  34.5 7.9 %collective-permute-start.15 = (bf16[160,512]{1,0:T(8,128)(2,1)S(1)}, bf16[160,512]{1,0:T(8,128)(2,1)S(1)}, u32[]{:S(2)}, u32[]{:S(2)}) collective-permute-start(bf16[160,512]{1,0:T(8,128)(2,1)S(1)} %stack.13.refs_0_), channel_id=1, source_target_pairs={{0,16},{4,20},{8,24},{12,28},{16,0},{20,4},{24,8},{28,12},{1,17},{... | collective-permute-start | bytes 491528 | tf_op jit(solution)/shard_map/ppermute | solution.py:31
  35.9 6.4 %collective-permute-start.14 = (bf16[160,512]{1,0:T(8,128)(2,1)S(1)}, bf16[160,512]{1,0:T(8,128)(2,1)S(1)}, u32[]{:S(2)}, u32[]{:S(2)}) collective-permute-start(bf16[160,512]{1,0:T(8,128)(2,1)S(1)} %stack.13.refs_0_), channel_id=1, source_target_pairs={{0,8},{4,12},{8,0},{12,4},{16,24},{20,28},{24,16},{28,20},{1,9},{5... | collective-permute-start | bytes 491528 | tf_op jit(solution)/shard_map/ppermute | solution.py:31
  37.4 6.5 %collective-permute-start.17 = (bf16[160,512]{1,0:T(8,128)(2,1)S(1)}, bf16[160,512]{1,0:T(8,128)(2,1)S(1)}, u32[]{:S(2)}, u32[]{:S(2)}) collective-permute-start(bf16[160,512]{1,0:T(8,128)(2,1)S(1)} %stack.13.refs_0_), channel_id=1, source_target_pairs={{0,4},{4,0},{8,12},{12,8},{16,20},{20,16},{24,28},{28,24},{1,5},{5... | collective-permute-start | bytes 491528 | tf_op jit(solution)/shard_map/ppermute | solution.py:31
  41.3 2.6 %collective-permute-start.20 = (bf16[160,512]{1,0:T(8,128)(2,1)S(1)}, bf16[160,512]{1,0:T(8,128)(2,1)S(1)}, u32[]{:S(2)}, u32[]{:S(2)}) collective-permute-start(bf16[160,512]{1,0:T(8,128)(2,1)S(1)} %collective-permute-done.16.refs_3_), channel_id=1, source_target_pairs={{0,4},{4,0},{8,12},{12,8},{16,20},{20,16},{24,28},{28,24},{1,5},{5... | collective-permute-start | bytes 491528 | tf_op jit(solution)/shard_map/ppermute | solution.py:31
  42.4 1.6 %collective-permute-start.19 = (bf16[160,512]{1,0:T(8,128)(2,1)S(1)}, bf16[160,512]{1,0:T(8,128)(2,1)S(1)}, u32[]{:S(2)}, u32[]{:S(2)}) collective-permute-start(bf16[160,512]{1,0:T(8,128)(2,1)S(1)} %collective-permute-done.15.refs_2_), channel_id=1, source_target_pairs={{0,4},{4,0},{8,12},{12,8},{16,20},{20,16},{24,28},{28,24},{1,5},{5... | collective-permute-start | bytes 491528 | tf_op jit(solution)/shard_map/ppermute | solution.py:31
  42.4 1.6 %collective-permute-start.18 = (bf16[160,512]{1,0:T(8,128)(2,1)S(1)}, bf16[160,512]{1,0:T(8,128)(2,1)S(1)}, u32[]{:S(2)}, u32[]{:S(2)}) collective-permute-start(bf16[160,512]{1,0:T(8,128)(2,1)S(1)} %collective-permute-done.14.refs_1_), channel_id=1, source_target_pairs={{0,4},{4,0},{8,12},{12,8},{16,20},{20,16},{24,28},{28,24},{1,5},{5... | collective-permute-start | bytes 491528 | tf_op jit(solution)/shard_map/ppermute | solution.py:31

commit v11 on v10

--- a/solution.py
+++ b/solution.py
@@ -194,7 +194,8 @@
     return pltpu.reciprocal(value, approx=True)
 
 
-def eliminate(tiles):
+def eliminate(tiles, aside):
+    share = -(-len(aside) // len(tiles))
     lane = lax.broadcasted_iota(jnp.int32, (SUB, LANE), 1)
     sub = lax.broadcasted_iota(jnp.int32, (SUB, LANE), 0)
     tiles = list(tiles)
@@ -290,6 +291,8 @@
             scale = jnp.where(sub >= k, roots[k], scale)
         tiles[tile] = new
         scales.append(scale)
+        for work in aside[tile * share : (tile + 1) * share]:
+            work()
     return tiles, scales
 
 
@@ -301,65 +304,94 @@
     return jnp.concatenate([parts[k] for k in order], axis=axis)
 
 
-def take_gram(rows_in, index_ref, piece_refs, sketch):
+def put_pieces(rows_in, index_ref, piece_refs, sketch):
     for m, ref in enumerate(piece_refs):
         at = jnp.bitwise_xor(jnp.right_shift(index_ref[0], 1), m) * rows_in
         sketch[pl.ds(pl.multiple_of(at, rows_in), rows_in), :] = ref[:rows_in, :]
-    rows = sketch[...]
-    return lax.dot_general(rows, rows, (((0,), (0,)), ((), ())), preferred_element_type=f32)
+
+
+def gram_rows(sketch, here):
+    return lax.dot_general(sketch[:, here], sketch[...], (((0,), (0,)), ((), ())), preferred_element_type=f32)
 
 
 def gram_kernel(rows_in, index_ref, *refs):
     piece_refs, (gram_ref, sketch) = refs[:-2], refs[-2:]
-    gram_ref[...] = take_gram(rows_in, index_ref, piece_refs, sketch)
+    put_pieces(rows_in, index_ref, piece_refs, sketch)
+    for at in range(0, gram_ref.shape[0], LANE):
+        gram_ref[at : at + LANE, :] = gram_rows(sketch, slice(at, at + LANE))
 
 
 def factor_kernel(ratio, rows_in, index_ref, gram_ref, *refs):
     piece_refs, (factor_ref, inverse_ref, sketch, work) = refs[:-4], refs[-4:]
-    cols = work.shape[0]
-    work[...] = gram_ref[...] + take_gram(rows_in, index_ref, piece_refs, sketch)
-    _, _, same = eye()
-    diagonal = []
-    for at in range(0, cols, LANE):
-        block = work[at : at + LANE, at : at + LANE]
-        diagonal.append(jnp.sum(jnp.where(same, block, 0.0), axis=0, keepdims=True))
-    unit = [lax.rsqrt(part) for part in diagonal]
-    level = jnp.concatenate([part * one for part, one in zip(diagonal, unit)], axis=1) * ratio
-    unit_row = jnp.concatenate(unit, axis=1)
-    for at, one in zip(range(0, cols, LANE), unit):
-        work[at : at + LANE, :] = work[at : at + LANE, :] * to_column(one, same) * unit_row
-
-    row_in = lax.broadcasted_iota(jnp.int32, (LANE, LANE), 0)
-    lane_in = lax.broadcasted_iota(jnp.int32, (LANE, LANE), 1)
-    for base in range(0, cols, LANE):
-        end = base + LANE
-        here = slice(base, end)
-        tiles = [work[base + SUB * i : base + SUB * (i + 1), here] for i in range(LANE // SUB)]
-        tiles, scales = eliminate(tiles)
+    count = work.shape[0] // LANE
+    spans = [slice(at, at + LANE) for at in range(0, work.shape[0], LANE)]
+    row_in, lane_in, same = eye()
+    diagonals, units = [None] * count, [None] * count
+    put_pieces(rows_in, index_ref, piece_refs, sketch)
+
+    def take_rows(i):
+        work[spans[i], :] = gram_ref[spans[i], :] + gram_rows(sketch, spans[i])
+
+    def take_unit(i):
+        diagonals[i] = jnp.sum(jnp.where(same, work[spans[i], spans[i]], 0.0), axis=0, keepdims=True)
+        units[i] = lax.rsqrt(diagonals[i])
+
+    def scale_rows(i):
+        work[spans[i], :] = work[spans[i], :] * to_column(units[i], same) * jnp.concatenate(units, axis=1)
+
+    take_rows(0)
+    take_unit(0)
+    fresh = work[spans[0], spans[0]] * to_column(units[0], same) * units[0]
+    aside = [functools.partial(take_rows, i) for i in range(1, count)]
+    aside += [functools.partial(take_unit, i) for i in range(1, count)]
+    aside += [functools.partial(scale_rows, i) for i in range(count)]
+    for b, here in enumerate(spans):
+        tiles, scales = eliminate([fresh[at : at + SUB] for at in range(0, LANE, SUB)], aside)
         scale = jnp.concatenate(scales)
         inner = jnp.concatenate(tiles) * scale
-        upper = jnp.where(lane_in >= row_in, inner, 0.0)
         lower = jnp.where(lane_in < row_in, inner, jnp.where(lane_in == row_in, scale, 0.0))
-        line = jnp.dot(parts_of(lower, LEFT, 1), parts_of(work[here, :], RIGHT, 0), preferred_element_type=f32)
-        if end < cols:
-            panel = parts_of(work[end:, here], LEFT, 1)
-            panel = lax.dot_general(panel, parts_of(lower, RIGHT, 1), NT, preferred_element_type=f32)
-            panel = parts_of(panel, LEFT, 1)
-            steps = ([line[:, :base]] if base else []) + [lower, line[:, end:]]
-            steps = parts_of(jnp.concatenate(steps, axis=1), RIGHT, 0)
-            work[end:, here] = jnp.zeros((cols - end, LANE), f32)
-            for start, stop in ((0, LANE), (LANE, cols - end)):
-                if start < stop:
-                    change = jnp.dot(panel[start:stop], steps, preferred_element_type=f32)
-                    work[end + start : end + stop, :] = work[end + start : end + stop, :] - change
-        factor_ref[here, here] = upper * level[:, here]
-        inverse_ref[here, here] = lower * unit_row[:, here]
-        if base:
-            factor_ref[here, :base] = jnp.zeros((LANE, base), f32)
-            inverse_ref[here, :base] = line[:, :base] * unit_row[:, :base]
-        if end < cols:
-            factor_ref[here, end:] = line[:, end:] * level[:, end:]
-            inverse_ref[here, end:] = jnp.zeros((LANE, cols - end), f32)
+        lower_left, lower_right = parts_of(lower, LEFT, 1), parts_of(lower, RIGHT, 1)
+        panels, steps = {}, {}
+
+        def take_line(j, b=b, here=here, lower_left=lower_left, steps=steps):
+            line = jnp.dot(lower_left, parts_of(work[here, spans[j]], RIGHT, 0), preferred_element_type=f32)
+            steps[j] = parts_of(line, RIGHT, 0)
+            if j > b:
+                factor_ref[here, spans[j]] = line * (diagonals[j] * units[j] * ratio)
+                inverse_ref[here, spans[j]] = jnp.zeros((LANE, LANE), f32)
+            else:
+                factor_ref[here, spans[j]] = jnp.zeros((LANE, LANE), f32)
+                inverse_ref[here, spans[j]] = line * units[j]
+
+        def take_panel(i, here=here, lower_right=lower_right, panels=panels):
+            panel = parts_of(work[spans[i], here], LEFT, 1)
+            panels[i] = parts_of(lax.dot_general(panel, lower_right, NT, preferred_element_type=f32), LEFT, 1)
+
+        def take_change(i, j, b=b, panels=panels, steps=steps):
+            change = jnp.dot(panels[i], steps[j], preferred_element_type=f32)
+            work[spans[i], spans[j]] = -change if j == b else work[spans[i], spans[j]] - change
+
+        def put_own(here=here, inner=inner, lower=lower, b=b, steps=steps):
+            steps[b] = parts_of(lower, RIGHT, 0)
+            factor_ref[here, here] = jnp.where(lane_in >= row_in, inner, 0.0) * (diagonals[b] * units[b] * ratio)
+            inverse_ref[here, here] = lower * units[b]
+
+        if b + 1 < count:
+            take_line(b + 1)
+            take_panel(b + 1)
+            fresh = work[spans[b + 1], spans[b + 1]]
+            fresh = fresh - jnp.dot(panels[b + 1], steps[b + 1], preferred_element_type=f32)
+        others = [j for j in range(count) if j not in (b, b + 1)]
+        aside = [put_own] + [functools.partial(take_line, j) for j in others]
+        aside += [functools.partial(take_panel, i) for i in range(b + 2, count)]
+        aside += [
+            functools.partial(take_change, i, j)
+            for i in range(b + 1, count)
+            for j in range(count)
+            if (i, j) != (b + 1, b + 1)
+        ]
+    for call_it in aside:
+        call_it()
 
 
 def solve_kernel(apart, rows_in, share, index_ref, inverse_ref, effects_ref, cov_ref, marks_ref, noise_ref, *refs):

time: 66 us -> 65.9 us (level)
  no operation moved by 1% of the time
where the time goes in v11:
time: 65.9 us; the launch traced here: 65.6 us
  Pallas kernels  27 us (41%)
  starting transfers between devices  18.1 us (27%)
  waiting for transfers between devices  16.5 us (25%)
  local copies, waits for them, and re-layouts  2.4 us (4%)
  other arithmetic  0.79 us (1%)
  between operations  0.72 us (1%)
    pallas_call x8, Pallas kernels, call(): pl.pallas_call(kernel, out_shape=[jax.ShapeDtypeStruct(shape, dtype) for...  27 us
    ppermute x21, starting transfers between devices, partner(): return lax.ppermute(value, axis, pairs)  18.1 us
    ppermute x21, waiting for transfers between devices, partner(): return lax.ppermute(value, axis, pairs)  16.5 us
    unnamed x10, local copies, waits for them, and re-layouts  2.4 us
  transfers between devices with their start and end apart: 21, of which 11 were waited for; matrix products, arithmetic and copies ran while one was open for 1% of the time, Pallas kernels for 3%

profile of v11, /device:TPU:0, one launch (start us, length us, event | category | flops | bytes accessed | tf_op | source)
XLA Modules:
  0.0 65.6 jit_solution(17865808645273904315)
XLA Ops:
  0.6 4.0 %collective-permute-start.5 = (s32[1,32]{1,0:T(1,128)}, s32[1,32]{1,0:T(1,128)S(1)}, u32[]{:S(2)}, u32[]{:S(2)}) collective-permute-start(s32[1,32]{1,0:T(1,128)} %bitcast.12), channel_id=1, source_target_pairs={{0,24},{4,28},{8,16},{12,20},{16,8},{20,12},{24,0},{28,4},{1,25},{... | collective-permute-start | bytes 392 | tf_op jit(solution)/shard_map/ppermute | solution.py:31
  4.6 0.5 collective-permute-start.3
  5.1 0.1 collective-permute-start.1
  5.2 0.0 collective-permute-start
  5.2 0.1 pad_add_fusion.index_ref
  5.3 0.7 %add_bitcast_fusion.marks_ref = s32[16,128]{1,0:T(8,128)S(1)} fusion(s32[2048]{0:T(1024)} %param.7, s32[2048]{0:T(1024)} %param.8), kind=kLoop, calls=%fused_computation | loop fusion | flops 4096 | bytes 24576 | tf_op jit(solution)/shard_map/reshape | solution.py:471
  6.0 0.0 copy-start
  6.0 1.0 %copy-done = bf16[2048,128]{1,0:T(8,128)(2,1)S(1)} copy-done((bf16[2048,128]{1,0:T(8,128)(2,1)S(1)}, bf16[2048,128]{1,0:T(8,128)(2,1)}, u32[]{:S(2)}) %copy-start) | copy-done | bytes 524312
  7.1 0.0 copy-start.2
  7.1 0.7 %copy-done.2 = f32[2048]{0:T(1024)S(1)} copy-done((f32[2048]{0:T(1024)S(1)}, f32[2048]{0:T(1024)}, u32[]{:S(2)}) %copy-start.2) | copy-done | bytes 8216
  7.8 1.0 %design.1 = (bf16[560,2048]{1,0:T(8,128)(2,1)S(1)}, f32[264,128]{1,0:T(8,128)S(1)}) custom-call(bf16[2048,128]{1,0:T(8,128)(2,1)S(1)} %copy-done, s32[16,128]{1,0:T(8,128)S(1)} %add_bitcast_fusion.marks_ref, f32[16,128]{1,0:T(8,128)S(1)} %bitcast.9), custom_call_target="tpu_custom_call" | custom-call | tf_op jit(solution)/shard_map/design/pallas_call | solution.py:453
  8.8 0.0 collective-permute-done.5.refs_6_
  8.8 0.6 collective-permute-start.6
  9.4 0.0 collective-permute-done.3.refs_4_
  9.4 0.1 collective-permute-start.4
  9.5 0.0 collective-permute-done.1.refs_2_
  9.5 0.4 collective-permute-start.2
  9.9 0.0 collective-permute-done.refs_1_
  9.9 0.3 collective-permute-done.6.refs_7_
  10.2 0.3 collective-permute-done.4.refs_5_
  10.5 0.2 collective-permute-done.2.refs_3_
  10.7 0.0 copy-start.4
  10.7 0.7 copy-done.4
  11.4 1.6 %local.1 = (bf16[256,512]{1,0:T(8,128)(2,1)S(1)}, bf16[256,512]{1,0:T(8,128)(2,1)S(1)}) custom-call(s32[2]{0:T(128)S(1)} %pad_add_fusion.index_ref, bf16[560,2048]{1,0:T(8,128)(2,1)S(1)} %get-tuple-element.15.design_ref, f32[264,128]{1,0:T(8,128)S(1)} %get-tuple-element.16.packed_ref, s32[16,128]{1,0:T(8,128)S(1)} %add_bitcast_fusion.marks_ref, ...), custom_call_target="tpu_custom_call" | custom-call | tf_op jit(solution)/shard_map/local/pallas_call | solution.py:453
  12.9 0.4 collective-permute-start.7
  13.3 1.2 %collective-permute-done.7.came_ref = bf16[256,512]{1,0:T(8,128)(2,1)S(1)} collective-permute-done((bf16[256,512]{1,0:T(8,128)(2,1)S(1)}, bf16[256,512]{1,0:T(8,128)(2,1)S(1)}, u32[]{:S(2)}, u32[]{:S(2)}) %collective-permute-start.7) | collective-permute-done | bytes 262176 | tf_op jit(solution)/shard_map/ppermute | solution.py:31
  14.5 0.0 copy-start.1
  14.6 0.0 copy-start.3
  14.6 0.7 pair.1
  15.2 2.0 %collective-permute-start.8 = (bf16[64,512]{1,0:T(8,128)(2,1)S(1)}, bf16[64,512]{1,0:T(8,128)(2,1)S(1)}, u32[]{:S(2)}, u32[]{:S(2)}) collective-permute-start(bf16[64,512]{1,0:T(8,128)(2,1)S(1)} %get-tuple-element.20), channel_id=1, source_target_pairs={{0,8},{4,12},{8,0},{12,4},{16,24},{20,28},{24,16},{28,20},{1,9},{5... | collective-permute-start | bytes 196616 | tf_op jit(solution)/shard_map/ppermute | solution.py:31
  17.2 1.5 %collective-permute-start.9 = (bf16[64,512]{1,0:T(8,128)(2,1)S(1)}, bf16[64,512]{1,0:T(8,128)(2,1)S(1)}, u32[]{:S(2)}, u32[]{:S(2)}) collective-permute-start(bf16[64,512]{1,0:T(8,128)(2,1)S(1)} %get-tuple-element.21), channel_id=1, source_target_pairs={{0,16},{4,20},{8,24},{12,28},{16,0},{20,4},{24,8},{28,12},{1,17},{... | collective-permute-start | bytes 196616 | tf_op jit(solution)/shard_map/ppermute | solution.py:31
  18.7 0.1 collective-permute-start.10
  18.8 1.0 %collective-permute-done.8.refs_1_ = bf16[64,512]{1,0:T(8,128)(2,1)S(1)} collective-permute-done((bf16[64,512]{1,0:T(8,128)(2,1)S(1)}, bf16[64,512]{1,0:T(8,128)(2,1)S(1)}, u32[]{:S(2)}, u32[]{:S(2)}) %collective-permute-start.8) | collective-permute-done | bytes 65568 | tf_op jit(solution)/shard_map/ppermute | solution.py:31
  19.7 1.7 %collective-permute-done.9.refs_2_ = bf16[64,512]{1,0:T(8,128)(2,1)S(1)} collective-permute-done((bf16[64,512]{1,0:T(8,128)(2,1)S(1)}, bf16[64,512]{1,0:T(8,128)(2,1)S(1)}, u32[]{:S(2)}, u32[]{:S(2)}) %collective-permute-start.9) | collective-permute-done | bytes 65568 | tf_op jit(solution)/shard_map/ppermute | solution.py:31
  21.4 2.4 %collective-permute-done.10.refs_3_ = bf16[64,512]{1,0:T(8,128)(2,1)S(1)} collective-permute-done((bf16[64,512]{1,0:T(8,128)(2,1)S(1)}, bf16[64,512]{1,0:T(8,128)(2,1)S(1)}, u32[]{:S(2)}, u32[]{:S(2)}) %collective-permute-start.10) | collective-permute-done | bytes 65568 | tf_op jit(solution)/shard_map/ppermute | solution.py:31
  23.8 0.6 mix.1.refs_0_
  24.5 3.7 %collective-permute-start.13 = (bf16[64,512]{1,0:T(8,128)(2,1)S(1)}, bf16[64,512]{1,0:T(8,128)(2,1)S(1)}, u32[]{:S(2)}, u32[]{:S(2)}) collective-permute-start(bf16[64,512]{1,0:T(8,128)(2,1)S(1)} %mix.1.refs_0_), channel_id=1, source_target_pairs={{0,3},{1,2},{2,1},{3,0},{4,7},{5,6},{6,5},{7,4},{8,11},{9,10},{10,... | collective-permute-start | bytes 196616 | tf_op jit(solution)/shard_map/ppermute | solution.py:31
  28.1 0.0 collective-permute-start.12
  28.1 0.8 %collective-permute-start.11 = (bf16[64,512]{1,0:T(8,128)(2,1)S(1)}, bf16[64,512]{1,0:T(8,128)(2,1)S(1)}, u32[]{:S(2)}, u32[]{:S(2)}) collective-permute-start(bf16[64,512]{1,0:T(8,128)(2,1)S(1)} %mix.1.refs_0_), channel_id=1, source_target_pairs={{0,1},{1,0},{2,3},{3,2},{4,5},{5,4},{6,7},{7,6},{8,9},{9,8},{10,11... | collective-permute-start | bytes 196616 | tf_op jit(solution)/shard_map/ppermute | solution.py:31
  28.9 1.7 %collective-permute-done.13.refs_3_ = bf16[64,512]{1,0:T(8,128)(2,1)S(1)} collective-permute-done((bf16[64,512]{1,0:T(8,128)(2,1)S(1)}, bf16[64,512]{1,0:T(8,128)(2,1)S(1)}, u32[]{:S(2)}, u32[]{:S(2)}) %collective-permute-start.13) | collective-permute-done | bytes 65568 | tf_op jit(solution)/shard_map/ppermute | solution.py:31
  30.6 2.7 %collective-permute-done.12.refs_2_ = bf16[64,512]{1,0:T(8,128)(2,1)S(1)} collective-permute-done((bf16[64,512]{1,0:T(8,128)(2,1)S(1)}, bf16[64,512]{1,0:T(8,128)(2,1)S(1)}, u32[]{:S(2)}, u32[]{:S(2)}) %collective-permute-start.12) | collective-permute-done | bytes 65568 | tf_op jit(solution)/shard_map/ppermute | solution.py:31
  33.3 0.0 collective-permute-done.11.refs_1_
  33.3 0.6 stack.13.refs_0_
  33.9 0.6 collective-permute-start.16
  34.5 1.5 %collective-permute-start.15 = (bf16[160,512]{1,0:T(8,128)(2,1)S(1)}, bf16[160,512]{1,0:T(8,128)(2,1)S(1)}, u32[]{:S(2)}, u32[]{:S(2)}) collective-permute-start(bf16[160,512]{1,0:T(8,128)(2,1)S(1)} %stack.13.refs_0_), channel_id=1, source_target_pairs={{0,16},{4,20},{8,24},{12,28},{16,0},{20,4},{24,8},{28,12},{1,17},{... | collective-permute-start | bytes 491528 | tf_op jit(solution)/shard_map/ppermute | solution.py:31
  35.9 1.5 %collective-permute-start.14 = (bf16[160,512]{1,0:T(8,128)(2,1)S(1)}, bf16[160,512]{1,0:T(8,128)(2,1)S(1)}, u32[]{:S(2)}, u32[]{:S(2)}) collective-permute-start(bf16[160,512]{1,0:T(8,128)(2,1)S(1)} %stack.13.refs_0_), channel_id=1, source_target_pairs={{0,8},{4,12},{8,0},{12,4},{16,24},{20,28},{24,16},{28,20},{1,9},{5... | collective-permute-start | bytes 491528 | tf_op jit(solution)/shard_map/ppermute | solution.py:31
  37.4 0.0 collective-permute-start.17
  37.4 3.9 %collective-permute-done.16.refs_3_ = bf16[160,512]{1,0:T(8,128)(2,1)S(1)} collective-permute-done((bf16[160,512]{1,0:T(8,128)(2,1)S(1)}, bf16[160,512]{1,0:T(8,128)(2,1)S(1)}, u32[]{:S(2)}, u32[]{:S(2)}) %collective-permute-start.16) | collective-permute-done | bytes 163872 | tf_op jit(solution)/shard_map/ppermute | solution.py:31
  41.3 0.0 collective-permute-start.20
  41.3 1.0 %collective-permute-done.15.refs_2_ = bf16[160,512]{1,0:T(8,128)(2,1)S(1)} collective-permute-done((bf16[160,512]{1,0:T(8,128)(2,1)S(1)}, bf16[160,512]{1,0:T(8,128)(2,1)S(1)}, u32[]{:S(2)}, u32[]{:S(2)}) %collective-permute-start.15) | collective-permute-done | bytes 163872 | tf_op jit(solution)/shard_map/ppermute | solution.py:31
  42.4 0.0 collective-permute-start.19
  42.4 0.0 collective-permute-done.14.refs_1_
  42.4 0.5 collective-permute-start.18
  42.9 1.0 %gram.1.gram_ref = f32[512,512]{1,0:T(8,128)S(1)} custom-call(s32[2]{0:T(128)S(1)} %pad_add_fusion.index_ref, bf16[160,512]{1,0:T(8,128)(2,1)S(1)} %stack.13.refs_0_, bf16[160,512]{1,0:T(8,128)(2,1)S(1)} %collective-permute-done.14.refs_1_, bf16[160,512]{1,0:T(8,128)(2,1)S(1)} %collective-permute-done.15.refs_2_, ...), custom_call_target="tpu_custom_call" | custom-call | tf_op jit(solution)/shard_map/gram/pallas_call | solution.py:453
  43.9 0.0 collective-permute-done.17.refs_0_.refs_4_
  44.0 0.0 collective-permute-done.20.refs_3_.refs_7_
  44.0 0.0 collective-permute-done.19.refs_2_.refs_6_
  44.0 0.0 collective-permute-done.18.refs_1_.refs_5_
  44.0 18.0 %factor.1 = (f32[512,512]{1,0:T(8,128)}, f32[512,512]{1,0:T(8,128)S(1)}) custom-call(s32[2]{0:T(128)S(1)} %pad_add_fusion.index_ref, f32[512,512]{1,0:T(8,128)S(1)} %gram.1.gram_ref, bf16[160,512]{1,0:T(8,128)(2,1)S(1)} %collective-permute-done.17.refs_0_.refs_4_, bf16[160,512]{1,0:T(8,128)(2,1)S(1)} %collective-permute-done.18.refs_1_.refs_5_, ...), custom_call_target="tpu_custom_call" | custom-call | tf_op jit(solution)/shard_map/factor/pallas_call | solution.py:453
  62.0 0.0 copy-done.1
  62.0 0.0 copy-done.3
  62.0 3.5 %solve.1 = (f32[4,128]{1,0:T(4,128)}, f32[16,128]{1,0:T(8,128)}) custom-call(s32[2]{0:T(128)S(1)} %pad_add_fusion.index_ref, f32[512,512]{1,0:T(8,128)S(1)} %get-tuple-element.23.inverse_ref, f32[4,128]{1,0:T(4,128)S(1)} %bitcast.11, bf16[2048,128]{1,0:T(8,128)(2,1)S(1)} %copy-done.1, s32[16,128]{1,0:T(8,128)S(1)} %add_bitcast_fusion.marks_ref, ...), custom_call_target="tpu_custom_call" | custom-call | tf_op jit(solution)/shard_map/solve/pallas_call | solution.py:453
Async XLA Ops:
  0.6 8.2 %collective-permute-start.5 = (s32[1,32]{1,0:T(1,128)}, s32[1,32]{1,0:T(1,128)S(1)}, u32[]{:S(2)}, u32[]{:S(2)}) collective-permute-start(s32[1,32]{1,0:T(1,128)} %bitcast.12), channel_id=1, source_target_pairs={{0,24},{4,28},{8,16},{12,20},{16,8},{20,12},{24,0},{28,4},{1,25},{... | collective-permute-start | bytes 392 | tf_op jit(solution)/shard_map/ppermute | solution.py:31
  4.6 4.8 %collective-permute-start.3 = (s32[1,32]{1,0:T(1,128)}, s32[1,32]{1,0:T(1,128)S(1)}, u32[]{:S(2)}, u32[]{:S(2)}) collective-permute-start(s32[1,32]{1,0:T(1,128)} %bitcast.13), channel_id=1, source_target_pairs={{0,16},{4,20},{8,24},{12,28},{16,0},{20,4},{24,8},{28,12},{1,17},{... | collective-permute-start | bytes 392 | tf_op jit(solution)/shard_map/ppermute | solution.py:31
  5.1 4.4 %collective-permute-start.1 = (s32[1,32]{1,0:T(1,128)}, s32[1,32]{1,0:T(1,128)S(1)}, u32[]{:S(2)}, u32[]{:S(2)}) collective-permute-start(s32[1,32]{1,0:T(1,128)} %bitcast.14), channel_id=1, source_target_pairs={{0,8},{4,12},{8,0},{12,4},{16,24},{20,28},{24,16},{28,20},{1,9},{5... | collective-permute-start | bytes 392 | tf_op jit(solution)/shard_map/ppermute | solution.py:31
  5.2 4.7 %collective-permute-start = (s32[1,32]{1,0:T(1,128)}, s32[1,32]{1,0:T(1,128)S(1)}, u32[]{:S(2)}, u32[]{:S(2)}) collective-permute-start(s32[1,32]{1,0:T(1,128)} %bitcast.15), channel_id=1, source_target_pairs={{0,4},{4,0},{8,12},{12,8},{16,20},{20,16},{24,28},{28,24},{1,5},{5... | collective-permute-start | bytes 392 | tf_op jit(solution)/shard_map/ppermute | solution.py:31
  6.0 1.0 %copy-start = (bf16[2048,128]{1,0:T(8,128)(2,1)S(1)}, bf16[2048,128]{1,0:T(8,128)(2,1)}, u32[]{:S(2)}) copy-start(bf16[2048,128]{1,0:T(8,128)(2,1)} %cov_ref.3) | copy-start | bytes 1572868
  7.1 0.7 %copy-start.2 = (f32[2048]{0:T(1024)S(1)}, f32[2048]{0:T(1024)}, u32[]{:S(2)}) copy-start(f32[2048]{0:T(1024)} %param.11) | copy-start | bytes 24580
  8.8 1.4 %collective-permute-start.6 = (s32[1,32]{1,0:T(1,128)S(1)}, s32[1,32]{1,0:T(1,128)S(1)}, u32[]{:S(2)}, u32[]{:S(2)}) collective-permute-start(s32[1,32]{1,0:T(1,128)S(1)} %collective-permute-done.5.refs_6_), channel_id=1, source_target_pairs={{0,4},{4,0},{8,12},{12,8},{16,20},{20,16},{24,28},{28,24},{1,5},{5... | collective-permute-start | bytes 392 | tf_op jit(solution)/shard_map/ppermute | solution.py:31
  9.4 1.1 %collective-permute-start.4 = (s32[1,32]{1,0:T(1,128)S(1)}, s32[1,32]{1,0:T(1,128)S(1)}, u32[]{:S(2)}, u32[]{:S(2)}) collective-permute-start(s32[1,32]{1,0:T(1,128)S(1)} %collective-permute-done.3.refs_4_), channel_id=1, source_target_pairs={{0,4},{4,0},{8,12},{12,8},{16,20},{20,16},{24,28},{28,24},{1,5},{5... | collective-permute-start | bytes 392 | tf_op jit(solution)/shard_map/ppermute | solution.py:31
  9.5 1.2 %collective-permute-start.2 = (s32[1,32]{1,0:T(1,128)S(1)}, s32[1,32]{1,0:T(1,128)S(1)}, u32[]{:S(2)}, u32[]{:S(2)}) collective-permute-start(s32[1,32]{1,0:T(1,128)S(1)} %collective-permute-done.1.refs_2_), channel_id=1, source_target_pairs={{0,4},{4,0},{8,12},{12,8},{16,20},{20,16},{24,28},{28,24},{1,5},{5... | collective-permute-start | bytes 392 | tf_op jit(solution)/shard_map/ppermute | solution.py:31
  10.7 0.7 copy-start.4
  12.9 1.6 %collective-permute-start.7 = (bf16[256,512]{1,0:T(8,128)(2,1)S(1)}, bf16[256,512]{1,0:T(8,128)(2,1)S(1)}, u32[]{:S(2)}, u32[]{:S(2)}) collective-permute-start(bf16[256,512]{1,0:T(8,128)(2,1)S(1)} %get-tuple-element.18), channel_id=1, source_target_pairs={{0,4},{4,0},{8,12},{12,8},{16,20},{20,16},{24,28},{28,24},{1,5},{5... | collective-permute-start | bytes 786440 | tf_op jit(solution)/shard_map/ppermute | solution.py:31
  14.5 47.5 %copy-start.1 = (bf16[2048,128]{1,0:T(8,128)(2,1)S(1)}, bf16[2048,128]{1,0:T(8,128)(2,1)}, u32[]{:S(2)}) copy-start(bf16[2048,128]{1,0:T(8,128)(2,1)} %cov_ref.3) | copy-start | bytes 1572868
  14.6 47.5 %copy-start.3 = (f32[512]{0:T(512)S(1)}, f32[512]{0:T(512)}, u32[]{:S(2)}) copy-start(f32[512]{0:T(512)} %param.10) | copy-start | bytes 6148
  15.2 4.5 %collective-permute-start.8 = (bf16[64,512]{1,0:T(8,128)(2,1)S(1)}, bf16[64,512]{1,0:T(8,128)(2,1)S(1)}, u32[]{:S(2)}, u32[]{:S(2)}) collective-permute-start(bf16[64,512]{1,0:T(8,128)(2,1)S(1)} %get-tuple-element.20), channel_id=1, source_target_pairs={{0,8},{4,12},{8,0},{12,4},{16,24},{20,28},{24,16},{28,20},{1,9},{5... | collective-permute-start | bytes 196616 | tf_op jit(solution)/shard_map/ppermute | solution.py:31
  17.2 4.3 %collective-permute-start.9 = (bf16[64,512]{1,0:T(8,128)(2,1)S(1)}, bf16[64,512]{1,0:T(8,128)(2,1)S(1)}, u32[]{:S(2)}, u32[]{:S(2)}) collective-permute-start(bf16[64,512]{1,0:T(8,128)(2,1)S(1)} %get-tuple-element.21), channel_id=1, source_target_pairs={{0,16},{4,20},{8,24},{12,28},{16,0},{20,4},{24,8},{28,12},{1,17},{... | collective-permute-start | bytes 196616 | tf_op jit(solution)/shard_map/ppermute | solution.py:31
  18.7 5.2 %collective-permute-start.10 = (bf16[64,512]{1,0:T(8,128)(2,1)S(1)}, bf16[64,512]{1,0:T(8,128)(2,1)S(1)}, u32[]{:S(2)}, u32[]{:S(2)}) collective-permute-start(bf16[64,512]{1,0:T(8,128)(2,1)S(1)} %get-tuple-element.22), channel_id=1, source_target_pairs={{0,24},{4,28},{8,16},{12,20},{16,8},{20,12},{24,0},{28,4},{1,25},{... | collective-permute-start | bytes 196616 | tf_op jit(solution)/shard_map/ppermute | solution.py:31
  24.5 6.1 %collective-permute-start.13 = (bf16[64,512]{1,0:T(8,128)(2,1)S(1)}, bf16[64,512]{1,0:T(8,128)(2,1)S(1)}, u32[]{:S(2)}, u32[]{:S(2)}) collective-permute-start(bf16[64,512]{1,0:T(8,128)(2,1)S(1)} %mix.1.refs_0_), channel_id=1, source_target_pairs={{0,3},{1,2},{2,1},{3,0},{4,7},{5,6},{6,5},{7,4},{8,11},{9,10},{10,... | collective-permute-start | bytes 196616 | tf_op jit(solution)/shard_map/ppermute | solution.py:31
  28.1 5.2 %collective-permute-start.12 = (bf16[64,512]{1,0:T(8,128)(2,1)S(1)}, bf16[64,512]{1,0:T(8,128)(2,1)S(1)}, u32[]{:S(2)}, u32[]{:S(2)}) collective-permute-start(bf16[64,512]{1,0:T(8,128)(2,1)S(1)} %mix.1.refs_0_), channel_id=1, source_target_pairs={{0,2},{1,3},{2,0},{3,1},{4,6},{5,7},{6,4},{7,5},{8,10},{9,11},{10,... | collective-permute-start | bytes 196616 | tf_op jit(solution)/shard_map/ppermute | solution.py:31
  28.1 5.2 %collective-permute-start.11 = (bf16[64,512]{1,0:T(8,128)(2,1)S(1)}, bf16[64,512]{1,0:T(8,128)(2,1)S(1)}, u32[]{:S(2)}, u32[]{:S(2)}) collective-permute-start(bf16[64,512]{1,0:T(8,128)(2,1)S(1)} %mix.1.refs_0_), channel_id=1, source_target_pairs={{0,1},{1,0},{2,3},{3,2},{4,5},{5,4},{6,7},{7,6},{8,9},{9,8},{10,11... | collective-permute-start | bytes 196616 | tf_op jit(solution)/shard_map/ppermute | solution.py:31
  33.9 7.5 %collective-permute-start.16 = (bf16[160,512]{1,0:T(8,128)(2,1)S(1)}, bf16[160,512]{1,0:T(8,128)(2,1)S(1)}, u32[]{:S(2)}, u32[]{:S(2)}) collective-permute-start(bf16[160,512]{1,0:T(8,128)(2,1)S(1)} %stack.13.refs_0_), channel_id=1, source_target_pairs={{0,24},{4,28},{8,16},{12,20},{16,8},{20,12},{24,0},{28,4},{1,25},{... | collective-permute-start | bytes 491528 | tf_op jit(solution)/shard_map/ppermute | solution.py:31
  34.5 7.9 %collective-permute-start.15 = (bf16[160,512]{1,0:T(8,128)(2,1)S(1)}, bf16[160,512]{1,0:T(8,128)(2,1)S(1)}, u32[]{:S(2)}, u32[]{:S(2)}) collective-permute-start(bf16[160,512]{1,0:T(8,128)(2,1)S(1)} %stack.13.refs_0_), channel_id=1, source_target_pairs={{0,16},{4,20},{8,24},{12,28},{16,0},{20,4},{24,8},{28,12},{1,17},{... | collective-permute-start | bytes 491528 | tf_op jit(solution)/shard_map/ppermute | solution.py:31
  35.9 6.4 %collective-permute-start.14 = (bf16[160,512]{1,0:T(8,128)(2,1)S(1)}, bf16[160,512]{1,0:T(8,128)(2,1)S(1)}, u32[]{:S(2)}, u32[]{:S(2)}) collective-permute-start(bf16[160,512]{1,0:T(8,128)(2,1)S(1)} %stack.13.refs_0_), channel_id=1, source_target_pairs={{0,8},{4,12},{8,0},{12,4},{16,24},{20,28},{24,16},{28,20},{1,9},{5... | collective-permute-start | bytes 491528 | tf_op jit(solution)/shard_map/ppermute | solution.py:31
  37.4 6.5 %collective-permute-start.17 = (bf16[160,512]{1,0:T(8,128)(2,1)S(1)}, bf16[160,512]{1,0:T(8,128)(2,1)S(1)}, u32[]{:S(2)}, u32[]{:S(2)}) collective-permute-start(bf16[160,512]{1,0:T(8,128)(2,1)S(1)} %stack.13.refs_0_), channel_id=1, source_target_pairs={{0,4},{4,0},{8,12},{12,8},{16,20},{20,16},{24,28},{28,24},{1,5},{5... | collective-permute-start | bytes 491528 | tf_op jit(solution)/shard_map/ppermute | solution.py:31
  41.3 2.6 %collective-permute-start.20 = (bf16[160,512]{1,0:T(8,128)(2,1)S(1)}, bf16[160,512]{1,0:T(8,128)(2,1)S(1)}, u32[]{:S(2)}, u32[]{:S(2)}) collective-permute-start(bf16[160,512]{1,0:T(8,128)(2,1)S(1)} %collective-permute-done.16.refs_3_), channel_id=1, source_target_pairs={{0,4},{4,0},{8,12},{12,8},{16,20},{20,16},{24,28},{28,24},{1,5},{5... | collective-permute-start | bytes 491528 | tf_op jit(solution)/shard_map/ppermute | solution.py:31
  42.4 1.6 %collective-permute-start.19 = (bf16[160,512]{1,0:T(8,128)(2,1)S(1)}, bf16[160,512]{1,0:T(8,128)(2,1)S(1)}, u32[]{:S(2)}, u32[]{:S(2)}) collective-permute-start(bf16[160,512]{1,0:T(8,128)(2,1)S(1)} %collective-permute-done.15.refs_2_), channel_id=1, source_target_pairs={{0,4},{4,0},{8,12},{12,8},{16,20},{20,16},{24,28},{28,24},{1,5},{5... | collective-permute-start | bytes 491528 | tf_op jit(solution)/shard_map/ppermute | solution.py:31
  42.4 1.6 %collective-permute-start.18 = (bf16[160,512]{1,0:T(8,128)(2,1)S(1)}, bf16[160,512]{1,0:T(8,128)(2,1)S(1)}, u32[]{:S(2)}, u32[]{:S(2)}) collective-permute-start(bf16[160,512]{1,0:T(8,128)(2,1)S(1)} %collective-permute-done.14.refs_1_), channel_id=1, source_target_pairs={{0,4},{4,0},{8,12},{12,8},{16,20},{20,16},{24,28},{28,24},{1,5},{5... | collective-permute-start | bytes 491528 | tf_op jit(solution)/shard_map/ppermute | solution.py:31

commit v12 on v11

--- a/solution.py
+++ b/solution.py
@@ -194,7 +194,7 @@
     return pltpu.reciprocal(value, approx=True)
 
 
-def eliminate(tiles, aside):
+def eliminate(tiles, aside, shelf):
     share = -(-len(aside) // len(tiles))
     lane = lax.broadcasted_iota(jnp.int32, (SUB, LANE), 1)
     sub = lax.broadcasted_iota(jnp.int32, (SUB, LANE), 0)
@@ -206,9 +206,17 @@
         marks = [lane == first + k for k in range(SUB)]
         old = tiles[tile]
         columns = [spread(old[:, first + k : first + k + 1]) for k in range(SUB)]
-        pivot = [[spread(columns[m][k : k + 1, :]) if m >= k else None for m in range(SUB)] for k in range(SUB)]
-        cleared = jnp.where(window, 0.0, old)
-        rows = [jnp.where(marks[k], 1.0, spread(cleared[k : k + 1, :])) for k in range(SUB)]
+        base = tile % 2 * (SUB + 1) * SUB
+        shelf[base : base + SUB, :] = jnp.where(window, 0.0, old)
+        for m in range(SUB):
+            shelf[base + (m + 1) * SUB : base + (m + 2) * SUB, :] = columns[m]
+
+        def take(m, k):
+            at = base + m * SUB + k
+            return spread(shelf[at : at + 1, :])
+
+        pivot = [[take(m + 1, k) if m >= k else None for m in range(SUB)] for k in range(SUB)]
+        rows = [jnp.where(marks[k], 1.0, take(0, k)) for k in range(SUB)]
         steps, near, far = [None] * SUB, {}, {}
         kept, roots = [None] * SUB, [None] * SUB
 
@@ -322,7 +330,7 @@
 
 
 def factor_kernel(ratio, rows_in, index_ref, gram_ref, *refs):
-    piece_refs, (factor_ref, inverse_ref, sketch, work) = refs[:-4], refs[-4:]
+    piece_refs, (factor_ref, inverse_ref, sketch, work, shelf) = refs[:-5], refs[-5:]
     count = work.shape[0] // LANE
     spans = [slice(at, at + LANE) for at in range(0, work.shape[0], LANE)]
     row_in, lane_in, same = eye()
@@ -346,7 +354,7 @@
     aside += [functools.partial(take_unit, i) for i in range(1, count)]
     aside += [functools.partial(scale_rows, i) for i in range(count)]
     for b, here in enumerate(spans):
-        tiles, scales = eliminate([fresh[at : at + SUB] for at in range(0, LANE, SUB)], aside)
+        tiles, scales = eliminate([fresh[at : at + SUB] for at in range(0, LANE, SUB)], aside, shelf)
         scale = jnp.concatenate(scales)
         inner = jnp.concatenate(tiles) * scale
         lower = jnp.where(lane_in < row_in, inner, jnp.where(lane_in == row_in, scale, 0.0))
@@ -525,7 +533,7 @@
         functools.partial(factor_kernel, math.sqrt(LEVELS / SKETCH), rows_in),
         "factor",
         [square] * 2,
-        sketch + [square],
+        sketch + [square, ((2 * (SUB + 1) * SUB, LANE), f32)],
         index,
         gram,
         *theirs,

time: 65.9 us -> 63.7 us (0.967)
  Pallas kernels: 27 us -> 24.8 us
    pallas_call x8, Pallas kernels: 27 us -> 24.8 us  [call(): pl.pallas_call(kernel, out_shape=[jax.ShapeDtypeStruct(shape, dtype) for...]
where the time goes in v12:
time: 63.7 us; the launch traced here: 63.4 us
  Pallas kernels  24.8 us (39%)
  starting transfers between devices  18.1 us (28%)
  waiting for transfers between devices  16.5 us (26%)
  local copies, waits for them, and re-layouts  2.4 us (4%)
  other arithmetic  0.79 us (1%)
  between operations  0.72 us (1%)
    pallas_call x8, Pallas kernels, call(): pl.pallas_call(kernel, out_shape=[jax.ShapeDtypeStruct(shape, dtype) for...  24.8 us
    ppermute x21, starting transfers between devices, partner(): return lax.ppermute(value, axis, pairs)  18.1 us
    ppermute x21, waiting for transfers between devices, partner(): return lax.ppermute(value, axis, pairs)  16.5 us
    unnamed x10, local copies, waits for them, and re-layouts  2.4 us
  transfers between devices with their start and end apart: 21, of which 11 were waited for; matrix products, arithmetic and copies ran while one was open for 1% of the time, Pallas kernels for 3%

profile of v12, /device:TPU:0, one launch (start us, length us, event | category | flops | bytes accessed | tf_op | source)
XLA Modules:
  0.0 63.4 jit_solution(17949837499964017825)
XLA Ops:
  0.6 4.0 %collective-permute-start.5 = (s32[1,32]{1,0:T(1,128)}, s32[1,32]{1,0:T(1,128)S(1)}, u32[]{:S(2)}, u32[]{:S(2)}) collective-permute-start(s32[1,32]{1,0:T(1,128)} %bitcast.12), channel_id=1, source_target_pairs={{0,24},{4,28},{8,16},{12,20},{16,8},{20,12},{24,0},{28,4},{1,25},{... | collective-permute-start | bytes 392 | tf_op jit(solution)/shard_map/ppermute | solution.py:31
  4.6 0.5 collective-permute-start.3
  5.1 0.1 collective-permute-start.1
  5.2 0.0 collective-permute-start
  5.2 0.1 pad_add_fusion.index_ref
  5.3 0.7 %add_bitcast_fusion.marks_ref = s32[16,128]{1,0:T(8,128)S(1)} fusion(s32[2048]{0:T(1024)} %param.7, s32[2048]{0:T(1024)} %param.8), kind=kLoop, calls=%fused_computation | loop fusion | flops 4096 | bytes 24576 | tf_op jit(solution)/shard_map/reshape | solution.py:479
  6.0 0.0 copy-start
  6.0 1.0 %copy-done = bf16[2048,128]{1,0:T(8,128)(2,1)S(1)} copy-done((bf16[2048,128]{1,0:T(8,128)(2,1)S(1)}, bf16[2048,128]{1,0:T(8,128)(2,1)}, u32[]{:S(2)}) %copy-start) | copy-done | bytes 524312
  7.1 0.0 copy-start.2
  7.1 0.7 %copy-done.2 = f32[2048]{0:T(1024)S(1)} copy-done((f32[2048]{0:T(1024)S(1)}, f32[2048]{0:T(1024)}, u32[]{:S(2)}) %copy-start.2) | copy-done | bytes 8216
  7.8 1.0 %design.1 = (bf16[560,2048]{1,0:T(8,128)(2,1)S(1)}, f32[264,128]{1,0:T(8,128)S(1)}) custom-call(bf16[2048,128]{1,0:T(8,128)(2,1)S(1)} %copy-done, s32[16,128]{1,0:T(8,128)S(1)} %add_bitcast_fusion.marks_ref, f32[16,128]{1,0:T(8,128)S(1)} %bitcast.9), custom_call_target="tpu_custom_call" | custom-call | tf_op jit(solution)/shard_map/design/pallas_call | solution.py:461
  8.8 0.0 collective-permute-done.5.refs_6_
  8.8 0.6 collective-permute-start.6
  9.4 0.0 collective-permute-done.3.refs_4_
  9.4 0.1 collective-permute-start.4
  9.5 0.0 collective-permute-done.1.refs_2_
  9.5 0.4 collective-permute-start.2
  9.9 0.0 collective-permute-done.refs_1_
  9.9 0.3 collective-permute-done.6.refs_7_
  10.2 0.3 collective-permute-done.4.refs_5_
  10.5 0.2 collective-permute-done.2.refs_3_
  10.7 0.0 copy-start.4
  10.7 0.7 %copy-done.4 = s32[32]{0:T(128)S(1)} copy-done((s32[32]{0:T(128)S(1)}, s32[32]{0:T(128)}, u32[]{:S(2)}) %copy-start.4) | copy-done | bytes 152
  11.4 1.6 %local.1 = (bf16[256,512]{1,0:T(8,128)(2,1)S(1)}, bf16[256,512]{1,0:T(8,128)(2,1)S(1)}) custom-call(s32[2]{0:T(128)S(1)} %pad_add_fusion.index_ref, bf16[560,2048]{1,0:T(8,128)(2,1)S(1)} %get-tuple-element.15.design_ref, f32[264,128]{1,0:T(8,128)S(1)} %get-tuple-element.16.packed_ref, s32[16,128]{1,0:T(8,128)S(1)} %add_bitcast_fusion.marks_ref, ...), custom_call_target="tpu_custom_call" | custom-call | tf_op jit(solution)/shard_map/local/pallas_call | solution.py:461
  12.9 0.4 collective-permute-start.7
  13.3 1.2 %collective-permute-done.7.came_ref = bf16[256,512]{1,0:T(8,128)(2,1)S(1)} collective-permute-done((bf16[256,512]{1,0:T(8,128)(2,1)S(1)}, bf16[256,512]{1,0:T(8,128)(2,1)S(1)}, u32[]{:S(2)}, u32[]{:S(2)}) %collective-permute-start.7) | collective-permute-done | bytes 262176 | tf_op jit(solution)/shard_map/ppermute | solution.py:31
  14.5 0.0 copy-start.1
  14.6 0.0 copy-start.3
  14.6 0.7 %pair.1 = (bf16[64,512]{1,0:T(8,128)(2,1)S(1)}, bf16[64,512]{1,0:T(8,128)(2,1)S(1)}, bf16[64,512]{1,0:T(8,128)(2,1)S(1)}, bf16[64,512]{1,0:T(8,128)(2,1)S(1)}) custom-call(s32[2]{0:T(128)S(1)} %pad_add_fusion.index_ref, bf16[256,512]{1,0:T(8,128)(2,1)S(1)} %get-tuple-element.17.stay_ref, bf16[256,512]{1,0:T(8,128)(2,1)S(1)} %collective-permute-done.7.came_ref), custom_call_target="tpu_custom_call" | custom-call | tf_op jit(solution)/shard_map/pair/pallas_call | solution.py:461
  15.2 2.0 %collective-permute-start.8 = (bf16[64,512]{1,0:T(8,128)(2,1)S(1)}, bf16[64,512]{1,0:T(8,128)(2,1)S(1)}, u32[]{:S(2)}, u32[]{:S(2)}) collective-permute-start(bf16[64,512]{1,0:T(8,128)(2,1)S(1)} %get-tuple-element.20), channel_id=1, source_target_pairs={{0,8},{4,12},{8,0},{12,4},{16,24},{20,28},{24,16},{28,20},{1,9},{5... | collective-permute-start | bytes 196616 | tf_op jit(solution)/shard_map/ppermute | solution.py:31
  17.2 1.5 %collective-permute-start.9 = (bf16[64,512]{1,0:T(8,128)(2,1)S(1)}, bf16[64,512]{1,0:T(8,128)(2,1)S(1)}, u32[]{:S(2)}, u32[]{:S(2)}) collective-permute-start(bf16[64,512]{1,0:T(8,128)(2,1)S(1)} %get-tuple-element.21), channel_id=1, source_target_pairs={{0,16},{4,20},{8,24},{12,28},{16,0},{20,4},{24,8},{28,12},{1,17},{... | collective-permute-start | bytes 196616 | tf_op jit(solution)/shard_map/ppermute | solution.py:31
  18.7 0.1 collective-permute-start.10
  18.8 1.0 %collective-permute-done.8.refs_1_ = bf16[64,512]{1,0:T(8,128)(2,1)S(1)} collective-permute-done((bf16[64,512]{1,0:T(8,128)(2,1)S(1)}, bf16[64,512]{1,0:T(8,128)(2,1)S(1)}, u32[]{:S(2)}, u32[]{:S(2)}) %collective-permute-start.8) | collective-permute-done | bytes 65568 | tf_op jit(solution)/shard_map/ppermute | solution.py:31
  19.7 1.7 %collective-permute-done.9.refs_2_ = bf16[64,512]{1,0:T(8,128)(2,1)S(1)} collective-permute-done((bf16[64,512]{1,0:T(8,128)(2,1)S(1)}, bf16[64,512]{1,0:T(8,128)(2,1)S(1)}, u32[]{:S(2)}, u32[]{:S(2)}) %collective-permute-start.9) | collective-permute-done | bytes 65568 | tf_op jit(solution)/shard_map/ppermute | solution.py:31
  21.4 2.4 %collective-permute-done.10.refs_3_ = bf16[64,512]{1,0:T(8,128)(2,1)S(1)} collective-permute-done((bf16[64,512]{1,0:T(8,128)(2,1)S(1)}, bf16[64,512]{1,0:T(8,128)(2,1)S(1)}, u32[]{:S(2)}, u32[]{:S(2)}) %collective-permute-start.10) | collective-permute-done | bytes 65568 | tf_op jit(solution)/shard_map/ppermute | solution.py:31
  23.8 0.6 mix.1.refs_0_
  24.5 3.7 %collective-permute-start.13 = (bf16[64,512]{1,0:T(8,128)(2,1)S(1)}, bf16[64,512]{1,0:T(8,128)(2,1)S(1)}, u32[]{:S(2)}, u32[]{:S(2)}) collective-permute-start(bf16[64,512]{1,0:T(8,128)(2,1)S(1)} %mix.1.refs_0_), channel_id=1, source_target_pairs={{0,3},{1,2},{2,1},{3,0},{4,7},{5,6},{6,5},{7,4},{8,11},{9,10},{10,... | collective-permute-start | bytes 196616 | tf_op jit(solution)/shard_map/ppermute | solution.py:31
  28.1 0.0 collective-permute-start.12
  28.1 0.8 %collective-permute-start.11 = (bf16[64,512]{1,0:T(8,128)(2,1)S(1)}, bf16[64,512]{1,0:T(8,128)(2,1)S(1)}, u32[]{:S(2)}, u32[]{:S(2)}) collective-permute-start(bf16[64,512]{1,0:T(8,128)(2,1)S(1)} %mix.1.refs_0_), channel_id=1, source_target_pairs={{0,1},{1,0},{2,3},{3,2},{4,5},{5,4},{6,7},{7,6},{8,9},{9,8},{10,11... | collective-permute-start | bytes 196616 | tf_op jit(solution)/shard_map/ppermute | solution.py:31
  28.9 1.7 %collective-permute-done.13.refs_3_ = bf16[64,512]{1,0:T(8,128)(2,1)S(1)} collective-permute-done((bf16[64,512]{1,0:T(8,128)(2,1)S(1)}, bf16[64,512]{1,0:T(8,128)(2,1)S(1)}, u32[]{:S(2)}, u32[]{:S(2)}) %collective-permute-start.13) | collective-permute-done | bytes 65568 | tf_op jit(solution)/shard_map/ppermute | solution.py:31
  30.6 2.7 %collective-permute-done.12.refs_2_ = bf16[64,512]{1,0:T(8,128)(2,1)S(1)} collective-permute-done((bf16[64,512]{1,0:T(8,128)(2,1)S(1)}, bf16[64,512]{1,0:T(8,128)(2,1)S(1)}, u32[]{:S(2)}, u32[]{:S(2)}) %collective-permute-start.12) | collective-permute-done | bytes 65568 | tf_op jit(solution)/shard_map/ppermute | solution.py:31
  33.3 0.0 collective-permute-done.11.refs_1_
  33.3 0.6 stack.13.refs_0_
  33.9 0.6 collective-permute-start.16
  34.5 1.5 %collective-permute-start.15 = (bf16[160,512]{1,0:T(8,128)(2,1)S(1)}, bf16[160,512]{1,0:T(8,128)(2,1)S(1)}, u32[]{:S(2)}, u32[]{:S(2)}) collective-permute-start(bf16[160,512]{1,0:T(8,128)(2,1)S(1)} %stack.13.refs_0_), channel_id=1, source_target_pairs={{0,16},{4,20},{8,24},{12,28},{16,0},{20,4},{24,8},{28,12},{1,17},{... | collective-permute-start | bytes 491528 | tf_op jit(solution)/shard_map/ppermute | solution.py:31
  35.9 1.5 %collective-permute-start.14 = (bf16[160,512]{1,0:T(8,128)(2,1)S(1)}, bf16[160,512]{1,0:T(8,128)(2,1)S(1)}, u32[]{:S(2)}, u32[]{:S(2)}) collective-permute-start(bf16[160,512]{1,0:T(8,128)(2,1)S(1)} %stack.13.refs_0_), channel_id=1, source_target_pairs={{0,8},{4,12},{8,0},{12,4},{16,24},{20,28},{24,16},{28,20},{1,9},{5... | collective-permute-start | bytes 491528 | tf_op jit(solution)/shard_map/ppermute | solution.py:31
  37.4 0.0 collective-permute-start.17
  37.4 3.9 %collective-permute-done.16.refs_3_ = bf16[160,512]{1,0:T(8,128)(2,1)S(1)} collective-permute-done((bf16[160,512]{1,0:T(8,128)(2,1)S(1)}, bf16[160,512]{1,0:T(8,128)(2,1)S(1)}, u32[]{:S(2)}, u32[]{:S(2)}) %collective-permute-start.16) | collective-permute-done | bytes 163872 | tf_op jit(solution)/shard_map/ppermute | solution.py:31
  41.3 0.0 collective-permute-start.20
  41.3 1.0 %collective-permute-done.15.refs_2_ = bf16[160,512]{1,0:T(8,128)(2,1)S(1)} collective-permute-done((bf16[160,512]{1,0:T(8,128)(2,1)S(1)}, bf16[160,512]{1,0:T(8,128)(2,1)S(1)}, u32[]{:S(2)}, u32[]{:S(2)}) %collective-permute-start.15) | collective-permute-done | bytes 163872 | tf_op jit(solution)/shard_map/ppermute | solution.py:31
  42.4 0.0 collective-permute-start.19
  42.4 0.0 collective-permute-done.14.refs_1_
  42.4 0.5 collective-permute-start.18
  42.9 1.0 %gram.1.gram_ref = f32[512,512]{1,0:T(8,128)S(1)} custom-call(s32[2]{0:T(128)S(1)} %pad_add_fusion.index_ref, bf16[160,512]{1,0:T(8,128)(2,1)S(1)} %stack.13.refs_0_, bf16[160,512]{1,0:T(8,128)(2,1)S(1)} %collective-permute-done.14.refs_1_, bf16[160,512]{1,0:T(8,128)(2,1)S(1)} %collective-permute-done.15.refs_2_, ...), custom_call_target="tpu_custom_call" | custom-call | tf_op jit(solution)/shard_map/gram/pallas_call | solution.py:461
  43.9 0.0 collective-permute-done.17.refs_0_.refs_4_
  44.0 0.0 collective-permute-done.20.refs_3_.refs_7_
  44.0 0.0 collective-permute-done.19.refs_2_.refs_6_
  44.0 0.0 collective-permute-done.18.refs_1_.refs_5_
  44.0 15.9 %factor.1 = (f32[512,512]{1,0:T(8,128)}, f32[512,512]{1,0:T(8,128)S(1)}) custom-call(s32[2]{0:T(128)S(1)} %pad_add_fusion.index_ref, f32[512,512]{1,0:T(8,128)S(1)} %gram.1.gram_ref, bf16[160,512]{1,0:T(8,128)(2,1)S(1)} %collective-permute-done.17.refs_0_.refs_4_, bf16[160,512]{1,0:T(8,128)(2,1)S(1)} %collective-permute-done.18.refs_1_.refs_5_, ...), custom_call_target="tpu_custom_call" | custom-call | tf_op jit(solution)/shard_map/factor/pallas_call | solution.py:461
  59.9 0.0 copy-done.1
  59.9 0.0 copy-done.3
  59.9 3.5 %solve.1 = (f32[4,128]{1,0:T(4,128)}, f32[16,128]{1,0:T(8,128)}) custom-call(s32[2]{0:T(128)S(1)} %pad_add_fusion.index_ref, f32[512,512]{1,0:T(8,128)S(1)} %get-tuple-element.23.inverse_ref, f32[4,128]{1,0:T(4,128)S(1)} %bitcast.11, bf16[2048,128]{1,0:T(8,128)(2,1)S(1)} %copy-done.1, s32[16,128]{1,0:T(8,128)S(1)} %add_bitcast_fusion.marks_ref, ...), custom_call_target="tpu_custom_call" | custom-call | tf_op jit(solution)/shard_map/solve/pallas_call | solution.py:461
Async XLA Ops:
  0.6 8.2 %collective-permute-start.5 = (s32[1,32]{1,0:T(1,128)}, s32[1,32]{1,0:T(1,128)S(1)}, u32[]{:S(2)}, u32[]{:S(2)}) collective-permute-start(s32[1,32]{1,0:T(1,128)} %bitcast.12), channel_id=1, source_target_pairs={{0,24},{4,28},{8,16},{12,20},{16,8},{20,12},{24,0},{28,4},{1,25},{... | collective-permute-start | bytes 392 | tf_op jit(solution)/shard_map/ppermute | solution.py:31
  4.6 4.8 %collective-permute-start.3 = (s32[1,32]{1,0:T(1,128)}, s32[1,32]{1,0:T(1,128)S(1)}, u32[]{:S(2)}, u32[]{:S(2)}) collective-permute-start(s32[1,32]{1,0:T(1,128)} %bitcast.13), channel_id=1, source_target_pairs={{0,16},{4,20},{8,24},{12,28},{16,0},{20,4},{24,8},{28,12},{1,17},{... | collective-permute-start | bytes 392 | tf_op jit(solution)/shard_map/ppermute | solution.py:31
  5.1 4.4 %collective-permute-start.1 = (s32[1,32]{1,0:T(1,128)}, s32[1,32]{1,0:T(1,128)S(1)}, u32[]{:S(2)}, u32[]{:S(2)}) collective-permute-start(s32[1,32]{1,0:T(1,128)} %bitcast.14), channel_id=1, source_target_pairs={{0,8},{4,12},{8,0},{12,4},{16,24},{20,28},{24,16},{28,20},{1,9},{5... | collective-permute-start | bytes 392 | tf_op jit(solution)/shard_map/ppermute | solution.py:31
  5.2 4.7 %collective-permute-start = (s32[1,32]{1,0:T(1,128)}, s32[1,32]{1,0:T(1,128)S(1)}, u32[]{:S(2)}, u32[]{:S(2)}) collective-permute-start(s32[1,32]{1,0:T(1,128)} %bitcast.15), channel_id=1, source_target_pairs={{0,4},{4,0},{8,12},{12,8},{16,20},{20,16},{24,28},{28,24},{1,5},{5... | collective-permute-start | bytes 392 | tf_op jit(solution)/shard_map/ppermute | solution.py:31
  6.0 1.0 %copy-start = (bf16[2048,128]{1,0:T(8,128)(2,1)S(1)}, bf16[2048,128]{1,0:T(8,128)(2,1)}, u32[]{:S(2)}) copy-start(bf16[2048,128]{1,0:T(8,128)(2,1)} %cov_ref.3) | copy-start | bytes 1572868
  7.1 0.7 %copy-start.2 = (f32[2048]{0:T(1024)S(1)}, f32[2048]{0:T(1024)}, u32[]{:S(2)}) copy-start(f32[2048]{0:T(1024)} %param.11) | copy-start | bytes 24580
  8.8 1.4 %collective-permute-start.6 = (s32[1,32]{1,0:T(1,128)S(1)}, s32[1,32]{1,0:T(1,128)S(1)}, u32[]{:S(2)}, u32[]{:S(2)}) collective-permute-start(s32[1,32]{1,0:T(1,128)S(1)} %collective-permute-done.5.refs_6_), channel_id=1, source_target_pairs={{0,4},{4,0},{8,12},{12,8},{16,20},{20,16},{24,28},{28,24},{1,5},{5... | collective-permute-start | bytes 392 | tf_op jit(solution)/shard_map/ppermute | solution.py:31
  9.4 1.1 %collective-permute-start.4 = (s32[1,32]{1,0:T(1,128)S(1)}, s32[1,32]{1,0:T(1,128)S(1)}, u32[]{:S(2)}, u32[]{:S(2)}) collective-permute-start(s32[1,32]{1,0:T(1,128)S(1)} %collective-permute-done.3.refs_4_), channel_id=1, source_target_pairs={{0,4},{4,0},{8,12},{12,8},{16,20},{20,16},{24,28},{28,24},{1,5},{5... | collective-permute-start | bytes 392 | tf_op jit(solution)/shard_map/ppermute | solution.py:31
  9.5 1.2 %collective-permute-start.2 = (s32[1,32]{1,0:T(1,128)S(1)}, s32[1,32]{1,0:T(1,128)S(1)}, u32[]{:S(2)}, u32[]{:S(2)}) collective-permute-start(s32[1,32]{1,0:T(1,128)S(1)} %collective-permute-done.1.refs_2_), channel_id=1, source_target_pairs={{0,4},{4,0},{8,12},{12,8},{16,20},{20,16},{24,28},{28,24},{1,5},{5... | collective-permute-start | bytes 392 | tf_op jit(solution)/shard_map/ppermute | solution.py:31
  10.7 0.7 %copy-start.4 = (s32[32]{0:T(128)S(1)}, s32[32]{0:T(128)}, u32[]{:S(2)}) copy-start(s32[32]{0:T(128)} %param.9) | copy-start | bytes 388
  12.9 1.6 %collective-permute-start.7 = (bf16[256,512]{1,0:T(8,128)(2,1)S(1)}, bf16[256,512]{1,0:T(8,128)(2,1)S(1)}, u32[]{:S(2)}, u32[]{:S(2)}) collective-permute-start(bf16[256,512]{1,0:T(8,128)(2,1)S(1)} %get-tuple-element.18), channel_id=1, source_target_pairs={{0,4},{4,0},{8,12},{12,8},{16,20},{20,16},{24,28},{28,24},{1,5},{5... | collective-permute-start | bytes 786440 | tf_op jit(solution)/shard_map/ppermute | solution.py:31
  14.5 45.3 %copy-start.1 = (bf16[2048,128]{1,0:T(8,128)(2,1)S(1)}, bf16[2048,128]{1,0:T(8,128)(2,1)}, u32[]{:S(2)}) copy-start(bf16[2048,128]{1,0:T(8,128)(2,1)} %cov_ref.3) | copy-start | bytes 1572868
  14.6 45.3 %copy-start.3 = (f32[512]{0:T(512)S(1)}, f32[512]{0:T(512)}, u32[]{:S(2)}) copy-start(f32[512]{0:T(512)} %param.10) | copy-start | bytes 6148
  15.2 4.5 %collective-permute-start.8 = (bf16[64,512]{1,0:T(8,128)(2,1)S(1)}, bf16[64,512]{1,0:T(8,128)(2,1)S(1)}, u32[]{:S(2)}, u32[]{:S(2)}) collective-permute-start(bf16[64,512]{1,0:T(8,128)(2,1)S(1)} %get-tuple-element.20), channel_id=1, source_target_pairs={{0,8},{4,12},{8,0},{12,4},{16,24},{20,28},{24,16},{28,20},{1,9},{5... | collective-permute-start | bytes 196616 | tf_op jit(solution)/shard_map/ppermute | solution.py:31
  17.2 4.3 %collective-permute-start.9 = (bf16[64,512]{1,0:T(8,128)(2,1)S(1)}, bf16[64,512]{1,0:T(8,128)(2,1)S(1)}, u32[]{:S(2)}, u32[]{:S(2)}) collective-permute-start(bf16[64,512]{1,0:T(8,128)(2,1)S(1)} %get-tuple-element.21), channel_id=1, source_target_pairs={{0,16},{4,20},{8,24},{12,28},{16,0},{20,4},{24,8},{28,12},{1,17},{... | collective-permute-start | bytes 196616 | tf_op jit(solution)/shard_map/ppermute | solution.py:31
  18.7 5.2 %collective-permute-start.10 = (bf16[64,512]{1,0:T(8,128)(2,1)S(1)}, bf16[64,512]{1,0:T(8,128)(2,1)S(1)}, u32[]{:S(2)}, u32[]{:S(2)}) collective-permute-start(bf16[64,512]{1,0:T(8,128)(2,1)S(1)} %get-tuple-element.22), channel_id=1, source_target_pairs={{0,24},{4,28},{8,16},{12,20},{16,8},{20,12},{24,0},{28,4},{1,25},{... | collective-permute-start | bytes 196616 | tf_op jit(solution)/shard_map/ppermute | solution.py:31
  24.5 6.1 %collective-permute-start.13 = (bf16[64,512]{1,0:T(8,128)(2,1)S(1)}, bf16[64,512]{1,0:T(8,128)(2,1)S(1)}, u32[]{:S(2)}, u32[]{:S(2)}) collective-permute-start(bf16[64,512]{1,0:T(8,128)(2,1)S(1)} %mix.1.refs_0_), channel_id=1, source_target_pairs={{0,3},{1,2},{2,1},{3,0},{4,7},{5,6},{6,5},{7,4},{8,11},{9,10},{10,... | collective-permute-start | bytes 196616 | tf_op jit(solution)/shard_map/ppermute | solution.py:31
  28.1 5.2 %collective-permute-start.12 = (bf16[64,512]{1,0:T(8,128)(2,1)S(1)}, bf16[64,512]{1,0:T(8,128)(2,1)S(1)}, u32[]{:S(2)}, u32[]{:S(2)}) collective-permute-start(bf16[64,512]{1,0:T(8,128)(2,1)S(1)} %mix.1.refs_0_), channel_id=1, source_target_pairs={{0,2},{1,3},{2,0},{3,1},{4,6},{5,7},{6,4},{7,5},{8,10},{9,11},{10,... | collective-permute-start | bytes 196616 | tf_op jit(solution)/shard_map/ppermute | solution.py:31
  28.1 5.2 %collective-permute-start.11 = (bf16[64,512]{1,0:T(8,128)(2,1)S(1)}, bf16[64,512]{1,0:T(8,128)(2,1)S(1)}, u32[]{:S(2)}, u32[]{:S(2)}) collective-permute-start(bf16[64,512]{1,0:T(8,128)(2,1)S(1)} %mix.1.refs_0_), channel_id=1, source_target_pairs={{0,1},{1,0},{2,3},{3,2},{4,5},{5,4},{6,7},{7,6},{8,9},{9,8},{10,11... | collective-permute-start | bytes 196616 | tf_op jit(solution)/shard_map/ppermute | solution.py:31
  33.9 7.5 %collective-permute-start.16 = (bf16[160,512]{1,0:T(8,128)(2,1)S(1)}, bf16[160,512]{1,0:T(8,128)(2,1)S(1)}, u32[]{:S(2)}, u32[]{:S(2)}) collective-permute-start(bf16[160,512]{1,0:T(8,128)(2,1)S(1)} %stack.13.refs_0_), channel_id=1, source_target_pairs={{0,24},{4,28},{8,16},{12,20},{16,8},{20,12},{24,0},{28,4},{1,25},{... | collective-permute-start | bytes 491528 | tf_op jit(solution)/shard_map/ppermute | solution.py:31
  34.5 7.9 %collective-permute-start.15 = (bf16[160,512]{1,0:T(8,128)(2,1)S(1)}, bf16[160,512]{1,0:T(8,128)(2,1)S(1)}, u32[]{:S(2)}, u32[]{:S(2)}) collective-permute-start(bf16[160,512]{1,0:T(8,128)(2,1)S(1)} %stack.13.refs_0_), channel_id=1, source_target_pairs={{0,16},{4,20},{8,24},{12,28},{16,0},{20,4},{24,8},{28,12},{1,17},{... | collective-permute-start | bytes 491528 | tf_op jit(solution)/shard_map/ppermute | solution.py:31
  35.9 6.4 %collective-permute-start.14 = (bf16[160,512]{1,0:T(8,128)(2,1)S(1)}, bf16[160,512]{1,0:T(8,128)(2,1)S(1)}, u32[]{:S(2)}, u32[]{:S(2)}) collective-permute-start(bf16[160,512]{1,0:T(8,128)(2,1)S(1)} %stack.13.refs_0_), channel_id=1, source_target_pairs={{0,8},{4,12},{8,0},{12,4},{16,24},{20,28},{24,16},{28,20},{1,9},{5... | collective-permute-start | bytes 491528 | tf_op jit(solution)/shard_map/ppermute | solution.py:31
  37.4 6.5 %collective-permute-start.17 = (bf16[160,512]{1,0:T(8,128)(2,1)S(1)}, bf16[160,512]{1,0:T(8,128)(2,1)S(1)}, u32[]{:S(2)}, u32[]{:S(2)}) collective-permute-start(bf16[160,512]{1,0:T(8,128)(2,1)S(1)} %stack.13.refs_0_), channel_id=1, source_target_pairs={{0,4},{4,0},{8,12},{12,8},{16,20},{20,16},{24,28},{28,24},{1,5},{5... | collective-permute-start | bytes 491528 | tf_op jit(solution)/shard_map/ppermute | solution.py:31
  41.3 2.6 %collective-permute-start.20 = (bf16[160,512]{1,0:T(8,128)(2,1)S(1)}, bf16[160,512]{1,0:T(8,128)(2,1)S(1)}, u32[]{:S(2)}, u32[]{:S(2)}) collective-permute-start(bf16[160,512]{1,0:T(8,128)(2,1)S(1)} %collective-permute-done.16.refs_3_), channel_id=1, source_target_pairs={{0,4},{4,0},{8,12},{12,8},{16,20},{20,16},{24,28},{28,24},{1,5},{5... | collective-permute-start | bytes 491528 | tf_op jit(solution)/shard_map/ppermute | solution.py:31
  42.4 1.6 %collective-permute-start.19 = (bf16[160,512]{1,0:T(8,128)(2,1)S(1)}, bf16[160,512]{1,0:T(8,128)(2,1)S(1)}, u32[]{:S(2)}, u32[]{:S(2)}) collective-permute-start(bf16[160,512]{1,0:T(8,128)(2,1)S(1)} %collective-permute-done.15.refs_2_), channel_id=1, source_target_pairs={{0,4},{4,0},{8,12},{12,8},{16,20},{20,16},{24,28},{28,24},{1,5},{5... | collective-permute-start | bytes 491528 | tf_op jit(solution)/shard_map/ppermute | solution.py:31
  42.4 1.6 %collective-permute-start.18 = (bf16[160,512]{1,0:T(8,128)(2,1)S(1)}, bf16[160,512]{1,0:T(8,128)(2,1)S(1)}, u32[]{:S(2)}, u32[]{:S(2)}) collective-permute-start(bf16[160,512]{1,0:T(8,128)(2,1)S(1)} %collective-permute-done.14.refs_1_), channel_id=1, source_target_pairs={{0,4},{4,0},{8,12},{12,8},{16,20},{20,16},{24,28},{28,24},{1,5},{5... | collective-permute-start | bytes 491528 | tf_op jit(solution)/shard_map/ppermute | solution.py:31

commit v13 on v12

--- a/solution.py
+++ b/solution.py
@@ -288,9 +288,26 @@
             for m in reversed(range(k + 2, SUB)):
                 steps[k] = steps[k] - near[k, m] * steps[m]
                 steps[k + 1] = steps[k + 1] - far[k, m] * steps[m]
-        for i in range(tile + 2, len(tiles)):
+        for i in range(tile + 2, min(tile + 3, len(tiles))):
             change = [spread(tiles[i][:, first + k : first + k + 1]) * steps[k] for k in range(SUB)]
             tiles[i] = jnp.where(window, 0.0, tiles[i]) - tree_sum(change[::-1])
+        if tile + 3 < len(tiles):
+            stacked = steps[0]
+            for k in range(1, SUB):
+                stacked = jnp.where(sub >= k, steps[k], stacked)
+            blank = jnp.zeros_like(stacked)
+            stacked = jnp.concatenate([stacked, blank] if tile % 2 == 0 else [blank, stacked])
+            none = jnp.zeros((PACK, LANE), bf16)
+            before, after = tile // 2, len(tiles) // 2 - 1 - tile // 2
+            parts = [jnp.concatenate([none] * before + [part] + [none] * after) for part in split(stacked)]
+            change = jnp.dot(
+                parts_of(jnp.concatenate(tiles[tile + 3 :]), LEFT, 1),
+                jnp.concatenate([parts[k] for k in RIGHT]),
+                preferred_element_type=f32,
+            )
+            for i in range(tile + 3, len(tiles)):
+                at = (i - tile - 3) * SUB
+                tiles[i] = jnp.where(window, 0.0, tiles[i]) - change[at : at + SUB]
         if tile + 1 < len(tiles):
             tiles[tile + 1] = fresh
         new, scale = kept[0], roots[0]

time: 63.7 us -> 64 us (level)
  no operation moved by 1% of the time
where the time goes in v13:
time: 64 us; the launch traced here: 63.6 us
  Pallas kernels  25 us (39%)
  starting transfers between devices  18.1 us (28%)
  waiting for transfers between devices  16.5 us (26%)
  local copies, waits for them, and re-layouts  2.4 us (4%)
  other arithmetic  0.79 us (1%)
  between operations  0.72 us (1%)
    pallas_call x8, Pallas kernels, call(): pl.pallas_call(kernel, out_shape=[jax.ShapeDtypeStruct(shape, dtype) for...  25 us
    ppermute x21, starting transfers between devices, partner(): return lax.ppermute(value, axis, pairs)  18.1 us
    ppermute x21, waiting for transfers between devices, partner(): return lax.ppermute(value, axis, pairs)  16.5 us
    unnamed x10, local copies, waits for them, and re-layouts  2.4 us
  transfers between devices with their start and end apart: 21, of which 11 were waited for; matrix products, arithmetic and copies ran while one was open for 1% of the time, Pallas kernels for 3%

profile of v13, /device:TPU:0, one launch (start us, length us, event | category | flops | bytes accessed | tf_op | source)
XLA Modules:
  0.0 63.6 jit_solution(17672865749106221596)
XLA Ops:
  0.6 4.0 %collective-permute-start.5 = (s32[1,32]{1,0:T(1,128)}, s32[1,32]{1,0:T(1,128)S(1)}, u32[]{:S(2)}, u32[]{:S(2)}) collective-permute-start(s32[1,32]{1,0:T(1,128)} %bitcast.12), channel_id=1, source_target_pairs={{0,24},{4,28},{8,16},{12,20},{16,8},{20,12},{24,0},{28,4},{1,25},{... | collective-permute-start | bytes 392 | tf_op jit(solution)/shard_map/ppermute | solution.py:31
  4.6 0.5 collective-permute-start.3
  5.1 0.1 collective-permute-start.1
  5.2 0.0 collective-permute-start
  5.2 0.1 pad_add_fusion.index_ref
  5.3 0.7 %add_bitcast_fusion.marks_ref = s32[16,128]{1,0:T(8,128)S(1)} fusion(s32[2048]{0:T(1024)} %param.7, s32[2048]{0:T(1024)} %param.8), kind=kLoop, calls=%fused_computation | loop fusion | flops 4096 | bytes 24576 | tf_op jit(solution)/shard_map/reshape | solution.py:496
  6.0 0.0 copy-start
  6.0 1.0 %copy-done = bf16[2048,128]{1,0:T(8,128)(2,1)S(1)} copy-done((bf16[2048,128]{1,0:T(8,128)(2,1)S(1)}, bf16[2048,128]{1,0:T(8,128)(2,1)}, u32[]{:S(2)}) %copy-start) | copy-done | bytes 524312
  7.1 0.0 copy-start.2
  7.1 0.7 %copy-done.2 = f32[2048]{0:T(1024)S(1)} copy-done((f32[2048]{0:T(1024)S(1)}, f32[2048]{0:T(1024)}, u32[]{:S(2)}) %copy-start.2) | copy-done | bytes 8216
  7.8 1.0 %design.1 = (bf16[560,2048]{1,0:T(8,128)(2,1)S(1)}, f32[264,128]{1,0:T(8,128)S(1)}) custom-call(bf16[2048,128]{1,0:T(8,128)(2,1)S(1)} %copy-done, s32[16,128]{1,0:T(8,128)S(1)} %add_bitcast_fusion.marks_ref, f32[16,128]{1,0:T(8,128)S(1)} %bitcast.9), custom_call_target="tpu_custom_call" | custom-call | tf_op jit(solution)/shard_map/design/pallas_call | solution.py:478
  8.8 0.0 collective-permute-done.5.refs_6_
  8.8 0.6 collective-permute-start.6
  9.4 0.0 collective-permute-done.3.refs_4_
  9.4 0.1 collective-permute-start.4
  9.5 0.0 collective-permute-done.1.refs_2_
  9.5 0.4 collective-permute-start.2
  9.9 0.0 collective-permute-done.refs_1_
  9.9 0.3 collective-permute-done.6.refs_7_
  10.2 0.3 collective-permute-done.4.refs_5_
  10.5 0.2 collective-permute-done.2.refs_3_
  10.7 0.0 copy-start.4
  10.7 0.7 %copy-done.4 = s32[32]{0:T(128)S(1)} copy-done((s32[32]{0:T(128)S(1)}, s32[32]{0:T(128)}, u32[]{:S(2)}) %copy-start.4) | copy-done | bytes 152
  11.4 1.6 %local.1 = (bf16[256,512]{1,0:T(8,128)(2,1)S(1)}, bf16[256,512]{1,0:T(8,128)(2,1)S(1)}) custom-call(s32[2]{0:T(128)S(1)} %pad_add_fusion.index_ref, bf16[560,2048]{1,0:T(8,128)(2,1)S(1)} %get-tuple-element.15.design_ref, f32[264,128]{1,0:T(8,128)S(1)} %get-tuple-element.16.packed_ref, s32[16,128]{1,0:T(8,128)S(1)} %add_bitcast_fusion.marks_ref, ...), custom_call_target="tpu_custom_call" | custom-call | tf_op jit(solution)/shard_map/local/pallas_call | solution.py:478
  12.9 0.4 collective-permute-start.7
  13.3 1.2 %collective-permute-done.7.came_ref = bf16[256,512]{1,0:T(8,128)(2,1)S(1)} collective-permute-done((bf16[256,512]{1,0:T(8,128)(2,1)S(1)}, bf16[256,512]{1,0:T(8,128)(2,1)S(1)}, u32[]{:S(2)}, u32[]{:S(2)}) %collective-permute-start.7) | collective-permute-done | bytes 262176 | tf_op jit(solution)/shard_map/ppermute | solution.py:31
  14.5 0.0 copy-start.1
  14.6 0.0 copy-start.3
  14.6 0.7 %pair.1 = (bf16[64,512]{1,0:T(8,128)(2,1)S(1)}, bf16[64,512]{1,0:T(8,128)(2,1)S(1)}, bf16[64,512]{1,0:T(8,128)(2,1)S(1)}, bf16[64,512]{1,0:T(8,128)(2,1)S(1)}) custom-call(s32[2]{0:T(128)S(1)} %pad_add_fusion.index_ref, bf16[256,512]{1,0:T(8,128)(2,1)S(1)} %get-tuple-element.17.stay_ref, bf16[256,512]{1,0:T(8,128)(2,1)S(1)} %collective-permute-done.7.came_ref), custom_call_target="tpu_custom_call" | custom-call | tf_op jit(solution)/shard_map/pair/pallas_call | solution.py:478
  15.2 2.0 %collective-permute-start.8 = (bf16[64,512]{1,0:T(8,128)(2,1)S(1)}, bf16[64,512]{1,0:T(8,128)(2,1)S(1)}, u32[]{:S(2)}, u32[]{:S(2)}) collective-permute-start(bf16[64,512]{1,0:T(8,128)(2,1)S(1)} %get-tuple-element.20), channel_id=1, source_target_pairs={{0,8},{4,12},{8,0},{12,4},{16,24},{20,28},{24,16},{28,20},{1,9},{5... | collective-permute-start | bytes 196616 | tf_op jit(solution)/shard_map/ppermute | solution.py:31
  17.2 1.5 %collective-permute-start.9 = (bf16[64,512]{1,0:T(8,128)(2,1)S(1)}, bf16[64,512]{1,0:T(8,128)(2,1)S(1)}, u32[]{:S(2)}, u32[]{:S(2)}) collective-permute-start(bf16[64,512]{1,0:T(8,128)(2,1)S(1)} %get-tuple-element.21), channel_id=1, source_target_pairs={{0,16},{4,20},{8,24},{12,28},{16,0},{20,4},{24,8},{28,12},{1,17},{... | collective-permute-start | bytes 196616 | tf_op jit(solution)/shard_map/ppermute | solution.py:31
  18.7 0.1 collective-permute-start.10
  18.8 1.0 %collective-permute-done.8.refs_1_ = bf16[64,512]{1,0:T(8,128)(2,1)S(1)} collective-permute-done((bf16[64,512]{1,0:T(8,128)(2,1)S(1)}, bf16[64,512]{1,0:T(8,128)(2,1)S(1)}, u32[]{:S(2)}, u32[]{:S(2)}) %collective-permute-start.8) | collective-permute-done | bytes 65568 | tf_op jit(solution)/shard_map/ppermute | solution.py:31
  19.7 1.7 %collective-permute-done.9.refs_2_ = bf16[64,512]{1,0:T(8,128)(2,1)S(1)} collective-permute-done((bf16[64,512]{1,0:T(8,128)(2,1)S(1)}, bf16[64,512]{1,0:T(8,128)(2,1)S(1)}, u32[]{:S(2)}, u32[]{:S(2)}) %collective-permute-start.9) | collective-permute-done | bytes 65568 | tf_op jit(solution)/shard_map/ppermute | solution.py:31
  21.4 2.4 %collective-permute-done.10.refs_3_ = bf16[64,512]{1,0:T(8,128)(2,1)S(1)} collective-permute-done((bf16[64,512]{1,0:T(8,128)(2,1)S(1)}, bf16[64,512]{1,0:T(8,128)(2,1)S(1)}, u32[]{:S(2)}, u32[]{:S(2)}) %collective-permute-start.10) | collective-permute-done | bytes 65568 | tf_op jit(solution)/shard_map/ppermute | solution.py:31
  23.8 0.6 mix.1.refs_0_
  24.5 3.7 %collective-permute-start.13 = (bf16[64,512]{1,0:T(8,128)(2,1)S(1)}, bf16[64,512]{1,0:T(8,128)(2,1)S(1)}, u32[]{:S(2)}, u32[]{:S(2)}) collective-permute-start(bf16[64,512]{1,0:T(8,128)(2,1)S(1)} %mix.1.refs_0_), channel_id=1, source_target_pairs={{0,3},{1,2},{2,1},{3,0},{4,7},{5,6},{6,5},{7,4},{8,11},{9,10},{10,... | collective-permute-start | bytes 196616 | tf_op jit(solution)/shard_map/ppermute | solution.py:31
  28.1 0.0 collective-permute-start.12
  28.1 0.8 %collective-permute-start.11 = (bf16[64,512]{1,0:T(8,128)(2,1)S(1)}, bf16[64,512]{1,0:T(8,128)(2,1)S(1)}, u32[]{:S(2)}, u32[]{:S(2)}) collective-permute-start(bf16[64,512]{1,0:T(8,128)(2,1)S(1)} %mix.1.refs_0_), channel_id=1, source_target_pairs={{0,1},{1,0},{2,3},{3,2},{4,5},{5,4},{6,7},{7,6},{8,9},{9,8},{10,11... | collective-permute-start | bytes 196616 | tf_op jit(solution)/shard_map/ppermute | solution.py:31
  28.9 1.7 %collective-permute-done.13.refs_3_ = bf16[64,512]{1,0:T(8,128)(2,1)S(1)} collective-permute-done((bf16[64,512]{1,0:T(8,128)(2,1)S(1)}, bf16[64,512]{1,0:T(8,128)(2,1)S(1)}, u32[]{:S(2)}, u32[]{:S(2)}) %collective-permute-start.13) | collective-permute-done | bytes 65568 | tf_op jit(solution)/shard_map/ppermute | solution.py:31
  30.6 2.7 %collective-permute-done.12.refs_2_ = bf16[64,512]{1,0:T(8,128)(2,1)S(1)} collective-permute-done((bf16[64,512]{1,0:T(8,128)(2,1)S(1)}, bf16[64,512]{1,0:T(8,128)(2,1)S(1)}, u32[]{:S(2)}, u32[]{:S(2)}) %collective-permute-start.12) | collective-permute-done | bytes 65568 | tf_op jit(solution)/shard_map/ppermute | solution.py:31
  33.3 0.0 collective-permute-done.11.refs_1_
  33.3 0.6 stack.13.refs_0_
  33.9 0.6 collective-permute-start.16
  34.5 1.5 %collective-permute-start.15 = (bf16[160,512]{1,0:T(8,128)(2,1)S(1)}, bf16[160,512]{1,0:T(8,128)(2,1)S(1)}, u32[]{:S(2)}, u32[]{:S(2)}) collective-permute-start(bf16[160,512]{1,0:T(8,128)(2,1)S(1)} %stack.13.refs_0_), channel_id=1, source_target_pairs={{0,16},{4,20},{8,24},{12,28},{16,0},{20,4},{24,8},{28,12},{1,17},{... | collective-permute-start | bytes 491528 | tf_op jit(solution)/shard_map/ppermute | solution.py:31
  35.9 1.5 %collective-permute-start.14 = (bf16[160,512]{1,0:T(8,128)(2,1)S(1)}, bf16[160,512]{1,0:T(8,128)(2,1)S(1)}, u32[]{:S(2)}, u32[]{:S(2)}) collective-permute-start(bf16[160,512]{1,0:T(8,128)(2,1)S(1)} %stack.13.refs_0_), channel_id=1, source_target_pairs={{0,8},{4,12},{8,0},{12,4},{16,24},{20,28},{24,16},{28,20},{1,9},{5... | collective-permute-start | bytes 491528 | tf_op jit(solution)/shard_map/ppermute | solution.py:31
  37.4 0.0 collective-permute-start.17
  37.4 3.9 %collective-permute-done.16.refs_3_ = bf16[160,512]{1,0:T(8,128)(2,1)S(1)} collective-permute-done((bf16[160,512]{1,0:T(8,128)(2,1)S(1)}, bf16[160,512]{1,0:T(8,128)(2,1)S(1)}, u32[]{:S(2)}, u32[]{:S(2)}) %collective-permute-start.16) | collective-permute-done | bytes 163872 | tf_op jit(solution)/shard_map/ppermute | solution.py:31
  41.3 0.0 collective-permute-start.20
  41.3 1.0 %collective-permute-done.15.refs_2_ = bf16[160,512]{1,0:T(8,128)(2,1)S(1)} collective-permute-done((bf16[160,512]{1,0:T(8,128)(2,1)S(1)}, bf16[160,512]{1,0:T(8,128)(2,1)S(1)}, u32[]{:S(2)}, u32[]{:S(2)}) %collective-permute-start.15) | collective-permute-done | bytes 163872 | tf_op jit(solution)/shard_map/ppermute | solution.py:31
  42.4 0.0 collective-permute-start.19
  42.4 0.0 collective-permute-done.14.refs_1_
  42.4 0.5 collective-permute-start.18
  42.9 1.0 %gram.1.gram_ref = f32[512,512]{1,0:T(8,128)S(1)} custom-call(s32[2]{0:T(128)S(1)} %pad_add_fusion.index_ref, bf16[160,512]{1,0:T(8,128)(2,1)S(1)} %stack.13.refs_0_, bf16[160,512]{1,0:T(8,128)(2,1)S(1)} %collective-permute-done.14.refs_1_, bf16[160,512]{1,0:T(8,128)(2,1)S(1)} %collective-permute-done.15.refs_2_, ...), custom_call_target="tpu_custom_call" | custom-call | tf_op jit(solution)/shard_map/gram/pallas_call | solution.py:478
  43.9 0.0 collective-permute-done.17.refs_0_.refs_4_
  44.0 0.0 collective-permute-done.20.refs_3_.refs_7_
  44.0 0.0 collective-permute-done.19.refs_2_.refs_6_
  44.0 0.0 collective-permute-done.18.refs_1_.refs_5_
  44.0 16.1 %factor.1 = (f32[512,512]{1,0:T(8,128)}, f32[512,512]{1,0:T(8,128)S(1)}) custom-call(s32[2]{0:T(128)S(1)} %pad_add_fusion.index_ref, f32[512,512]{1,0:T(8,128)S(1)} %gram.1.gram_ref, bf16[160,512]{1,0:T(8,128)(2,1)S(1)} %collective-permute-done.17.refs_0_.refs_4_, bf16[160,512]{1,0:T(8,128)(2,1)S(1)} %collective-permute-done.18.refs_1_.refs_5_, ...), custom_call_target="tpu_custom_call" | custom-call | tf_op jit(solution)/shard_map/factor/pallas_call | solution.py:478
  60.1 0.0 copy-done.1
  60.1 0.0 copy-done.3
  60.1 3.5 %solve.1 = (f32[4,128]{1,0:T(4,128)}, f32[16,128]{1,0:T(8,128)}) custom-call(s32[2]{0:T(128)S(1)} %pad_add_fusion.index_ref, f32[512,512]{1,0:T(8,128)S(1)} %get-tuple-element.23.inverse_ref, f32[4,128]{1,0:T(4,128)S(1)} %bitcast.11, bf16[2048,128]{1,0:T(8,128)(2,1)S(1)} %copy-done.1, s32[16,128]{1,0:T(8,128)S(1)} %add_bitcast_fusion.marks_ref, ...), custom_call_target="tpu_custom_call" | custom-call | tf_op jit(solution)/shard_map/solve/pallas_call | solution.py:478
Async XLA Ops:
  0.6 8.2 %collective-permute-start.5 = (s32[1,32]{1,0:T(1,128)}, s32[1,32]{1,0:T(1,128)S(1)}, u32[]{:S(2)}, u32[]{:S(2)}) collective-permute-start(s32[1,32]{1,0:T(1,128)} %bitcast.12), channel_id=1, source_target_pairs={{0,24},{4,28},{8,16},{12,20},{16,8},{20,12},{24,0},{28,4},{1,25},{... | collective-permute-start | bytes 392 | tf_op jit(solution)/shard_map/ppermute | solution.py:31
  4.6 4.8 %collective-permute-start.3 = (s32[1,32]{1,0:T(1,128)}, s32[1,32]{1,0:T(1,128)S(1)}, u32[]{:S(2)}, u32[]{:S(2)}) collective-permute-start(s32[1,32]{1,0:T(1,128)} %bitcast.13), channel_id=1, source_target_pairs={{0,16},{4,20},{8,24},{12,28},{16,0},{20,4},{24,8},{28,12},{1,17},{... | collective-permute-start | bytes 392 | tf_op jit(solution)/shard_map/ppermute | solution.py:31
  5.1 4.4 %collective-permute-start.1 = (s32[1,32]{1,0:T(1,128)}, s32[1,32]{1,0:T(1,128)S(1)}, u32[]{:S(2)}, u32[]{:S(2)}) collective-permute-start(s32[1,32]{1,0:T(1,128)} %bitcast.14), channel_id=1, source_target_pairs={{0,8},{4,12},{8,0},{12,4},{16,24},{20,28},{24,16},{28,20},{1,9},{5... | collective-permute-start | bytes 392 | tf_op jit(solution)/shard_map/ppermute | solution.py:31
  5.2 4.7 %collective-permute-start = (s32[1,32]{1,0:T(1,128)}, s32[1,32]{1,0:T(1,128)S(1)}, u32[]{:S(2)}, u32[]{:S(2)}) collective-permute-start(s32[1,32]{1,0:T(1,128)} %bitcast.15), channel_id=1, source_target_pairs={{0,4},{4,0},{8,12},{12,8},{16,20},{20,16},{24,28},{28,24},{1,5},{5... | collective-permute-start | bytes 392 | tf_op jit(solution)/shard_map/ppermute | solution.py:31
  6.0 1.0 %copy-start = (bf16[2048,128]{1,0:T(8,128)(2,1)S(1)}, bf16[2048,128]{1,0:T(8,128)(2,1)}, u32[]{:S(2)}) copy-start(bf16[2048,128]{1,0:T(8,128)(2,1)} %cov_ref.3) | copy-start | bytes 1572868
  7.1 0.7 %copy-start.2 = (f32[2048]{0:T(1024)S(1)}, f32[2048]{0:T(1024)}, u32[]{:S(2)}) copy-start(f32[2048]{0:T(1024)} %param.11) | copy-start | bytes 24580
  8.8 1.4 %collective-permute-start.6 = (s32[1,32]{1,0:T(1,128)S(1)}, s32[1,32]{1,0:T(1,128)S(1)}, u32[]{:S(2)}, u32[]{:S(2)}) collective-permute-start(s32[1,32]{1,0:T(1,128)S(1)} %collective-permute-done.5.refs_6_), channel_id=1, source_target_pairs={{0,4},{4,0},{8,12},{12,8},{16,20},{20,16},{24,28},{28,24},{1,5},{5... | collective-permute-start | bytes 392 | tf_op jit(solution)/shard_map/ppermute | solution.py:31
  9.4 1.1 %collective-permute-start.4 = (s32[1,32]{1,0:T(1,128)S(1)}, s32[1,32]{1,0:T(1,128)S(1)}, u32[]{:S(2)}, u32[]{:S(2)}) collective-permute-start(s32[1,32]{1,0:T(1,128)S(1)} %collective-permute-done.3.refs_4_), channel_id=1, source_target_pairs={{0,4},{4,0},{8,12},{12,8},{16,20},{20,16},{24,28},{28,24},{1,5},{5... | collective-permute-start | bytes 392 | tf_op jit(solution)/shard_map/ppermute | solution.py:31
  9.5 1.2 %collective-permute-start.2 = (s32[1,32]{1,0:T(1,128)S(1)}, s32[1,32]{1,0:T(1,128)S(1)}, u32[]{:S(2)}, u32[]{:S(2)}) collective-permute-start(s32[1,32]{1,0:T(1,128)S(1)} %collective-permute-done.1.refs_2_), channel_id=1, source_target_pairs={{0,4},{4,0},{8,12},{12,8},{16,20},{20,16},{24,28},{28,24},{1,5},{5... | collective-permute-start | bytes 392 | tf_op jit(solution)/shard_map/ppermute | solution.py:31
  10.7 0.7 %copy-start.4 = (s32[32]{0:T(128)S(1)}, s32[32]{0:T(128)}, u32[]{:S(2)}) copy-start(s32[32]{0:T(128)} %param.9) | copy-start | bytes 388
  12.9 1.6 %collective-permute-start.7 = (bf16[256,512]{1,0:T(8,128)(2,1)S(1)}, bf16[256,512]{1,0:T(8,128)(2,1)S(1)}, u32[]{:S(2)}, u32[]{:S(2)}) collective-permute-start(bf16[256,512]{1,0:T(8,128)(2,1)S(1)} %get-tuple-element.18), channel_id=1, source_target_pairs={{0,4},{4,0},{8,12},{12,8},{16,20},{20,16},{24,28},{28,24},{1,5},{5... | collective-permute-start | bytes 786440 | tf_op jit(solution)/shard_map/ppermute | solution.py:31
  14.5 45.5 %copy-start.1 = (bf16[2048,128]{1,0:T(8,128)(2,1)S(1)}, bf16[2048,128]{1,0:T(8,128)(2,1)}, u32[]{:S(2)}) copy-start(bf16[2048,128]{1,0:T(8,128)(2,1)} %cov_ref.3) | copy-start | bytes 1572868
  14.6 45.5 %copy-start.3 = (f32[512]{0:T(512)S(1)}, f32[512]{0:T(512)}, u32[]{:S(2)}) copy-start(f32[512]{0:T(512)} %param.10) | copy-start | bytes 6148
  15.2 4.5 %collective-permute-start.8 = (bf16[64,512]{1,0:T(8,128)(2,1)S(1)}, bf16[64,512]{1,0:T(8,128)(2,1)S(1)}, u32[]{:S(2)}, u32[]{:S(2)}) collective-permute-start(bf16[64,512]{1,0:T(8,128)(2,1)S(1)} %get-tuple-element.20), channel_id=1, source_target_pairs={{0,8},{4,12},{8,0},{12,4},{16,24},{20,28},{24,16},{28,20},{1,9},{5... | collective-permute-start | bytes 196616 | tf_op jit(solution)/shard_map/ppermute | solution.py:31
  17.2 4.3 %collective-permute-start.9 = (bf16[64,512]{1,0:T(8,128)(2,1)S(1)}, bf16[64,512]{1,0:T(8,128)(2,1)S(1)}, u32[]{:S(2)}, u32[]{:S(2)}) collective-permute-start(bf16[64,512]{1,0:T(8,128)(2,1)S(1)} %get-tuple-element.21), channel_id=1, source_target_pairs={{0,16},{4,20},{8,24},{12,28},{16,0},{20,4},{24,8},{28,12},{1,17},{... | collective-permute-start | bytes 196616 | tf_op jit(solution)/shard_map/ppermute | solution.py:31
  18.7 5.2 %collective-permute-start.10 = (bf16[64,512]{1,0:T(8,128)(2,1)S(1)}, bf16[64,512]{1,0:T(8,128)(2,1)S(1)}, u32[]{:S(2)}, u32[]{:S(2)}) collective-permute-start(bf16[64,512]{1,0:T(8,128)(2,1)S(1)} %get-tuple-element.22), channel_id=1, source_target_pairs={{0,24},{4,28},{8,16},{12,20},{16,8},{20,12},{24,0},{28,4},{1,25},{... | collective-permute-start | bytes 196616 | tf_op jit(solution)/shard_map/ppermute | solution.py:31
  24.5 6.1 %collective-permute-start.13 = (bf16[64,512]{1,0:T(8,128)(2,1)S(1)}, bf16[64,512]{1,0:T(8,128)(2,1)S(1)}, u32[]{:S(2)}, u32[]{:S(2)}) collective-permute-start(bf16[64,512]{1,0:T(8,128)(2,1)S(1)} %mix.1.refs_0_), channel_id=1, source_target_pairs={{0,3},{1,2},{2,1},{3,0},{4,7},{5,6},{6,5},{7,4},{8,11},{9,10},{10,... | collective-permute-start | bytes 196616 | tf_op jit(solution)/shard_map/ppermute | solution.py:31
  28.1 5.2 %collective-permute-start.12 = (bf16[64,512]{1,0:T(8,128)(2,1)S(1)}, bf16[64,512]{1,0:T(8,128)(2,1)S(1)}, u32[]{:S(2)}, u32[]{:S(2)}) collective-permute-start(bf16[64,512]{1,0:T(8,128)(2,1)S(1)} %mix.1.refs_0_), channel_id=1, source_target_pairs={{0,2},{1,3},{2,0},{3,1},{4,6},{5,7},{6,4},{7,5},{8,10},{9,11},{10,... | collective-permute-start | bytes 196616 | tf_op jit(solution)/shard_map/ppermute | solution.py:31
  28.1 5.2 %collective-permute-start.11 = (bf16[64,512]{1,0:T(8,128)(2,1)S(1)}, bf16[64,512]{1,0:T(8,128)(2,1)S(1)}, u32[]{:S(2)}, u32[]{:S(2)}) collective-permute-start(bf16[64,512]{1,0:T(8,128)(2,1)S(1)} %mix.1.refs_0_), channel_id=1, source_target_pairs={{0,1},{1,0},{2,3},{3,2},{4,5},{5,4},{6,7},{7,6},{8,9},{9,8},{10,11... | collective-permute-start | bytes 196616 | tf_op jit(solution)/shard_map/ppermute | solution.py:31
  33.9 7.5 %collective-permute-start.16 = (bf16[160,512]{1,0:T(8,128)(2,1)S(1)}, bf16[160,512]{1,0:T(8,128)(2,1)S(1)}, u32[]{:S(2)}, u32[]{:S(2)}) collective-permute-start(bf16[160,512]{1,0:T(8,128)(2,1)S(1)} %stack.13.refs_0_), channel_id=1, source_target_pairs={{0,24},{4,28},{8,16},{12,20},{16,8},{20,12},{24,0},{28,4},{1,25},{... | collective-permute-start | bytes 491528 | tf_op jit(solution)/shard_map/ppermute | solution.py:31
  34.5 7.9 %collective-permute-start.15 = (bf16[160,512]{1,0:T(8,128)(2,1)S(1)}, bf16[160,512]{1,0:T(8,128)(2,1)S(1)}, u32[]{:S(2)}, u32[]{:S(2)}) collective-permute-start(bf16[160,512]{1,0:T(8,128)(2,1)S(1)} %stack.13.refs_0_), channel_id=1, source_target_pairs={{0,16},{4,20},{8,24},{12,28},{16,0},{20,4},{24,8},{28,12},{1,17},{... | collective-permute-start | bytes 491528 | tf_op jit(solution)/shard_map/ppermute | solution.py:31
  35.9 6.4 %collective-permute-start.14 = (bf16[160,512]{1,0:T(8,128)(2,1)S(1)}, bf16[160,512]{1,0:T(8,128)(2,1)S(1)}, u32[]{:S(2)}, u32[]{:S(2)}) collective-permute-start(bf16[160,512]{1,0:T(8,128)(2,1)S(1)} %stack.13.refs_0_), channel_id=1, source_target_pairs={{0,8},{4,12},{8,0},{12,4},{16,24},{20,28},{24,16},{28,20},{1,9},{5... | collective-permute-start | bytes 491528 | tf_op jit(solution)/shard_map/ppermute | solution.py:31
  37.4 6.5 %collective-permute-start.17 = (bf16[160,512]{1,0:T(8,128)(2,1)S(1)}, bf16[160,512]{1,0:T(8,128)(2,1)S(1)}, u32[]{:S(2)}, u32[]{:S(2)}) collective-permute-start(bf16[160,512]{1,0:T(8,128)(2,1)S(1)} %stack.13.refs_0_), channel_id=1, source_target_pairs={{0,4},{4,0},{8,12},{12,8},{16,20},{20,16},{24,28},{28,24},{1,5},{5... | collective-permute-start | bytes 491528 | tf_op jit(solution)/shard_map/ppermute | solution.py:31
  41.3 2.6 %collective-permute-start.20 = (bf16[160,512]{1,0:T(8,128)(2,1)S(1)}, bf16[160,512]{1,0:T(8,128)(2,1)S(1)}, u32[]{:S(2)}, u32[]{:S(2)}) collective-permute-start(bf16[160,512]{1,0:T(8,128)(2,1)S(1)} %collective-permute-done.16.refs_3_), channel_id=1, source_target_pairs={{0,4},{4,0},{8,12},{12,8},{16,20},{20,16},{24,28},{28,24},{1,5},{5... | collective-permute-start | bytes 491528 | tf_op jit(solution)/shard_map/ppermute | solution.py:31
  42.4 1.6 %collective-permute-start.19 = (bf16[160,512]{1,0:T(8,128)(2,1)S(1)}, bf16[160,512]{1,0:T(8,128)(2,1)S(1)}, u32[]{:S(2)}, u32[]{:S(2)}) collective-permute-start(bf16[160,512]{1,0:T(8,128)(2,1)S(1)} %collective-permute-done.15.refs_2_), channel_id=1, source_target_pairs={{0,4},{4,0},{8,12},{12,8},{16,20},{20,16},{24,28},{28,24},{1,5},{5... | collective-permute-start | bytes 491528 | tf_op jit(solution)/shard_map/ppermute | solution.py:31
  42.4 1.6 %collective-permute-start.18 = (bf16[160,512]{1,0:T(8,128)(2,1)S(1)}, bf16[160,512]{1,0:T(8,128)(2,1)S(1)}, u32[]{:S(2)}, u32[]{:S(2)}) collective-permute-start(bf16[160,512]{1,0:T(8,128)(2,1)S(1)} %collective-permute-done.14.refs_1_), channel_id=1, source_target_pairs={{0,4},{4,0},{8,12},{12,8},{16,20},{20,16},{24,28},{28,24},{1,5},{5... | collective-permute-start | bytes 491528 | tf_op jit(solution)/shard_map/ppermute | solution.py:31

commit v14 on v13

--- a/solution.py
+++ b/solution.py
@@ -346,13 +346,16 @@
         gram_ref[at : at + LANE, :] = gram_rows(sketch, slice(at, at + LANE))
 
 
-def factor_kernel(ratio, rows_in, index_ref, gram_ref, *refs):
-    piece_refs, (factor_ref, inverse_ref, sketch, work, shelf) = refs[:-5], refs[-5:]
+def solve_kernel(
+    ratio, apart, rows_in, share, index_ref, gram_ref, effects_ref, cov_ref, marks_ref, noise_ref, *refs
+):
+    piece_refs, (factor_hbm, solved_ref, resid_ref), scratch = refs[:-11], refs[-11:-8], refs[-8:]
+    sketch, work, shelf, factor_ref, inverse_ref, packed, normal, sent = scratch
     count = work.shape[0] // LANE
     spans = [slice(at, at + LANE) for at in range(0, work.shape[0], LANE)]
     row_in, lane_in, same = eye()
     diagonals, units = [None] * count, [None] * count
-    put_pieces(rows_in, index_ref, piece_refs, sketch)
+    put_pieces(rows_in, index_ref, piece_refs[len(piece_refs) // 2 :], sketch)
 
     def take_rows(i):
         work[spans[i], :] = gram_ref[spans[i], :] + gram_rows(sketch, spans[i])
@@ -363,6 +366,28 @@
 
     def scale_rows(i):
         work[spans[i], :] = work[spans[i], :] * to_column(units[i], same) * jnp.concatenate(units, axis=1)
+
+    extras, gradient = [], [None] * LEVELS
+
+    def take_share(mask, ref):
+        at = pl.multiple_of(jnp.bitwise_xor(index_ref[0], mask) * share, share)
+        packed[pl.ds(at, share), :], extra = take_sums(ref, rows_in, share)
+        extras.append(extra)
+
+    def unpack(pair):
+        both = packed[spans[pair], :]
+        turned = both.T
+        normal[spans[2 * pair], :] = jnp.where(row_in >= lane_in, both, turned)
+        diagonal = jnp.where(same, extras[0][LEVELS + pair : LEVELS + pair + 1], turned)
+        normal[spans[2 * pair + 1], :] = jnp.where(row_in < lane_in, both, diagonal)
+
+    def take_gradient(level):
+        column = to_column(effects_ref[level : level + 1, :], same)
+        image = jnp.sum(normal[spans[level], :] * column, axis=0, keepdims=True)
+        gradient[level] = image + extras[0][level : level + 1]
+
+    def send_factor(i):
+        return pltpu.make_async_copy(factor_ref.at[spans[i], :], factor_hbm.at[spans[i], :], sent.at[i])
 
     take_rows(0)
     take_unit(0)
@@ -370,6 +395,9 @@
     aside = [functools.partial(take_rows, i) for i in range(1, count)]
     aside += [functools.partial(take_unit, i) for i in range(1, count)]
     aside += [functools.partial(scale_rows, i) for i in range(count)]
+    later = [functools.partial(take_share, mask, ref) for mask, ref in zip(apart, piece_refs)]
+    later += [functools.partial(unpack, pair) for pair in range(LEVELS // 2)]
+    later += [functools.partial(take_gradient, level) for level in range(LEVELS)]
     for b, here in enumerate(spans):
         tiles, scales = eliminate([fresh[at : at + SUB] for at in range(0, LANE, SUB)], aside, shelf)
         scale = jnp.concatenate(scales)
@@ -415,32 +443,13 @@
             for j in range(count)
             if (i, j) != (b + 1, b + 1)
         ]
+        aside.append(lambda b=b: send_factor(b).start())
+        if b == 1:
+            aside += later
     for call_it in aside:
         call_it()
 
-
-def solve_kernel(apart, rows_in, share, index_ref, inverse_ref, effects_ref, cov_ref, marks_ref, noise_ref, *refs):
-    piece_refs, (solved_ref, resid_ref, packed) = refs[:-3], refs[-3:]
-    rows, lanes, same = eye()
-    extra = None
-    for mask, ref in zip(apart, piece_refs):
-        at = pl.multiple_of(jnp.bitwise_xor(index_ref[0], mask) * share, share)
-        packed[pl.ds(at, share), :], more = take_sums(ref, rows_in, share)
-        extra = more if extra is None else extra
-    normal = []
-    for pair in range(LEVELS // 2):
-        both = packed[pair * LANE : (pair + 1) * LANE, :]
-        turned = both.T
-        normal.append(jnp.where(rows >= lanes, both, turned))
-        diagonal = jnp.where(same, extra[LEVELS + pair : LEVELS + pair + 1], turned)
-        normal.append(jnp.where(rows < lanes, both, diagonal))
-
     inverse = inverse_ref[...]
-    spans = [slice(level * LANE, (level + 1) * LANE) for level in range(LEVELS)]
-    gradient = []
-    for level in range(LEVELS):
-        column = to_column(effects_ref[level : level + 1, :], same)
-        gradient.append(jnp.sum(normal[level] * column, axis=0, keepdims=True) + extra[level : level + 1])
     steer = jnp.sum(inverse * jnp.concatenate(gradient, axis=1), axis=1, keepdims=True)
     direction = steer
     gamma = jnp.sum(steer * steer, axis=0, keepdims=True)
@@ -448,8 +457,8 @@
     for step in range(ITERS):
         move = jnp.sum(inverse * direction, axis=0, keepdims=True)
         image = []
-        for level, span in enumerate(spans):
-            image.append(jnp.sum(normal[level] * to_column(move[:, span], same), axis=0, keepdims=True))
+        for span in spans:
+            image.append(jnp.sum(normal[span, :] * to_column(move[:, span], same), axis=0, keepdims=True))
         image = jnp.concatenate(image, axis=1)
         alpha = gamma / jnp.sum(move * image, axis=1, keepdims=True)
         solved = solved + alpha * move
@@ -462,16 +471,18 @@
     solved = jnp.concatenate([solved[:, span] for span in spans])
     solved_ref[...] = solved
 
-    left = jnp.concatenate([effects_ref[...] - solved, jnp.zeros((PACK - LEVELS, LANE), f32)])
-    values = jnp.zeros((SUB, cov_ref.shape[0]), f32)
-    for part in split(left):
-        values = values + lax.dot_general(part, cov_ref[...], NT, preferred_element_type=f32)[:SUB]
+    left = [part.astype(f32) for part in split(effects_ref[...] - solved)]
+    left = jnp.concatenate(left + [jnp.zeros((PACK - 3 * LEVELS, LANE), f32)]).astype(bf16)
+    values = lax.dot_general(left, cov_ref[...], NT, preferred_element_type=f32)
+    values = values[:LEVELS] + values[LEVELS : 2 * LEVELS] + values[2 * LEVELS : 3 * LEVELS]
     for r in range(marks_ref.shape[0]):
         code = jnp.bitwise_and(marks_ref[r : r + 1, :], LEVELS - 1)
         total = noise_ref[r : r + 1, :]
         for level in range(LEVELS):
             total = total + jnp.where(code == level, values[level : level + 1, r * LANE : (r + 1) * LANE], 0.0)
         resid_ref[r : r + 1, :] = total
+    for i in range(count):
+        send_factor(i).wait()
 
 
 def call(kernel, name, outs, scratch, *operands):
@@ -546,30 +557,26 @@
     sketch = [((rows_in * (wide // 2), cols), bf16)]
     square = ((cols, cols), f32)
     (gram,) = call(functools.partial(gram_kernel, rows_in), "gram", [square], sketch, index, *pieces)
-    factor, inverse = call(
-        functools.partial(factor_kernel, math.sqrt(LEVELS / SKETCH), rows_in),
-        "factor",
-        [square] * 2,
-        sketch + [square, ((2 * (SUB + 1) * SUB, LANE), f32)],
-        index,
-        gram,
-        *theirs,
-    )
-    pieces += theirs
     apart = [2 * m + core for core in range(2) for m in range(wide // 2)]
-    solved, resid = call(
-        functools.partial(solve_kernel, apart, rows_in, share),
-        "solve",
-        [((LEVELS, COV), f32), (noise.shape, f32)],
-        [((share * wide, LANE), f32)],
-        index,
-        inverse,
-        effects,
-        covariates,
-        marks,
-        noise,
-        *pieces,
-    )
+    operands = (gram, effects, covariates, marks, noise, *pieces, *theirs)
+    scratch = sketch + [
+        square,
+        ((2 * (SUB + 1) * SUB, LANE), f32),
+        square,
+        square,
+        ((share * wide, LANE), f32),
+        ((cols, LANE), f32),
+    ]
+    factor, solved, resid = pl.pallas_call(
+        functools.partial(solve_kernel, math.sqrt(LEVELS / SKETCH), apart, rows_in, share),
+        out_shape=[jax.ShapeDtypeStruct(shape, f32) for shape in ((cols, cols), (LEVELS, COV), noise.shape)],
+        in_specs=[SMEM] + [VMEM] * len(operands),
+        out_specs=[pl.BlockSpec(memory_space=pl.ANY), VMEM, VMEM],
+        scratch_shapes=[pltpu.VMEM(shape, dtype) for shape, dtype in scratch]
+        + [pltpu.SemaphoreType.DMA((cols // LANE,))],
+        compiler_params=pltpu.CompilerParams(vmem_limit_bytes=40 * 2**20),
+        name="solve",
+    )(index, *operands)
     return solved.reshape(-1), resid.reshape(-1), factor
 
 

time: 64 us -> 62.3 us (0.973)
  Pallas kernels: 25 us -> 23.1 us
    pallas_call x8 -> x6, Pallas kernels: 25 us -> 5.46 us  [call(): pl.pallas_call(kernel, out_shape=[jax.ShapeDtypeStruct(shape, dtype) for...]
    pallas_call x0 -> x1, Pallas kernels: none -> 17.6 us  [body(): pl.pallas_call(functools.partial(solve_kernel, math.sqrt(LEVELS / SKETCH)...]
where the time goes in v14:
time: 62.3 us; the launch traced here: 61.9 us
  Pallas kernels  23.1 us (37%)
  starting transfers between devices  18.1 us (29%)
  waiting for transfers between devices  16.6 us (27%)
  local copies, waits for them, and re-layouts  2.4 us (4%)
  between operations  0.88 us (1%)
  other arithmetic  0.79 us (1%)
    ppermute x21, starting transfers between devices, partner(): return lax.ppermute(value, axis, pairs)  18.1 us
    pallas_call x1, Pallas kernels, body(): pl.pallas_call(functools.partial(solve_kernel, math.sqrt(LEVELS / SKETCH)...  17.6 us
    ppermute x21, waiting for transfers between devices, partner(): return lax.ppermute(value, axis, pairs)  16.6 us
    pallas_call x6, Pallas kernels, call(): pl.pallas_call(kernel, out_shape=[jax.ShapeDtypeStruct(shape, dtype) for...  5.46 us
    unnamed x10, local copies, waits for them, and re-layouts  2.4 us
  transfers between devices with their start and end apart: 21, of which 11 were waited for; matrix products, arithmetic and copies ran while one was open for 1% of the time, Pallas kernels for 3%

profile of v14, /device:TPU:0, one launch (start us, length us, event | category | flops | bytes accessed | tf_op | source)
XLA Modules:
  0.0 61.9 jit_solution(8380014945041094872)
XLA Ops:
  0.6 4.0 %collective-permute-start.5 = (s32[1,32]{1,0:T(1,128)}, s32[1,32]{1,0:T(1,128)S(1)}, u32[]{:S(2)}, u32[]{:S(2)}) collective-permute-start(s32[1,32]{1,0:T(1,128)} %bitcast.12), channel_id=1, source_target_pairs={{0,24},{4,28},{8,16},{12,20},{16,8},{20,12},{24,0},{28,4},{1,25},{... | collective-permute-start | bytes 392 | tf_op jit(solution)/shard_map/ppermute | solution.py:31
  4.6 0.5 collective-permute-start.3
  5.1 0.1 collective-permute-start.1
  5.2 0.0 collective-permute-start
  5.2 0.1 pad_add_fusion.index_ref
  5.3 0.7 %add_bitcast_fusion.marks_ref = s32[16,128]{1,0:T(8,128)S(1)} fusion(s32[2048]{0:T(1024)} %param.7, s32[2048]{0:T(1024)} %param.8), kind=kLoop, calls=%fused_computation | loop fusion | flops 4096 | bytes 24576 | tf_op jit(solution)/shard_map/reshape | solution.py:507
  6.0 0.0 copy-start
  6.0 1.0 %copy-done = bf16[2048,128]{1,0:T(8,128)(2,1)S(1)} copy-done((bf16[2048,128]{1,0:T(8,128)(2,1)S(1)}, bf16[2048,128]{1,0:T(8,128)(2,1)}, u32[]{:S(2)}) %copy-start) | copy-done | bytes 524312
  7.1 0.0 copy-start.2
  7.1 0.7 %copy-done.2 = f32[2048]{0:T(1024)S(1)} copy-done((f32[2048]{0:T(1024)S(1)}, f32[2048]{0:T(1024)}, u32[]{:S(2)}) %copy-start.2) | copy-done | bytes 8216
  7.8 1.0 %design.1 = (bf16[560,2048]{1,0:T(8,128)(2,1)S(1)}, f32[264,128]{1,0:T(8,128)S(1)}) custom-call(bf16[2048,128]{1,0:T(8,128)(2,1)S(1)} %copy-done, s32[16,128]{1,0:T(8,128)S(1)} %add_bitcast_fusion.marks_ref, f32[16,128]{1,0:T(8,128)S(1)} %bitcast.9), custom_call_target="tpu_custom_call" | custom-call | tf_op jit(solution)/shard_map/design/pallas_call | solution.py:489
  8.8 0.0 collective-permute-done.5.refs_6_
  8.8 0.6 collective-permute-start.6
  9.4 0.0 collective-permute-done.3.refs_4_
  9.4 0.1 collective-permute-start.4
  9.5 0.0 collective-permute-done.1.refs_2_
  9.5 0.4 collective-permute-start.2
  9.9 0.0 collective-permute-done.refs_1_
  9.9 0.3 collective-permute-done.6.refs_7_
  10.2 0.3 collective-permute-done.4.refs_5_
  10.5 0.2 collective-permute-done.2.refs_3_
  10.7 0.0 copy-start.4
  10.7 0.7 %copy-done.4 = s32[32]{0:T(128)S(1)} copy-done((s32[32]{0:T(128)S(1)}, s32[32]{0:T(128)}, u32[]{:S(2)}) %copy-start.4) | copy-done | bytes 152
  11.4 0.0 copy-start.1
  11.4 0.0 copy-start.3
  11.4 1.6 %local.1 = (bf16[256,512]{1,0:T(8,128)(2,1)S(1)}, bf16[256,512]{1,0:T(8,128)(2,1)S(1)}) custom-call(s32[2]{0:T(128)S(1)} %pad_add_fusion.index_ref, bf16[560,2048]{1,0:T(8,128)(2,1)S(1)} %get-tuple-element.14.design_ref, f32[264,128]{1,0:T(8,128)S(1)} %get-tuple-element.15.packed_ref, s32[16,128]{1,0:T(8,128)S(1)} %add_bitcast_fusion.marks_ref, ...), custom_call_target="tpu_custom_call" | custom-call | tf_op jit(solution)/shard_map/local/pallas_call | solution.py:489
  13.0 0.4 collective-permute-start.7
  13.3 1.2 %collective-permute-done.7.came_ref = bf16[256,512]{1,0:T(8,128)(2,1)S(1)} collective-permute-done((bf16[256,512]{1,0:T(8,128)(2,1)S(1)}, bf16[256,512]{1,0:T(8,128)(2,1)S(1)}, u32[]{:S(2)}, u32[]{:S(2)}) %collective-permute-start.7) | collective-permute-done | bytes 262176 | tf_op jit(solution)/shard_map/ppermute | solution.py:31
  14.6 0.7 %pair.1 = (bf16[64,512]{1,0:T(8,128)(2,1)S(1)}, bf16[64,512]{1,0:T(8,128)(2,1)S(1)}, bf16[64,512]{1,0:T(8,128)(2,1)S(1)}, bf16[64,512]{1,0:T(8,128)(2,1)S(1)}) custom-call(s32[2]{0:T(128)S(1)} %pad_add_fusion.index_ref, bf16[256,512]{1,0:T(8,128)(2,1)S(1)} %get-tuple-element.16.stay_ref, bf16[256,512]{1,0:T(8,128)(2,1)S(1)} %collective-permute-done.7.came_ref), custom_call_target="tpu_custom_call" | custom-call | tf_op jit(solution)/shard_map/pair/pallas_call | solution.py:489
  15.2 1.9 %collective-permute-start.8 = (bf16[64,512]{1,0:T(8,128)(2,1)S(1)}, bf16[64,512]{1,0:T(8,128)(2,1)S(1)}, u32[]{:S(2)}, u32[]{:S(2)}) collective-permute-start(bf16[64,512]{1,0:T(8,128)(2,1)S(1)} %get-tuple-element.19), channel_id=1, source_target_pairs={{0,8},{4,12},{8,0},{12,4},{16,24},{20,28},{24,16},{28,20},{1,9},{5... | collective-permute-start | bytes 196616 | tf_op jit(solution)/shard_map/ppermute | solution.py:31
  17.2 1.5 %collective-permute-start.9 = (bf16[64,512]{1,0:T(8,128)(2,1)S(1)}, bf16[64,512]{1,0:T(8,128)(2,1)S(1)}, u32[]{:S(2)}, u32[]{:S(2)}) collective-permute-start(bf16[64,512]{1,0:T(8,128)(2,1)S(1)} %get-tuple-element.20), channel_id=1, source_target_pairs={{0,16},{4,20},{8,24},{12,28},{16,0},{20,4},{24,8},{28,12},{1,17},{... | collective-permute-start | bytes 196616 | tf_op jit(solution)/shard_map/ppermute | solution.py:31
  18.7 0.1 collective-permute-start.10
  18.8 0.9 %collective-permute-done.8.refs_1_ = bf16[64,512]{1,0:T(8,128)(2,1)S(1)} collective-permute-done((bf16[64,512]{1,0:T(8,128)(2,1)S(1)}, bf16[64,512]{1,0:T(8,128)(2,1)S(1)}, u32[]{:S(2)}, u32[]{:S(2)}) %collective-permute-start.8) | collective-permute-done | bytes 65568 | tf_op jit(solution)/shard_map/ppermute | solution.py:31
  19.7 1.7 %collective-permute-done.9.refs_2_ = bf16[64,512]{1,0:T(8,128)(2,1)S(1)} collective-permute-done((bf16[64,512]{1,0:T(8,128)(2,1)S(1)}, bf16[64,512]{1,0:T(8,128)(2,1)S(1)}, u32[]{:S(2)}, u32[]{:S(2)}) %collective-permute-start.9) | collective-permute-done | bytes 65568 | tf_op jit(solution)/shard_map/ppermute | solution.py:31
  21.4 2.4 %collective-permute-done.10.refs_3_ = bf16[64,512]{1,0:T(8,128)(2,1)S(1)} collective-permute-done((bf16[64,512]{1,0:T(8,128)(2,1)S(1)}, bf16[64,512]{1,0:T(8,128)(2,1)S(1)}, u32[]{:S(2)}, u32[]{:S(2)}) %collective-permute-start.10) | collective-permute-done | bytes 65568 | tf_op jit(solution)/shard_map/ppermute | solution.py:31
  23.8 0.6 mix.1.refs_0_
  24.5 3.7 %collective-permute-start.13 = (bf16[64,512]{1,0:T(8,128)(2,1)S(1)}, bf16[64,512]{1,0:T(8,128)(2,1)S(1)}, u32[]{:S(2)}, u32[]{:S(2)}) collective-permute-start(bf16[64,512]{1,0:T(8,128)(2,1)S(1)} %mix.1.refs_0_), channel_id=1, source_target_pairs={{0,3},{1,2},{2,1},{3,0},{4,7},{5,6},{6,5},{7,4},{8,11},{9,10},{10,... | collective-permute-start | bytes 196616 | tf_op jit(solution)/shard_map/ppermute | solution.py:31
  28.1 0.0 collective-permute-start.12
  28.1 0.8 %collective-permute-start.11 = (bf16[64,512]{1,0:T(8,128)(2,1)S(1)}, bf16[64,512]{1,0:T(8,128)(2,1)S(1)}, u32[]{:S(2)}, u32[]{:S(2)}) collective-permute-start(bf16[64,512]{1,0:T(8,128)(2,1)S(1)} %mix.1.refs_0_), channel_id=1, source_target_pairs={{0,1},{1,0},{2,3},{3,2},{4,5},{5,4},{6,7},{7,6},{8,9},{9,8},{10,11... | collective-permute-start | bytes 196616 | tf_op jit(solution)/shard_map/ppermute | solution.py:31
  28.9 1.7 %collective-permute-done.13.refs_3_ = bf16[64,512]{1,0:T(8,128)(2,1)S(1)} collective-permute-done((bf16[64,512]{1,0:T(8,128)(2,1)S(1)}, bf16[64,512]{1,0:T(8,128)(2,1)S(1)}, u32[]{:S(2)}, u32[]{:S(2)}) %collective-permute-start.13) | collective-permute-done | bytes 65568 | tf_op jit(solution)/shard_map/ppermute | solution.py:31
  30.6 2.7 %collective-permute-done.12.refs_2_ = bf16[64,512]{1,0:T(8,128)(2,1)S(1)} collective-permute-done((bf16[64,512]{1,0:T(8,128)(2,1)S(1)}, bf16[64,512]{1,0:T(8,128)(2,1)S(1)}, u32[]{:S(2)}, u32[]{:S(2)}) %collective-permute-start.12) | collective-permute-done | bytes 65568 | tf_op jit(solution)/shard_map/ppermute | solution.py:31
  33.3 0.0 collective-permute-done.11.refs_1_
  33.3 0.6 stack.13.refs_0_
  33.9 0.6 collective-permute-start.16
  34.5 1.5 %collective-permute-start.15 = (bf16[160,512]{1,0:T(8,128)(2,1)S(1)}, bf16[160,512]{1,0:T(8,128)(2,1)S(1)}, u32[]{:S(2)}, u32[]{:S(2)}) collective-permute-start(bf16[160,512]{1,0:T(8,128)(2,1)S(1)} %stack.13.refs_0_), channel_id=1, source_target_pairs={{0,16},{4,20},{8,24},{12,28},{16,0},{20,4},{24,8},{28,12},{1,17},{... | collective-permute-start | bytes 491528 | tf_op jit(solution)/shard_map/ppermute | solution.py:31
  35.9 1.5 %collective-permute-start.14 = (bf16[160,512]{1,0:T(8,128)(2,1)S(1)}, bf16[160,512]{1,0:T(8,128)(2,1)S(1)}, u32[]{:S(2)}, u32[]{:S(2)}) collective-permute-start(bf16[160,512]{1,0:T(8,128)(2,1)S(1)} %stack.13.refs_0_), channel_id=1, source_target_pairs={{0,8},{4,12},{8,0},{12,4},{16,24},{20,28},{24,16},{28,20},{1,9},{5... | collective-permute-start | bytes 491528 | tf_op jit(solution)/shard_map/ppermute | solution.py:31
  37.4 0.0 collective-permute-start.17
  37.4 3.9 %collective-permute-done.16.refs_3_ = bf16[160,512]{1,0:T(8,128)(2,1)S(1)} collective-permute-done((bf16[160,512]{1,0:T(8,128)(2,1)S(1)}, bf16[160,512]{1,0:T(8,128)(2,1)S(1)}, u32[]{:S(2)}, u32[]{:S(2)}) %collective-permute-start.16) | collective-permute-done | bytes 163872 | tf_op jit(solution)/shard_map/ppermute | solution.py:31
  41.3 0.0 collective-permute-start.20
  41.4 1.1 %collective-permute-done.15.refs_2_ = bf16[160,512]{1,0:T(8,128)(2,1)S(1)} collective-permute-done((bf16[160,512]{1,0:T(8,128)(2,1)S(1)}, bf16[160,512]{1,0:T(8,128)(2,1)S(1)}, u32[]{:S(2)}, u32[]{:S(2)}) %collective-permute-start.15) | collective-permute-done | bytes 163872 | tf_op jit(solution)/shard_map/ppermute | solution.py:31
  42.5 0.0 collective-permute-start.19
  42.5 0.0 collective-permute-done.14.refs_1_
  42.5 0.5 collective-permute-start.18
  43.0 1.0 %gram.1.gram_ref = f32[512,512]{1,0:T(8,128)S(1)} custom-call(s32[2]{0:T(128)S(1)} %pad_add_fusion.index_ref, bf16[160,512]{1,0:T(8,128)(2,1)S(1)} %stack.13.refs_0_, bf16[160,512]{1,0:T(8,128)(2,1)S(1)} %collective-permute-done.14.refs_1_, bf16[160,512]{1,0:T(8,128)(2,1)S(1)} %collective-permute-done.15.refs_2_, ...), custom_call_target="tpu_custom_call" | custom-call | tf_op jit(solution)/shard_map/gram/pallas_call | solution.py:489
  44.0 0.0 collective-permute-done.17.refs_4_
  44.0 0.0 collective-permute-done.20.refs_7_
  44.1 0.0 collective-permute-done.19.refs_6_
  44.1 0.0 collective-permute-done.18.refs_5_
  44.1 0.0 copy-done.1
  44.1 0.0 copy-done.3
  44.1 17.6 %solve.1 = (f32[512,512]{1,0:T(8,128)}, f32[4,128]{1,0:T(4,128)}, f32[16,128]{1,0:T(8,128)}) custom-call(s32[2]{0:T(128)S(1)} %pad_add_fusion.index_ref, f32[512,512]{1,0:T(8,128)S(1)} %gram.1.gram_ref, f32[4,128]{1,0:T(4,128)S(1)} %bitcast.11, bf16[2048,128]{1,0:T(8,128)(2,1)S(1)} %copy-done.1, s32[16,128]{1,0:T(8,128)S(1)} %add_bitcast_fusion.marks_ref, ...), custom_call_target="tpu_custom_call" | custom-call | tf_op jit(solution)/shard_map/solve/pallas_call | solution.py:570
Async XLA Ops:
  0.6 8.2 %collective-permute-start.5 = (s32[1,32]{1,0:T(1,128)}, s32[1,32]{1,0:T(1,128)S(1)}, u32[]{:S(2)}, u32[]{:S(2)}) collective-permute-start(s32[1,32]{1,0:T(1,128)} %bitcast.12), channel_id=1, source_target_pairs={{0,24},{4,28},{8,16},{12,20},{16,8},{20,12},{24,0},{28,4},{1,25},{... | collective-permute-start | bytes 392 | tf_op jit(solution)/shard_map/ppermute | solution.py:31
  4.6 4.8 %collective-permute-start.3 = (s32[1,32]{1,0:T(1,128)}, s32[1,32]{1,0:T(1,128)S(1)}, u32[]{:S(2)}, u32[]{:S(2)}) collective-permute-start(s32[1,32]{1,0:T(1,128)} %bitcast.13), channel_id=1, source_target_pairs={{0,16},{4,20},{8,24},{12,28},{16,0},{20,4},{24,8},{28,12},{1,17},{... | collective-permute-start | bytes 392 | tf_op jit(solution)/shard_map/ppermute | solution.py:31
  5.1 4.4 %collective-permute-start.1 = (s32[1,32]{1,0:T(1,128)}, s32[1,32]{1,0:T(1,128)S(1)}, u32[]{:S(2)}, u32[]{:S(2)}) collective-permute-start(s32[1,32]{1,0:T(1,128)} %bitcast.14), channel_id=1, source_target_pairs={{0,8},{4,12},{8,0},{12,4},{16,24},{20,28},{24,16},{28,20},{1,9},{5... | collective-permute-start | bytes 392 | tf_op jit(solution)/shard_map/ppermute | solution.py:31
  5.2 4.7 %collective-permute-start = (s32[1,32]{1,0:T(1,128)}, s32[1,32]{1,0:T(1,128)S(1)}, u32[]{:S(2)}, u32[]{:S(2)}) collective-permute-start(s32[1,32]{1,0:T(1,128)} %bitcast.15), channel_id=1, source_target_pairs={{0,4},{4,0},{8,12},{12,8},{16,20},{20,16},{24,28},{28,24},{1,5},{5... | collective-permute-start | bytes 392 | tf_op jit(solution)/shard_map/ppermute | solution.py:31
  6.0 1.0 %copy-start = (bf16[2048,128]{1,0:T(8,128)(2,1)S(1)}, bf16[2048,128]{1,0:T(8,128)(2,1)}, u32[]{:S(2)}) copy-start(bf16[2048,128]{1,0:T(8,128)(2,1)} %cov_ref.3) | copy-start | bytes 1572868
  7.1 0.7 %copy-start.2 = (f32[2048]{0:T(1024)S(1)}, f32[2048]{0:T(1024)}, u32[]{:S(2)}) copy-start(f32[2048]{0:T(1024)} %param.11) | copy-start | bytes 24580
  8.8 1.4 %collective-permute-start.6 = (s32[1,32]{1,0:T(1,128)S(1)}, s32[1,32]{1,0:T(1,128)S(1)}, u32[]{:S(2)}, u32[]{:S(2)}) collective-permute-start(s32[1,32]{1,0:T(1,128)S(1)} %collective-permute-done.5.refs_6_), channel_id=1, source_target_pairs={{0,4},{4,0},{8,12},{12,8},{16,20},{20,16},{24,28},{28,24},{1,5},{5... | collective-permute-start | bytes 392 | tf_op jit(solution)/shard_map/ppermute | solution.py:31
  9.4 1.1 %collective-permute-start.4 = (s32[1,32]{1,0:T(1,128)S(1)}, s32[1,32]{1,0:T(1,128)S(1)}, u32[]{:S(2)}, u32[]{:S(2)}) collective-permute-start(s32[1,32]{1,0:T(1,128)S(1)} %collective-permute-done.3.refs_4_), channel_id=1, source_target_pairs={{0,4},{4,0},{8,12},{12,8},{16,20},{20,16},{24,28},{28,24},{1,5},{5... | collective-permute-start | bytes 392 | tf_op jit(solution)/shard_map/ppermute | solution.py:31
  9.5 1.2 %collective-permute-start.2 = (s32[1,32]{1,0:T(1,128)S(1)}, s32[1,32]{1,0:T(1,128)S(1)}, u32[]{:S(2)}, u32[]{:S(2)}) collective-permute-start(s32[1,32]{1,0:T(1,128)S(1)} %collective-permute-done.1.refs_2_), channel_id=1, source_target_pairs={{0,4},{4,0},{8,12},{12,8},{16,20},{20,16},{24,28},{28,24},{1,5},{5... | collective-permute-start | bytes 392 | tf_op jit(solution)/shard_map/ppermute | solution.py:31
  10.7 0.7 %copy-start.4 = (s32[32]{0:T(128)S(1)}, s32[32]{0:T(128)}, u32[]{:S(2)}) copy-start(s32[32]{0:T(128)} %param.9) | copy-start | bytes 388
  11.4 32.7 %copy-start.1 = (bf16[2048,128]{1,0:T(8,128)(2,1)S(1)}, bf16[2048,128]{1,0:T(8,128)(2,1)}, u32[]{:S(2)}) copy-start(bf16[2048,128]{1,0:T(8,128)(2,1)} %cov_ref.3) | copy-start | bytes 1572868
  11.4 32.7 %copy-start.3 = (f32[512]{0:T(512)S(1)}, f32[512]{0:T(512)}, u32[]{:S(2)}) copy-start(f32[512]{0:T(512)} %param.10) | copy-start | bytes 6148
  13.0 1.6 %collective-permute-start.7 = (bf16[256,512]{1,0:T(8,128)(2,1)S(1)}, bf16[256,512]{1,0:T(8,128)(2,1)S(1)}, u32[]{:S(2)}, u32[]{:S(2)}) collective-permute-start(bf16[256,512]{1,0:T(8,128)(2,1)S(1)} %get-tuple-element.17), channel_id=1, source_target_pairs={{0,4},{4,0},{8,12},{12,8},{16,20},{20,16},{24,28},{28,24},{1,5},{5... | collective-permute-start | bytes 786440 | tf_op jit(solution)/shard_map/ppermute | solution.py:31
  15.2 4.5 %collective-permute-start.8 = (bf16[64,512]{1,0:T(8,128)(2,1)S(1)}, bf16[64,512]{1,0:T(8,128)(2,1)S(1)}, u32[]{:S(2)}, u32[]{:S(2)}) collective-permute-start(bf16[64,512]{1,0:T(8,128)(2,1)S(1)} %get-tuple-element.19), channel_id=1, source_target_pairs={{0,8},{4,12},{8,0},{12,4},{16,24},{20,28},{24,16},{28,20},{1,9},{5... | collective-permute-start | bytes 196616 | tf_op jit(solution)/shard_map/ppermute | solution.py:31
  17.2 4.3 %collective-permute-start.9 = (bf16[64,512]{1,0:T(8,128)(2,1)S(1)}, bf16[64,512]{1,0:T(8,128)(2,1)S(1)}, u32[]{:S(2)}, u32[]{:S(2)}) collective-permute-start(bf16[64,512]{1,0:T(8,128)(2,1)S(1)} %get-tuple-element.20), channel_id=1, source_target_pairs={{0,16},{4,20},{8,24},{12,28},{16,0},{20,4},{24,8},{28,12},{1,17},{... | collective-permute-start | bytes 196616 | tf_op jit(solution)/shard_map/ppermute | solution.py:31
  18.7 5.2 %collective-permute-start.10 = (bf16[64,512]{1,0:T(8,128)(2,1)S(1)}, bf16[64,512]{1,0:T(8,128)(2,1)S(1)}, u32[]{:S(2)}, u32[]{:S(2)}) collective-permute-start(bf16[64,512]{1,0:T(8,128)(2,1)S(1)} %get-tuple-element.21), channel_id=1, source_target_pairs={{0,24},{4,28},{8,16},{12,20},{16,8},{20,12},{24,0},{28,4},{1,25},{... | collective-permute-start | bytes 196616 | tf_op jit(solution)/shard_map/ppermute | solution.py:31
  24.5 6.1 %collective-permute-start.13 = (bf16[64,512]{1,0:T(8,128)(2,1)S(1)}, bf16[64,512]{1,0:T(8,128)(2,1)S(1)}, u32[]{:S(2)}, u32[]{:S(2)}) collective-permute-start(bf16[64,512]{1,0:T(8,128)(2,1)S(1)} %mix.1.refs_0_), channel_id=1, source_target_pairs={{0,3},{1,2},{2,1},{3,0},{4,7},{5,6},{6,5},{7,4},{8,11},{9,10},{10,... | collective-permute-start | bytes 196616 | tf_op jit(solution)/shard_map/ppermute | solution.py:31
  28.1 5.2 %collective-permute-start.12 = (bf16[64,512]{1,0:T(8,128)(2,1)S(1)}, bf16[64,512]{1,0:T(8,128)(2,1)S(1)}, u32[]{:S(2)}, u32[]{:S(2)}) collective-permute-start(bf16[64,512]{1,0:T(8,128)(2,1)S(1)} %mix.1.refs_0_), channel_id=1, source_target_pairs={{0,2},{1,3},{2,0},{3,1},{4,6},{5,7},{6,4},{7,5},{8,10},{9,11},{10,... | collective-permute-start | bytes 196616 | tf_op jit(solution)/shard_map/ppermute | solution.py:31
  28.1 5.2 %collective-permute-start.11 = (bf16[64,512]{1,0:T(8,128)(2,1)S(1)}, bf16[64,512]{1,0:T(8,128)(2,1)S(1)}, u32[]{:S(2)}, u32[]{:S(2)}) collective-permute-start(bf16[64,512]{1,0:T(8,128)(2,1)S(1)} %mix.1.refs_0_), channel_id=1, source_target_pairs={{0,1},{1,0},{2,3},{3,2},{4,5},{5,4},{6,7},{7,6},{8,9},{9,8},{10,11... | collective-permute-start | bytes 196616 | tf_op jit(solution)/shard_map/ppermute | solution.py:31
  33.9 7.5 %collective-permute-start.16 = (bf16[160,512]{1,0:T(8,128)(2,1)S(1)}, bf16[160,512]{1,0:T(8,128)(2,1)S(1)}, u32[]{:S(2)}, u32[]{:S(2)}) collective-permute-start(bf16[160,512]{1,0:T(8,128)(2,1)S(1)} %stack.13.refs_0_), channel_id=1, source_target_pairs={{0,24},{4,28},{8,16},{12,20},{16,8},{20,12},{24,0},{28,4},{1,25},{... | collective-permute-start | bytes 491528 | tf_op jit(solution)/shard_map/ppermute | solution.py:31
  34.5 8.0 %collective-permute-start.15 = (bf16[160,512]{1,0:T(8,128)(2,1)S(1)}, bf16[160,512]{1,0:T(8,128)(2,1)S(1)}, u32[]{:S(2)}, u32[]{:S(2)}) collective-permute-start(bf16[160,512]{1,0:T(8,128)(2,1)S(1)} %stack.13.refs_0_), channel_id=1, source_target_pairs={{0,16},{4,20},{8,24},{12,28},{16,0},{20,4},{24,8},{28,12},{1,17},{... | collective-permute-start | bytes 491528 | tf_op jit(solution)/shard_map/ppermute | solution.py:31
  35.9 6.5 %collective-permute-start.14 = (bf16[160,512]{1,0:T(8,128)(2,1)S(1)}, bf16[160,512]{1,0:T(8,128)(2,1)S(1)}, u32[]{:S(2)}, u32[]{:S(2)}) collective-permute-start(bf16[160,512]{1,0:T(8,128)(2,1)S(1)} %stack.13.refs_0_), channel_id=1, source_target_pairs={{0,8},{4,12},{8,0},{12,4},{16,24},{20,28},{24,16},{28,20},{1,9},{5... | collective-permute-start | bytes 491528 | tf_op jit(solution)/shard_map/ppermute | solution.py:31
  37.4 6.6 %collective-permute-start.17 = (bf16[160,512]{1,0:T(8,128)(2,1)S(1)}, bf16[160,512]{1,0:T(8,128)(2,1)S(1)}, u32[]{:S(2)}, u32[]{:S(2)}) collective-permute-start(bf16[160,512]{1,0:T(8,128)(2,1)S(1)} %stack.13.refs_0_), channel_id=1, source_target_pairs={{0,4},{4,0},{8,12},{12,8},{16,20},{20,16},{24,28},{28,24},{1,5},{5... | collective-permute-start | bytes 491528 | tf_op jit(solution)/shard_map/ppermute | solution.py:31
  41.3 2.7 %collective-permute-start.20 = (bf16[160,512]{1,0:T(8,128)(2,1)S(1)}, bf16[160,512]{1,0:T(8,128)(2,1)S(1)}, u32[]{:S(2)}, u32[]{:S(2)}) collective-permute-start(bf16[160,512]{1,0:T(8,128)(2,1)S(1)} %collective-permute-done.16.refs_3_), channel_id=1, source_target_pairs={{0,4},{4,0},{8,12},{12,8},{16,20},{20,16},{24,28},{28,24},{1,5},{5... | collective-permute-start | bytes 491528 | tf_op jit(solution)/shard_map/ppermute | solution.py:31
  42.5 1.6 %collective-permute-start.19 = (bf16[160,512]{1,0:T(8,128)(2,1)S(1)}, bf16[160,512]{1,0:T(8,128)(2,1)S(1)}, u32[]{:S(2)}, u32[]{:S(2)}) collective-permute-start(bf16[160,512]{1,0:T(8,128)(2,1)S(1)} %collective-permute-done.15.refs_2_), channel_id=1, source_target_pairs={{0,4},{4,0},{8,12},{12,8},{16,20},{20,16},{24,28},{28,24},{1,5},{5... | collective-permute-start | bytes 491528 | tf_op jit(solution)/shard_map/ppermute | solution.py:31
  42.5 1.6 %collective-permute-start.18 = (bf16[160,512]{1,0:T(8,128)(2,1)S(1)}, bf16[160,512]{1,0:T(8,128)(2,1)S(1)}, u32[]{:S(2)}, u32[]{:S(2)}) collective-permute-start(bf16[160,512]{1,0:T(8,128)(2,1)S(1)} %collective-permute-done.14.refs_1_), channel_id=1, source_target_pairs={{0,4},{4,0},{8,12},{12,8},{16,20},{20,16},{24,28},{28,24},{1,5},{5... | collective-permute-start | bytes 491528 | tf_op jit(solution)/shard_map/ppermute | solution.py:31

commit v15 on v14

--- a/solution.py
+++ b/solution.py
@@ -229,6 +229,11 @@
             for m in range(k + 1, SUB):
                 kept[k + 1] = jnp.where(marks[m], others[m], kept[k + 1])
             roots[k], roots[k + 1] = lax.rsqrt(low), lax.rsqrt(last)
+
+        ahead = []
+        if tile + 1 < len(tiles):
+            ahead = [spread(tiles[tile + 1][:, first + k : first + k + 1]) for k in range(SUB)]
+            fresh = jnp.where(window, 0.0, tiles[tile + 1])
 
         for k in range(0, SUB, 4):
             low, cross, high = pivot[k][k], pivot[k][k + 1], pivot[k + 1][k + 1]
@@ -252,17 +257,29 @@
                 for n in range(m, SUB):
                     drop2 = grown[c, m] * near[c, n] + grown[d, m] * far[c, n]
                     pivot[m][n] = pivot[m][n] - over * (drop[m, n] + over2 * drop2)
+
+            def past(lines):
+                pair = [area * lines[m] - (near[k, m] * lines[k] + far[k, m] * lines[k + 1]) for m in (c, d)]
+                for m in range(k + 4, SUB):
+                    inner = near[c, m] * pair[0] + far[c, m] * pair[1]
+                    lines[m] = lines[m] - over * (near[k, m] * lines[k] + far[k, m] * lines[k + 1] + over2 * inner)
+                return pair
+
+            wide = past(rows)
+            first_pair = [high * rows[k] - cross * rows[k + 1], low * rows[k + 1] - cross * rows[k]]
+            second_pair = [high2 * wide[0] - cross2 * wide[1], low2 * wide[1] - cross2 * wide[0]]
+            if ahead:
+                tall = past(ahead)
+                inner = tall[0] * second_pair[0] + tall[1] * second_pair[1]
+                outer = ahead[k] * first_pair[0] + ahead[k + 1] * first_pair[1]
+                fresh = fresh - over * (outer + over2 * inner)
+            steps[k], steps[k + 1] = [over * value for value in first_pair]
+            steps[c], steps[d] = [over2 * value for value in second_pair]
+            rows[c], rows[d] = [over * value for value in wide]
             for m in range(k + 2, SUB):
                 near[k, m], far[k, m] = over * near[k, m], over * far[k, m]
-                rows[m] = rows[m] - (near[k, m] * rows[k] + far[k, m] * rows[k + 1])
             for m in range(k + 4, SUB):
                 near[c, m], far[c, m] = over2 * near[c, m], over2 * far[c, m]
-                rows[m] = rows[m] - (near[c, m] * rows[c] + far[c, m] * rows[d])
-            steps[k] = over * (high * rows[k] - cross * rows[k + 1])
-            steps[k + 1] = over * (low * rows[k + 1] - cross * rows[k])
-            both = area * over2
-            steps[c] = both * (high2 * rows[c] - cross2 * rows[d])
-            steps[d] = both * (low2 * rows[d] - cross2 * rows[c])
 
             inner = reciprocal(low)
             ratio = cross * inner
@@ -276,14 +293,6 @@
             others = {m: over * (grown[d, m] - ratio * grown[c, m]) for m in range(c + 2, SUB)}
             others[d] = over * (area2 * inner)
             keep(c, values[c], ratio, values, others)
-        if tile + 1 < len(tiles):
-            after = tiles[tile + 1]
-            ahead = [spread(after[:, first + k : first + k + 1]) for k in range(SUB)]
-            fresh = jnp.where(window, 0.0, after)
-            for k in range(0, SUB, 2):
-                for m in range(k + 2, SUB):
-                    ahead[m] = ahead[m] - (near[k, m] * ahead[k] + far[k, m] * ahead[k + 1])
-                fresh = fresh - (ahead[k] * steps[k] + ahead[k + 1] * steps[k + 1])
         for k in reversed(range(0, SUB, 2)):
             for m in reversed(range(k + 2, SUB)):
                 steps[k] = steps[k] - near[k, m] * steps[m]

time: 62.3 us -> 62.7 us (level)
  no operation moved by 1% of the time
where the time goes in v15:
time: 62.7 us; the launch traced here: 62.3 us
  Pallas kernels  23.5 us (37%)
  starting transfers between devices  18.1 us (29%)
  waiting for transfers between devices  16.6 us (26%)
  local copies, waits for them, and re-layouts  2.4 us (4%)
  between operations  0.88 us (1%)
  other arithmetic  0.79 us (1%)
    ppermute x21, starting transfers between devices, partner(): return lax.ppermute(value, axis, pairs)  18.1 us
    pallas_call x1, Pallas kernels, body(): pl.pallas_call(functools.partial(solve_kernel, math.sqrt(LEVELS / SKETCH)...  18.1 us
    ppermute x21, waiting for transfers between devices, partner(): return lax.ppermute(value, axis, pairs)  16.6 us
    pallas_call x6, Pallas kernels, call(): pl.pallas_call(kernel, out_shape=[jax.ShapeDtypeStruct(shape, dtype) for...  5.46 us
    unnamed x10, local copies, waits for them, and re-layouts  2.4 us
  transfers between devices with their start and end apart: 21, of which 11 were waited for; matrix products, arithmetic and copies ran while one was open for 1% of the time, Pallas kernels for 3%

profile of v15, /device:TPU:0, one launch (start us, length us, event | category | flops | bytes accessed | tf_op | source)
XLA Modules:
  0.0 62.3 jit_solution(13963807188684951964)
XLA Ops:
  0.6 4.0 %collective-permute-start.5 = (s32[1,32]{1,0:T(1,128)}, s32[1,32]{1,0:T(1,128)S(1)}, u32[]{:S(2)}, u32[]{:S(2)}) collective-permute-start(s32[1,32]{1,0:T(1,128)} %bitcast.12), channel_id=1, source_target_pairs={{0,24},{4,28},{8,16},{12,20},{16,8},{20,12},{24,0},{28,4},{1,25},{... | collective-permute-start | bytes 392 | tf_op jit(solution)/shard_map/ppermute | solution.py:31
  4.6 0.5 collective-permute-start.3
  5.1 0.1 collective-permute-start.1
  5.2 0.0 collective-permute-start
  5.2 0.1 pad_add_fusion.index_ref
  5.3 0.7 %add_bitcast_fusion.marks_ref = s32[16,128]{1,0:T(8,128)S(1)} fusion(s32[2048]{0:T(1024)} %param.7, s32[2048]{0:T(1024)} %param.8), kind=kLoop, calls=%fused_computation | loop fusion | flops 4096 | bytes 24576 | tf_op jit(solution)/shard_map/reshape | solution.py:516
  6.0 0.0 copy-start
  6.0 1.0 %copy-done = bf16[2048,128]{1,0:T(8,128)(2,1)S(1)} copy-done((bf16[2048,128]{1,0:T(8,128)(2,1)S(1)}, bf16[2048,128]{1,0:T(8,128)(2,1)}, u32[]{:S(2)}) %copy-start) | copy-done | bytes 524312
  7.1 0.0 copy-start.2
  7.1 0.7 %copy-done.2 = f32[2048]{0:T(1024)S(1)} copy-done((f32[2048]{0:T(1024)S(1)}, f32[2048]{0:T(1024)}, u32[]{:S(2)}) %copy-start.2) | copy-done | bytes 8216
  7.8 1.0 %design.1 = (bf16[560,2048]{1,0:T(8,128)(2,1)S(1)}, f32[264,128]{1,0:T(8,128)S(1)}) custom-call(bf16[2048,128]{1,0:T(8,128)(2,1)S(1)} %copy-done, s32[16,128]{1,0:T(8,128)S(1)} %add_bitcast_fusion.marks_ref, f32[16,128]{1,0:T(8,128)S(1)} %bitcast.9), custom_call_target="tpu_custom_call" | custom-call | tf_op jit(solution)/shard_map/design/pallas_call | solution.py:498
  8.8 0.0 collective-permute-done.5.refs_6_
  8.8 0.6 collective-permute-start.6
  9.4 0.0 collective-permute-done.3.refs_4_
  9.4 0.1 collective-permute-start.4
  9.5 0.0 collective-permute-done.1.refs_2_
  9.5 0.4 collective-permute-start.2
  9.9 0.0 collective-permute-done.refs_1_
  9.9 0.3 collective-permute-done.6.refs_7_
  10.2 0.3 collective-permute-done.4.refs_5_
  10.5 0.2 collective-permute-done.2.refs_3_
  10.7 0.0 copy-start.4
  10.7 0.7 %copy-done.4 = s32[32]{0:T(128)S(1)} copy-done((s32[32]{0:T(128)S(1)}, s32[32]{0:T(128)}, u32[]{:S(2)}) %copy-start.4) | copy-done | bytes 152
  11.4 0.0 copy-start.1
  11.4 0.0 copy-start.3
  11.4 1.6 %local.1 = (bf16[256,512]{1,0:T(8,128)(2,1)S(1)}, bf16[256,512]{1,0:T(8,128)(2,1)S(1)}) custom-call(s32[2]{0:T(128)S(1)} %pad_add_fusion.index_ref, bf16[560,2048]{1,0:T(8,128)(2,1)S(1)} %get-tuple-element.14.design_ref, f32[264,128]{1,0:T(8,128)S(1)} %get-tuple-element.15.packed_ref, s32[16,128]{1,0:T(8,128)S(1)} %add_bitcast_fusion.marks_ref, ...), custom_call_target="tpu_custom_call" | custom-call | tf_op jit(solution)/shard_map/local/pallas_call | solution.py:498
  13.0 0.4 collective-permute-start.7
  13.3 1.2 %collective-permute-done.7.came_ref = bf16[256,512]{1,0:T(8,128)(2,1)S(1)} collective-permute-done((bf16[256,512]{1,0:T(8,128)(2,1)S(1)}, bf16[256,512]{1,0:T(8,128)(2,1)S(1)}, u32[]{:S(2)}, u32[]{:S(2)}) %collective-permute-start.7) | collective-permute-done | bytes 262176 | tf_op jit(solution)/shard_map/ppermute | solution.py:31
  14.6 0.7 %pair.1 = (bf16[64,512]{1,0:T(8,128)(2,1)S(1)}, bf16[64,512]{1,0:T(8,128)(2,1)S(1)}, bf16[64,512]{1,0:T(8,128)(2,1)S(1)}, bf16[64,512]{1,0:T(8,128)(2,1)S(1)}) custom-call(s32[2]{0:T(128)S(1)} %pad_add_fusion.index_ref, bf16[256,512]{1,0:T(8,128)(2,1)S(1)} %get-tuple-element.16.stay_ref, bf16[256,512]{1,0:T(8,128)(2,1)S(1)} %collective-permute-done.7.came_ref), custom_call_target="tpu_custom_call" | custom-call | tf_op jit(solution)/shard_map/pair/pallas_call | solution.py:498
  15.2 1.9 %collective-permute-start.8 = (bf16[64,512]{1,0:T(8,128)(2,1)S(1)}, bf16[64,512]{1,0:T(8,128)(2,1)S(1)}, u32[]{:S(2)}, u32[]{:S(2)}) collective-permute-start(bf16[64,512]{1,0:T(8,128)(2,1)S(1)} %get-tuple-element.19), channel_id=1, source_target_pairs={{0,8},{4,12},{8,0},{12,4},{16,24},{20,28},{24,16},{28,20},{1,9},{5... | collective-permute-start | bytes 196616 | tf_op jit(solution)/shard_map/ppermute | solution.py:31
  17.2 1.5 %collective-permute-start.9 = (bf16[64,512]{1,0:T(8,128)(2,1)S(1)}, bf16[64,512]{1,0:T(8,128)(2,1)S(1)}, u32[]{:S(2)}, u32[]{:S(2)}) collective-permute-start(bf16[64,512]{1,0:T(8,128)(2,1)S(1)} %get-tuple-element.20), channel_id=1, source_target_pairs={{0,16},{4,20},{8,24},{12,28},{16,0},{20,4},{24,8},{28,12},{1,17},{... | collective-permute-start | bytes 196616 | tf_op jit(solution)/shard_map/ppermute | solution.py:31
  18.7 0.1 collective-permute-start.10
  18.8 0.9 %collective-permute-done.8.refs_1_ = bf16[64,512]{1,0:T(8,128)(2,1)S(1)} collective-permute-done((bf16[64,512]{1,0:T(8,128)(2,1)S(1)}, bf16[64,512]{1,0:T(8,128)(2,1)S(1)}, u32[]{:S(2)}, u32[]{:S(2)}) %collective-permute-start.8) | collective-permute-done | bytes 65568 | tf_op jit(solution)/shard_map/ppermute | solution.py:31
  19.7 1.7 %collective-permute-done.9.refs_2_ = bf16[64,512]{1,0:T(8,128)(2,1)S(1)} collective-permute-done((bf16[64,512]{1,0:T(8,128)(2,1)S(1)}, bf16[64,512]{1,0:T(8,128)(2,1)S(1)}, u32[]{:S(2)}, u32[]{:S(2)}) %collective-permute-start.9) | collective-permute-done | bytes 65568 | tf_op jit(solution)/shard_map/ppermute | solution.py:31
  21.4 2.4 %collective-permute-done.10.refs_3_ = bf16[64,512]{1,0:T(8,128)(2,1)S(1)} collective-permute-done((bf16[64,512]{1,0:T(8,128)(2,1)S(1)}, bf16[64,512]{1,0:T(8,128)(2,1)S(1)}, u32[]{:S(2)}, u32[]{:S(2)}) %collective-permute-start.10) | collective-permute-done | bytes 65568 | tf_op jit(solution)/shard_map/ppermute | solution.py:31
  23.8 0.6 mix.1.refs_0_
  24.5 3.7 %collective-permute-start.13 = (bf16[64,512]{1,0:T(8,128)(2,1)S(1)}, bf16[64,512]{1,0:T(8,128)(2,1)S(1)}, u32[]{:S(2)}, u32[]{:S(2)}) collective-permute-start(bf16[64,512]{1,0:T(8,128)(2,1)S(1)} %mix.1.refs_0_), channel_id=1, source_target_pairs={{0,3},{1,2},{2,1},{3,0},{4,7},{5,6},{6,5},{7,4},{8,11},{9,10},{10,... | collective-permute-start | bytes 196616 | tf_op jit(solution)/shard_map/ppermute | solution.py:31
  28.1 0.0 collective-permute-start.12
  28.1 0.8 %collective-permute-start.11 = (bf16[64,512]{1,0:T(8,128)(2,1)S(1)}, bf16[64,512]{1,0:T(8,128)(2,1)S(1)}, u32[]{:S(2)}, u32[]{:S(2)}) collective-permute-start(bf16[64,512]{1,0:T(8,128)(2,1)S(1)} %mix.1.refs_0_), channel_id=1, source_target_pairs={{0,1},{1,0},{2,3},{3,2},{4,5},{5,4},{6,7},{7,6},{8,9},{9,8},{10,11... | collective-permute-start | bytes 196616 | tf_op jit(solution)/shard_map/ppermute | solution.py:31
  28.9 1.7 %collective-permute-done.13.refs_3_ = bf16[64,512]{1,0:T(8,128)(2,1)S(1)} collective-permute-done((bf16[64,512]{1,0:T(8,128)(2,1)S(1)}, bf16[64,512]{1,0:T(8,128)(2,1)S(1)}, u32[]{:S(2)}, u32[]{:S(2)}) %collective-permute-start.13) | collective-permute-done | bytes 65568 | tf_op jit(solution)/shard_map/ppermute | solution.py:31
  30.6 2.7 %collective-permute-done.12.refs_2_ = bf16[64,512]{1,0:T(8,128)(2,1)S(1)} collective-permute-done((bf16[64,512]{1,0:T(8,128)(2,1)S(1)}, bf16[64,512]{1,0:T(8,128)(2,1)S(1)}, u32[]{:S(2)}, u32[]{:S(2)}) %collective-permute-start.12) | collective-permute-done | bytes 65568 | tf_op jit(solution)/shard_map/ppermute | solution.py:31
  33.3 0.0 collective-permute-done.11.refs_1_
  33.3 0.6 stack.13.refs_0_
  33.9 0.6 collective-permute-start.16
  34.5 1.5 %collective-permute-start.15 = (bf16[160,512]{1,0:T(8,128)(2,1)S(1)}, bf16[160,512]{1,0:T(8,128)(2,1)S(1)}, u32[]{:S(2)}, u32[]{:S(2)}) collective-permute-start(bf16[160,512]{1,0:T(8,128)(2,1)S(1)} %stack.13.refs_0_), channel_id=1, source_target_pairs={{0,16},{4,20},{8,24},{12,28},{16,0},{20,4},{24,8},{28,12},{1,17},{... | collective-permute-start | bytes 491528 | tf_op jit(solution)/shard_map/ppermute | solution.py:31
  35.9 1.5 %collective-permute-start.14 = (bf16[160,512]{1,0:T(8,128)(2,1)S(1)}, bf16[160,512]{1,0:T(8,128)(2,1)S(1)}, u32[]{:S(2)}, u32[]{:S(2)}) collective-permute-start(bf16[160,512]{1,0:T(8,128)(2,1)S(1)} %stack.13.refs_0_), channel_id=1, source_target_pairs={{0,8},{4,12},{8,0},{12,4},{16,24},{20,28},{24,16},{28,20},{1,9},{5... | collective-permute-start | bytes 491528 | tf_op jit(solution)/shard_map/ppermute | solution.py:31
  37.4 0.0 collective-permute-start.17
  37.4 3.9 %collective-permute-done.16.refs_3_ = bf16[160,512]{1,0:T(8,128)(2,1)S(1)} collective-permute-done((bf16[160,512]{1,0:T(8,128)(2,1)S(1)}, bf16[160,512]{1,0:T(8,128)(2,1)S(1)}, u32[]{:S(2)}, u32[]{:S(2)}) %collective-permute-start.16) | collective-permute-done | bytes 163872 | tf_op jit(solution)/shard_map/ppermute | solution.py:31
  41.3 0.0 collective-permute-start.20
  41.4 1.1 %collective-permute-done.15.refs_2_ = bf16[160,512]{1,0:T(8,128)(2,1)S(1)} collective-permute-done((bf16[160,512]{1,0:T(8,128)(2,1)S(1)}, bf16[160,512]{1,0:T(8,128)(2,1)S(1)}, u32[]{:S(2)}, u32[]{:S(2)}) %collective-permute-start.15) | collective-permute-done | bytes 163872 | tf_op jit(solution)/shard_map/ppermute | solution.py:31
  42.5 0.0 collective-permute-start.19
  42.5 0.0 collective-permute-done.14.refs_1_
  42.5 0.5 collective-permute-start.18
  43.0 1.0 %gram.1.gram_ref = f32[512,512]{1,0:T(8,128)S(1)} custom-call(s32[2]{0:T(128)S(1)} %pad_add_fusion.index_ref, bf16[160,512]{1,0:T(8,128)(2,1)S(1)} %stack.13.refs_0_, bf16[160,512]{1,0:T(8,128)(2,1)S(1)} %collective-permute-done.14.refs_1_, bf16[160,512]{1,0:T(8,128)(2,1)S(1)} %collective-permute-done.15.refs_2_, ...), custom_call_target="tpu_custom_call" | custom-call | tf_op jit(solution)/shard_map/gram/pallas_call | solution.py:498
  44.0 0.0 collective-permute-done.17.refs_4_
  44.0 0.0 collective-permute-done.20.refs_7_
  44.1 0.0 collective-permute-done.19.refs_6_
  44.1 0.0 collective-permute-done.18.refs_5_
  44.1 0.0 copy-done.1
  44.1 0.0 copy-done.3
  44.1 18.1 %solve.1 = (f32[512,512]{1,0:T(8,128)}, f32[4,128]{1,0:T(4,128)}, f32[16,128]{1,0:T(8,128)}) custom-call(s32[2]{0:T(128)S(1)} %pad_add_fusion.index_ref, f32[512,512]{1,0:T(8,128)S(1)} %gram.1.gram_ref, f32[4,128]{1,0:T(4,128)S(1)} %bitcast.11, bf16[2048,128]{1,0:T(8,128)(2,1)S(1)} %copy-done.1, s32[16,128]{1,0:T(8,128)S(1)} %add_bitcast_fusion.marks_ref, ...), custom_call_target="tpu_custom_call" | custom-call | tf_op jit(solution)/shard_map/solve/pallas_call | solution.py:579
Async XLA Ops:
  0.6 8.2 %collective-permute-start.5 = (s32[1,32]{1,0:T(1,128)}, s32[1,32]{1,0:T(1,128)S(1)}, u32[]{:S(2)}, u32[]{:S(2)}) collective-permute-start(s32[1,32]{1,0:T(1,128)} %bitcast.12), channel_id=1, source_target_pairs={{0,24},{4,28},{8,16},{12,20},{16,8},{20,12},{24,0},{28,4},{1,25},{... | collective-permute-start | bytes 392 | tf_op jit(solution)/shard_map/ppermute | solution.py:31
  4.6 4.8 %collective-permute-start.3 = (s32[1,32]{1,0:T(1,128)}, s32[1,32]{1,0:T(1,128)S(1)}, u32[]{:S(2)}, u32[]{:S(2)}) collective-permute-start(s32[1,32]{1,0:T(1,128)} %bitcast.13), channel_id=1, source_target_pairs={{0,16},{4,20},{8,24},{12,28},{16,0},{20,4},{24,8},{28,12},{1,17},{... | collective-permute-start | bytes 392 | tf_op jit(solution)/shard_map/ppermute | solution.py:31
  5.1 4.4 %collective-permute-start.1 = (s32[1,32]{1,0:T(1,128)}, s32[1,32]{1,0:T(1,128)S(1)}, u32[]{:S(2)}, u32[]{:S(2)}) collective-permute-start(s32[1,32]{1,0:T(1,128)} %bitcast.14), channel_id=1, source_target_pairs={{0,8},{4,12},{8,0},{12,4},{16,24},{20,28},{24,16},{28,20},{1,9},{5... | collective-permute-start | bytes 392 | tf_op jit(solution)/shard_map/ppermute | solution.py:31
  5.2 4.7 %collective-permute-start = (s32[1,32]{1,0:T(1,128)}, s32[1,32]{1,0:T(1,128)S(1)}, u32[]{:S(2)}, u32[]{:S(2)}) collective-permute-start(s32[1,32]{1,0:T(1,128)} %bitcast.15), channel_id=1, source_target_pairs={{0,4},{4,0},{8,12},{12,8},{16,20},{20,16},{24,28},{28,24},{1,5},{5... | collective-permute-start | bytes 392 | tf_op jit(solution)/shard_map/ppermute | solution.py:31
  6.0 1.0 %copy-start = (bf16[2048,128]{1,0:T(8,128)(2,1)S(1)}, bf16[2048,128]{1,0:T(8,128)(2,1)}, u32[]{:S(2)}) copy-start(bf16[2048,128]{1,0:T(8,128)(2,1)} %cov_ref.3) | copy-start | bytes 1572868
  7.1 0.7 %copy-start.2 = (f32[2048]{0:T(1024)S(1)}, f32[2048]{0:T(1024)}, u32[]{:S(2)}) copy-start(f32[2048]{0:T(1024)} %param.11) | copy-start | bytes 24580
  8.8 1.4 %collective-permute-start.6 = (s32[1,32]{1,0:T(1,128)S(1)}, s32[1,32]{1,0:T(1,128)S(1)}, u32[]{:S(2)}, u32[]{:S(2)}) collective-permute-start(s32[1,32]{1,0:T(1,128)S(1)} %collective-permute-done.5.refs_6_), channel_id=1, source_target_pairs={{0,4},{4,0},{8,12},{12,8},{16,20},{20,16},{24,28},{28,24},{1,5},{5... | collective-permute-start | bytes 392 | tf_op jit(solution)/shard_map/ppermute | solution.py:31
  9.4 1.1 %collective-permute-start.4 = (s32[1,32]{1,0:T(1,128)S(1)}, s32[1,32]{1,0:T(1,128)S(1)}, u32[]{:S(2)}, u32[]{:S(2)}) collective-permute-start(s32[1,32]{1,0:T(1,128)S(1)} %collective-permute-done.3.refs_4_), channel_id=1, source_target_pairs={{0,4},{4,0},{8,12},{12,8},{16,20},{20,16},{24,28},{28,24},{1,5},{5... | collective-permute-start | bytes 392 | tf_op jit(solution)/shard_map/ppermute | solution.py:31
  9.5 1.2 %collective-permute-start.2 = (s32[1,32]{1,0:T(1,128)S(1)}, s32[1,32]{1,0:T(1,128)S(1)}, u32[]{:S(2)}, u32[]{:S(2)}) collective-permute-start(s32[1,32]{1,0:T(1,128)S(1)} %collective-permute-done.1.refs_2_), channel_id=1, source_target_pairs={{0,4},{4,0},{8,12},{12,8},{16,20},{20,16},{24,28},{28,24},{1,5},{5... | collective-permute-start | bytes 392 | tf_op jit(solution)/shard_map/ppermute | solution.py:31
  10.7 0.7 %copy-start.4 = (s32[32]{0:T(128)S(1)}, s32[32]{0:T(128)}, u32[]{:S(2)}) copy-start(s32[32]{0:T(128)} %param.9) | copy-start | bytes 388
  11.4 32.7 %copy-start.1 = (bf16[2048,128]{1,0:T(8,128)(2,1)S(1)}, bf16[2048,128]{1,0:T(8,128)(2,1)}, u32[]{:S(2)}) copy-start(bf16[2048,128]{1,0:T(8,128)(2,1)} %cov_ref.3) | copy-start | bytes 1572868
  11.4 32.7 %copy-start.3 = (f32[512]{0:T(512)S(1)}, f32[512]{0:T(512)}, u32[]{:S(2)}) copy-start(f32[512]{0:T(512)} %param.10) | copy-start | bytes 6148
  13.0 1.6 %collective-permute-start.7 = (bf16[256,512]{1,0:T(8,128)(2,1)S(1)}, bf16[256,512]{1,0:T(8,128)(2,1)S(1)}, u32[]{:S(2)}, u32[]{:S(2)}) collective-permute-start(bf16[256,512]{1,0:T(8,128)(2,1)S(1)} %get-tuple-element.17), channel_id=1, source_target_pairs={{0,4},{4,0},{8,12},{12,8},{16,20},{20,16},{24,28},{28,24},{1,5},{5... | collective-permute-start | bytes 786440 | tf_op jit(solution)/shard_map/ppermute | solution.py:31
  15.2 4.5 %collective-permute-start.8 = (bf16[64,512]{1,0:T(8,128)(2,1)S(1)}, bf16[64,512]{1,0:T(8,128)(2,1)S(1)}, u32[]{:S(2)}, u32[]{:S(2)}) collective-permute-start(bf16[64,512]{1,0:T(8,128)(2,1)S(1)} %get-tuple-element.19), channel_id=1, source_target_pairs={{0,8},{4,12},{8,0},{12,4},{16,24},{20,28},{24,16},{28,20},{1,9},{5... | collective-permute-start | bytes 196616 | tf_op jit(solution)/shard_map/ppermute | solution.py:31
  17.2 4.3 %collective-permute-start.9 = (bf16[64,512]{1,0:T(8,128)(2,1)S(1)}, bf16[64,512]{1,0:T(8,128)(2,1)S(1)}, u32[]{:S(2)}, u32[]{:S(2)}) collective-permute-start(bf16[64,512]{1,0:T(8,128)(2,1)S(1)} %get-tuple-element.20), channel_id=1, source_target_pairs={{0,16},{4,20},{8,24},{12,28},{16,0},{20,4},{24,8},{28,12},{1,17},{... | collective-permute-start | bytes 196616 | tf_op jit(solution)/shard_map/ppermute | solution.py:31
  18.7 5.2 %collective-permute-start.10 = (bf16[64,512]{1,0:T(8,128)(2,1)S(1)}, bf16[64,512]{1,0:T(8,128)(2,1)S(1)}, u32[]{:S(2)}, u32[]{:S(2)}) collective-permute-start(bf16[64,512]{1,0:T(8,128)(2,1)S(1)} %get-tuple-element.21), channel_id=1, source_target_pairs={{0,24},{4,28},{8,16},{12,20},{16,8},{20,12},{24,0},{28,4},{1,25},{... | collective-permute-start | bytes 196616 | tf_op jit(solution)/shard_map/ppermute | solution.py:31
  24.5 6.1 %collective-permute-start.13 = (bf16[64,512]{1,0:T(8,128)(2,1)S(1)}, bf16[64,512]{1,0:T(8,128)(2,1)S(1)}, u32[]{:S(2)}, u32[]{:S(2)}) collective-permute-start(bf16[64,512]{1,0:T(8,128)(2,1)S(1)} %mix.1.refs_0_), channel_id=1, source_target_pairs={{0,3},{1,2},{2,1},{3,0},{4,7},{5,6},{6,5},{7,4},{8,11},{9,10},{10,... | collective-permute-start | bytes 196616 | tf_op jit(solution)/shard_map/ppermute | solution.py:31
  28.1 5.2 %collective-permute-start.12 = (bf16[64,512]{1,0:T(8,128)(2,1)S(1)}, bf16[64,512]{1,0:T(8,128)(2,1)S(1)}, u32[]{:S(2)}, u32[]{:S(2)}) collective-permute-start(bf16[64,512]{1,0:T(8,128)(2,1)S(1)} %mix.1.refs_0_), channel_id=1, source_target_pairs={{0,2},{1,3},{2,0},{3,1},{4,6},{5,7},{6,4},{7,5},{8,10},{9,11},{10,... | collective-permute-start | bytes 196616 | tf_op jit(solution)/shard_map/ppermute | solution.py:31
  28.1 5.2 %collective-permute-start.11 = (bf16[64,512]{1,0:T(8,128)(2,1)S(1)}, bf16[64,512]{1,0:T(8,128)(2,1)S(1)}, u32[]{:S(2)}, u32[]{:S(2)}) collective-permute-start(bf16[64,512]{1,0:T(8,128)(2,1)S(1)} %mix.1.refs_0_), channel_id=1, source_target_pairs={{0,1},{1,0},{2,3},{3,2},{4,5},{5,4},{6,7},{7,6},{8,9},{9,8},{10,11... | collective-permute-start | bytes 196616 | tf_op jit(solution)/shard_map/ppermute | solution.py:31
  33.9 7.5 %collective-permute-start.16 = (bf16[160,512]{1,0:T(8,128)(2,1)S(1)}, bf16[160,512]{1,0:T(8,128)(2,1)S(1)}, u32[]{:S(2)}, u32[]{:S(2)}) collective-permute-start(bf16[160,512]{1,0:T(8,128)(2,1)S(1)} %stack.13.refs_0_), channel_id=1, source_target_pairs={{0,24},{4,28},{8,16},{12,20},{16,8},{20,12},{24,0},{28,4},{1,25},{... | collective-permute-start | bytes 491528 | tf_op jit(solution)/shard_map/ppermute | solution.py:31
  34.5 8.0 %collective-permute-start.15 = (bf16[160,512]{1,0:T(8,128)(2,1)S(1)}, bf16[160,512]{1,0:T(8,128)(2,1)S(1)}, u32[]{:S(2)}, u32[]{:S(2)}) collective-permute-start(bf16[160,512]{1,0:T(8,128)(2,1)S(1)} %stack.13.refs_0_), channel_id=1, source_target_pairs={{0,16},{4,20},{8,24},{12,28},{16,0},{20,4},{24,8},{28,12},{1,17},{... | collective-permute-start | bytes 491528 | tf_op jit(solution)/shard_map/ppermute | solution.py:31
  35.9 6.5 %collective-permute-start.14 = (bf16[160,512]{1,0:T(8,128)(2,1)S(1)}, bf16[160,512]{1,0:T(8,128)(2,1)S(1)}, u32[]{:S(2)}, u32[]{:S(2)}) collective-permute-start(bf16[160,512]{1,0:T(8,128)(2,1)S(1)} %stack.13.refs_0_), channel_id=1, source_target_pairs={{0,8},{4,12},{8,0},{12,4},{16,24},{20,28},{24,16},{28,20},{1,9},{5... | collective-permute-start | bytes 491528 | tf_op jit(solution)/shard_map/ppermute | solution.py:31
  37.4 6.6 %collective-permute-start.17 = (bf16[160,512]{1,0:T(8,128)(2,1)S(1)}, bf16[160,512]{1,0:T(8,128)(2,1)S(1)}, u32[]{:S(2)}, u32[]{:S(2)}) collective-permute-start(bf16[160,512]{1,0:T(8,128)(2,1)S(1)} %stack.13.refs_0_), channel_id=1, source_target_pairs={{0,4},{4,0},{8,12},{12,8},{16,20},{20,16},{24,28},{28,24},{1,5},{5... | collective-permute-start | bytes 491528 | tf_op jit(solution)/shard_map/ppermute | solution.py:31
  41.3 2.7 %collective-permute-start.20 = (bf16[160,512]{1,0:T(8,128)(2,1)S(1)}, bf16[160,512]{1,0:T(8,128)(2,1)S(1)}, u32[]{:S(2)}, u32[]{:S(2)}) collective-permute-start(bf16[160,512]{1,0:T(8,128)(2,1)S(1)} %collective-permute-done.16.refs_3_), channel_id=1, source_target_pairs={{0,4},{4,0},{8,12},{12,8},{16,20},{20,16},{24,28},{28,24},{1,5},{5... | collective-permute-start | bytes 491528 | tf_op jit(solution)/shard_map/ppermute | solution.py:31
  42.5 1.6 %collective-permute-start.19 = (bf16[160,512]{1,0:T(8,128)(2,1)S(1)}, bf16[160,512]{1,0:T(8,128)(2,1)S(1)}, u32[]{:S(2)}, u32[]{:S(2)}) collective-permute-start(bf16[160,512]{1,0:T(8,128)(2,1)S(1)} %collective-permute-done.15.refs_2_), channel_id=1, source_target_pairs={{0,4},{4,0},{8,12},{12,8},{16,20},{20,16},{24,28},{28,24},{1,5},{5... | collective-permute-start | bytes 491528 | tf_op jit(solution)/shard_map/ppermute | solution.py:31
  42.5 1.6 %collective-permute-start.18 = (bf16[160,512]{1,0:T(8,128)(2,1)S(1)}, bf16[160,512]{1,0:T(8,128)(2,1)S(1)}, u32[]{:S(2)}, u32[]{:S(2)}) collective-permute-start(bf16[160,512]{1,0:T(8,128)(2,1)S(1)} %collective-permute-done.14.refs_1_), channel_id=1, source_target_pairs={{0,4},{4,0},{8,12},{12,8},{16,20},{20,16},{24,28},{28,24},{1,5},{5... | collective-permute-start | bytes 491528 | tf_op jit(solution)/shard_map/ppermute | solution.py:31

commit v16 on v15

--- a/solution.py
+++ b/solution.py
@@ -194,10 +194,80 @@
     return pltpu.reciprocal(value, approx=True)
 
 
+def finish(tiles, scales, tile, window, marks, pivot, rows, near, far, quads, aside):
+    first = tile * SUB
+    sub = lax.broadcasted_iota(jnp.int32, (SUB, LANE), 0)
+    kept, roots, steps = [None] * SUB, [None] * SUB, [None] * SUB
+
+    def keep(k, low, ratio, values, others):
+        last = others[k + 1]
+        kept[k] = rows[k]
+        for m in range(k, SUB):
+            kept[k] = jnp.where(marks[m], values[m], kept[k])
+        kept[k + 1] = rows[k + 1] - ratio * rows[k]
+        for m in range(k + 1, SUB):
+            kept[k + 1] = jnp.where(marks[m], others[m], kept[k + 1])
+        roots[k], roots[k + 1] = lax.rsqrt(low), lax.rsqrt(last)
+
+    for k, low, cross, area, low2, cross2, area2, over, over2, grown, first_pair, second_pair, wide in quads:
+        c, d = k + 2, k + 3
+        steps[k], steps[k + 1] = [over * value for value in first_pair]
+        steps[c], steps[d] = [over2 * value for value in second_pair]
+        rows[c], rows[d] = [over * value for value in wide]
+        for m in range(k + 2, SUB):
+            near[k, m], far[k, m] = over * near[k, m], over * far[k, m]
+        for m in range(k + 4, SUB):
+            near[c, m], far[c, m] = over2 * near[c, m], over2 * far[c, m]
+        inner = reciprocal(low)
+        ratio = cross * inner
+        values = {m: pivot[k][m] for m in range(k, SUB)}
+        others = {m: pivot[k + 1][m] - ratio * pivot[k][m] for m in range(k + 2, SUB)}
+        others[k + 1] = area * inner
+        keep(k, low, ratio, values, others)
+        inner = reciprocal(low2)
+        ratio = cross2 * inner
+        values = {m: over * grown[c, m] for m in range(c, SUB)}
+        others = {m: over * (grown[d, m] - ratio * grown[c, m]) for m in range(c + 2, SUB)}
+        others[d] = over * (area2 * inner)
+        keep(c, values[c], ratio, values, others)
+    for k in reversed(range(0, SUB, 2)):
+        for m in reversed(range(k + 2, SUB)):
+            steps[k] = steps[k] - near[k, m] * steps[m]
+            steps[k + 1] = steps[k + 1] - far[k, m] * steps[m]
+    for i in range(tile + 2, min(tile + 3, len(tiles))):
+        change = [spread(tiles[i][:, first + k : first + k + 1]) * steps[k] for k in range(SUB)]
+        tiles[i] = jnp.where(window, 0.0, tiles[i]) - tree_sum(change[::-1])
+    if tile + 3 < len(tiles):
+        stacked = steps[0]
+        for k in range(1, SUB):
+            stacked = jnp.where(sub >= k, steps[k], stacked)
+        blank = jnp.zeros_like(stacked)
+        stacked = jnp.concatenate([stacked, blank] if tile % 2 == 0 else [blank, stacked])
+        none = jnp.zeros((PACK, LANE), bf16)
+        before, after = tile // 2, len(tiles) // 2 - 1 - tile // 2
+        parts = [jnp.concatenate([none] * before + [part] + [none] * after) for part in split(stacked)]
+        change = jnp.dot(
+            parts_of(jnp.concatenate(tiles[tile + 3 :]), LEFT, 1),
+            jnp.concatenate([parts[k] for k in RIGHT]),
+            preferred_element_type=f32,
+        )
+        for i in range(tile + 3, len(tiles)):
+            at = (i - tile - 3) * SUB
+            tiles[i] = jnp.where(window, 0.0, tiles[i]) - change[at : at + SUB]
+    new, scale = kept[0], roots[0]
+    for k in range(1, SUB):
+        new = jnp.where(sub >= k, kept[k], new)
+        scale = jnp.where(sub >= k, roots[k], scale)
+    tiles[tile] = new
+    scales.append(scale)
+    for work in aside:
+        work()
+
+
 def eliminate(tiles, aside, shelf):
     share = -(-len(aside) // len(tiles))
+    behind = None
     lane = lax.broadcasted_iota(jnp.int32, (SUB, LANE), 1)
-    sub = lax.broadcasted_iota(jnp.int32, (SUB, LANE), 0)
     tiles = list(tiles)
     scales = []
     for tile in range(len(tiles)):
@@ -217,18 +287,9 @@
 
         pivot = [[take(m + 1, k) if m >= k else None for m in range(SUB)] for k in range(SUB)]
         rows = [jnp.where(marks[k], 1.0, take(0, k)) for k in range(SUB)]
-        steps, near, far = [None] * SUB, {}, {}
-        kept, roots = [None] * SUB, [None] * SUB
-
-        def keep(k, low, ratio, values, others):
-            last = others[k + 1]
-            kept[k] = rows[k]
-            for m in range(k, SUB):
-                kept[k] = jnp.where(marks[m], values[m], kept[k])
-            kept[k + 1] = rows[k + 1] - ratio * rows[k]
-            for m in range(k + 1, SUB):
-                kept[k + 1] = jnp.where(marks[m], others[m], kept[k + 1])
-            roots[k], roots[k + 1] = lax.rsqrt(low), lax.rsqrt(last)
+        near, far, quads = {}, {}, []
+        if behind:
+            behind()
 
         ahead = []
         if tile + 1 < len(tiles):
@@ -273,60 +334,13 @@
                 inner = tall[0] * second_pair[0] + tall[1] * second_pair[1]
                 outer = ahead[k] * first_pair[0] + ahead[k + 1] * first_pair[1]
                 fresh = fresh - over * (outer + over2 * inner)
-            steps[k], steps[k + 1] = [over * value for value in first_pair]
-            steps[c], steps[d] = [over2 * value for value in second_pair]
-            rows[c], rows[d] = [over * value for value in wide]
-            for m in range(k + 2, SUB):
-                near[k, m], far[k, m] = over * near[k, m], over * far[k, m]
-            for m in range(k + 4, SUB):
-                near[c, m], far[c, m] = over2 * near[c, m], over2 * far[c, m]
-
-            inner = reciprocal(low)
-            ratio = cross * inner
-            values = {m: pivot[k][m] for m in range(k, SUB)}
-            others = {m: pivot[k + 1][m] - ratio * pivot[k][m] for m in range(k + 2, SUB)}
-            others[k + 1] = area * inner
-            keep(k, low, ratio, values, others)
-            inner = reciprocal(low2)
-            ratio = cross2 * inner
-            values = {m: over * grown[c, m] for m in range(c, SUB)}
-            others = {m: over * (grown[d, m] - ratio * grown[c, m]) for m in range(c + 2, SUB)}
-            others[d] = over * (area2 * inner)
-            keep(c, values[c], ratio, values, others)
-        for k in reversed(range(0, SUB, 2)):
-            for m in reversed(range(k + 2, SUB)):
-                steps[k] = steps[k] - near[k, m] * steps[m]
-                steps[k + 1] = steps[k + 1] - far[k, m] * steps[m]
-        for i in range(tile + 2, min(tile + 3, len(tiles))):
-            change = [spread(tiles[i][:, first + k : first + k + 1]) * steps[k] for k in range(SUB)]
-            tiles[i] = jnp.where(window, 0.0, tiles[i]) - tree_sum(change[::-1])
-        if tile + 3 < len(tiles):
-            stacked = steps[0]
-            for k in range(1, SUB):
-                stacked = jnp.where(sub >= k, steps[k], stacked)
-            blank = jnp.zeros_like(stacked)
-            stacked = jnp.concatenate([stacked, blank] if tile % 2 == 0 else [blank, stacked])
-            none = jnp.zeros((PACK, LANE), bf16)
-            before, after = tile // 2, len(tiles) // 2 - 1 - tile // 2
-            parts = [jnp.concatenate([none] * before + [part] + [none] * after) for part in split(stacked)]
-            change = jnp.dot(
-                parts_of(jnp.concatenate(tiles[tile + 3 :]), LEFT, 1),
-                jnp.concatenate([parts[k] for k in RIGHT]),
-                preferred_element_type=f32,
-            )
-            for i in range(tile + 3, len(tiles)):
-                at = (i - tile - 3) * SUB
-                tiles[i] = jnp.where(window, 0.0, tiles[i]) - change[at : at + SUB]
-        if tile + 1 < len(tiles):
+            quads.append((k, low, cross, area, low2, cross2, area2, over, over2, grown, first_pair, second_pair, wide))
+        if ahead:
             tiles[tile + 1] = fresh
-        new, scale = kept[0], roots[0]
-        for k in range(1, SUB):
-            new = jnp.where(sub >= k, kept[k], new)
-            scale = jnp.where(sub >= k, roots[k], scale)
-        tiles[tile] = new
-        scales.append(scale)
-        for work in aside[tile * share : (tile + 1) * share]:
-            work()
+        behind = functools.partial(
+            finish, tiles, scales, tile, window, marks, pivot, rows, near, far, quads, aside[tile * share :][:share]
+        )
+    behind()
     return tiles, scales
 
 

time: 62.7 us -> 62.7 us (level)
  no operation moved by 1% of the time
where the time goes in v16:
time: 62.7 us; the launch traced here: 62.4 us
  Pallas kernels  23.6 us (38%)
  starting transfers between devices  18.1 us (29%)
  waiting for transfers between devices  16.6 us (26%)
  local copies, waits for them, and re-layouts  2.4 us (4%)
  between operations  0.88 us (1%)
  other arithmetic  0.79 us (1%)
    ppermute x21, starting transfers between devices, partner(): return lax.ppermute(value, axis, pairs)  18.1 us
    pallas_call x1, Pallas kernels, body(): pl.pallas_call(functools.partial(solve_kernel, math.sqrt(LEVELS / SKETCH)...  18.1 us
    ppermute x21, waiting for transfers between devices, partner(): return lax.ppermute(value, axis, pairs)  16.6 us
    pallas_call x6, Pallas kernels, call(): pl.pallas_call(kernel, out_shape=[jax.ShapeDtypeStruct(shape, dtype) for...  5.46 us
    unnamed x10, local copies, waits for them, and re-layouts  2.4 us
  transfers between devices with their start and end apart: 21, of which 11 were waited for; matrix products, arithmetic and copies ran while one was open for 1% of the time, Pallas kernels for 3%

profile of v16, /device:TPU:0, one launch (start us, length us, event | category | flops | bytes accessed | tf_op | source)
XLA Modules:
  0.0 62.4 jit_solution(10854119420684930287)
XLA Ops:
  0.6 4.0 %collective-permute-start.5 = (s32[1,32]{1,0:T(1,128)}, s32[1,32]{1,0:T(1,128)S(1)}, u32[]{:S(2)}, u32[]{:S(2)}) collective-permute-start(s32[1,32]{1,0:T(1,128)} %bitcast.12), channel_id=1, source_target_pairs={{0,24},{4,28},{8,16},{12,20},{16,8},{20,12},{24,0},{28,4},{1,25},{... | collective-permute-start | bytes 392 | tf_op jit(solution)/shard_map/ppermute | solution.py:31
  4.6 0.5 collective-permute-start.3
  5.1 0.1 collective-permute-start.1
  5.2 0.0 collective-permute-start
  5.2 0.1 pad_add_fusion.index_ref
  5.3 0.7 %add_bitcast_fusion.marks_ref = s32[16,128]{1,0:T(8,128)S(1)} fusion(s32[2048]{0:T(1024)} %param.7, s32[2048]{0:T(1024)} %param.8), kind=kLoop, calls=%fused_computation | loop fusion | flops 4096 | bytes 24576 | tf_op jit(solution)/shard_map/reshape | solution.py:530
  6.0 0.0 copy-start
  6.0 1.0 %copy-done = bf16[2048,128]{1,0:T(8,128)(2,1)S(1)} copy-done((bf16[2048,128]{1,0:T(8,128)(2,1)S(1)}, bf16[2048,128]{1,0:T(8,128)(2,1)}, u32[]{:S(2)}) %copy-start) | copy-done | bytes 524312
  7.1 0.0 copy-start.2
  7.1 0.7 %copy-done.2 = f32[2048]{0:T(1024)S(1)} copy-done((f32[2048]{0:T(1024)S(1)}, f32[2048]{0:T(1024)}, u32[]{:S(2)}) %copy-start.2) | copy-done | bytes 8216
  7.8 1.0 %design.1 = (bf16[560,2048]{1,0:T(8,128)(2,1)S(1)}, f32[264,128]{1,0:T(8,128)S(1)}) custom-call(bf16[2048,128]{1,0:T(8,128)(2,1)S(1)} %copy-done, s32[16,128]{1,0:T(8,128)S(1)} %add_bitcast_fusion.marks_ref, f32[16,128]{1,0:T(8,128)S(1)} %bitcast.9), custom_call_target="tpu_custom_call" | custom-call | tf_op jit(solution)/shard_map/design/pallas_call | solution.py:512
  8.8 0.0 collective-permute-done.5.refs_6_
  8.8 0.6 collective-permute-start.6
  9.4 0.0 collective-permute-done.3.refs_4_
  9.4 0.1 collective-permute-start.4
  9.5 0.0 collective-permute-done.1.refs_2_
  9.5 0.4 collective-permute-start.2
  9.9 0.0 collective-permute-done.refs_1_
  9.9 0.3 collective-permute-done.6.refs_7_
  10.2 0.3 collective-permute-done.4.refs_5_
  10.5 0.2 collective-permute-done.2.refs_3_
  10.7 0.0 copy-start.4
  10.7 0.7 %copy-done.4 = s32[32]{0:T(128)S(1)} copy-done((s32[32]{0:T(128)S(1)}, s32[32]{0:T(128)}, u32[]{:S(2)}) %copy-start.4) | copy-done | bytes 152
  11.4 0.0 copy-start.1
  11.4 0.0 copy-start.3
  11.4 1.6 %local.1 = (bf16[256,512]{1,0:T(8,128)(2,1)S(1)}, bf16[256,512]{1,0:T(8,128)(2,1)S(1)}) custom-call(s32[2]{0:T(128)S(1)} %pad_add_fusion.index_ref, bf16[560,2048]{1,0:T(8,128)(2,1)S(1)} %get-tuple-element.14.design_ref, f32[264,128]{1,0:T(8,128)S(1)} %get-tuple-element.15.packed_ref, s32[16,128]{1,0:T(8,128)S(1)} %add_bitcast_fusion.marks_ref, ...), custom_call_target="tpu_custom_call" | custom-call | tf_op jit(solution)/shard_map/local/pallas_call | solution.py:512
  13.0 0.4 collective-permute-start.7
  13.3 1.2 %collective-permute-done.7.came_ref = bf16[256,512]{1,0:T(8,128)(2,1)S(1)} collective-permute-done((bf16[256,512]{1,0:T(8,128)(2,1)S(1)}, bf16[256,512]{1,0:T(8,128)(2,1)S(1)}, u32[]{:S(2)}, u32[]{:S(2)}) %collective-permute-start.7) | collective-permute-done | bytes 262176 | tf_op jit(solution)/shard_map/ppermute | solution.py:31
  14.6 0.7 %pair.1 = (bf16[64,512]{1,0:T(8,128)(2,1)S(1)}, bf16[64,512]{1,0:T(8,128)(2,1)S(1)}, bf16[64,512]{1,0:T(8,128)(2,1)S(1)}, bf16[64,512]{1,0:T(8,128)(2,1)S(1)}) custom-call(s32[2]{0:T(128)S(1)} %pad_add_fusion.index_ref, bf16[256,512]{1,0:T(8,128)(2,1)S(1)} %get-tuple-element.16.stay_ref, bf16[256,512]{1,0:T(8,128)(2,1)S(1)} %collective-permute-done.7.came_ref), custom_call_target="tpu_custom_call" | custom-call | tf_op jit(solution)/shard_map/pair/pallas_call | solution.py:512
  15.2 1.9 %collective-permute-start.8 = (bf16[64,512]{1,0:T(8,128)(2,1)S(1)}, bf16[64,512]{1,0:T(8,128)(2,1)S(1)}, u32[]{:S(2)}, u32[]{:S(2)}) collective-permute-start(bf16[64,512]{1,0:T(8,128)(2,1)S(1)} %get-tuple-element.19), channel_id=1, source_target_pairs={{0,8},{4,12},{8,0},{12,4},{16,24},{20,28},{24,16},{28,20},{1,9},{5... | collective-permute-start | bytes 196616 | tf_op jit(solution)/shard_map/ppermute | solution.py:31
  17.2 1.5 %collective-permute-start.9 = (bf16[64,512]{1,0:T(8,128)(2,1)S(1)}, bf16[64,512]{1,0:T(8,128)(2,1)S(1)}, u32[]{:S(2)}, u32[]{:S(2)}) collective-permute-start(bf16[64,512]{1,0:T(8,128)(2,1)S(1)} %get-tuple-element.20), channel_id=1, source_target_pairs={{0,16},{4,20},{8,24},{12,28},{16,0},{20,4},{24,8},{28,12},{1,17},{... | collective-permute-start | bytes 196616 | tf_op jit(solution)/shard_map/ppermute | solution.py:31
  18.7 0.1 collective-permute-start.10
  18.8 0.9 %collective-permute-done.8.refs_1_ = bf16[64,512]{1,0:T(8,128)(2,1)S(1)} collective-permute-done((bf16[64,512]{1,0:T(8,128)(2,1)S(1)}, bf16[64,512]{1,0:T(8,128)(2,1)S(1)}, u32[]{:S(2)}, u32[]{:S(2)}) %collective-permute-start.8) | collective-permute-done | bytes 65568 | tf_op jit(solution)/shard_map/ppermute | solution.py:31
  19.7 1.7 %collective-permute-done.9.refs_2_ = bf16[64,512]{1,0:T(8,128)(2,1)S(1)} collective-permute-done((bf16[64,512]{1,0:T(8,128)(2,1)S(1)}, bf16[64,512]{1,0:T(8,128)(2,1)S(1)}, u32[]{:S(2)}, u32[]{:S(2)}) %collective-permute-start.9) | collective-permute-done | bytes 65568 | tf_op jit(solution)/shard_map/ppermute | solution.py:31
  21.4 2.4 %collective-permute-done.10.refs_3_ = bf16[64,512]{1,0:T(8,128)(2,1)S(1)} collective-permute-done((bf16[64,512]{1,0:T(8,128)(2,1)S(1)}, bf16[64,512]{1,0:T(8,128)(2,1)S(1)}, u32[]{:S(2)}, u32[]{:S(2)}) %collective-permute-start.10) | collective-permute-done | bytes 65568 | tf_op jit(solution)/shard_map/ppermute | solution.py:31
  23.8 0.6 mix.1.refs_0_
  24.5 3.7 %collective-permute-start.13 = (bf16[64,512]{1,0:T(8,128)(2,1)S(1)}, bf16[64,512]{1,0:T(8,128)(2,1)S(1)}, u32[]{:S(2)}, u32[]{:S(2)}) collective-permute-start(bf16[64,512]{1,0:T(8,128)(2,1)S(1)} %mix.1.refs_0_), channel_id=1, source_target_pairs={{0,3},{1,2},{2,1},{3,0},{4,7},{5,6},{6,5},{7,4},{8,11},{9,10},{10,... | collective-permute-start | bytes 196616 | tf_op jit(solution)/shard_map/ppermute | solution.py:31
  28.1 0.0 collective-permute-start.12
  28.1 0.8 %collective-permute-start.11 = (bf16[64,512]{1,0:T(8,128)(2,1)S(1)}, bf16[64,512]{1,0:T(8,128)(2,1)S(1)}, u32[]{:S(2)}, u32[]{:S(2)}) collective-permute-start(bf16[64,512]{1,0:T(8,128)(2,1)S(1)} %mix.1.refs_0_), channel_id=1, source_target_pairs={{0,1},{1,0},{2,3},{3,2},{4,5},{5,4},{6,7},{7,6},{8,9},{9,8},{10,11... | collective-permute-start | bytes 196616 | tf_op jit(solution)/shard_map/ppermute | solution.py:31
  28.9 1.7 %collective-permute-done.13.refs_3_ = bf16[64,512]{1,0:T(8,128)(2,1)S(1)} collective-permute-done((bf16[64,512]{1,0:T(8,128)(2,1)S(1)}, bf16[64,512]{1,0:T(8,128)(2,1)S(1)}, u32[]{:S(2)}, u32[]{:S(2)}) %collective-permute-start.13) | collective-permute-done | bytes 65568 | tf_op jit(solution)/shard_map/ppermute | solution.py:31
  30.6 2.7 %collective-permute-done.12.refs_2_ = bf16[64,512]{1,0:T(8,128)(2,1)S(1)} collective-permute-done((bf16[64,512]{1,0:T(8,128)(2,1)S(1)}, bf16[64,512]{1,0:T(8,128)(2,1)S(1)}, u32[]{:S(2)}, u32[]{:S(2)}) %collective-permute-start.12) | collective-permute-done | bytes 65568 | tf_op jit(solution)/shard_map/ppermute | solution.py:31
  33.3 0.0 collective-permute-done.11.refs_1_
  33.3 0.6 stack.13.refs_0_
  33.9 0.6 collective-permute-start.16
  34.5 1.5 %collective-permute-start.15 = (bf16[160,512]{1,0:T(8,128)(2,1)S(1)}, bf16[160,512]{1,0:T(8,128)(2,1)S(1)}, u32[]{:S(2)}, u32[]{:S(2)}) collective-permute-start(bf16[160,512]{1,0:T(8,128)(2,1)S(1)} %stack.13.refs_0_), channel_id=1, source_target_pairs={{0,16},{4,20},{8,24},{12,28},{16,0},{20,4},{24,8},{28,12},{1,17},{... | collective-permute-start | bytes 491528 | tf_op jit(solution)/shard_map/ppermute | solution.py:31
  35.9 1.5 %collective-permute-start.14 = (bf16[160,512]{1,0:T(8,128)(2,1)S(1)}, bf16[160,512]{1,0:T(8,128)(2,1)S(1)}, u32[]{:S(2)}, u32[]{:S(2)}) collective-permute-start(bf16[160,512]{1,0:T(8,128)(2,1)S(1)} %stack.13.refs_0_), channel_id=1, source_target_pairs={{0,8},{4,12},{8,0},{12,4},{16,24},{20,28},{24,16},{28,20},{1,9},{5... | collective-permute-start | bytes 491528 | tf_op jit(solution)/shard_map/ppermute | solution.py:31
  37.4 0.0 collective-permute-start.17
  37.4 3.9 %collective-permute-done.16.refs_3_ = bf16[160,512]{1,0:T(8,128)(2,1)S(1)} collective-permute-done((bf16[160,512]{1,0:T(8,128)(2,1)S(1)}, bf16[160,512]{1,0:T(8,128)(2,1)S(1)}, u32[]{:S(2)}, u32[]{:S(2)}) %collective-permute-start.16) | collective-permute-done | bytes 163872 | tf_op jit(solution)/shard_map/ppermute | solution.py:31
  41.3 0.0 collective-permute-start.20
  41.4 1.1 %collective-permute-done.15.refs_2_ = bf16[160,512]{1,0:T(8,128)(2,1)S(1)} collective-permute-done((bf16[160,512]{1,0:T(8,128)(2,1)S(1)}, bf16[160,512]{1,0:T(8,128)(2,1)S(1)}, u32[]{:S(2)}, u32[]{:S(2)}) %collective-permute-start.15) | collective-permute-done | bytes 163872 | tf_op jit(solution)/shard_map/ppermute | solution.py:31
  42.5 0.0 collective-permute-start.19
  42.5 0.0 collective-permute-done.14.refs_1_
  42.5 0.5 collective-permute-start.18
  43.0 1.0 %gram.1.gram_ref = f32[512,512]{1,0:T(8,128)S(1)} custom-call(s32[2]{0:T(128)S(1)} %pad_add_fusion.index_ref, bf16[160,512]{1,0:T(8,128)(2,1)S(1)} %stack.13.refs_0_, bf16[160,512]{1,0:T(8,128)(2,1)S(1)} %collective-permute-done.14.refs_1_, bf16[160,512]{1,0:T(8,128)(2,1)S(1)} %collective-permute-done.15.refs_2_, ...), custom_call_target="tpu_custom_call" | custom-call | tf_op jit(solution)/shard_map/gram/pallas_call | solution.py:512
  44.0 0.0 collective-permute-done.17.refs_4_
  44.0 0.0 collective-permute-done.20.refs_7_
  44.1 0.0 collective-permute-done.19.refs_6_
  44.1 0.0 collective-permute-done.18.refs_5_
  44.1 0.0 copy-done.1
  44.1 0.0 copy-done.3
  44.1 18.1 %solve.1 = (f32[512,512]{1,0:T(8,128)}, f32[4,128]{1,0:T(4,128)}, f32[16,128]{1,0:T(8,128)}) custom-call(s32[2]{0:T(128)S(1)} %pad_add_fusion.index_ref, f32[512,512]{1,0:T(8,128)S(1)} %gram.1.gram_ref, f32[4,128]{1,0:T(4,128)S(1)} %bitcast.11, bf16[2048,128]{1,0:T(8,128)(2,1)S(1)} %copy-done.1, s32[16,128]{1,0:T(8,128)S(1)} %add_bitcast_fusion.marks_ref, ...), custom_call_target="tpu_custom_call" | custom-call | tf_op jit(solution)/shard_map/solve/pallas_call | solution.py:593
Async XLA Ops:
  0.6 8.2 %collective-permute-start.5 = (s32[1,32]{1,0:T(1,128)}, s32[1,32]{1,0:T(1,128)S(1)}, u32[]{:S(2)}, u32[]{:S(2)}) collective-permute-start(s32[1,32]{1,0:T(1,128)} %bitcast.12), channel_id=1, source_target_pairs={{0,24},{4,28},{8,16},{12,20},{16,8},{20,12},{24,0},{28,4},{1,25},{... | collective-permute-start | bytes 392 | tf_op jit(solution)/shard_map/ppermute | solution.py:31
  4.6 4.8 %collective-permute-start.3 = (s32[1,32]{1,0:T(1,128)}, s32[1,32]{1,0:T(1,128)S(1)}, u32[]{:S(2)}, u32[]{:S(2)}) collective-permute-start(s32[1,32]{1,0:T(1,128)} %bitcast.13), channel_id=1, source_target_pairs={{0,16},{4,20},{8,24},{12,28},{16,0},{20,4},{24,8},{28,12},{1,17},{... | collective-permute-start | bytes 392 | tf_op jit(solution)/shard_map/ppermute | solution.py:31
  5.1 4.4 %collective-permute-start.1 = (s32[1,32]{1,0:T(1,128)}, s32[1,32]{1,0:T(1,128)S(1)}, u32[]{:S(2)}, u32[]{:S(2)}) collective-permute-start(s32[1,32]{1,0:T(1,128)} %bitcast.14), channel_id=1, source_target_pairs={{0,8},{4,12},{8,0},{12,4},{16,24},{20,28},{24,16},{28,20},{1,9},{5... | collective-permute-start | bytes 392 | tf_op jit(solution)/shard_map/ppermute | solution.py:31
  5.2 4.7 %collective-permute-start = (s32[1,32]{1,0:T(1,128)}, s32[1,32]{1,0:T(1,128)S(1)}, u32[]{:S(2)}, u32[]{:S(2)}) collective-permute-start(s32[1,32]{1,0:T(1,128)} %bitcast.15), channel_id=1, source_target_pairs={{0,4},{4,0},{8,12},{12,8},{16,20},{20,16},{24,28},{28,24},{1,5},{5... | collective-permute-start | bytes 392 | tf_op jit(solution)/shard_map/ppermute | solution.py:31
  6.0 1.0 %copy-start = (bf16[2048,128]{1,0:T(8,128)(2,1)S(1)}, bf16[2048,128]{1,0:T(8,128)(2,1)}, u32[]{:S(2)}) copy-start(bf16[2048,128]{1,0:T(8,128)(2,1)} %cov_ref.3) | copy-start | bytes 1572868
  7.1 0.7 %copy-start.2 = (f32[2048]{0:T(1024)S(1)}, f32[2048]{0:T(1024)}, u32[]{:S(2)}) copy-start(f32[2048]{0:T(1024)} %param.11) | copy-start | bytes 24580
  8.8 1.4 %collective-permute-start.6 = (s32[1,32]{1,0:T(1,128)S(1)}, s32[1,32]{1,0:T(1,128)S(1)}, u32[]{:S(2)}, u32[]{:S(2)}) collective-permute-start(s32[1,32]{1,0:T(1,128)S(1)} %collective-permute-done.5.refs_6_), channel_id=1, source_target_pairs={{0,4},{4,0},{8,12},{12,8},{16,20},{20,16},{24,28},{28,24},{1,5},{5... | collective-permute-start | bytes 392 | tf_op jit(solution)/shard_map/ppermute | solution.py:31
  9.4 1.1 %collective-permute-start.4 = (s32[1,32]{1,0:T(1,128)S(1)}, s32[1,32]{1,0:T(1,128)S(1)}, u32[]{:S(2)}, u32[]{:S(2)}) collective-permute-start(s32[1,32]{1,0:T(1,128)S(1)} %collective-permute-done.3.refs_4_), channel_id=1, source_target_pairs={{0,4},{4,0},{8,12},{12,8},{16,20},{20,16},{24,28},{28,24},{1,5},{5... | collective-permute-start | bytes 392 | tf_op jit(solution)/shard_map/ppermute | solution.py:31
  9.5 1.2 %collective-permute-start.2 = (s32[1,32]{1,0:T(1,128)S(1)}, s32[1,32]{1,0:T(1,128)S(1)}, u32[]{:S(2)}, u32[]{:S(2)}) collective-permute-start(s32[1,32]{1,0:T(1,128)S(1)} %collective-permute-done.1.refs_2_), channel_id=1, source_target_pairs={{0,4},{4,0},{8,12},{12,8},{16,20},{20,16},{24,28},{28,24},{1,5},{5... | collective-permute-start | bytes 392 | tf_op jit(solution)/shard_map/ppermute | solution.py:31
  10.7 0.7 %copy-start.4 = (s32[32]{0:T(128)S(1)}, s32[32]{0:T(128)}, u32[]{:S(2)}) copy-start(s32[32]{0:T(128)} %param.9) | copy-start | bytes 388
  11.4 32.7 %copy-start.1 = (bf16[2048,128]{1,0:T(8,128)(2,1)S(1)}, bf16[2048,128]{1,0:T(8,128)(2,1)}, u32[]{:S(2)}) copy-start(bf16[2048,128]{1,0:T(8,128)(2,1)} %cov_ref.3) | copy-start | bytes 1572868
  11.4 32.7 %copy-start.3 = (f32[512]{0:T(512)S(1)}, f32[512]{0:T(512)}, u32[]{:S(2)}) copy-start(f32[512]{0:T(512)} %param.10) | copy-start | bytes 6148
  13.0 1.6 %collective-permute-start.7 = (bf16[256,512]{1,0:T(8,128)(2,1)S(1)}, bf16[256,512]{1,0:T(8,128)(2,1)S(1)}, u32[]{:S(2)}, u32[]{:S(2)}) collective-permute-start(bf16[256,512]{1,0:T(8,128)(2,1)S(1)} %get-tuple-element.17), channel_id=1, source_target_pairs={{0,4},{4,0},{8,12},{12,8},{16,20},{20,16},{24,28},{28,24},{1,5},{5... | collective-permute-start | bytes 786440 | tf_op jit(solution)/shard_map/ppermute | solution.py:31
  15.2 4.5 %collective-permute-start.8 = (bf16[64,512]{1,0:T(8,128)(2,1)S(1)}, bf16[64,512]{1,0:T(8,128)(2,1)S(1)}, u32[]{:S(2)}, u32[]{:S(2)}) collective-permute-start(bf16[64,512]{1,0:T(8,128)(2,1)S(1)} %get-tuple-element.19), channel_id=1, source_target_pairs={{0,8},{4,12},{8,0},{12,4},{16,24},{20,28},{24,16},{28,20},{1,9},{5... | collective-permute-start | bytes 196616 | tf_op jit(solution)/shard_map/ppermute | solution.py:31
  17.2 4.3 %collective-permute-start.9 = (bf16[64,512]{1,0:T(8,128)(2,1)S(1)}, bf16[64,512]{1,0:T(8,128)(2,1)S(1)}, u32[]{:S(2)}, u32[]{:S(2)}) collective-permute-start(bf16[64,512]{1,0:T(8,128)(2,1)S(1)} %get-tuple-element.20), channel_id=1, source_target_pairs={{0,16},{4,20},{8,24},{12,28},{16,0},{20,4},{24,8},{28,12},{1,17},{... | collective-permute-start | bytes 196616 | tf_op jit(solution)/shard_map/ppermute | solution.py:31
  18.7 5.2 %collective-permute-start.10 = (bf16[64,512]{1,0:T(8,128)(2,1)S(1)}, bf16[64,512]{1,0:T(8,128)(2,1)S(1)}, u32[]{:S(2)}, u32[]{:S(2)}) collective-permute-start(bf16[64,512]{1,0:T(8,128)(2,1)S(1)} %get-tuple-element.21), channel_id=1, source_target_pairs={{0,24},{4,28},{8,16},{12,20},{16,8},{20,12},{24,0},{28,4},{1,25},{... | collective-permute-start | bytes 196616 | tf_op jit(solution)/shard_map/ppermute | solution.py:31
  24.5 6.1 %collective-permute-start.13 = (bf16[64,512]{1,0:T(8,128)(2,1)S(1)}, bf16[64,512]{1,0:T(8,128)(2,1)S(1)}, u32[]{:S(2)}, u32[]{:S(2)}) collective-permute-start(bf16[64,512]{1,0:T(8,128)(2,1)S(1)} %mix.1.refs_0_), channel_id=1, source_target_pairs={{0,3},{1,2},{2,1},{3,0},{4,7},{5,6},{6,5},{7,4},{8,11},{9,10},{10,... | collective-permute-start | bytes 196616 | tf_op jit(solution)/shard_map/ppermute | solution.py:31
  28.1 5.2 %collective-permute-start.12 = (bf16[64,512]{1,0:T(8,128)(2,1)S(1)}, bf16[64,512]{1,0:T(8,128)(2,1)S(1)}, u32[]{:S(2)}, u32[]{:S(2)}) collective-permute-start(bf16[64,512]{1,0:T(8,128)(2,1)S(1)} %mix.1.refs_0_), channel_id=1, source_target_pairs={{0,2},{1,3},{2,0},{3,1},{4,6},{5,7},{6,4},{7,5},{8,10},{9,11},{10,... | collective-permute-start | bytes 196616 | tf_op jit(solution)/shard_map/ppermute | solution.py:31
  28.1 5.2 %collective-permute-start.11 = (bf16[64,512]{1,0:T(8,128)(2,1)S(1)}, bf16[64,512]{1,0:T(8,128)(2,1)S(1)}, u32[]{:S(2)}, u32[]{:S(2)}) collective-permute-start(bf16[64,512]{1,0:T(8,128)(2,1)S(1)} %mix.1.refs_0_), channel_id=1, source_target_pairs={{0,1},{1,0},{2,3},{3,2},{4,5},{5,4},{6,7},{7,6},{8,9},{9,8},{10,11... | collective-permute-start | bytes 196616 | tf_op jit(solution)/shard_map/ppermute | solution.py:31
  33.9 7.5 %collective-permute-start.16 = (bf16[160,512]{1,0:T(8,128)(2,1)S(1)}, bf16[160,512]{1,0:T(8,128)(2,1)S(1)}, u32[]{:S(2)}, u32[]{:S(2)}) collective-permute-start(bf16[160,512]{1,0:T(8,128)(2,1)S(1)} %stack.13.refs_0_), channel_id=1, source_target_pairs={{0,24},{4,28},{8,16},{12,20},{16,8},{20,12},{24,0},{28,4},{1,25},{... | collective-permute-start | bytes 491528 | tf_op jit(solution)/shard_map/ppermute | solution.py:31
  34.5 8.0 %collective-permute-start.15 = (bf16[160,512]{1,0:T(8,128)(2,1)S(1)}, bf16[160,512]{1,0:T(8,128)(2,1)S(1)}, u32[]{:S(2)}, u32[]{:S(2)}) collective-permute-start(bf16[160,512]{1,0:T(8,128)(2,1)S(1)} %stack.13.refs_0_), channel_id=1, source_target_pairs={{0,16},{4,20},{8,24},{12,28},{16,0},{20,4},{24,8},{28,12},{1,17},{... | collective-permute-start | bytes 491528 | tf_op jit(solution)/shard_map/ppermute | solution.py:31
  35.9 6.5 %collective-permute-start.14 = (bf16[160,512]{1,0:T(8,128)(2,1)S(1)}, bf16[160,512]{1,0:T(8,128)(2,1)S(1)}, u32[]{:S(2)}, u32[]{:S(2)}) collective-permute-start(bf16[160,512]{1,0:T(8,128)(2,1)S(1)} %stack.13.refs_0_), channel_id=1, source_target_pairs={{0,8},{4,12},{8,0},{12,4},{16,24},{20,28},{24,16},{28,20},{1,9},{5... | collective-permute-start | bytes 491528 | tf_op jit(solution)/shard_map/ppermute | solution.py:31
  37.4 6.6 %collective-permute-start.17 = (bf16[160,512]{1,0:T(8,128)(2,1)S(1)}, bf16[160,512]{1,0:T(8,128)(2,1)S(1)}, u32[]{:S(2)}, u32[]{:S(2)}) collective-permute-start(bf16[160,512]{1,0:T(8,128)(2,1)S(1)} %stack.13.refs_0_), channel_id=1, source_target_pairs={{0,4},{4,0},{8,12},{12,8},{16,20},{20,16},{24,28},{28,24},{1,5},{5... | collective-permute-start | bytes 491528 | tf_op jit(solution)/shard_map/ppermute | solution.py:31
  41.3 2.7 %collective-permute-start.20 = (bf16[160,512]{1,0:T(8,128)(2,1)S(1)}, bf16[160,512]{1,0:T(8,128)(2,1)S(1)}, u32[]{:S(2)}, u32[]{:S(2)}) collective-permute-start(bf16[160,512]{1,0:T(8,128)(2,1)S(1)} %collective-permute-done.16.refs_3_), channel_id=1, source_target_pairs={{0,4},{4,0},{8,12},{12,8},{16,20},{20,16},{24,28},{28,24},{1,5},{5... | collective-permute-start | bytes 491528 | tf_op jit(solution)/shard_map/ppermute | solution.py:31
  42.5 1.6 %collective-permute-start.19 = (bf16[160,512]{1,0:T(8,128)(2,1)S(1)}, bf16[160,512]{1,0:T(8,128)(2,1)S(1)}, u32[]{:S(2)}, u32[]{:S(2)}) collective-permute-start(bf16[160,512]{1,0:T(8,128)(2,1)S(1)} %collective-permute-done.15.refs_2_), channel_id=1, source_target_pairs={{0,4},{4,0},{8,12},{12,8},{16,20},{20,16},{24,28},{28,24},{1,5},{5... | collective-permute-start | bytes 491528 | tf_op jit(solution)/shard_map/ppermute | solution.py:31
  42.5 1.6 %collective-permute-start.18 = (bf16[160,512]{1,0:T(8,128)(2,1)S(1)}, bf16[160,512]{1,0:T(8,128)(2,1)S(1)}, u32[]{:S(2)}, u32[]{:S(2)}) collective-permute-start(bf16[160,512]{1,0:T(8,128)(2,1)S(1)} %collective-permute-done.14.refs_1_), channel_id=1, source_target_pairs={{0,4},{4,0},{8,12},{12,8},{16,20},{20,16},{24,28},{28,24},{1,5},{5... | collective-permute-start | bytes 491528 | tf_op jit(solution)/shard_map/ppermute | solution.py:31

commit v17 on v14

--- a/solution.py
+++ b/solution.py
@@ -511,6 +511,7 @@
     want = sample_rows[None, :]
     want = [want] + [partner(want, "wide", m) for m in range(2, MATES, 2)]
     want = [one for piece in want for one in (piece, partner(piece, "wide", 1))]
+    want[0] = jnp.maximum(want[0], -1)
 
     design, packed = call(
         design_kernel,

time: 62.3 us -> 62.3 us (level)
  other arithmetic: 0.79 us -> 1.48 us
  local copies, waits for them, and re-layouts: 2.4 us -> 1.74 us
    max x0 -> x1, other arithmetic: none -> 0.69 us  [body(): want[0] = jnp.maximum(want[0], -1)]
    unnamed x10 -> x8, local copies, waits for them, and re-layouts: 2.4 us -> 1.74 us
  transfers between devices with their start and end apart: 21 -> 21, of which waited for: 11 -> 11; matrix products, arithmetic and copies ran while one was open for 1% -> 2% of each run, Pallas kernels for 3% -> 3%
where the time goes in v17:
time: 62.3 us; the launch traced here: 61.9 us
  Pallas kernels  23.1 us (37%)
  starting transfers between devices  18.1 us (29%)
  waiting for transfers between devices  16.6 us (27%)
  local copies, waits for them, and re-layouts  1.74 us (3%)
  other arithmetic  1.48 us (2%)
  between operations  0.88 us (1%)
    ppermute x21, starting transfers between devices, partner(): return lax.ppermute(value, axis, pairs)  18.1 us
    pallas_call x1, Pallas kernels, body(): pl.pallas_call(functools.partial(solve_kernel, math.sqrt(LEVELS / SKETCH)...  17.6 us
    ppermute x21, waiting for transfers between devices, partner(): return lax.ppermute(value, axis, pairs)  16.6 us
    pallas_call x6, Pallas kernels, call(): pl.pallas_call(kernel, out_shape=[jax.ShapeDtypeStruct(shape, dtype) for...  5.46 us
    unnamed x8, local copies, waits for them, and re-layouts  1.74 us
  transfers between devices with their start and end apart: 21, of which 11 were waited for; matrix products, arithmetic and copies ran while one was open for 2% of the time, Pallas kernels for 3%

profile of v17, /device:TPU:0, one launch (start us, length us, event | category | flops | bytes accessed | tf_op | source)
XLA Modules:
  0.0 61.9 jit_solution(8498260168645910789)
XLA Ops:
  0.6 4.0 %collective-permute-start.5 = (s32[1,32]{1,0:T(1,128)}, s32[1,32]{1,0:T(1,128)S(1)}, u32[]{:S(2)}, u32[]{:S(2)}) collective-permute-start(s32[1,32]{1,0:T(1,128)} %bitcast.16), channel_id=1, source_target_pairs={{0,24},{4,28},{8,16},{12,20},{16,8},{20,12},{24,0},{28,4},{1,25},{... | collective-permute-start | bytes 392 | tf_op jit(solution)/shard_map/ppermute | solution.py:31
  4.6 0.5 collective-permute-start.3
  5.1 0.1 collective-permute-start.1
  5.2 0.0 collective-permute-start
  5.2 0.7 %maximum_bitcast_fusion.refs_0_ = s32[1,32]{1,0:T(1,128)S(1)} fusion(s32[32]{0:T(128)} %param.9), kind=kLoop, calls=%fused_computation.2 | loop fusion | flops 32 | bytes 256 | tf_op jit(solution)/shard_map/max | solution.py:514
  5.9 0.1 pad_add_fusion.index_ref
  6.0 0.7 %add_bitcast_fusion.marks_ref = s32[16,128]{1,0:T(8,128)S(1)} fusion(s32[2048]{0:T(1024)} %param.7, s32[2048]{0:T(1024)} %param.8), kind=kLoop, calls=%fused_computation | loop fusion | flops 4096 | bytes 24576 | tf_op jit(solution)/shard_map/reshape | solution.py:507
  6.7 0.0 copy-start
  6.7 1.0 %copy-done = bf16[2048,128]{1,0:T(8,128)(2,1)S(1)} copy-done((bf16[2048,128]{1,0:T(8,128)(2,1)S(1)}, bf16[2048,128]{1,0:T(8,128)(2,1)}, u32[]{:S(2)}) %copy-start) | copy-done | bytes 524312
  7.8 0.0 copy-start.2
  7.8 0.7 %copy-done.2 = f32[2048]{0:T(1024)S(1)} copy-done((f32[2048]{0:T(1024)S(1)}, f32[2048]{0:T(1024)}, u32[]{:S(2)}) %copy-start.2) | copy-done | bytes 8216
  8.5 1.0 %design.1 = (bf16[560,2048]{1,0:T(8,128)(2,1)S(1)}, f32[264,128]{1,0:T(8,128)S(1)}) custom-call(bf16[2048,128]{1,0:T(8,128)(2,1)S(1)} %copy-done, s32[16,128]{1,0:T(8,128)S(1)} %add_bitcast_fusion.marks_ref, f32[16,128]{1,0:T(8,128)S(1)} %bitcast.11), custom_call_target="tpu_custom_call" | custom-call | tf_op jit(solution)/shard_map/design/pallas_call | solution.py:489
  9.5 0.0 collective-permute-done.5.refs_6_
  9.5 0.5 collective-permute-start.6
  10.0 0.0 collective-permute-done.3.refs_4_
  10.0 0.1 collective-permute-start.4
  10.1 0.0 collective-permute-done.1.refs_2_
  10.1 0.4 collective-permute-start.2
  10.5 0.0 collective-permute-done.refs_1_
  10.5 0.3 collective-permute-done.6.refs_7_
  10.8 0.3 collective-permute-done.4.refs_5_
  11.1 0.2 collective-permute-done.2.refs_3_
  11.4 0.0 copy-start.1
  11.4 0.0 copy-start.3
  11.4 1.6 %local.1 = (bf16[256,512]{1,0:T(8,128)(2,1)S(1)}, bf16[256,512]{1,0:T(8,128)(2,1)S(1)}) custom-call(s32[2]{0:T(128)S(1)} %pad_add_fusion.index_ref, bf16[560,2048]{1,0:T(8,128)(2,1)S(1)} %get-tuple-element.14.design_ref, f32[264,128]{1,0:T(8,128)S(1)} %get-tuple-element.15.packed_ref, s32[16,128]{1,0:T(8,128)S(1)} %add_bitcast_fusion.marks_ref, ...), custom_call_target="tpu_custom_call" | custom-call | tf_op jit(solution)/shard_map/local/pallas_call | solution.py:489
  13.0 0.4 collective-permute-start.7
  13.3 1.2 %collective-permute-done.7.came_ref = bf16[256,512]{1,0:T(8,128)(2,1)S(1)} collective-permute-done((bf16[256,512]{1,0:T(8,128)(2,1)S(1)}, bf16[256,512]{1,0:T(8,128)(2,1)S(1)}, u32[]{:S(2)}, u32[]{:S(2)}) %collective-permute-start.7) | collective-permute-done | bytes 262176 | tf_op jit(solution)/shard_map/ppermute | solution.py:31
  14.6 0.7 %pair.1 = (bf16[64,512]{1,0:T(8,128)(2,1)S(1)}, bf16[64,512]{1,0:T(8,128)(2,1)S(1)}, bf16[64,512]{1,0:T(8,128)(2,1)S(1)}, bf16[64,512]{1,0:T(8,128)(2,1)S(1)}) custom-call(s32[2]{0:T(128)S(1)} %pad_add_fusion.index_ref, bf16[256,512]{1,0:T(8,128)(2,1)S(1)} %get-tuple-element.16.stay_ref, bf16[256,512]{1,0:T(8,128)(2,1)S(1)} %collective-permute-done.7.came_ref), custom_call_target="tpu_custom_call" | custom-call | tf_op jit(solution)/shard_map/pair/pallas_call | solution.py:489
  15.2 2.0 %collective-permute-start.8 = (bf16[64,512]{1,0:T(8,128)(2,1)S(1)}, bf16[64,512]{1,0:T(8,128)(2,1)S(1)}, u32[]{:S(2)}, u32[]{:S(2)}) collective-permute-start(bf16[64,512]{1,0:T(8,128)(2,1)S(1)} %get-tuple-element.19), channel_id=1, source_target_pairs={{0,8},{4,12},{8,0},{12,4},{16,24},{20,28},{24,16},{28,20},{1,9},{5... | collective-permute-start | bytes 196616 | tf_op jit(solution)/shard_map/ppermute | solution.py:31
  17.2 1.5 %collective-permute-start.9 = (bf16[64,512]{1,0:T(8,128)(2,1)S(1)}, bf16[64,512]{1,0:T(8,128)(2,1)S(1)}, u32[]{:S(2)}, u32[]{:S(2)}) collective-permute-start(bf16[64,512]{1,0:T(8,128)(2,1)S(1)} %get-tuple-element.20), channel_id=1, source_target_pairs={{0,16},{4,20},{8,24},{12,28},{16,0},{20,4},{24,8},{28,12},{1,17},{... | collective-permute-start | bytes 196616 | tf_op jit(solution)/shard_map/ppermute | solution.py:31
  18.7 0.1 collective-permute-start.10
  18.8 1.0 %collective-permute-done.8.refs_1_ = bf16[64,512]{1,0:T(8,128)(2,1)S(1)} collective-permute-done((bf16[64,512]{1,0:T(8,128)(2,1)S(1)}, bf16[64,512]{1,0:T(8,128)(2,1)S(1)}, u32[]{:S(2)}, u32[]{:S(2)}) %collective-permute-start.8) | collective-permute-done | bytes 65568 | tf_op jit(solution)/shard_map/ppermute | solution.py:31
  19.7 1.7 %collective-permute-done.9.refs_2_ = bf16[64,512]{1,0:T(8,128)(2,1)S(1)} collective-permute-done((bf16[64,512]{1,0:T(8,128)(2,1)S(1)}, bf16[64,512]{1,0:T(8,128)(2,1)S(1)}, u32[]{:S(2)}, u32[]{:S(2)}) %collective-permute-start.9) | collective-permute-done | bytes 65568 | tf_op jit(solution)/shard_map/ppermute | solution.py:31
  21.4 2.4 %collective-permute-done.10.refs_3_ = bf16[64,512]{1,0:T(8,128)(2,1)S(1)} collective-permute-done((bf16[64,512]{1,0:T(8,128)(2,1)S(1)}, bf16[64,512]{1,0:T(8,128)(2,1)S(1)}, u32[]{:S(2)}, u32[]{:S(2)}) %collective-permute-start.10) | collective-permute-done | bytes 65568 | tf_op jit(solution)/shard_map/ppermute | solution.py:31
  23.8 0.6 mix.1.refs_0_
  24.5 3.7 %collective-permute-start.13 = (bf16[64,512]{1,0:T(8,128)(2,1)S(1)}, bf16[64,512]{1,0:T(8,128)(2,1)S(1)}, u32[]{:S(2)}, u32[]{:S(2)}) collective-permute-start(bf16[64,512]{1,0:T(8,128)(2,1)S(1)} %mix.1.refs_0_), channel_id=1, source_target_pairs={{0,3},{1,2},{2,1},{3,0},{4,7},{5,6},{6,5},{7,4},{8,11},{9,10},{10,... | collective-permute-start | bytes 196616 | tf_op jit(solution)/shard_map/ppermute | solution.py:31
  28.1 0.0 collective-permute-start.12
  28.1 0.8 %collective-permute-start.11 = (bf16[64,512]{1,0:T(8,128)(2,1)S(1)}, bf16[64,512]{1,0:T(8,128)(2,1)S(1)}, u32[]{:S(2)}, u32[]{:S(2)}) collective-permute-start(bf16[64,512]{1,0:T(8,128)(2,1)S(1)} %mix.1.refs_0_), channel_id=1, source_target_pairs={{0,1},{1,0},{2,3},{3,2},{4,5},{5,4},{6,7},{7,6},{8,9},{9,8},{10,11... | collective-permute-start | bytes 196616 | tf_op jit(solution)/shard_map/ppermute | solution.py:31
  28.9 1.7 %collective-permute-done.13.refs_3_ = bf16[64,512]{1,0:T(8,128)(2,1)S(1)} collective-permute-done((bf16[64,512]{1,0:T(8,128)(2,1)S(1)}, bf16[64,512]{1,0:T(8,128)(2,1)S(1)}, u32[]{:S(2)}, u32[]{:S(2)}) %collective-permute-start.13) | collective-permute-done | bytes 65568 | tf_op jit(solution)/shard_map/ppermute | solution.py:31
  30.6 2.7 %collective-permute-done.12.refs_2_ = bf16[64,512]{1,0:T(8,128)(2,1)S(1)} collective-permute-done((bf16[64,512]{1,0:T(8,128)(2,1)S(1)}, bf16[64,512]{1,0:T(8,128)(2,1)S(1)}, u32[]{:S(2)}, u32[]{:S(2)}) %collective-permute-start.12) | collective-permute-done | bytes 65568 | tf_op jit(solution)/shard_map/ppermute | solution.py:31
  33.3 0.0 collective-permute-done.11.refs_1_
  33.3 0.6 stack.13.refs_0_
  33.9 0.6 collective-permute-start.16
  34.5 1.5 %collective-permute-start.15 = (bf16[160,512]{1,0:T(8,128)(2,1)S(1)}, bf16[160,512]{1,0:T(8,128)(2,1)S(1)}, u32[]{:S(2)}, u32[]{:S(2)}) collective-permute-start(bf16[160,512]{1,0:T(8,128)(2,1)S(1)} %stack.13.refs_0_), channel_id=1, source_target_pairs={{0,16},{4,20},{8,24},{12,28},{16,0},{20,4},{24,8},{28,12},{1,17},{... | collective-permute-start | bytes 491528 | tf_op jit(solution)/shard_map/ppermute | solution.py:31
  35.9 1.5 %collective-permute-start.14 = (bf16[160,512]{1,0:T(8,128)(2,1)S(1)}, bf16[160,512]{1,0:T(8,128)(2,1)S(1)}, u32[]{:S(2)}, u32[]{:S(2)}) collective-permute-start(bf16[160,512]{1,0:T(8,128)(2,1)S(1)} %stack.13.refs_0_), channel_id=1, source_target_pairs={{0,8},{4,12},{8,0},{12,4},{16,24},{20,28},{24,16},{28,20},{1,9},{5... | collective-permute-start | bytes 491528 | tf_op jit(solution)/shard_map/ppermute | solution.py:31
  37.4 0.0 collective-permute-start.17
  37.4 3.9 %collective-permute-done.16.refs_3_ = bf16[160,512]{1,0:T(8,128)(2,1)S(1)} collective-permute-done((bf16[160,512]{1,0:T(8,128)(2,1)S(1)}, bf16[160,512]{1,0:T(8,128)(2,1)S(1)}, u32[]{:S(2)}, u32[]{:S(2)}) %collective-permute-start.16) | collective-permute-done | bytes 163872 | tf_op jit(solution)/shard_map/ppermute | solution.py:31
  41.3 0.0 collective-permute-start.20
  41.3 1.1 %collective-permute-done.15.refs_2_ = bf16[160,512]{1,0:T(8,128)(2,1)S(1)} collective-permute-done((bf16[160,512]{1,0:T(8,128)(2,1)S(1)}, bf16[160,512]{1,0:T(8,128)(2,1)S(1)}, u32[]{:S(2)}, u32[]{:S(2)}) %collective-permute-start.15) | collective-permute-done | bytes 163872 | tf_op jit(solution)/shard_map/ppermute | solution.py:31
  42.5 0.0 collective-permute-start.19
  42.5 0.0 collective-permute-done.14.refs_1_
  42.5 0.5 collective-permute-start.18
  43.0 1.0 %gram.1.gram_ref = f32[512,512]{1,0:T(8,128)S(1)} custom-call(s32[2]{0:T(128)S(1)} %pad_add_fusion.index_ref, bf16[160,512]{1,0:T(8,128)(2,1)S(1)} %stack.13.refs_0_, bf16[160,512]{1,0:T(8,128)(2,1)S(1)} %collective-permute-done.14.refs_1_, bf16[160,512]{1,0:T(8,128)(2,1)S(1)} %collective-permute-done.15.refs_2_, ...), custom_call_target="tpu_custom_call" | custom-call | tf_op jit(solution)/shard_map/gram/pallas_call | solution.py:489
  44.0 0.0 collective-permute-done.17.refs_4_
  44.0 0.0 collective-permute-done.20.refs_7_
  44.1 0.0 collective-permute-done.19.refs_6_
  44.1 0.0 collective-permute-done.18.refs_5_
  44.1 0.0 copy-done.1
  44.1 0.0 copy-done.3
  44.1 17.6 %solve.1 = (f32[512,512]{1,0:T(8,128)}, f32[4,128]{1,0:T(4,128)}, f32[16,128]{1,0:T(8,128)}) custom-call(s32[2]{0:T(128)S(1)} %pad_add_fusion.index_ref, f32[512,512]{1,0:T(8,128)S(1)} %gram.1.gram_ref, f32[4,128]{1,0:T(4,128)S(1)} %bitcast.13, bf16[2048,128]{1,0:T(8,128)(2,1)S(1)} %copy-done.1, s32[16,128]{1,0:T(8,128)S(1)} %add_bitcast_fusion.marks_ref, ...), custom_call_target="tpu_custom_call" | custom-call | tf_op jit(solution)/shard_map/solve/pallas_call | solution.py:571
Async XLA Ops:
  0.6 8.8 %collective-permute-start.5 = (s32[1,32]{1,0:T(1,128)}, s32[1,32]{1,0:T(1,128)S(1)}, u32[]{:S(2)}, u32[]{:S(2)}) collective-permute-start(s32[1,32]{1,0:T(1,128)} %bitcast.16), channel_id=1, source_target_pairs={{0,24},{4,28},{8,16},{12,20},{16,8},{20,12},{24,0},{28,4},{1,25},{... | collective-permute-start | bytes 392 | tf_op jit(solution)/shard_map/ppermute | solution.py:31
  4.6 5.4 %collective-permute-start.3 = (s32[1,32]{1,0:T(1,128)}, s32[1,32]{1,0:T(1,128)S(1)}, u32[]{:S(2)}, u32[]{:S(2)}) collective-permute-start(s32[1,32]{1,0:T(1,128)} %bitcast.17), channel_id=1, source_target_pairs={{0,16},{4,20},{8,24},{12,28},{16,0},{20,4},{24,8},{28,12},{1,17},{... | collective-permute-start | bytes 392 | tf_op jit(solution)/shard_map/ppermute | solution.py:31
  5.1 5.0 %collective-permute-start.1 = (s32[1,32]{1,0:T(1,128)}, s32[1,32]{1,0:T(1,128)S(1)}, u32[]{:S(2)}, u32[]{:S(2)}) collective-permute-start(s32[1,32]{1,0:T(1,128)} %bitcast.18), channel_id=1, source_target_pairs={{0,8},{4,12},{8,0},{12,4},{16,24},{20,28},{24,16},{28,20},{1,9},{5... | collective-permute-start | bytes 392 | tf_op jit(solution)/shard_map/ppermute | solution.py:31
  5.2 5.3 %collective-permute-start = (s32[1,32]{1,0:T(1,128)}, s32[1,32]{1,0:T(1,128)S(1)}, u32[]{:S(2)}, u32[]{:S(2)}) collective-permute-start(s32[1,32]{1,0:T(1,128)} %bitcast.19), channel_id=1, source_target_pairs={{0,4},{4,0},{8,12},{12,8},{16,20},{20,16},{24,28},{28,24},{1,5},{5... | collective-permute-start | bytes 392 | tf_op jit(solution)/shard_map/ppermute | solution.py:31
  6.7 1.0 %copy-start = (bf16[2048,128]{1,0:T(8,128)(2,1)S(1)}, bf16[2048,128]{1,0:T(8,128)(2,1)}, u32[]{:S(2)}) copy-start(bf16[2048,128]{1,0:T(8,128)(2,1)} %cov_ref.3) | copy-start | bytes 1572868
  7.8 0.7 %copy-start.2 = (f32[2048]{0:T(1024)S(1)}, f32[2048]{0:T(1024)}, u32[]{:S(2)}) copy-start(f32[2048]{0:T(1024)} %param.11) | copy-start | bytes 24580
  9.5 1.4 %collective-permute-start.6 = (s32[1,32]{1,0:T(1,128)S(1)}, s32[1,32]{1,0:T(1,128)S(1)}, u32[]{:S(2)}, u32[]{:S(2)}) collective-permute-start(s32[1,32]{1,0:T(1,128)S(1)} %collective-permute-done.5.refs_6_), channel_id=1, source_target_pairs={{0,4},{4,0},{8,12},{12,8},{16,20},{20,16},{24,28},{28,24},{1,5},{5... | collective-permute-start | bytes 392 | tf_op jit(solution)/shard_map/ppermute | solution.py:31
  10.0 1.1 %collective-permute-start.4 = (s32[1,32]{1,0:T(1,128)S(1)}, s32[1,32]{1,0:T(1,128)S(1)}, u32[]{:S(2)}, u32[]{:S(2)}) collective-permute-start(s32[1,32]{1,0:T(1,128)S(1)} %collective-permute-done.3.refs_4_), channel_id=1, source_target_pairs={{0,4},{4,0},{8,12},{12,8},{16,20},{20,16},{24,28},{28,24},{1,5},{5... | collective-permute-start | bytes 392 | tf_op jit(solution)/shard_map/ppermute | solution.py:31
  10.1 1.2 %collective-permute-start.2 = (s32[1,32]{1,0:T(1,128)S(1)}, s32[1,32]{1,0:T(1,128)S(1)}, u32[]{:S(2)}, u32[]{:S(2)}) collective-permute-start(s32[1,32]{1,0:T(1,128)S(1)} %collective-permute-done.1.refs_2_), channel_id=1, source_target_pairs={{0,4},{4,0},{8,12},{12,8},{16,20},{20,16},{24,28},{28,24},{1,5},{5... | collective-permute-start | bytes 392 | tf_op jit(solution)/shard_map/ppermute | solution.py:31
  11.4 32.7 %copy-start.1 = (bf16[2048,128]{1,0:T(8,128)(2,1)S(1)}, bf16[2048,128]{1,0:T(8,128)(2,1)}, u32[]{:S(2)}) copy-start(bf16[2048,128]{1,0:T(8,128)(2,1)} %cov_ref.3) | copy-start | bytes 1572868
  11.4 32.7 %copy-start.3 = (f32[512]{0:T(512)S(1)}, f32[512]{0:T(512)}, u32[]{:S(2)}) copy-start(f32[512]{0:T(512)} %param.10) | copy-start | bytes 6148
  13.0 1.6 %collective-permute-start.7 = (bf16[256,512]{1,0:T(8,128)(2,1)S(1)}, bf16[256,512]{1,0:T(8,128)(2,1)S(1)}, u32[]{:S(2)}, u32[]{:S(2)}) collective-permute-start(bf16[256,512]{1,0:T(8,128)(2,1)S(1)} %get-tuple-element.17), channel_id=1, source_target_pairs={{0,4},{4,0},{8,12},{12,8},{16,20},{20,16},{24,28},{28,24},{1,5},{5... | collective-permute-start | bytes 786440 | tf_op jit(solution)/shard_map/ppermute | solution.py:31
  15.2 4.5 %collective-permute-start.8 = (bf16[64,512]{1,0:T(8,128)(2,1)S(1)}, bf16[64,512]{1,0:T(8,128)(2,1)S(1)}, u32[]{:S(2)}, u32[]{:S(2)}) collective-permute-start(bf16[64,512]{1,0:T(8,128)(2,1)S(1)} %get-tuple-element.19), channel_id=1, source_target_pairs={{0,8},{4,12},{8,0},{12,4},{16,24},{20,28},{24,16},{28,20},{1,9},{5... | collective-permute-start | bytes 196616 | tf_op jit(solution)/shard_map/ppermute | solution.py:31
  17.2 4.3 %collective-permute-start.9 = (bf16[64,512]{1,0:T(8,128)(2,1)S(1)}, bf16[64,512]{1,0:T(8,128)(2,1)S(1)}, u32[]{:S(2)}, u32[]{:S(2)}) collective-permute-start(bf16[64,512]{1,0:T(8,128)(2,1)S(1)} %get-tuple-element.20), channel_id=1, source_target_pairs={{0,16},{4,20},{8,24},{12,28},{16,0},{20,4},{24,8},{28,12},{1,17},{... | collective-permute-start | bytes 196616 | tf_op jit(solution)/shard_map/ppermute | solution.py:31
  18.7 5.2 %collective-permute-start.10 = (bf16[64,512]{1,0:T(8,128)(2,1)S(1)}, bf16[64,512]{1,0:T(8,128)(2,1)S(1)}, u32[]{:S(2)}, u32[]{:S(2)}) collective-permute-start(bf16[64,512]{1,0:T(8,128)(2,1)S(1)} %get-tuple-element.21), channel_id=1, source_target_pairs={{0,24},{4,28},{8,16},{12,20},{16,8},{20,12},{24,0},{28,4},{1,25},{... | collective-permute-start | bytes 196616 | tf_op jit(solution)/shard_map/ppermute | solution.py:31
  24.5 6.1 %collective-permute-start.13 = (bf16[64,512]{1,0:T(8,128)(2,1)S(1)}, bf16[64,512]{1,0:T(8,128)(2,1)S(1)}, u32[]{:S(2)}, u32[]{:S(2)}) collective-permute-start(bf16[64,512]{1,0:T(8,128)(2,1)S(1)} %mix.1.refs_0_), channel_id=1, source_target_pairs={{0,3},{1,2},{2,1},{3,0},{4,7},{5,6},{6,5},{7,4},{8,11},{9,10},{10,... | collective-permute-start | bytes 196616 | tf_op jit(solution)/shard_map/ppermute | solution.py:31
  28.1 5.2 %collective-permute-start.12 = (bf16[64,512]{1,0:T(8,128)(2,1)S(1)}, bf16[64,512]{1,0:T(8,128)(2,1)S(1)}, u32[]{:S(2)}, u32[]{:S(2)}) collective-permute-start(bf16[64,512]{1,0:T(8,128)(2,1)S(1)} %mix.1.refs_0_), channel_id=1, source_target_pairs={{0,2},{1,3},{2,0},{3,1},{4,6},{5,7},{6,4},{7,5},{8,10},{9,11},{10,... | collective-permute-start | bytes 196616 | tf_op jit(solution)/shard_map/ppermute | solution.py:31
  28.1 5.2 %collective-permute-start.11 = (bf16[64,512]{1,0:T(8,128)(2,1)S(1)}, bf16[64,512]{1,0:T(8,128)(2,1)S(1)}, u32[]{:S(2)}, u32[]{:S(2)}) collective-permute-start(bf16[64,512]{1,0:T(8,128)(2,1)S(1)} %mix.1.refs_0_), channel_id=1, source_target_pairs={{0,1},{1,0},{2,3},{3,2},{4,5},{5,4},{6,7},{7,6},{8,9},{9,8},{10,11... | collective-permute-start | bytes 196616 | tf_op jit(solution)/shard_map/ppermute | solution.py:31
  33.9 7.5 %collective-permute-start.16 = (bf16[160,512]{1,0:T(8,128)(2,1)S(1)}, bf16[160,512]{1,0:T(8,128)(2,1)S(1)}, u32[]{:S(2)}, u32[]{:S(2)}) collective-permute-start(bf16[160,512]{1,0:T(8,128)(2,1)S(1)} %stack.13.refs_0_), channel_id=1, source_target_pairs={{0,24},{4,28},{8,16},{12,20},{16,8},{20,12},{24,0},{28,4},{1,25},{... | collective-permute-start | bytes 491528 | tf_op jit(solution)/shard_map/ppermute | solution.py:31
  34.5 8.0 %collective-permute-start.15 = (bf16[160,512]{1,0:T(8,128)(2,1)S(1)}, bf16[160,512]{1,0:T(8,128)(2,1)S(1)}, u32[]{:S(2)}, u32[]{:S(2)}) collective-permute-start(bf16[160,512]{1,0:T(8,128)(2,1)S(1)} %stack.13.refs_0_), channel_id=1, source_target_pairs={{0,16},{4,20},{8,24},{12,28},{16,0},{20,4},{24,8},{28,12},{1,17},{... | collective-permute-start | bytes 491528 | tf_op jit(solution)/shard_map/ppermute | solution.py:31
  35.9 6.5 %collective-permute-start.14 = (bf16[160,512]{1,0:T(8,128)(2,1)S(1)}, bf16[160,512]{1,0:T(8,128)(2,1)S(1)}, u32[]{:S(2)}, u32[]{:S(2)}) collective-permute-start(bf16[160,512]{1,0:T(8,128)(2,1)S(1)} %stack.13.refs_0_), channel_id=1, source_target_pairs={{0,8},{4,12},{8,0},{12,4},{16,24},{20,28},{24,16},{28,20},{1,9},{5... | collective-permute-start | bytes 491528 | tf_op jit(solution)/shard_map/ppermute | solution.py:31
  37.4 6.6 %collective-permute-start.17 = (bf16[160,512]{1,0:T(8,128)(2,1)S(1)}, bf16[160,512]{1,0:T(8,128)(2,1)S(1)}, u32[]{:S(2)}, u32[]{:S(2)}) collective-permute-start(bf16[160,512]{1,0:T(8,128)(2,1)S(1)} %stack.13.refs_0_), channel_id=1, source_target_pairs={{0,4},{4,0},{8,12},{12,8},{16,20},{20,16},{24,28},{28,24},{1,5},{5... | collective-permute-start | bytes 491528 | tf_op jit(solution)/shard_map/ppermute | solution.py:31
  41.3 2.7 %collective-permute-start.20 = (bf16[160,512]{1,0:T(8,128)(2,1)S(1)}, bf16[160,512]{1,0:T(8,128)(2,1)S(1)}, u32[]{:S(2)}, u32[]{:S(2)}) collective-permute-start(bf16[160,512]{1,0:T(8,128)(2,1)S(1)} %collective-permute-done.16.refs_3_), channel_id=1, source_target_pairs={{0,4},{4,0},{8,12},{12,8},{16,20},{20,16},{24,28},{28,24},{1,5},{5... | collective-permute-start | bytes 491528 | tf_op jit(solution)/shard_map/ppermute | solution.py:31
  42.5 1.6 %collective-permute-start.19 = (bf16[160,512]{1,0:T(8,128)(2,1)S(1)}, bf16[160,512]{1,0:T(8,128)(2,1)S(1)}, u32[]{:S(2)}, u32[]{:S(2)}) collective-permute-start(bf16[160,512]{1,0:T(8,128)(2,1)S(1)} %collective-permute-done.15.refs_2_), channel_id=1, source_target_pairs={{0,4},{4,0},{8,12},{12,8},{16,20},{20,16},{24,28},{28,24},{1,5},{5... | collective-permute-start | bytes 491528 | tf_op jit(solution)/shard_map/ppermute | solution.py:31
  42.5 1.6 %collective-permute-start.18 = (bf16[160,512]{1,0:T(8,128)(2,1)S(1)}, bf16[160,512]{1,0:T(8,128)(2,1)S(1)}, u32[]{:S(2)}, u32[]{:S(2)}) collective-permute-start(bf16[160,512]{1,0:T(8,128)(2,1)S(1)} %collective-permute-done.14.refs_1_), channel_id=1, source_target_pairs={{0,4},{4,0},{8,12},{12,8},{16,20},{20,16},{24,28},{28,24},{1,5},{5... | collective-permute-start | bytes 491528 | tf_op jit(solution)/shard_map/ppermute | solution.py:31

commit v18 on v17

--- a/solution.py
+++ b/solution.py
@@ -411,7 +411,6 @@
             steps[j] = parts_of(line, RIGHT, 0)
             if j > b:
                 factor_ref[here, spans[j]] = line * (diagonals[j] * units[j] * ratio)
-                inverse_ref[here, spans[j]] = jnp.zeros((LANE, LANE), f32)
             else:
                 factor_ref[here, spans[j]] = jnp.zeros((LANE, LANE), f32)
                 inverse_ref[here, spans[j]] = line * units[j]
@@ -449,13 +448,24 @@
     for call_it in aside:
         call_it()
 
-    inverse = inverse_ref[...]
-    steer = jnp.sum(inverse * jnp.concatenate(gradient, axis=1), axis=1, keepdims=True)
+    def forward(row):
+        sums = []
+        for span in spans:
+            sums.append(jnp.sum(inverse_ref[span, : span.stop] * row[:, : span.stop], axis=1, keepdims=True))
+        return jnp.concatenate(sums)
+
+    def backward(column):
+        sums = []
+        for span in spans:
+            sums.append(jnp.sum(inverse_ref[span.start :, span] * column[span.start :], axis=0, keepdims=True))
+        return jnp.concatenate(sums, axis=1)
+
+    steer = forward(jnp.concatenate(gradient, axis=1))
     direction = steer
     gamma = jnp.sum(steer * steer, axis=0, keepdims=True)
     solved = jnp.zeros((1, cov_ref.shape[1] * LEVELS), f32)
     for step in range(ITERS):
-        move = jnp.sum(inverse * direction, axis=0, keepdims=True)
+        move = backward(direction)
         image = []
         for span in spans:
             image.append(jnp.sum(normal[span, :] * to_column(move[:, span], same), axis=0, keepdims=True))
@@ -464,7 +474,7 @@
         solved = solved + alpha * move
         if step == ITERS - 1:
             break
-        steer = steer - alpha * jnp.sum(inverse * image, axis=1, keepdims=True)
+        steer = steer - alpha * forward(image)
         gamma_new = jnp.sum(steer * steer, axis=0, keepdims=True)
         direction = steer + gamma_new / gamma * direction
         gamma = gamma_new

time: 62.3 us -> 62.6 us (level)
  no operation moved by 1% of the time
where the time goes in v18:
time: 62.6 us; the launch traced here: 62.3 us
  Pallas kernels  23.5 us (38%)
  starting transfers between devices  18.1 us (29%)
  waiting for transfers between devices  16.6 us (27%)
  local copies, waits for them, and re-layouts  1.74 us (3%)
  other arithmetic  1.48 us (2%)
  between operations  0.88 us (1%)
    ppermute x21, starting transfers between devices, partner(): return lax.ppermute(value, axis, pairs)  18.1 us
    pallas_call x1, Pallas kernels, body(): pl.pallas_call(functools.partial(solve_kernel, math.sqrt(LEVELS / SKETCH)...  18 us
    ppermute x21, waiting for transfers between devices, partner(): return lax.ppermute(value, axis, pairs)  16.6 us
    pallas_call x6, Pallas kernels, call(): pl.pallas_call(kernel, out_shape=[jax.ShapeDtypeStruct(shape, dtype) for...  5.46 us
    unnamed x8, local copies, waits for them, and re-layouts  1.74 us
  transfers between devices with their start and end apart: 21, of which 11 were waited for; matrix products, arithmetic and copies ran while one was open for 2% of the time, Pallas kernels for 3%

profile of v18, /device:TPU:0, one launch (start us, length us, event | category | flops | bytes accessed | tf_op | source)
XLA Modules:
  0.0 62.3 jit_solution(17730408284816970186)
XLA Ops:
  0.6 4.0 %collective-permute-start.5 = (s32[1,32]{1,0:T(1,128)}, s32[1,32]{1,0:T(1,128)S(1)}, u32[]{:S(2)}, u32[]{:S(2)}) collective-permute-start(s32[1,32]{1,0:T(1,128)} %bitcast.16), channel_id=1, source_target_pairs={{0,24},{4,28},{8,16},{12,20},{16,8},{20,12},{24,0},{28,4},{1,25},{... | collective-permute-start | bytes 392 | tf_op jit(solution)/shard_map/ppermute | solution.py:31
  4.6 0.5 collective-permute-start.3
  5.1 0.1 collective-permute-start.1
  5.2 0.0 collective-permute-start
  5.2 0.7 %maximum_bitcast_fusion.refs_0_ = s32[1,32]{1,0:T(1,128)S(1)} fusion(s32[32]{0:T(128)} %param.9), kind=kLoop, calls=%fused_computation.2 | loop fusion | flops 32 | bytes 256 | tf_op jit(solution)/shard_map/max | solution.py:524
  5.9 0.1 pad_add_fusion.index_ref
  6.0 0.7 %add_bitcast_fusion.marks_ref = s32[16,128]{1,0:T(8,128)S(1)} fusion(s32[2048]{0:T(1024)} %param.7, s32[2048]{0:T(1024)} %param.8), kind=kLoop, calls=%fused_computation | loop fusion | flops 4096 | bytes 24576 | tf_op jit(solution)/shard_map/reshape | solution.py:517
  6.7 0.0 copy-start
  6.7 1.0 %copy-done = bf16[2048,128]{1,0:T(8,128)(2,1)S(1)} copy-done((bf16[2048,128]{1,0:T(8,128)(2,1)S(1)}, bf16[2048,128]{1,0:T(8,128)(2,1)}, u32[]{:S(2)}) %copy-start) | copy-done | bytes 524312
  7.8 0.0 copy-start.2
  7.8 0.7 %copy-done.2 = f32[2048]{0:T(1024)S(1)} copy-done((f32[2048]{0:T(1024)S(1)}, f32[2048]{0:T(1024)}, u32[]{:S(2)}) %copy-start.2) | copy-done | bytes 8216
  8.5 1.0 %design.1 = (bf16[560,2048]{1,0:T(8,128)(2,1)S(1)}, f32[264,128]{1,0:T(8,128)S(1)}) custom-call(bf16[2048,128]{1,0:T(8,128)(2,1)S(1)} %copy-done, s32[16,128]{1,0:T(8,128)S(1)} %add_bitcast_fusion.marks_ref, f32[16,128]{1,0:T(8,128)S(1)} %bitcast.11), custom_call_target="tpu_custom_call" | custom-call | tf_op jit(solution)/shard_map/design/pallas_call | solution.py:499
  9.5 0.0 collective-permute-done.5.refs_6_
  9.5 0.5 collective-permute-start.6
  10.0 0.0 collective-permute-done.3.refs_4_
  10.0 0.1 collective-permute-start.4
  10.1 0.0 collective-permute-done.1.refs_2_
  10.1 0.4 collective-permute-start.2
  10.5 0.0 collective-permute-done.refs_1_
  10.5 0.3 collective-permute-done.6.refs_7_
  10.8 0.3 collective-permute-done.4.refs_5_
  11.1 0.2 collective-permute-done.2.refs_3_
  11.4 0.0 copy-start.1
  11.4 0.0 copy-start.3
  11.4 1.6 %local.1 = (bf16[256,512]{1,0:T(8,128)(2,1)S(1)}, bf16[256,512]{1,0:T(8,128)(2,1)S(1)}) custom-call(s32[2]{0:T(128)S(1)} %pad_add_fusion.index_ref, bf16[560,2048]{1,0:T(8,128)(2,1)S(1)} %get-tuple-element.14.design_ref, f32[264,128]{1,0:T(8,128)S(1)} %get-tuple-element.15.packed_ref, s32[16,128]{1,0:T(8,128)S(1)} %add_bitcast_fusion.marks_ref, ...), custom_call_target="tpu_custom_call" | custom-call | tf_op jit(solution)/shard_map/local/pallas_call | solution.py:499
  13.0 0.4 collective-permute-start.7
  13.3 1.2 %collective-permute-done.7.came_ref = bf16[256,512]{1,0:T(8,128)(2,1)S(1)} collective-permute-done((bf16[256,512]{1,0:T(8,128)(2,1)S(1)}, bf16[256,512]{1,0:T(8,128)(2,1)S(1)}, u32[]{:S(2)}, u32[]{:S(2)}) %collective-permute-start.7) | collective-permute-done | bytes 262176 | tf_op jit(solution)/shard_map/ppermute | solution.py:31
  14.6 0.7 %pair.1 = (bf16[64,512]{1,0:T(8,128)(2,1)S(1)}, bf16[64,512]{1,0:T(8,128)(2,1)S(1)}, bf16[64,512]{1,0:T(8,128)(2,1)S(1)}, bf16[64,512]{1,0:T(8,128)(2,1)S(1)}) custom-call(s32[2]{0:T(128)S(1)} %pad_add_fusion.index_ref, bf16[256,512]{1,0:T(8,128)(2,1)S(1)} %get-tuple-element.16.stay_ref, bf16[256,512]{1,0:T(8,128)(2,1)S(1)} %collective-permute-done.7.came_ref), custom_call_target="tpu_custom_call" | custom-call | tf_op jit(solution)/shard_map/pair/pallas_call | solution.py:499
  15.2 2.0 %collective-permute-start.8 = (bf16[64,512]{1,0:T(8,128)(2,1)S(1)}, bf16[64,512]{1,0:T(8,128)(2,1)S(1)}, u32[]{:S(2)}, u32[]{:S(2)}) collective-permute-start(bf16[64,512]{1,0:T(8,128)(2,1)S(1)} %get-tuple-element.19), channel_id=1, source_target_pairs={{0,8},{4,12},{8,0},{12,4},{16,24},{20,28},{24,16},{28,20},{1,9},{5... | collective-permute-start | bytes 196616 | tf_op jit(solution)/shard_map/ppermute | solution.py:31
  17.2 1.5 %collective-permute-start.9 = (bf16[64,512]{1,0:T(8,128)(2,1)S(1)}, bf16[64,512]{1,0:T(8,128)(2,1)S(1)}, u32[]{:S(2)}, u32[]{:S(2)}) collective-permute-start(bf16[64,512]{1,0:T(8,128)(2,1)S(1)} %get-tuple-element.20), channel_id=1, source_target_pairs={{0,16},{4,20},{8,24},{12,28},{16,0},{20,4},{24,8},{28,12},{1,17},{... | collective-permute-start | bytes 196616 | tf_op jit(solution)/shard_map/ppermute | solution.py:31
  18.7 0.1 collective-permute-start.10
  18.8 1.0 %collective-permute-done.8.refs_1_ = bf16[64,512]{1,0:T(8,128)(2,1)S(1)} collective-permute-done((bf16[64,512]{1,0:T(8,128)(2,1)S(1)}, bf16[64,512]{1,0:T(8,128)(2,1)S(1)}, u32[]{:S(2)}, u32[]{:S(2)}) %collective-permute-start.8) | collective-permute-done | bytes 65568 | tf_op jit(solution)/shard_map/ppermute | solution.py:31
  19.7 1.7 %collective-permute-done.9.refs_2_ = bf16[64,512]{1,0:T(8,128)(2,1)S(1)} collective-permute-done((bf16[64,512]{1,0:T(8,128)(2,1)S(1)}, bf16[64,512]{1,0:T(8,128)(2,1)S(1)}, u32[]{:S(2)}, u32[]{:S(2)}) %collective-permute-start.9) | collective-permute-done | bytes 65568 | tf_op jit(solution)/shard_map/ppermute | solution.py:31
  21.4 2.4 %collective-permute-done.10.refs_3_ = bf16[64,512]{1,0:T(8,128)(2,1)S(1)} collective-permute-done((bf16[64,512]{1,0:T(8,128)(2,1)S(1)}, bf16[64,512]{1,0:T(8,128)(2,1)S(1)}, u32[]{:S(2)}, u32[]{:S(2)}) %collective-permute-start.10) | collective-permute-done | bytes 65568 | tf_op jit(solution)/shard_map/ppermute | solution.py:31
  23.8 0.6 mix.1.refs_0_
  24.5 3.7 %collective-permute-start.13 = (bf16[64,512]{1,0:T(8,128)(2,1)S(1)}, bf16[64,512]{1,0:T(8,128)(2,1)S(1)}, u32[]{:S(2)}, u32[]{:S(2)}) collective-permute-start(bf16[64,512]{1,0:T(8,128)(2,1)S(1)} %mix.1.refs_0_), channel_id=1, source_target_pairs={{0,3},{1,2},{2,1},{3,0},{4,7},{5,6},{6,5},{7,4},{8,11},{9,10},{10,... | collective-permute-start | bytes 196616 | tf_op jit(solution)/shard_map/ppermute | solution.py:31
  28.1 0.0 collective-permute-start.12
  28.1 0.8 %collective-permute-start.11 = (bf16[64,512]{1,0:T(8,128)(2,1)S(1)}, bf16[64,512]{1,0:T(8,128)(2,1)S(1)}, u32[]{:S(2)}, u32[]{:S(2)}) collective-permute-start(bf16[64,512]{1,0:T(8,128)(2,1)S(1)} %mix.1.refs_0_), channel_id=1, source_target_pairs={{0,1},{1,0},{2,3},{3,2},{4,5},{5,4},{6,7},{7,6},{8,9},{9,8},{10,11... | collective-permute-start | bytes 196616 | tf_op jit(solution)/shard_map/ppermute | solution.py:31
  28.9 1.7 %collective-permute-done.13.refs_3_ = bf16[64,512]{1,0:T(8,128)(2,1)S(1)} collective-permute-done((bf16[64,512]{1,0:T(8,128)(2,1)S(1)}, bf16[64,512]{1,0:T(8,128)(2,1)S(1)}, u32[]{:S(2)}, u32[]{:S(2)}) %collective-permute-start.13) | collective-permute-done | bytes 65568 | tf_op jit(solution)/shard_map/ppermute | solution.py:31
  30.6 2.7 %collective-permute-done.12.refs_2_ = bf16[64,512]{1,0:T(8,128)(2,1)S(1)} collective-permute-done((bf16[64,512]{1,0:T(8,128)(2,1)S(1)}, bf16[64,512]{1,0:T(8,128)(2,1)S(1)}, u32[]{:S(2)}, u32[]{:S(2)}) %collective-permute-start.12) | collective-permute-done | bytes 65568 | tf_op jit(solution)/shard_map/ppermute | solution.py:31
  33.3 0.0 collective-permute-done.11.refs_1_
  33.3 0.6 stack.13.refs_0_
  33.9 0.6 collective-permute-start.16
  34.5 1.5 %collective-permute-start.15 = (bf16[160,512]{1,0:T(8,128)(2,1)S(1)}, bf16[160,512]{1,0:T(8,128)(2,1)S(1)}, u32[]{:S(2)}, u32[]{:S(2)}) collective-permute-start(bf16[160,512]{1,0:T(8,128)(2,1)S(1)} %stack.13.refs_0_), channel_id=1, source_target_pairs={{0,16},{4,20},{8,24},{12,28},{16,0},{20,4},{24,8},{28,12},{1,17},{... | collective-permute-start | bytes 491528 | tf_op jit(solution)/shard_map/ppermute | solution.py:31
  35.9 1.5 %collective-permute-start.14 = (bf16[160,512]{1,0:T(8,128)(2,1)S(1)}, bf16[160,512]{1,0:T(8,128)(2,1)S(1)}, u32[]{:S(2)}, u32[]{:S(2)}) collective-permute-start(bf16[160,512]{1,0:T(8,128)(2,1)S(1)} %stack.13.refs_0_), channel_id=1, source_target_pairs={{0,8},{4,12},{8,0},{12,4},{16,24},{20,28},{24,16},{28,20},{1,9},{5... | collective-permute-start | bytes 491528 | tf_op jit(solution)/shard_map/ppermute | solution.py:31
  37.4 0.0 collective-permute-start.17
  37.4 3.9 %collective-permute-done.16.refs_3_ = bf16[160,512]{1,0:T(8,128)(2,1)S(1)} collective-permute-done((bf16[160,512]{1,0:T(8,128)(2,1)S(1)}, bf16[160,512]{1,0:T(8,128)(2,1)S(1)}, u32[]{:S(2)}, u32[]{:S(2)}) %collective-permute-start.16) | collective-permute-done | bytes 163872 | tf_op jit(solution)/shard_map/ppermute | solution.py:31
  41.3 0.0 collective-permute-start.20
  41.3 1.1 %collective-permute-done.15.refs_2_ = bf16[160,512]{1,0:T(8,128)(2,1)S(1)} collective-permute-done((bf16[160,512]{1,0:T(8,128)(2,1)S(1)}, bf16[160,512]{1,0:T(8,128)(2,1)S(1)}, u32[]{:S(2)}, u32[]{:S(2)}) %collective-permute-start.15) | collective-permute-done | bytes 163872 | tf_op jit(solution)/shard_map/ppermute | solution.py:31
  42.5 0.0 collective-permute-start.19
  42.5 0.0 collective-permute-done.14.refs_1_
  42.5 0.5 collective-permute-start.18
  43.0 1.0 %gram.1.gram_ref = f32[512,512]{1,0:T(8,128)S(1)} custom-call(s32[2]{0:T(128)S(1)} %pad_add_fusion.index_ref, bf16[160,512]{1,0:T(8,128)(2,1)S(1)} %stack.13.refs_0_, bf16[160,512]{1,0:T(8,128)(2,1)S(1)} %collective-permute-done.14.refs_1_, bf16[160,512]{1,0:T(8,128)(2,1)S(1)} %collective-permute-done.15.refs_2_, ...), custom_call_target="tpu_custom_call" | custom-call | tf_op jit(solution)/shard_map/gram/pallas_call | solution.py:499
  44.0 0.0 collective-permute-done.17.refs_4_
  44.0 0.0 collective-permute-done.20.refs_7_
  44.1 0.0 collective-permute-done.19.refs_6_
  44.1 0.0 collective-permute-done.18.refs_5_
  44.1 0.0 copy-done.1
  44.1 0.0 copy-done.3
  44.1 18.0 %solve.1 = (f32[512,512]{1,0:T(8,128)}, f32[4,128]{1,0:T(4,128)}, f32[16,128]{1,0:T(8,128)}) custom-call(s32[2]{0:T(128)S(1)} %pad_add_fusion.index_ref, f32[512,512]{1,0:T(8,128)S(1)} %gram.1.gram_ref, f32[4,128]{1,0:T(4,128)S(1)} %bitcast.13, bf16[2048,128]{1,0:T(8,128)(2,1)S(1)} %copy-done.1, s32[16,128]{1,0:T(8,128)S(1)} %add_bitcast_fusion.marks_ref, ...), custom_call_target="tpu_custom_call" | custom-call | tf_op jit(solution)/shard_map/solve/pallas_call | solution.py:581
Async XLA Ops:
  0.6 8.8 %collective-permute-start.5 = (s32[1,32]{1,0:T(1,128)}, s32[1,32]{1,0:T(1,128)S(1)}, u32[]{:S(2)}, u32[]{:S(2)}) collective-permute-start(s32[1,32]{1,0:T(1,128)} %bitcast.16), channel_id=1, source_target_pairs={{0,24},{4,28},{8,16},{12,20},{16,8},{20,12},{24,0},{28,4},{1,25},{... | collective-permute-start | bytes 392 | tf_op jit(solution)/shard_map/ppermute | solution.py:31
  4.6 5.4 %collective-permute-start.3 = (s32[1,32]{1,0:T(1,128)}, s32[1,32]{1,0:T(1,128)S(1)}, u32[]{:S(2)}, u32[]{:S(2)}) collective-permute-start(s32[1,32]{1,0:T(1,128)} %bitcast.17), channel_id=1, source_target_pairs={{0,16},{4,20},{8,24},{12,28},{16,0},{20,4},{24,8},{28,12},{1,17},{... | collective-permute-start | bytes 392 | tf_op jit(solution)/shard_map/ppermute | solution.py:31
  5.1 5.0 %collective-permute-start.1 = (s32[1,32]{1,0:T(1,128)}, s32[1,32]{1,0:T(1,128)S(1)}, u32[]{:S(2)}, u32[]{:S(2)}) collective-permute-start(s32[1,32]{1,0:T(1,128)} %bitcast.18), channel_id=1, source_target_pairs={{0,8},{4,12},{8,0},{12,4},{16,24},{20,28},{24,16},{28,20},{1,9},{5... | collective-permute-start | bytes 392 | tf_op jit(solution)/shard_map/ppermute | solution.py:31
  5.2 5.3 %collective-permute-start = (s32[1,32]{1,0:T(1,128)}, s32[1,32]{1,0:T(1,128)S(1)}, u32[]{:S(2)}, u32[]{:S(2)}) collective-permute-start(s32[1,32]{1,0:T(1,128)} %bitcast.19), channel_id=1, source_target_pairs={{0,4},{4,0},{8,12},{12,8},{16,20},{20,16},{24,28},{28,24},{1,5},{5... | collective-permute-start | bytes 392 | tf_op jit(solution)/shard_map/ppermute | solution.py:31
  6.7 1.0 %copy-start = (bf16[2048,128]{1,0:T(8,128)(2,1)S(1)}, bf16[2048,128]{1,0:T(8,128)(2,1)}, u32[]{:S(2)}) copy-start(bf16[2048,128]{1,0:T(8,128)(2,1)} %cov_ref.3) | copy-start | bytes 1572868
  7.8 0.7 %copy-start.2 = (f32[2048]{0:T(1024)S(1)}, f32[2048]{0:T(1024)}, u32[]{:S(2)}) copy-start(f32[2048]{0:T(1024)} %param.11) | copy-start | bytes 24580
  9.5 1.4 %collective-permute-start.6 = (s32[1,32]{1,0:T(1,128)S(1)}, s32[1,32]{1,0:T(1,128)S(1)}, u32[]{:S(2)}, u32[]{:S(2)}) collective-permute-start(s32[1,32]{1,0:T(1,128)S(1)} %collective-permute-done.5.refs_6_), channel_id=1, source_target_pairs={{0,4},{4,0},{8,12},{12,8},{16,20},{20,16},{24,28},{28,24},{1,5},{5... | collective-permute-start | bytes 392 | tf_op jit(solution)/shard_map/ppermute | solution.py:31
  10.0 1.1 %collective-permute-start.4 = (s32[1,32]{1,0:T(1,128)S(1)}, s32[1,32]{1,0:T(1,128)S(1)}, u32[]{:S(2)}, u32[]{:S(2)}) collective-permute-start(s32[1,32]{1,0:T(1,128)S(1)} %collective-permute-done.3.refs_4_), channel_id=1, source_target_pairs={{0,4},{4,0},{8,12},{12,8},{16,20},{20,16},{24,28},{28,24},{1,5},{5... | collective-permute-start | bytes 392 | tf_op jit(solution)/shard_map/ppermute | solution.py:31
  10.1 1.2 %collective-permute-start.2 = (s32[1,32]{1,0:T(1,128)S(1)}, s32[1,32]{1,0:T(1,128)S(1)}, u32[]{:S(2)}, u32[]{:S(2)}) collective-permute-start(s32[1,32]{1,0:T(1,128)S(1)} %collective-permute-done.1.refs_2_), channel_id=1, source_target_pairs={{0,4},{4,0},{8,12},{12,8},{16,20},{20,16},{24,28},{28,24},{1,5},{5... | collective-permute-start | bytes 392 | tf_op jit(solution)/shard_map/ppermute | solution.py:31
  11.4 32.7 %copy-start.1 = (bf16[2048,128]{1,0:T(8,128)(2,1)S(1)}, bf16[2048,128]{1,0:T(8,128)(2,1)}, u32[]{:S(2)}) copy-start(bf16[2048,128]{1,0:T(8,128)(2,1)} %cov_ref.3) | copy-start | bytes 1572868
  11.4 32.7 %copy-start.3 = (f32[512]{0:T(512)S(1)}, f32[512]{0:T(512)}, u32[]{:S(2)}) copy-start(f32[512]{0:T(512)} %param.10) | copy-start | bytes 6148
  13.0 1.6 %collective-permute-start.7 = (bf16[256,512]{1,0:T(8,128)(2,1)S(1)}, bf16[256,512]{1,0:T(8,128)(2,1)S(1)}, u32[]{:S(2)}, u32[]{:S(2)}) collective-permute-start(bf16[256,512]{1,0:T(8,128)(2,1)S(1)} %get-tuple-element.17), channel_id=1, source_target_pairs={{0,4},{4,0},{8,12},{12,8},{16,20},{20,16},{24,28},{28,24},{1,5},{5... | collective-permute-start | bytes 786440 | tf_op jit(solution)/shard_map/ppermute | solution.py:31
  15.2 4.5 %collective-permute-start.8 = (bf16[64,512]{1,0:T(8,128)(2,1)S(1)}, bf16[64,512]{1,0:T(8,128)(2,1)S(1)}, u32[]{:S(2)}, u32[]{:S(2)}) collective-permute-start(bf16[64,512]{1,0:T(8,128)(2,1)S(1)} %get-tuple-element.19), channel_id=1, source_target_pairs={{0,8},{4,12},{8,0},{12,4},{16,24},{20,28},{24,16},{28,20},{1,9},{5... | collective-permute-start | bytes 196616 | tf_op jit(solution)/shard_map/ppermute | solution.py:31
  17.2 4.3 %collective-permute-start.9 = (bf16[64,512]{1,0:T(8,128)(2,1)S(1)}, bf16[64,512]{1,0:T(8,128)(2,1)S(1)}, u32[]{:S(2)}, u32[]{:S(2)}) collective-permute-start(bf16[64,512]{1,0:T(8,128)(2,1)S(1)} %get-tuple-element.20), channel_id=1, source_target_pairs={{0,16},{4,20},{8,24},{12,28},{16,0},{20,4},{24,8},{28,12},{1,17},{... | collective-permute-start | bytes 196616 | tf_op jit(solution)/shard_map/ppermute | solution.py:31
  18.7 5.2 %collective-permute-start.10 = (bf16[64,512]{1,0:T(8,128)(2,1)S(1)}, bf16[64,512]{1,0:T(8,128)(2,1)S(1)}, u32[]{:S(2)}, u32[]{:S(2)}) collective-permute-start(bf16[64,512]{1,0:T(8,128)(2,1)S(1)} %get-tuple-element.21), channel_id=1, source_target_pairs={{0,24},{4,28},{8,16},{12,20},{16,8},{20,12},{24,0},{28,4},{1,25},{... | collective-permute-start | bytes 196616 | tf_op jit(solution)/shard_map/ppermute | solution.py:31
  24.5 6.1 %collective-permute-start.13 = (bf16[64,512]{1,0:T(8,128)(2,1)S(1)}, bf16[64,512]{1,0:T(8,128)(2,1)S(1)}, u32[]{:S(2)}, u32[]{:S(2)}) collective-permute-start(bf16[64,512]{1,0:T(8,128)(2,1)S(1)} %mix.1.refs_0_), channel_id=1, source_target_pairs={{0,3},{1,2},{2,1},{3,0},{4,7},{5,6},{6,5},{7,4},{8,11},{9,10},{10,... | collective-permute-start | bytes 196616 | tf_op jit(solution)/shard_map/ppermute | solution.py:31
  28.1 5.2 %collective-permute-start.12 = (bf16[64,512]{1,0:T(8,128)(2,1)S(1)}, bf16[64,512]{1,0:T(8,128)(2,1)S(1)}, u32[]{:S(2)}, u32[]{:S(2)}) collective-permute-start(bf16[64,512]{1,0:T(8,128)(2,1)S(1)} %mix.1.refs_0_), channel_id=1, source_target_pairs={{0,2},{1,3},{2,0},{3,1},{4,6},{5,7},{6,4},{7,5},{8,10},{9,11},{10,... | collective-permute-start | bytes 196616 | tf_op jit(solution)/shard_map/ppermute | solution.py:31
  28.1 5.2 %collective-permute-start.11 = (bf16[64,512]{1,0:T(8,128)(2,1)S(1)}, bf16[64,512]{1,0:T(8,128)(2,1)S(1)}, u32[]{:S(2)}, u32[]{:S(2)}) collective-permute-start(bf16[64,512]{1,0:T(8,128)(2,1)S(1)} %mix.1.refs_0_), channel_id=1, source_target_pairs={{0,1},{1,0},{2,3},{3,2},{4,5},{5,4},{6,7},{7,6},{8,9},{9,8},{10,11... | collective-permute-start | bytes 196616 | tf_op jit(solution)/shard_map/ppermute | solution.py:31
  33.9 7.5 %collective-permute-start.16 = (bf16[160,512]{1,0:T(8,128)(2,1)S(1)}, bf16[160,512]{1,0:T(8,128)(2,1)S(1)}, u32[]{:S(2)}, u32[]{:S(2)}) collective-permute-start(bf16[160,512]{1,0:T(8,128)(2,1)S(1)} %stack.13.refs_0_), channel_id=1, source_target_pairs={{0,24},{4,28},{8,16},{12,20},{16,8},{20,12},{24,0},{28,4},{1,25},{... | collective-permute-start | bytes 491528 | tf_op jit(solution)/shard_map/ppermute | solution.py:31
  34.5 8.0 %collective-permute-start.15 = (bf16[160,512]{1,0:T(8,128)(2,1)S(1)}, bf16[160,512]{1,0:T(8,128)(2,1)S(1)}, u32[]{:S(2)}, u32[]{:S(2)}) collective-permute-start(bf16[160,512]{1,0:T(8,128)(2,1)S(1)} %stack.13.refs_0_), channel_id=1, source_target_pairs={{0,16},{4,20},{8,24},{12,28},{16,0},{20,4},{24,8},{28,12},{1,17},{... | collective-permute-start | bytes 491528 | tf_op jit(solution)/shard_map/ppermute | solution.py:31
  35.9 6.5 %collective-permute-start.14 = (bf16[160,512]{1,0:T(8,128)(2,1)S(1)}, bf16[160,512]{1,0:T(8,128)(2,1)S(1)}, u32[]{:S(2)}, u32[]{:S(2)}) collective-permute-start(bf16[160,512]{1,0:T(8,128)(2,1)S(1)} %stack.13.refs_0_), channel_id=1, source_target_pairs={{0,8},{4,12},{8,0},{12,4},{16,24},{20,28},{24,16},{28,20},{1,9},{5... | collective-permute-start | bytes 491528 | tf_op jit(solution)/shard_map/ppermute | solution.py:31
  37.4 6.6 %collective-permute-start.17 = (bf16[160,512]{1,0:T(8,128)(2,1)S(1)}, bf16[160,512]{1,0:T(8,128)(2,1)S(1)}, u32[]{:S(2)}, u32[]{:S(2)}) collective-permute-start(bf16[160,512]{1,0:T(8,128)(2,1)S(1)} %stack.13.refs_0_), channel_id=1, source_target_pairs={{0,4},{4,0},{8,12},{12,8},{16,20},{20,16},{24,28},{28,24},{1,5},{5... | collective-permute-start | bytes 491528 | tf_op jit(solution)/shard_map/ppermute | solution.py:31
  41.3 2.7 %collective-permute-start.20 = (bf16[160,512]{1,0:T(8,128)(2,1)S(1)}, bf16[160,512]{1,0:T(8,128)(2,1)S(1)}, u32[]{:S(2)}, u32[]{:S(2)}) collective-permute-start(bf16[160,512]{1,0:T(8,128)(2,1)S(1)} %collective-permute-done.16.refs_3_), channel_id=1, source_target_pairs={{0,4},{4,0},{8,12},{12,8},{16,20},{20,16},{24,28},{28,24},{1,5},{5... | collective-permute-start | bytes 491528 | tf_op jit(solution)/shard_map/ppermute | solution.py:31
  42.5 1.6 %collective-permute-start.19 = (bf16[160,512]{1,0:T(8,128)(2,1)S(1)}, bf16[160,512]{1,0:T(8,128)(2,1)S(1)}, u32[]{:S(2)}, u32[]{:S(2)}) collective-permute-start(bf16[160,512]{1,0:T(8,128)(2,1)S(1)} %collective-permute-done.15.refs_2_), channel_id=1, source_target_pairs={{0,4},{4,0},{8,12},{12,8},{16,20},{20,16},{24,28},{28,24},{1,5},{5... | collective-permute-start | bytes 491528 | tf_op jit(solution)/shard_map/ppermute | solution.py:31
  42.5 1.6 %collective-permute-start.18 = (bf16[160,512]{1,0:T(8,128)(2,1)S(1)}, bf16[160,512]{1,0:T(8,128)(2,1)S(1)}, u32[]{:S(2)}, u32[]{:S(2)}) collective-permute-start(bf16[160,512]{1,0:T(8,128)(2,1)S(1)} %collective-permute-done.14.refs_1_), channel_id=1, source_target_pairs={{0,4},{4,0},{8,12},{12,8},{16,20},{20,16},{24,28},{28,24},{1,5},{5... | collective-permute-start | bytes 491528 | tf_op jit(solution)/shard_map/ppermute | solution.py:31
